TPU v7x, 32 devices: a whole 2x2x4 slice. The times are simulated.
32 devices in a mesh: dp: 4 (over z), ctx: 8 (over y, x, core).
Axes of the slice: x: 2, y: 2, z: 4, core: 2. Of those that a mesh axis runs over, the one named last changes fastest.
Arguments:
- inputs: bfloat16 [4, 1024, 2048], P('dp', 'ctx'), may hold values from -12 to 12
- cotangent: bfloat16 [4, 1024, 2048], P('dp', 'ctx'), may hold values from -6 to 6
- documents: int32 [4, 1024], P('dp'), may hold values from 0 to 4, as said below
- block_place: int32 [8], replicated, may hold values from 0 to 7, as said below
- params: float32 [2048, 32768], P(('dp', 'ctx'))
- first_moment: float32 [2048, 32768], P(('dp', 'ctx'))
- second_moment: float32 [2048, 32768], P(('dp', 'ctx')), as said below
- gains: float32 [4, 2048], replicated, as said below
- gains_first: float32 [4, 2048], replicated
- gains_second: float32 [4, 2048], replicated, as said below
Outputs:
- output: bfloat16 [4, 1024, 2048], P('dp', 'ctx')
- input_grad: bfloat16 [4, 1024, 2048], P('dp', 'ctx')
- grad_norm: float32 [], replicated
- new_params: float32 [2048, 32768], P(('dp', 'ctx'))
- new_first: float32 [2048, 32768], P(('dp', 'ctx'))
- new_second: float32 [2048, 32768], P(('dp', 'ctx'))
- new_gains: float32 [4, 2048], replicated
- new_gains_first: float32 [4, 2048], replicated
- new_gains_second: float32 [4, 2048], replicated
Inputs may be any that keep to these rules, and one draw needn't show every extreme that they name: A permutation: ctx index c holds sequence block block_place[c] of its row. `documents`: along sequence positions the ids never fall; in each row one document has tokens in every block. `second_moment`: positive. `gains`: positive. `gains_second`: positive.
All inputs are finite; a program needn't handle non-finite values.
Results may differ from a plain program's by a relative error of at most 0.015.
Values may be sent and summed in bfloat16 or wider, within the bound.
A program may use at most 1 GiB of HBM per device.

v0:
```python
import jax
import jax.numpy as jnp
from jax import lax
from jax.sharding import PartitionSpec as P

HD = 128
STEP = 10


EPS = 1e-06
THETA = 500000.0
CLIP = 1.0
BETA1 = 0.9
BETA2 = 0.95
RATE = 0.03
GAIN_RATE = 0.8
DECAY = 0.1
ADAM_EPS = 1e-08


def rms_scale(values):
    return lax.rsqrt(jnp.mean(values * values, axis=-1, keepdims=True) + EPS)


def norm_back(upstream, source, scale):
    return scale * (
        upstream - source * scale * scale * jnp.mean(upstream * source, axis=-1, keepdims=True)
    )


def rope_tables(positions, head_size):
    half_size = head_size // 2
    freqs = THETA ** (-jnp.arange(half_size, dtype=jnp.float32) * 2.0 / head_size)
    angles = positions.astype(jnp.float32)[:, None] * freqs[None, :]
    return (jnp.cos(angles), jnp.sin(angles))


def rotate(values, cos_tab, sine_tab):
    half_size = values.shape[-1] // 2
    first_half = values[..., :half_size]
    second_half = values[..., half_size:]
    cos_b = cos_tab[:, None, :]
    sine_b = sine_tab[:, None, :]
    return jnp.concatenate(
        [first_half * cos_b - second_half * sine_b, second_half * cos_b + first_half * sine_b],
        axis=-1,
    )


def split_weights(wide_bf, model_width):
    ff_width = (wide_bf.shape[1] - 4 * model_width) // 3
    w_qkv = wide_bf[:, : 3 * model_width]
    wo_t = wide_bf[:, 3 * model_width : 4 * model_width]
    w_gu = wide_bf[:, 4 * model_width : 4 * model_width + 2 * ff_width]
    wd_t = wide_bf[:, 4 * model_width + 2 * ff_width :]
    return (w_qkv, wo_t, w_gu, wd_t)


def adam_update(weight, first_in, second_in, clipped, rate, decay):
    new_first = BETA1 * first_in + (1.0 - BETA1) * clipped
    new_second = BETA2 * second_in + (1.0 - BETA2) * clipped * clipped
    first_hat = new_first / (1.0 - BETA1**STEP)
    second_hat = new_second / (1.0 - BETA2**STEP)
    new_weight = weight - rate * (first_hat / (jnp.sqrt(second_hat) + ADAM_EPS) + decay * weight)
    return (new_weight, new_first, new_second)


def score_terms(query_blk, key_blk, value_blk, lse_blk, delta_blk, dout_blk, visible):
    scores = jnp.einsum("qhd,khd->hqk", query_blk, key_blk, preferred_element_type=jnp.float32)
    probs = jnp.exp(jnp.where(visible[None], scores - lse_blk[:, :, None], -jnp.inf))
    d_probs = jnp.einsum("hqd,khd->hqk", dout_blk, value_blk, preferred_element_type=jnp.float32)
    d_scores = (probs * (d_probs - delta_blk[:, :, None])).astype(jnp.bfloat16)
    return (probs, d_scores)


def shards(
    inputs,
    cotangent,
    documents,
    block_place,
    params,
    first_moment,
    second_moment,
    gains,
    gains_first,
    gains_second,
):
    tokens = inputs[0]
    upstream = cotangent[0].astype(jnp.float32)
    length, model_width = tokens.shape
    n_ctx = lax.axis_size("ctx")
    me_ctx = lax.axis_index("ctx")
    seq_len = length * n_ctx
    head_count = model_width // HD
    indices = jnp.arange(seq_len, dtype=jnp.int32)
    owners = indices // length
    placed = jnp.sum(
        jnp.where(
            owners[:, None] == jnp.arange(n_ctx, dtype=jnp.int32)[None, :], block_place[None, :], 0
        ),
        axis=1,
    )
    all_pos = placed * length + indices % length
    all_docs = documents[0]
    my_pos = lax.dynamic_slice_in_dim(all_pos, me_ctx * length, length)
    my_docs = lax.dynamic_slice_in_dim(all_docs, me_ctx * length, length)
    cos_tab, sine_tab = rope_tables(my_pos, HD)
    wide_bf = lax.all_gather(params.astype(jnp.bfloat16), ("dp", "ctx"), axis=0, tiled=True)
    w_qkv, wo_t, w_gu, wd_t = split_weights(wide_bf, model_width)
    projected = jnp.dot(tokens, w_qkv, preferred_element_type=jnp.float32)
    q_pre = projected[:, :model_width]
    k_pre = projected[:, model_width : 2 * model_width]
    values_loc = projected[:, 2 * model_width :].astype(jnp.bfloat16)
    q_scale = rms_scale(q_pre)
    k_scale = rms_scale(k_pre)
    queries = (
        rotate((q_pre * q_scale * gains[0]).reshape(length, head_count, HD), cos_tab, sine_tab)
        * HD ** (-0.5)
    ).astype(jnp.bfloat16)
    keys_loc = (
        rotate((k_pre * k_scale * gains[1]).reshape(length, head_count, HD), cos_tab, sine_tab)
        .astype(jnp.bfloat16)
        .reshape(length, model_width)
    )
    q_heads = jnp.transpose(queries, (1, 0, 2))
    init_state = (
        jnp.full((head_count, length), -jnp.inf, jnp.float32),
        jnp.zeros((head_count, length), jnp.float32),
        jnp.zeros((head_count, length, HD), jnp.float32),
    )
    key_piece = lax.all_gather(keys_loc, "ctx", axis=0, tiled=True)
    value_piece = lax.all_gather(values_loc, "ctx", axis=0, tiled=True)
    row_count = key_piece.shape[0]
    key_pos = all_pos
    key_docs = all_docs
    visible = (key_docs[None, :] == my_docs[:, None]) & (key_pos[None, :] <= my_pos[:, None])
    key_heads = jnp.transpose(key_piece.reshape(row_count, head_count, HD), (1, 0, 2))
    value_heads = jnp.transpose(value_piece.reshape(row_count, head_count, HD), (1, 0, 2))

    def one_head(pieces_h):
        query_h, key_h, value_h, run_max, run_sum, run_acc = pieces_h
        scores = jnp.dot(query_h, key_h.T, preferred_element_type=jnp.float32)
        scores = jnp.where(visible, scores, -jnp.inf)
        new_max = jnp.maximum(run_max, jnp.max(scores, axis=1))
        safe_max = jnp.where(new_max == -jnp.inf, jnp.float32(0.0), new_max)
        shrink = jnp.exp(run_max - safe_max)
        weights = jnp.exp(scores - safe_max[:, None])
        new_sum = run_sum * shrink + jnp.sum(weights, axis=1)
        new_acc = run_acc * shrink[:, None] + jnp.dot(
            weights, value_h.astype(jnp.float32), precision=lax.Precision.HIGHEST
        )
        return (new_max, new_sum, new_acc)

    run_max, run_sum, run_acc = lax.map(
        one_head, (q_heads, key_heads, value_heads) + tuple(init_state)
    )
    lse_rows = run_max + jnp.log(run_sum)
    attn_heads = run_acc / run_sum[:, :, None]
    attn_low = (
        jnp.transpose(attn_heads, (1, 0, 2)).reshape(length, model_width).astype(jnp.bfloat16)
    )
    branch = jnp.einsum("ta,da->td", attn_low, wo_t, preferred_element_type=jnp.float32)
    a_scale = rms_scale(branch)
    hidden1 = tokens.astype(jnp.float32) + branch * a_scale * gains[2]
    h1_low = hidden1.astype(jnp.bfloat16)
    gate_up = jnp.dot(h1_low, w_gu, preferred_element_type=jnp.float32)
    ff_width = gate_up.shape[1] // 2
    gate_pre = gate_up[:, :ff_width]
    up_pre = gate_up[:, ff_width:]
    gate_sig = jax.nn.sigmoid(gate_pre)
    silu_val = gate_pre * gate_sig
    inner_act = (silu_val * up_pre).astype(jnp.bfloat16)
    mlp_out = jnp.einsum("tf,df->td", inner_act, wd_t, preferred_element_type=jnp.float32)
    m_scale = rms_scale(mlp_out)
    result = hidden1 + mlp_out * m_scale * gains[3]
    wide_bf = lax.all_gather(params.astype(jnp.bfloat16), ("dp", "ctx"), axis=0, tiled=True)
    w_qkv, wo_t, w_gu, wd_t = split_weights(wide_bf, model_width)
    g_ff_part = jnp.sum(upstream * mlp_out * m_scale, axis=0)
    d_mlp = norm_back(upstream * gains[3], mlp_out, m_scale).astype(jnp.bfloat16)
    d_inner = jnp.dot(d_mlp, wd_t, preferred_element_type=jnp.float32)
    d_gate = d_inner * up_pre * gate_sig * (1.0 + gate_pre * (1.0 - gate_sig))
    d_upper = d_inner * silu_val
    d_gu = jnp.concatenate([d_gate, d_upper], axis=1).astype(jnp.bfloat16)
    d_h1 = upstream + jnp.einsum("tk,dk->td", d_gu, w_gu, preferred_element_type=jnp.float32)
    g_attn_part = jnp.sum(d_h1 * branch * a_scale, axis=0)
    d_branch = norm_back(d_h1 * gains[2], branch, a_scale).astype(jnp.bfloat16)
    d_attn = jnp.dot(d_branch, wo_t, preferred_element_type=jnp.float32).astype(jnp.bfloat16)
    d_heads = jnp.transpose(d_attn.reshape(length, head_count, HD), (1, 0, 2))
    d_heads_wide = d_heads.astype(jnp.float32)
    row_delta = jnp.sum(d_heads_wide * attn_heads, axis=2)
    key_all, value_all = (
        lax.all_gather(keys_loc, "ctx", axis=0, tiled=True),
        lax.all_gather(values_loc, "ctx", axis=0, tiled=True),
    )
    key_span = min(512, seq_len)
    block_total = seq_len // key_span
    dq_start = jnp.zeros((head_count, length, HD), jnp.float32)

    def key_slices(offset):
        key_blk = lax.dynamic_slice_in_dim(key_all, offset, key_span).reshape(
            key_span, head_count, HD
        )
        value_blk = lax.dynamic_slice_in_dim(value_all, offset, key_span).reshape(
            key_span, head_count, HD
        )
        key_pos = lax.dynamic_slice_in_dim(all_pos, offset, key_span)
        key_docs = lax.dynamic_slice_in_dim(all_docs, offset, key_span)
        visible = (key_docs[None, :] == my_docs[:, None]) & (key_pos[None, :] <= my_pos[:, None])
        return (key_blk, value_blk, visible)

    def back_block(d_query, block_index):
        key_blk, value_blk, visible = key_slices(block_index * key_span)
        probs, d_scores = score_terms(
            queries, key_blk, value_blk, lse_rows, row_delta, d_heads, visible
        )
        d_value = jnp.einsum("hqk,hqd->khd", probs, d_heads_wide, precision=lax.Precision.HIGHEST)
        new_dq = d_query + jnp.einsum(
            "hqk,khd->hqd", d_scores, key_blk, preferred_element_type=jnp.float32
        )
        d_key = jnp.einsum("hqk,qhd->khd", d_scores, queries, preferred_element_type=jnp.float32)
        return (
            new_dq,
            (d_key.reshape(key_span, model_width), d_value.reshape(key_span, model_width)),
        )

    d_query_all, (dk_blocks, dv_blocks) = lax.scan(
        back_block, dq_start, jnp.arange(block_total, dtype=jnp.int32)
    )
    d_keys, d_values = (
        lax.psum_scatter(
            dk_blocks.reshape(seq_len, model_width), "ctx", scatter_dimension=0, tiled=True
        ),
        lax.psum_scatter(
            dv_blocks.reshape(seq_len, model_width), "ctx", scatter_dimension=0, tiled=True
        ),
    )
    d_qn = rotate(jnp.transpose(d_query_all, (1, 0, 2)) * HD ** (-0.5), cos_tab, -sine_tab).reshape(
        length, model_width
    )
    g_q_part = jnp.sum(d_qn * q_pre * q_scale, axis=0)
    d_q_pre = norm_back(d_qn * gains[0], q_pre, q_scale)
    d_kn = rotate(d_keys.reshape(length, head_count, HD), cos_tab, -sine_tab).reshape(
        length, model_width
    )
    g_k_part = jnp.sum(d_kn * k_pre * k_scale, axis=0)
    d_k_pre = norm_back(d_kn * gains[1], k_pre, k_scale)
    d_qkv = jnp.concatenate([d_q_pre, d_k_pre, d_values], axis=1).astype(jnp.bfloat16)
    d_input = d_h1 + jnp.einsum("tk,dk->td", d_qkv, w_qkv, preferred_element_type=jnp.float32)
    gain_part = jnp.stack([g_q_part, g_k_part, g_attn_part, g_ff_part], axis=0)
    pieces = [
        jnp.einsum("tr,tk->rk", tokens, d_qkv, preferred_element_type=jnp.float32),
        jnp.einsum("tr,tk->rk", d_branch, attn_low, preferred_element_type=jnp.float32),
        jnp.einsum("tr,tk->rk", h1_low, d_gu, preferred_element_type=jnp.float32),
        jnp.einsum("tr,tk->rk", d_mlp, inner_act, preferred_element_type=jnp.float32),
    ]
    grad_rows = lax.psum_scatter(
        jnp.concatenate(pieces, axis=1), ("dp", "ctx"), scatter_dimension=0, tiled=True
    )
    squares = jnp.sum(grad_rows * grad_rows)
    square_total, gain_total = lax.psum((squares, gain_part), ("dp", "ctx"))
    square_sum = square_total + jnp.sum(gain_total * gain_total)
    grad_norm = jnp.sqrt(square_sum)
    factor = CLIP / (grad_norm + 1e-06)
    new_params, new_first, new_second = adam_update(
        params, first_moment, second_moment, grad_rows * factor, RATE, DECAY
    )
    new_gains, new_gains_first, new_gains_second = adam_update(
        gains, gains_first, gains_second, gain_total * factor, GAIN_RATE, 0.0
    )
    return (
        result.astype(jnp.bfloat16)[None],
        d_input.astype(jnp.bfloat16)[None],
        grad_norm,
        new_params,
        new_first,
        new_second,
        new_gains,
        new_gains_first,
        new_gains_second,
    )


def solution(mesh):
    return jax.shard_map(
        shards,
        mesh=mesh,
        in_specs=(
            P("dp", "ctx", None),
            P("dp", "ctx", None),
            P("dp", None),
            P(),
            P(("dp", "ctx"), None),
            P(("dp", "ctx"), None),
            P(("dp", "ctx"), None),
            P(),
            P(),
            P(),
        ),
        out_specs=(
            P("dp", "ctx", None),
            P("dp", "ctx", None),
            P(),
            P(("dp", "ctx"), None),
            P(("dp", "ctx"), None),
            P(("dp", "ctx"), None),
            P(),
            P(),
            P(),
        ),
        check_vma=False,
    )
```

profile of v0, /device:TPU:0, one launch (start us, length us, event | category | flops | bytes accessed | tf_op | source)
XLA Modules:
  0.0 4325.2 jit_solution(4144230771603573625)
XLA Ops:
  7.2 5.8 convert_element_type.65
  14.7 679.9 %all-gather.4.cloned.1.call-done = bf16[2048,32768]{1,0:T(8,128)(2,1)} async-done(((bf16[64,32768]{1,0:T(8,128)(2,1)}), bf16[2048,32768]{1,0:T(8,128)(2,1)}) %all-gather.4.cloned.1.call-update) | async-done | bytes 134217744 | tf_op jit(solution)/shard_map/all_gather | solution.py:108
  694.6 10.3 fusion.35
  705.2 1.9 multiply_multiply_fusion.1
  707.0 2.5 copy.102
  709.6 2.5 copy.101
  712.1 2.8 subtract_convert_fusion
  719.9 31.7 all-gather.6.cloned.1.call-done
  751.6 6.4 copy.75
  758.0 32.3 all-gather.8.cloned.1.call-done
  790.2 5.3 bitcast_bitcast_fusion
  795.5 51.5 %while.30 = (s32[]{:T(128)}, f32[16,128]{1,0:T(8,128)S(1)}, f32[16,128]{1,0:T(8,128)S(1)}, f32[16,128,128]{1,2,0:T(8,128)S(1)}, bf16[16,128,128]{1,2,0:T(8,128)(...) while((s32[]{:T(128)}, f32[16,128]{1,0:T(8,128)S(1)}, ...), condition=%wide.region_6.7_spmd.clone, body=%wide.region_3.6_spmd.clone.sunk | while | flops 235946880 | bytes 2475669 | solution.py:154
  800.3 1.4 fusion.141
  803.5 1.4 fusion.141
  806.7 1.4 fusion.141
  819.6 1.4 fusion.141
  822.8 1.4 fusion.141
  826.0 1.4 fusion.141
  829.2 1.4 fusion.141
  848.0 6.5 multiply_reduce_fusion.9
  855.8 26.8 fusion.27
  882.7 4.6 multiply_convert_fusion.2
  887.3 17.0 multiply_reduce_fusion.8
  905.3 18.0 multiply_convert_fusion.1
  923.3 31.1 multiply_reduce_fusion.1
  954.4 2.9 multiply_convert_fusion.5
  957.3 4.9 fusion.53
  964.9 79.1 %while.31 = (s32[]{:T(128)}, f32[16,128,128]{2,1,0:T(8,128)}, f32[2,512,2048]{2,1,0:T(8,128)}, f32[2,512,2048]{2,1,0:T(8,128)}, s32[2]{0:T(128)S(1)}, /*index=5*...) while((s32[]{:T(128)}, f32[16,128,128]{2,1,0:T(8,128)}, ...), condition=%wide.region_13.14_spmd.clone, body=%wide.region_12.13_spmd.clone.sunk | while | flops 2692415488 | bytes 105616760 | solution.py:226
  966.7 1.7 constant_dynamic-slice_fusion.5
  968.4 2.5 copy.136
  970.9 1.7 constant_dynamic-slice_fusion.4
  974.2 1.6 fusion.153
  977.1 6.0 fusion.154
  983.1 5.3 copy.137
  988.4 2.7 fusion.155
  991.2 5.4 copy.138
  996.5 8.0 constant_dynamic-update-slice_fusion.6
  1006.1 1.7 constant_dynamic-slice_fusion.5
  1007.8 2.5 copy.136
  1010.3 1.7 constant_dynamic-slice_fusion.4
  1013.7 1.6 fusion.153
  1016.5 6.0 fusion.154
  1022.5 5.3 copy.137
  1027.9 2.7 fusion.155
  1030.6 5.4 copy.138
  1036.0 8.0 constant_dynamic-update-slice_fusion.6
  1045.8 10.9 fusion.96
  1056.7 26.5 fusion.91
  1083.2 52.1 %fusion.43 = f32[2048,16384]{1,0:T(8,128)} fusion(bf16[128,2048]{1,0:T(8,128)(2,1)} %copy-done.20, bf16[128,8192]{1,0:T(8,128)(2,1)} %get-tuple-element.375, bf16[128,8192]{1,0:T(8,128)(2,1)S(1)} %copy-done.19), kind=kOutput, calls=%fused_computation.68 | convolution fusion | flops 8598323200 | bytes 138936320 | tf_op jit(solution)/shard_map/tr,tk->rk/dot_general | solution.py:253
  1135.3 1.6 copy.85
  1139.2 2.8 copy.99
  1142.1 2.3 pad_maximum_fusion.8
  1144.3 2.9 copy.100
  1147.3 2.9 multiply_reduce_fusion.3
  1150.1 1.5 multiply_convert_fusion.4
  1151.7 39.4 reduce-scatter.6.cloned.1.call-done
  1192.4 20.8 convolution_bitcast_fusion
  1213.2 49.2 %copy.88 = f32[2048,6144]{1,0:T(8,128)} copy(f32[2048,6144]{0,1:T(8,128)} %convolution_bitcast_fusion) | data formatting | bytes 100663296 | tf_op jit(solution)/shard_map/tr,tk->rk/dot_general | solution.py:251
  1262.4 169.8 %pad_maximum_fusion = f32[2048,32768]{1,0:T(8,128)} fusion(f32[2048,8192]{1,0:T(8,128)} %fusion.91, f32[2048,16384]{1,0:T(8,128)} %fusion.43, f32[2048,2048]{1,0:T(8,128)} %fusion.96, f32[2048,6144]{1,0:T(8,128)} %copy.88), kind=kLoop, calls=%fused_computation.38 | loop fusion | flops 201326592 | bytes 536870912 | tf_op jit(solution)/shard_map/concatenate | solution.py:257
  1433.1 2791.7 %reduce-scatter.8.cloned.1.call-done = f32[64,32768]{1,0:T(8,128)} async-done(((f32[2048,32768]{1,0:T(8,128)}), f32[64,32768]{1,0:T(8,128)}) %reduce-scatter.8.cloned.1.call-update) | async-done | bytes 8388624 | tf_op jit(solution)/shard_map/reduce_scatter | solution.py:256
  4224.8 6.1 multiply_reduce_fusion
  4231.0 13.6 fusion.56
  4244.6 47.4 %all-reduce = (f32[]{:T(128)}, f32[4,2048]{1,0:T(4,128)S(1)}) all-reduce(f32[]{:T(128)} %multiply_reduce_fusion, f32[4,2048]{1,0:T(4,128)S(1)} %pad_maximum_fusion.12), channel_id=1, replica_groups=mesh['dp'=4,'ctx'=8] {'dp','ctx'}, use_global_device_ids=true, to_apply=%region_20.21 | all-reduce | flops 8193 | bytes 65544 | tf_op jit(solution)/shard_map/psum | solution.py:260
  4294.8 22.2 multiply_subtract_fusion
  (322 shorter events, 68.2 us)
Async XLA Ops:
  7.2 687.4 %all-gather.4.cloned.1.call-start = ((), (), s32[]{:S(2)}) async-start(), calls=%async_computation.3 | async-start | bytes 138412032 | tf_op jit(solution)/shard_map/all_gather | solution.py:108
  13.0 0.7 copy-start.53
  13.0 1.6 copy-start.38
  13.1 738.5 %all-gather.6.cloned.1.call-start = ((), (), s32[]{:S(2)}) async-start(), calls=%async_computation.4 | async-start | bytes 4718592 | tf_op jit(solution)/shard_map/all_gather | solution.py:131
  14.7 697.4 %copy-start.31 = (f32[128,64]{0,1:T(8,128)}, f32[128,64]{0,1:T(8,128)S(1)}, u32[]{:S(2)}) copy-start(f32[128,64]{0,1:T(8,128)S(1)} %get-tuple-element.400) | copy-start | bytes 98308
  14.7 690.4 %copy-start.33 = (f32[1,2048]{1,0:T(1,128)}, f32[1,2048]{1,0:T(1,128)S(1)}, u32[]{:S(2)}) copy-start(f32[1,2048]{1,0:T(1,128)S(1)} %get-tuple-element.396) | copy-start | bytes 24580
  14.7 690.4 %copy-start.35 = (f32[1,2048]{1,0:T(1,128)}, f32[1,2048]{1,0:T(1,128)S(1)}, u32[]{:S(2)}) copy-start(f32[1,2048]{1,0:T(1,128)S(1)} %get-tuple-element.397) | copy-start | bytes 24580
  704.9 11.0 copy-start.5
  705.1 4.4 copy-start.49
  705.1 7.0 copy-start.51
  709.6 7.6 copy-start.45
  715.8 74.4 %all-gather.8.cloned.1.call-start = ((), (), s32[]{:S(2)}) async-start(), calls=%async_computation.5 | async-start | bytes 4718592 | tf_op jit(solution)/shard_map/all_gather | solution.py:132
  716.8 418.6 %reduce-scatter.4.cloned.1.call-start = ((), (), s32[]{:S(2)}) async-start(), calls=%async_computation.6 | async-start | bytes 9437184 | tf_op jit(solution)/shard_map/reduce_scatter | solution.py:230
  847.0 1.0 copy-start.14
  848.0 6.5 copy-start.26
  848.0 7.6 copy-start.13
  854.5 1.1 copy-start.16
  855.8 26.9 copy-start.20
  887.3 17.0 copy-start.11
  887.3 17.0 copy-start.25
  904.3 50.1 %copy-start.7 = (f32[128,2048]{1,0:T(8,128)}, f32[128,2048]{1,0:T(8,128)S(1)}, u32[]{:S(2)}) copy-start(f32[128,2048]{1,0:T(8,128)S(1)} %get-tuple-element.404) | copy-start | bytes 3145732
  905.3 18.0 copy-start.46
  957.3 4.9 copy-start.17
  957.3 6.1 copy-start.15
  962.2 0.8 copy-start.28
  962.9 1.8 copy-start.29
  972.6 1.6 copy-start
  974.2 1.6 copy-start.1
  975.9 1.2 copy-start.4
  977.1 6.0 copy-start.2
  1012.1 1.6 copy-start
  1013.7 1.6 copy-start.1
  1015.3 1.2 copy-start.4
  1016.5 6.0 copy-start.2
  1044.0 147.1 %reduce-scatter.6.cloned.1.call-start = ((), (), s32[]{:S(2)}) async-start(), calls=%async_computation.7 | async-start | bytes 9437184 | tf_op jit(solution)/shard_map/reduce_scatter | solution.py:233
  1044.0 1.2 copy-start.3
  1044.5 1.1 copy-start.18
  1044.6 1.3 copy-start.27
  1044.6 3180.3 %reduce-scatter.8.cloned.1.call-start = ((), (), s32[]{:S(2)}) async-start(), calls=%async_computation.8 | async-start | bytes 276824064 | tf_op jit(solution)/shard_map/reduce_scatter | solution.py:256
  1045.8 10.9 copy-start.8
  1045.8 10.9 copy-start.12
  1045.8 10.9 copy-start.47
  1056.7 26.5 copy-start.19
  1083.2 53.7 %copy-start.32 = (f32[128,64]{0,1:T(8,128)S(1)}, f32[128,64]{0,1:T(8,128)}, u32[]{:S(2)}) copy-start(f32[128,64]{0,1:T(8,128)} %copy-done.31) | copy-start | bytes 98308
  1083.2 53.7 %copy-start.37 = (f32[128,64]{0,1:T(8,128)S(1)}, f32[128,64]{0,1:T(8,128)}, u32[]{:S(2)}) copy-start(f32[128,64]{0,1:T(8,128)} %get-tuple-element.398) | copy-start | bytes 98308
  1138.2 9.0 copy-start.6
  1138.2 9.0 copy-start.34
  1138.2 9.0 copy-start.36
  1138.2 9.0 copy-start.50
  1138.2 9.0 copy-start.52
  1147.2 2.9 copy-start.9
  1147.3 2.9 copy-start.10
  1192.4 20.8 copy-start.23
  1432.3 0.7 copy-start.40
  1432.3 0.7 copy-start.41
  1432.3 0.7 copy-start.42
  1432.3 0.7 copy-start.48
  1433.1 2797.9 %copy-start.21 = (bf16[128,2048]{1,0:T(8,128)(2,1)S(1)}, bf16[128,2048]{1,0:T(8,128)(2,1)}, u32[]{:S(2)}) copy-start(bf16[128,2048]{1,0:T(8,128)(2,1)} %get-tuple-element.376) | copy-start | bytes 1572868
  1433.1 2797.9 %copy-start.22 = (bf16[128,2048]{1,0:T(8,128)(2,1)S(1)}, bf16[128,2048]{1,0:T(8,128)(2,1)}, u32[]{:S(2)}) copy-start(bf16[128,2048]{1,0:T(8,128)(2,1)} %get-tuple-element.377) | copy-start | bytes 1572868
  1433.1 2797.9 %copy-start.24 = (bf16[128,2048]{1,0:T(8,128)(2,1)S(1)}, bf16[128,2048]{1,0:T(8,128)(2,1)}, u32[]{:S(2)}) copy-start(bf16[128,2048]{1,0:T(8,128)(2,1)} %copy-done.23) | copy-start | bytes 1572868
  1433.1 2797.9 %copy-start.30 = (f32[128,2048]{1,0:T(8,128)S(1)}, f32[128,2048]{1,0:T(8,128)}, u32[]{:S(2)}) copy-start(f32[128,2048]{1,0:T(8,128)} %get-tuple-element.405) | copy-start | bytes 3145732
  4231.0 63.1 %copy-start.39 = (f32[4,2048]{1,0:T(4,128)S(1)}, f32[4,2048]{1,0:T(4,128)}, u32[]{:S(2)}) copy-start(f32[4,2048]{1,0:T(4,128)} %param.21) | copy-start | bytes 98308
  4231.0 63.1 %copy-start.43 = (f32[4,2048]{1,0:T(4,128)S(1)}, f32[4,2048]{1,0:T(4,128)}, u32[]{:S(2)}) copy-start(f32[4,2048]{1,0:T(4,128)} %param.22) | copy-start | bytes 98308
  4231.0 63.1 %copy-start.44 = (f32[4,2048]{1,0:T(4,128)S(1)}, f32[4,2048]{1,0:T(4,128)}, u32[]{:S(2)}) copy-start(f32[4,2048]{1,0:T(4,128)} %param.23) | copy-start | bytes 98308
Sparse Core Ops, SparseCore 0:
  13.2 681.3 all-gather.3
  715.9 35.6 all-gather.5
  753.5 36.7 all-gather.7
  1044.1 71.3 reduce-scatter.3
  1119.8 71.2 reduce-scatter.5
  1432.5 2792.3 reduce-scatter.7
where the time goes:
time: 4330 us
  waiting for transfers between devices  3580 us (83%)
  matrix products  307 us (7%)
  other arithmetic  240 us (6%)
  local copies, waits for them, and re-layouts  136 us (3%)
  blocking collectives  47.4 us (1%)
    reduce_scatter x1, waiting for transfers between devices, shards(): lax.psum_scatter(jnp.concatenate(pieces, axis=1), ('dp', 'ctx'), scatter_...  2790 us
    all_gather x1, waiting for transfers between devices, shards(): lax.all_gather(params.astype(jnp.bfloat16), ('dp', 'ctx'), axis=0, tiled=...  680 us
    concatenate x1, other arithmetic, shards(): jnp.concatenate(pieces, axis=1)  170 us
  transfers between devices with their start and end apart: 6, of which 5 were waited for; matrix products, arithmetic and copies ran while one was open for 3% of the time, Pallas kernels for 0%

commit v1 on v0

v1 whole, which is shorter than its diff:
```python
import jax
import jax.numpy as jnp
from jax import lax
from jax.sharding import PartitionSpec as P

HD = 128
STEP = 10
EPS = 1e-06
THETA = 500000.0
CLIP = 1.0
BETA1 = 0.9
BETA2 = 0.95
RATE = 0.03
GAIN_RATE = 0.8
DECAY = 0.1
ADAM_EPS = 1e-08
BF = jnp.bfloat16
F32 = jnp.float32


def rms_scale(values):
    return lax.rsqrt(jnp.mean(values * values, axis=-1, keepdims=True) + EPS)


def norm_back(upstream, source, scale):
    return scale * (
        upstream - source * scale * scale * jnp.mean(upstream * source, axis=-1, keepdims=True)
    )


def rope_tables(positions, head_size):
    half_size = head_size // 2
    freqs = THETA ** (-jnp.arange(half_size, dtype=jnp.float32) * 2.0 / head_size)
    angles = positions.astype(jnp.float32)[:, None] * freqs[None, :]
    return (jnp.cos(angles), jnp.sin(angles))


def rotate(values, cos_tab, sine_tab):
    shape = values.shape
    values = values.reshape(shape[0], shape[1] // HD, HD)
    half_size = HD // 2
    first_half = values[..., :half_size]
    second_half = values[..., half_size:]
    cos_b = cos_tab[:, None, :]
    sine_b = sine_tab[:, None, :]
    return jnp.concatenate(
        [first_half * cos_b - second_half * sine_b, second_half * cos_b + first_half * sine_b],
        axis=-1,
    ).reshape(shape)


def adam_update(weight, first_in, second_in, clipped, rate, decay):
    new_first = BETA1 * first_in + (1.0 - BETA1) * clipped
    new_second = BETA2 * second_in + (1.0 - BETA2) * clipped * clipped
    first_hat = new_first / (1.0 - BETA1**STEP)
    second_hat = new_second / (1.0 - BETA2**STEP)
    new_weight = weight - rate * (first_hat / (jnp.sqrt(second_hat) + ADAM_EPS) + decay * weight)
    return (new_weight, new_first, new_second)


def dot(a, b):
    return jnp.dot(a, b, preferred_element_type=F32)


def dot_t(a, b):
    return lax.dot_general(a, b, (((1,), (1,)), ((), ())), preferred_element_type=F32)


def t_dot(a, b):
    return lax.dot_general(a, b, (((0,), (0,)), ((), ())), preferred_element_type=F32)


def shards(
    inputs,
    cotangent,
    documents,
    block_place,
    params,
    first_moment,
    second_moment,
    gains,
    gains_first,
    gains_second,
):
    tokens = inputs[0]
    upstream = cotangent[0].astype(F32)
    length, width = tokens.shape
    n_ctx = lax.axis_size("ctx")
    n_dp = lax.axis_size("dp")
    me_ctx = lax.axis_index("ctx")
    seq = length * n_ctx
    rows = params.shape[0]
    ff = (params.shape[1] - 4 * width) // 3
    hc = width // n_ctx
    heads = hc // HD
    fs = ff // n_dp

    def mix(values):
        t = values.shape[0]
        return (
            values.reshape(t, n_dp, n_ctx, rows).transpose(0, 2, 1, 3).reshape(t, width)
        )

    def unmix(values):
        t = values.shape[0]
        return (
            values.reshape(t, n_ctx, n_dp, rows).transpose(0, 2, 1, 3).reshape(t, width)
        )

    low = params.astype(BF)
    wa = low[:, : 4 * width].reshape(rows, 4, n_ctx, hc).transpose(2, 0, 1, 3)
    wa = lax.all_to_all(wa.reshape(n_ctx * rows, 4 * hc), "ctx", 0, 0, tiled=True)
    wa = lax.all_gather(wa, "dp", axis=0, tiled=True)
    w_qkv, w_o = wa[:, : 3 * hc], wa[:, 3 * hc :]
    x_all = lax.all_gather(tokens, "ctx", axis=0, tiled=True)
    wf = low[:, 4 * width :].reshape(rows, 3, n_dp, fs).transpose(2, 0, 1, 3)
    wf = lax.all_to_all(wf.reshape(n_dp * rows, 3 * fs), "dp", 0, 0, tiled=True)
    wf = lax.all_gather(wf, "ctx", axis=0, tiled=True)
    w_gu, w_d = wf[:, : 2 * fs], wf[:, 2 * fs :]

    indices = jnp.arange(seq, dtype=jnp.int32)
    owners = indices // length
    placed = jnp.sum(
        jnp.where(
            owners[:, None] == jnp.arange(n_ctx, dtype=jnp.int32)[None, :], block_place[None, :], 0
        ),
        axis=1,
    )
    pos = placed * length + indices % length
    docs = documents[0]
    visible = (docs[None, :] == docs[:, None]) & (pos[None, :] <= pos[:, None])
    cos_tab, sine_tab = rope_tables(pos, HD)

    my_gains = lax.dynamic_slice_in_dim(gains, me_ctx * hc, hc, axis=1)
    projected = dot(x_all, w_qkv)
    qk_pre = projected[:, : 2 * hc].reshape(seq, 2, hc)
    values = projected[:, 2 * hc :].astype(BF)
    squares = lax.psum(jnp.sum(qk_pre * qk_pre, axis=-1), "ctx")
    scales = lax.rsqrt(squares / width + EPS)
    q_pre, k_pre = qk_pre[:, 0], qk_pre[:, 1]
    q_scale, k_scale = scales[:, :1], scales[:, 1:]
    queries = (rotate(q_pre * q_scale * my_gains[0], cos_tab, sine_tab) * HD ** (-0.5)).astype(BF)
    keys = rotate(k_pre * k_scale * my_gains[1], cos_tab, sine_tab).astype(BF)

    def split(v):
        return v.reshape(seq, heads, HD).transpose(1, 0, 2)

    def join(v):
        return v.transpose(1, 0, 2).reshape(seq, hc)

    qh, kh, vh = split(queries), split(keys), split(values)
    scores = jnp.einsum("hqd,hkd->hqk", qh, kh, preferred_element_type=F32)
    scores = jnp.where(visible[None], scores, -jnp.inf)
    top = jnp.max(scores, axis=-1, keepdims=True)
    weights = jnp.exp(scores - top)
    total = jnp.sum(weights, axis=-1, keepdims=True)
    probs = weights / total
    probs_low = probs.astype(BF)
    attn = jnp.einsum("hqk,hkd->hqd", probs_low, vh, preferred_element_type=F32)
    attn_low = join(attn).astype(BF)
    branch = lax.psum_scatter(
        dot_t(attn_low, w_o).astype(BF), "ctx", scatter_dimension=0, tiled=True
    ).astype(F32)
    a_scale = rms_scale(branch)
    hidden1 = tokens.astype(F32) + branch * a_scale * gains[2]

    h1_all = lax.all_gather(mix(hidden1.astype(BF)), "dp", axis=0, tiled=True)
    gate_up = dot(h1_all, w_gu)
    gate_pre, up_pre = gate_up[:, :fs], gate_up[:, fs:]
    gate_sig = jax.nn.sigmoid(gate_pre)
    silu_val = gate_pre * gate_sig
    inner = (silu_val * up_pre).astype(BF)
    mlp_out = unmix(
        lax.psum_scatter(
            dot_t(inner, w_d).astype(BF), "dp", scatter_dimension=0, tiled=True
        ).astype(F32)
    )
    m_scale = rms_scale(mlp_out)
    result = hidden1 + mlp_out * m_scale * gains[3]

    g_ff_part = jnp.sum(upstream * mlp_out * m_scale, axis=0)
    d_mlp = norm_back(upstream * gains[3], mlp_out, m_scale).astype(BF)
    d_mlp_all = lax.all_gather(mix(d_mlp), "dp", axis=0, tiled=True)
    d_inner = dot(d_mlp_all, w_d)
    d_gate = d_inner * up_pre * gate_sig * (1.0 + gate_pre * (1.0 - gate_sig))
    d_upper = d_inner * silu_val
    d_gu = jnp.concatenate([d_gate, d_upper], axis=1).astype(BF)
    d_h1 = upstream + unmix(
        lax.psum_scatter(
            dot_t(d_gu, w_gu).astype(BF), "dp", scatter_dimension=0, tiled=True
        ).astype(F32)
    )
    ff_grad = jnp.concatenate([t_dot(h1_all, d_gu), t_dot(d_mlp_all, inner)], axis=1).astype(BF)

    g_attn_part = jnp.sum(d_h1 * branch * a_scale, axis=0)
    d_branch = norm_back(d_h1 * gains[2], branch, a_scale).astype(BF)
    d_branch_all = lax.all_gather(d_branch, "ctx", axis=0, tiled=True)
    ff_grad = lax.psum_scatter(ff_grad, "ctx", scatter_dimension=0, tiled=True)
    ff_grad = lax.all_to_all(ff_grad, "dp", 0, 0, tiled=True)
    d_attn = dot(d_branch_all, w_o).astype(BF)
    dh = split(d_attn)
    delta = jnp.sum(dh.astype(F32) * attn, axis=-1, keepdims=True)
    d_probs = jnp.einsum("hqd,hkd->hqk", dh, vh, preferred_element_type=F32)
    d_scores = (probs * (d_probs - delta)).astype(BF)
    d_query = join(jnp.einsum("hqk,hkd->hqd", d_scores, kh, preferred_element_type=F32))
    d_key = join(jnp.einsum("hqk,hqd->hkd", d_scores, qh, preferred_element_type=F32))
    d_value = join(jnp.einsum("hqk,hqd->hkd", probs_low, dh, preferred_element_type=F32))
    d_qn = rotate(d_query * HD ** (-0.5), cos_tab, -sine_tab)
    d_kn = rotate(d_key, cos_tab, -sine_tab)
    g_q_part = jnp.sum(d_qn * q_pre * q_scale, axis=0)
    g_k_part = jnp.sum(d_kn * k_pre * k_scale, axis=0)
    e_q, e_k = d_qn * my_gains[0], d_kn * my_gains[1]
    means = (
        lax.psum(jnp.stack([jnp.sum(e_q * q_pre, -1), jnp.sum(e_k * k_pre, -1)], -1), "ctx") / width
    )
    d_q_pre = q_scale * (e_q - q_pre * q_scale * q_scale * means[:, :1])
    d_k_pre = k_scale * (e_k - k_pre * k_scale * k_scale * means[:, 1:])
    d_qkv = jnp.concatenate([d_q_pre, d_k_pre, d_value], axis=1).astype(BF)
    attn_grad = jnp.concatenate([t_dot(x_all, d_qkv), t_dot(d_branch_all, attn_low)], axis=1)
    attn_grad = lax.psum_scatter(attn_grad.astype(BF), "dp", scatter_dimension=0, tiled=True)
    attn_grad = lax.all_to_all(attn_grad, "ctx", 0, 0, tiled=True)
    d_input = d_h1 + lax.psum_scatter(
        dot_t(d_qkv, w_qkv).astype(BF), "ctx", scatter_dimension=0, tiled=True
    ).astype(F32)

    grad = jnp.concatenate(
        [
            attn_grad.reshape(n_ctx, rows, 4, hc).transpose(1, 2, 0, 3).reshape(rows, 4 * width),
            ff_grad.reshape(n_dp, rows, 3, fs).transpose(1, 2, 0, 3).reshape(rows, 3 * ff),
        ],
        axis=1,
    ).astype(F32)
    gain_part = jnp.stack(
        [
            lax.dynamic_update_slice(jnp.zeros(width, F32), g_q_part, (me_ctx * hc,)),
            lax.dynamic_update_slice(jnp.zeros(width, F32), g_k_part, (me_ctx * hc,)),
            g_attn_part,
            g_ff_part,
        ],
        axis=0,
    )
    square_total, gain_total = lax.psum((jnp.sum(grad * grad), gain_part), ("dp", "ctx"))
    grad_norm = jnp.sqrt(square_total + jnp.sum(gain_total * gain_total))
    factor = CLIP / (grad_norm + 1e-06)
    new_params, new_first, new_second = adam_update(
        params, first_moment, second_moment, grad * factor, RATE, DECAY
    )
    new_gains, new_gains_first, new_gains_second = adam_update(
        gains, gains_first, gains_second, gain_total * factor, GAIN_RATE, 0.0
    )
    return (
        result.astype(BF)[None],
        d_input.astype(BF)[None],
        grad_norm,
        new_params,
        new_first,
        new_second,
        new_gains,
        new_gains_first,
        new_gains_second,
    )


def solution(mesh):
    split, whole = P("dp", "ctx", None), P(("dp", "ctx"), None)
    return jax.shard_map(
        shards,
        mesh=mesh,
        in_specs=(split, split, P("dp", None), P(), whole, whole, whole, P(), P(), P()),
        out_specs=(split, split, P(), whole, whole, whole, P(), P(), P()),
        check_vma=False,
    )
```

time: 4330 us -> 1180 us (0.27)
  waiting for transfers between devices: 3580 us -> 734 us
  matrix products: 307 us -> 111 us
  other arithmetic: 240 us -> 94.9 us
  blocking collectives: 47.4 us -> 104 us
    reduce_scatter x3 -> x6, waiting for transfers between devices: 2830 us -> 271 us  [the longest x1 139 us: shards(): ff_grad = lax.psum_scatter(ff_grad, 'ctx', scatter_dimension=0, tiled=True)]
    all_gather x3 -> x6, waiting for transfers between devices: 744 us -> 318 us  [the longest x1 125 us: shards(): wf = lax.all_gather(wf, 'ctx', axis=0, tiled=True)]
    dot_general x54 -> x18, matrix products: 307 us -> 111 us  [the longest x4 35.1 us: dot_t(): lax.dot_general(a, b, (((1,), (1,)), ((), ())), preferred_element_type=F32)]
    concatenate x1 -> x2, other arithmetic: 170 us -> 19.4 us  [the longest x1 17.1 us: shards(): jnp.concatenate([t_dot(h1_all, d_gu), t_dot(d_mlp_all, inner)], axis=1)]
    all_to_all x0 -> x2, waiting for transfers between devices: none -> 145 us  [the longest x1 78.8 us: shards(): wf = lax.all_to_all(wf.reshape(n_dp * rows, 3 * fs), 'dp', 0, 0, tiled=True)]
    dot_general x1 -> x0, local copies, waits for them, and re-layouts: 49.2 us -> none  [shards(): jnp.einsum('tr,tk->rk', tokens, d_qkv, preferred_element_type=jnp.float32)]
  transfers between devices with their start and end apart: 6 -> 14, of which waited for: 5 -> 12; matrix products, arithmetic and copies ran while one was open for 3% -> 10% of each run, Pallas kernels for 0% -> 0%
where the time goes in v1:
time: 1180 us; the launch traced here: 1170 us
  waiting for transfers between devices  734 us (62%)
  matrix products  111 us (9%)
  blocking collectives  104 us (9%)
  other arithmetic  94.9 us (8%)
  local copies, waits for them, and re-layouts  94.3 us (8%)
  between operations  17.9 us (2%)
    reduce_scatter x1, waiting for transfers between devices, shards(): ff_grad = lax.psum_scatter(ff_grad, 'ctx', scatter_dimension=0, tiled=True)  139 us
    all_gather x1, waiting for transfers between devices, shards(): wf = lax.all_gather(wf, 'ctx', axis=0, tiled=True)  125 us
    all_to_all x1, waiting for transfers between devices, shards(): wf = lax.all_to_all(wf.reshape(n_dp * rows, 3 * fs), 'dp', 0, 0, tiled=True)  78.8 us
    all_gather x1, waiting for transfers between devices, shards(): wa = lax.all_gather(wa, 'dp', axis=0, tiled=True)  74.3 us
    all_to_all x1, waiting for transfers between devices, shards(): ff_grad = lax.all_to_all(ff_grad, 'dp', 0, 0, tiled=True)  65.7 us
    all_gather x1, waiting for transfers between devices, shards(): d_mlp_all = lax.all_gather(mix(d_mlp), 'dp', axis=0, tiled=True)  45.7 us
    reduce_scatter x1, waiting for transfers between devices, shards(): lax.psum_scatter(dot_t(inner, w_d).astype(BF), 'dp', scatter_dimension=0,...  42.7 us
    reduce_scatter x1, waiting for transfers between devices, shards(): lax.psum_scatter(dot_t(d_gu, w_gu).astype(BF), 'dp', scatter_dimension=0,...  38.5 us
  transfers between devices with their start and end apart: 14, of which 12 were waited for; matrix products, arithmetic and copies ran while one was open for 10% of the time, Pallas kernels for 0%

profile of v1, /device:TPU:0, one launch (start us, length us, event | category | flops | bytes accessed | tf_op | source)
XLA Modules:
  0.0 1166.6 jit_solution(2757129951516957364)
XLA Ops:
  7.2 3.8 convert_element_type.102
  11.0 2.0 copy-done.2
  14.6 20.4 %all_to_all.42 = bf16[8,64,1024]{2,1,0:T(8,128)(2,1)} all-to-all(bf16[8,64,1024]{2,1,0:T(8,128)(2,1)S(1)} %all_to_all.28), channel_id=1, replica_groups=mesh['dp'=4,'ctx'=8] {'ctx'}, dimensions={0} | all-to-all | bytes 2097152 | tf_op jit(solution)/shard_map/all_to_all | solution.py:112
  36.1 3.1 fusion.73
  39.1 1.9 compare_and_fusion
  41.1 74.3 %all-gather.8.cloned.1.call-done = bf16[2048,1024]{1,0:T(8,128)(2,1)} async-done(((bf16[512,1024]{1,0:T(8,128)(2,1)}), bf16[2048,1024]{1,0:T(8,128)(2,1)}) %all-gather.8.cloned.1.call-update) | async-done | bytes 4194320 | tf_op jit(solution)/shard_map/all_gather | solution.py:113
  115.3 37.2 %all-gather.18.cloned.1.call-done = bf16[1,1024,2048]{2,1,0:T(8,128)(2,1)} async-done(((bf16[1,128,2048]{2,1,0:T(8,128)(2,1)}), bf16[1,1024,2048]{2,1,0:T(8,128)(2,1)}) %all-gather.18.cloned.1.call-update) | async-done | bytes 4194320 | tf_op jit(solution)/shard_map/all_gather | solution.py:115
  152.5 6.2 fusion.18
  160.7 2.6 copy.176
  163.3 2.5 copy.177
  165.8 13.3 %psum.28 = f32[1024,2]{0,1:T(2,128)S(1)} all-reduce(f32[1024,2]{0,1:T(2,128)S(1)} %multiply_reduce_fusion), channel_id=1, replica_groups=mesh['dp'=4,'ctx'=8] {'ctx'}, use_global_device_ids=true, to_apply=%region_2.3 | all-reduce | flops 2048 | bytes 16384 | tf_op jit(solution)/shard_map/psum | solution.py:138
  179.2 1.9 multiply_multiply_fusion.1
  184.5 7.6 fusion.99
  192.1 4.6 fusion.23
  196.8 1.9 copy-done
  201.2 4.6 convolution_convert_fusion.2
  205.8 3.7 slice.130
  209.5 5.4 reshape.409
  214.9 6.9 copy.233
  221.8 9.7 all_to_all.31
  231.6 4.8 all-to-all-start.1
  236.4 20.8 %reduce-scatter.7.cloned.1.call-done = bf16[128,2048]{1,0:T(8,128)(2,1)} async-done(((bf16[1024,2048]{1,0:T(8,128)(2,1)}), bf16[128,2048]{1,0:T(8,128)(2,1)}) %reduce-scatter.7.cloned.1.call-update) | async-done | bytes 524304 | tf_op jit(solution)/shard_map/reduce_scatter | solution.py:161
  261.0 78.8 %all-to-all-done.1 = bf16[4,64,6144]{2,1,0:T(8,128)(2,1)} async-done(((bf16[4,64,6144]{2,1,0:T(8,128)(2,1)}), bf16[4,64,6144]{2,1,0:T(8,128)(2,1)}, u32[]{:S(2)}, u32[]{:S(2)}) %all-to-all-start.1) | async-done | bytes 3145760 | tf_op jit(solution)/shard_map/all_to_all | solution.py:117
  340.0 124.7 %all-gather.12.cloned.1.call-done = bf16[2048,6144]{1,0:T(8,128)(2,1)} async-done(((bf16[256,6144]{1,0:T(8,128)(2,1)}), bf16[2048,6144]{1,0:T(8,128)(2,1)}) %all-gather.12.cloned.1.call-update) | async-done | bytes 25165840 | tf_op jit(solution)/shard_map/all_gather | solution.py:118
  464.7 12.5 %fusion.3 = f32[512,4096]{1,0:T(8,128)S(1)} fusion(bf16[512,2048]{0,1:T(8,128)(2,1)} %all-gather.10.cloned.1.call-done, bf16[2048,6144]{1,0:T(8,128)(2,1)} %all-gather.12.cloned.1.call-done), kind=kOutput, calls=%fused_computation.5 | convolution fusion | flops 8589934592 | bytes 27262976 | tf_op jit(solution)/shard_map/dot_general | solution.py:62
  478.5 2.1 copy-done.6
  481.9 9.2 fusion.33
  492.4 42.7 %reduce-scatter.9.cloned.1.call-done = bf16[128,2048]{1,0:T(8,128)(2,1)} async-done(((bf16[512,2048]{1,0:T(8,128)(2,1)}), bf16[128,2048]{1,0:T(8,128)(2,1)}) %reduce-scatter.9.cloned.1.call-update) | async-done | bytes 524304 | tf_op jit(solution)/shard_map/reduce_scatter | solution.py:174
  536.7 1.9 multiply_reduce_fusion.1
  539.8 45.7 %all-gather.14.cloned.1.call-done = bf16[512,2048]{0,1:T(8,128)(2,1)} async-done(((bf16[128,2048]{0,1:T(8,128)(2,1)}), bf16[512,2048]{0,1:T(8,128)(2,1)}) %all-gather.14.cloned.1.call-update) | async-done | bytes 2097168 | tf_op jit(solution)/shard_map/all_gather | solution.py:183
  585.5 10.9 multiply_convert_fusion.2
  598.4 13.4 %fusion.27 = bf16[512,2048]{1,0:T(8,128)(2,1)} fusion(bf16[2048,6144]{1,0:T(8,128)(2,1)} %all-gather.12.cloned.1.call-done, bf16[512,2048]{1,0:T(8,128)(2,1)S(1)} %get-tuple-element.26, bf16[512,2048]{1,0:T(8,128)(2,1)S(1)} %get-tuple-element.25), kind=kOutput, calls=%fused_computation.45 | convolution fusion | flops 8599371776 | bytes 23068672 | tf_op jit(solution)/shard_map/dot_general | solution.py:66
  613.0 2.6 copy.184
  615.5 38.5 %reduce-scatter.11.cloned.1.call-done = bf16[128,2048]{1,0:T(8,128)(2,1)} async-done(((bf16[512,2048]{1,0:T(8,128)(2,1)}), bf16[128,2048]{1,0:T(8,128)(2,1)}) %reduce-scatter.11.cloned.1.call-update) | async-done | bytes 524304 | tf_op jit(solution)/shard_map/reduce_scatter | solution.py:189
  657.9 2.0 fusion.49
  659.9 3.2 fusion.45
  663.7 35.7 %all-gather.16.cloned.1.call-done = bf16[1024,2048]{1,0:T(8,128)(2,1)} async-done(((bf16[128,2048]{1,0:T(8,128)(2,1)}), bf16[1024,2048]{1,0:T(8,128)(2,1)}) %all-gather.16.cloned.1.call-update) | async-done | bytes 4194320 | tf_op jit(solution)/shard_map/all_gather | solution.py:197
  699.3 4.2 multiply_reduce_fusion.2
  703.6 4.8 multiply_convert_fusion
  709.7 2.0 fusion.38
  711.9 2.3 convolution_convert_fusion.5
  714.2 1.9 multiply_subtract_fusion.2
  719.1 2.9 pad_maximum_fusion.7
  722.0 2.5 copy.197
  726.0 13.5 %psum.29 = f32[1024,2]{0,1:T(2,128)S(1)} all-reduce(f32[1024,2]{0,1:T(2,128)S(1)} %pad_maximum_fusion.12), channel_id=1, replica_groups=mesh['dp'=4,'ctx'=8] {'ctx'}, use_global_device_ids=true, to_apply=%region_15.16 | all-reduce | flops 2048 | bytes 16384 | tf_op jit(solution)/shard_map/psum | solution.py:214
  745.0 5.1 fusion.30
  750.1 2.3 pad_maximum_fusion.2
  752.5 10.3 convolution_convert_fusion.1
  762.8 11.7 %convolution_convert_fusion = bf16[2048,4096]{1,0:T(8,128)(2,1)} fusion(bf16[512,2048]{0,1:T(8,128)(2,1)S(1)} %copy-done.36, bf16[512,2048]{1,0:T(8,128)(2,1)S(1)} %copy-done.40, bf16[512,2048]{1,0:T(8,128)(2,1)S(1)} %copy-done.38), kind=kOutput, calls=%fused_computation.2 | convolution fusion | flops 8606711808 | bytes 23068672 | tf_op jit(solution)/shard_map/dot_general | solution.py:70
  774.5 17.1 %pad_maximum_fusion = bf16[2048,6144]{1,0:T(8,128)(2,1)} fusion(bf16[2048,2048]{1,0:T(8,128)(2,1)} %convolution_convert_fusion.1, bf16[2048,4096]{1,0:T(8,128)(2,1)} %convolution_convert_fusion), kind=kLoop, calls=%fused_computation.1 | loop fusion | flops 50331648 | bytes 50331648 | tf_op jit(solution)/shard_map/concatenate | solution.py:193
  791.6 7.9 convolution_convert_fusion.3
  799.6 29.7 %reduce-scatter.15.cloned.1.call-done = bf16[512,1024]{0,1:T(8,128)(2,1)} async-done(((bf16[2048,1024]{0,1:T(8,128)(2,1)}), bf16[512,1024]{0,1:T(8,128)(2,1)}) %reduce-scatter.15.cloned.1.call-update) | async-done | bytes 1048592 | tf_op jit(solution)/shard_map/reduce_scatter | solution.py:220
  829.3 2.3 copy.203
  831.6 19.6 %all_to_all.43 = bf16[8,64,1024]{2,1,0:T(8,128)(2,1)} all-to-all(bf16[8,64,1024]{2,1,0:T(8,128)(2,1)} %bitcast.204), channel_id=1, replica_groups=mesh['dp'=4,'ctx'=8] {'ctx'}, dimensions={0} | all-to-all | bytes 2097152 | tf_op jit(solution)/shard_map/all_to_all | solution.py:221
  851.2 139.2 %reduce-scatter.17.cloned.1.call-done = bf16[256,6144]{1,0:T(8,128)(2,1)} async-done(((bf16[2048,6144]{1,0:T(8,128)(2,1)}), bf16[256,6144]{1,0:T(8,128)(2,1)}) %reduce-scatter.17.cloned.1.call-update) | async-done | bytes 3145744 | tf_op jit(solution)/shard_map/reduce_scatter | solution.py:198
  990.4 4.9 all-to-all-start.3
  1000.5 65.7 %all-to-all-done.3 = bf16[4,64,6144]{2,1,0:T(8,128)(2,1)} async-done(((bf16[4,64,6144]{2,1,0:T(8,128)(2,1)}), bf16[4,64,6144]{2,1,0:T(8,128)(2,1)}, u32[]{:S(2)}, u32[]{:S(2)}) %all-to-all-start.3) | async-done | bytes 3145760 | tf_op jit(solution)/shard_map/all_to_all | solution.py:199
  1066.2 10.1 reshape.422
  1076.3 10.0 copy.206
  1086.3 5.3 reshape.423
  1091.7 4.2 fusion.7
  1095.9 2.0 fusion.71
  1097.9 37.6 %all-reduce = (f32[]{:T(128)}, f32[4,2048]{1,0:T(4,128)S(1)}) all-reduce(f32[]{:T(128)} %fusion.7, f32[4,2048]{1,0:T(4,128)S(1)} %pad_maximum_fusion.11), channel_id=1, replica_groups=mesh['dp'=4,'ctx'=8] {'dp','ctx'}, use_global_device_ids=true, to_apply=%region_20.21 | all-reduce | flops 8193 | bytes 65544 | tf_op jit(solution)/shard_map/psum | solution.py:242
  1138.2 20.0 %multiply_subtract_fusion = (f32[64,32768]{1,0:T(8,128)}, f32[64,32768]{1,0:T(8,128)}, f32[64,32768]{1,0:T(8,128)}) fusion(f32[64,32768]{1,0:T(8,128)} %param.14, f32[]{:T(128)S(6)} %div.89, bf16[64,24576]{1,0:T(8,128)(2,1)} %reshape.423, bf16[64,8192]{1,0:T(8,128)(2,1)S(1)} %bitcast.195, f32[64,32768]{1,0:T(8,128)} %param.15, f32[64,32768]{1,0:T(8,128)} %param.16), kind=kLoop, calls=%fused_computation.14 | loop fusion | flops 41943040 | bytes 54525956 | tf_op jit(solution)/shard_map/sub | solution.py:57
  (166 shorter events, 46.4 us)
Async XLA Ops:
  7.2 108.2 %all-gather.8.cloned.1.call-start = ((), (), s32[]{:S(2)}) async-start(), calls=%async_computation.10 | async-start | bytes 5242880 | tf_op jit(solution)/shard_map/all_gather | solution.py:113
  11.0 2.0 copy-start.2
  13.4 22.5 %copy-start.28 = (f32[4,2048]{1,0:T(4,128)S(1)}, f32[4,2048]{1,0:T(4,128)}, u32[]{:S(2)}) copy-start(f32[4,2048]{1,0:T(4,128)} %param.17) | copy-start | bytes 98308
  13.4 22.6 %copy-start.33 = (s32[8]{0:T(128)S(1)}, s32[8]{0:T(128)}, u32[]{:S(2)}) copy-start(s32[8]{0:T(128)} %param.13) | copy-start | bytes 100
  13.8 25.3 %copy-start.32 = (s32[1,1024]{1,0:T(1,128)S(1)}, s32[1,1024]{1,0:T(1,128)}, u32[]{:S(2)}) copy-start(s32[1,1024]{1,0:T(1,128)} %param.12) | copy-start | bytes 12292
  35.0 117.5 %all-gather.18.cloned.1.call-start = ((), (), s32[]{:S(2)}) async-start(), calls=%async_computation.21 | async-start | bytes 4718592 | tf_op jit(solution)/shard_map/all_gather | solution.py:115
  35.8 221.5 %reduce-scatter.7.cloned.1.call-start = ((), (), s32[]{:S(2)}) async-start(), calls=%async_computation.11 | async-start | bytes 4718592 | tf_op jit(solution)/shard_map/reduce_scatter | solution.py:161
  39.1 142.0 %copy-start.13 = (f32[1024,64]{1,0:T(8,128)}, f32[1024,64]{1,0:T(8,128)S(1)}, u32[]{:S(2)}) copy-start(f32[1024,64]{1,0:T(8,128)S(1)} %get-tuple-element.56) | copy-start | bytes 786436
  159.2 37.6 %copy-start.22 = (bf16[1024,256]{0,1:T(8,128)(2,1)}, bf16[1024,256]{0,1:T(8,128)(2,1)S(1)}, u32[]{:S(2)}) copy-start(bf16[1024,256]{0,1:T(8,128)(2,1)S(1)} %slice.194) | copy-start | bytes 1572868
  179.2 2.0 copy-start.24
  182.0 0.8 copy-start.9
  182.0 1.0 copy-start.11
  182.4 0.8 copy-start.15
  196.8 1.9 copy-start
  200.4 0.8 copy-start.18
  231.6 27.0 %copy-start.17 = (bf16[1,128,2048]{2,1,0:T(8,128)(2,1)S(1)}, bf16[1,128,2048]{2,1,0:T(8,128)(2,1)}, u32[]{:S(2)}) copy-start(bf16[1,128,2048]{2,1,0:T(8,128)(2,1)} %param.10) | copy-start | bytes 1572868
  231.6 108.3 %all-to-all-start.1 = ((bf16[4,64,6144]{2,1,0:T(8,128)(2,1)}), bf16[4,64,6144]{2,1,0:T(8,128)(2,1)}, u32[]{:S(2)}, u32[]{:S(2)}) async-start(bf16[4,64,6144]{2,1,0:T(8,128)(2,1)} %all_to_all.31), calls=%async_computation.2 | async-start | bytes 6291456 | tf_op jit(solution)/shard_map/all_to_all | solution.py:117
  236.4 103.6 %all-gather.10.cloned.1.call-start = ((), (), s32[]{:S(2)}) async-start(), calls=%async_computation.12 | async-start | bytes 2621440 | tf_op jit(solution)/shard_map/all_gather | solution.py:167
  261.0 203.7 %all-gather.12.cloned.1.call-start = ((), (), s32[]{:S(2)}) async-start(), calls=%async_computation.13 | async-start | bytes 28311552 | tf_op jit(solution)/shard_map/all_gather | solution.py:118
  339.9 195.2 %reduce-scatter.9.cloned.1.call-start = ((), (), s32[]{:S(2)}) async-start(), calls=%async_computation.14 | async-start | bytes 2621440 | tf_op jit(solution)/shard_map/reduce_scatter | solution.py:174
  477.2 3.4 copy-start.6
  480.6 1.3 copy-start.20
  481.9 9.3 copy-start.7
  491.1 94.4 %all-gather.14.cloned.1.call-start = ((), (), s32[]{:S(2)}) async-start(), calls=%async_computation.15 | async-start | bytes 2621440 | tf_op jit(solution)/shard_map/all_gather | solution.py:183
  536.4 2.2 copy-start.5
  539.8 114.3 %reduce-scatter.11.cloned.1.call-start = ((), (), s32[]{:S(2)}) async-start(), calls=%async_computation.16 | async-start | bytes 2621440 | tf_op jit(solution)/shard_map/reduce_scatter | solution.py:189
  596.4 1.3 copy-start.37
  596.4 2.0 copy-start.39
  611.8 87.5 %all-gather.16.cloned.1.call-start = ((), (), s32[]{:S(2)}) async-start(), calls=%async_computation.17 | async-start | bytes 4718592 | tf_op jit(solution)/shard_map/all_gather | solution.py:197
  657.9 45.6 %copy-start.3 = (f32[128,2048]{1,0:T(8,128)}, f32[128,2048]{1,0:T(8,128)S(1)}, u32[]{:S(2)}) copy-start(f32[128,2048]{1,0:T(8,128)S(1)} %copy.190) | copy-start | bytes 3145732
  663.1 166.2 %reduce-scatter.15.cloned.1.call-start = ((), (), s32[]{:S(2)}) async-start(), calls=%async_computation.19 | async-start | bytes 5242880 | tf_op jit(solution)/shard_map/reduce_scatter | solution.py:220
  699.3 4.2 copy-start.23
  703.5 4.8 copy-start.16
  708.4 1.3 copy-start.10
  708.4 1.3 copy-start.12
  709.7 2.2 copy-start.1
  711.8 2.3 copy-start.14
  711.9 2.3 copy-start.21
  739.6 1.9 copy-start.19
  739.6 2.7 copy-start.35
  742.2 1.3 copy-start.26
  742.2 1.3 copy-start.27
  742.2 1.4 copy-start.25
  742.2 2.7 copy-start.34
  752.4 237.9 %reduce-scatter.17.cloned.1.call-start = ((), (), s32[]{:S(2)}) async-start(), calls=%async_computation.20 | async-start | bytes 28311552 | tf_op jit(solution)/shard_map/reduce_scatter | solution.py:198
  752.5 10.3 copy-start.36
  752.5 10.3 copy-start.38
  752.5 10.3 copy-start.40
  791.6 304.3 %reduce-scatter.13.cloned.1.call-start = ((), (), s32[]{:S(2)}) async-start(), calls=%async_computation.18 | async-start | bytes 4718592 | tf_op jit(solution)/shard_map/reduce_scatter | solution.py:222
  990.4 75.9 %all-to-all-start.3 = ((bf16[4,64,6144]{2,1,0:T(8,128)(2,1)}), bf16[4,64,6144]{2,1,0:T(8,128)(2,1)}, u32[]{:S(2)}, u32[]{:S(2)}) async-start(bf16[4,64,6144]{2,1,0:T(8,128)(2,1)} %bitcast.212), calls=%async_computation.9 | async-start | bytes 6291456 | tf_op jit(solution)/shard_map/all_to_all | solution.py:199
  1086.3 9.6 copy-start.4
  1086.3 9.6 copy-start.8
  1091.7 45.8 %copy-start.29 = (f32[4,2048]{1,0:T(4,128)S(1)}, f32[4,2048]{1,0:T(4,128)}, u32[]{:S(2)}) copy-start(f32[4,2048]{1,0:T(4,128)} %param.17) | copy-start | bytes 98308
  1091.7 45.8 %copy-start.30 = (f32[4,2048]{1,0:T(4,128)S(1)}, f32[4,2048]{1,0:T(4,128)}, u32[]{:S(2)}) copy-start(f32[4,2048]{1,0:T(4,128)} %param.18) | copy-start | bytes 98308
  1091.7 45.8 %copy-start.31 = (f32[4,2048]{1,0:T(4,128)S(1)}, f32[4,2048]{1,0:T(4,128)}, u32[]{:S(2)}) copy-start(f32[4,2048]{1,0:T(4,128)} %param.19) | copy-start | bytes 98308
Sparse Core Ops, SparseCore 0:
  35.2 80.1 all-gather.7
  117.2 35.2 all-gather.17
  205.9 51.3 reduce-scatter.6
  261.1 78.1 all-gather.9
  341.2 123.4 all-gather.11
  491.2 43.8 reduce-scatter.8
  539.9 45.5 all-gather.13
  612.0 42.0 reduce-scatter.10
  663.3 36.0 all-gather.15
  752.5 76.7 reduce-scatter.14
  832.9 157.3 reduce-scatter.16
  994.1 51.3 reduce-scatter.12

commit v2 on v1

--- a/solution.py
+++ b/solution.py
@@ -1,6 +1,10 @@
+import functools
+
 import jax
 import jax.numpy as jnp
 from jax import lax
+from jax.experimental import pallas as pl
+from jax.experimental.pallas import tpu as pltpu
 from jax.sharding import PartitionSpec as P
 
 HD = 128
@@ -16,6 +20,9 @@
 ADAM_EPS = 1e-08
 BF = jnp.bfloat16
 F32 = jnp.float32
+MESH = pl.DeviceIdType.MESH
+ANY = pl.BlockSpec(memory_space=pl.ANY)
+VMEM = pl.BlockSpec(memory_space=pltpu.VMEM)
 
 
 def rms_scale(values):
@@ -68,6 +75,675 @@
 
 def t_dot(a, b):
     return lax.dot_general(a, b, (((0,), (0,)), ((), ())), preferred_element_type=F32)
+
+
+def greet(peers):
+    barrier = pltpu.get_barrier_semaphore()
+    for peer in peers:
+        pl.semaphore_signal(barrier, inc=1, device_id=peer, device_id_type=MESH)
+    pl.semaphore_wait(barrier, len(peers))
+
+
+def remote(src, dst, send, recv, peer):
+    return pltpu.make_async_remote_copy(
+        src_ref=src, dst_ref=dst, send_sem=send, recv_sem=recv, device_id=peer, device_id_type=MESH
+    )
+
+
+def params_of(number, vmem=48):
+    return pltpu.CompilerParams(
+        collective_id=number, has_side_effects=True, vmem_limit_bytes=vmem * 1024 * 1024
+    )
+
+
+def line_steps(n, me, make_right, make_left):
+    for s in range(n - 1):
+
+        @pl.when((me < n - 1) & (me >= s))
+        def _():
+            make_right(s).start()
+
+        @pl.when((me > 0) & (me + s < n))
+        def _():
+            make_left(s).start()
+
+        @pl.when(me - 1 - s >= 0)
+        def _():
+            make_right(s, me - 1 - s).wait_recv()
+
+        @pl.when(me + 1 + s < n)
+        def _():
+            make_left(s, me + 1 + s).wait_recv()
+
+    for s in range(n - 1):
+
+        @pl.when((me < n - 1) & (me >= s))
+        def _():
+            make_right(s).wait_send()
+
+        @pl.when((me > 0) & (me + s < n))
+        def _():
+            make_left(s).wait_send()
+
+
+def pairs_of(n, me):
+    half = n // 2
+    parity, pair = me % 2, me // 2
+    partner = me + 1 - 2 * parity
+    ahead = [2 * ((pair + k) % half) + parity for k in range(1, half)]
+    behind = [2 * ((pair + half - k) % half) + parity for k in range(1, half)]
+    return half, parity, pair, partner, ahead, behind
+
+
+def gather_dp_kernel(n, x_ref, o_ref, local, sr, rr, sl, rl):
+    me, ctx = lax.axis_index("dp"), lax.axis_index("ctx")
+
+    def here(d):
+        return (d, ctx)
+
+    greet([here((me + 1) % n), here((me + n - 1) % n)])
+    own = pltpu.make_async_copy(x_ref, o_ref.at[me], local)
+    own.start()
+
+    def right(s, block=None):
+        b = me - s if block is None else block
+        return remote(x_ref if s == 0 else o_ref.at[b], o_ref.at[b], sr.at[s], rr.at[s], here(me + 1))
+
+    def left(s, block=None):
+        b = me + s if block is None else block
+        return remote(x_ref if s == 0 else o_ref.at[b], o_ref.at[b], sl.at[s], rl.at[s], here(me - 1))
+
+    line_steps(n, me, right, left)
+    own.wait()
+
+
+def gather_dp(x, number):
+    n = lax.axis_size("dp")
+    out = pl.pallas_call(
+        functools.partial(gather_dp_kernel, n),
+        out_shape=jax.ShapeDtypeStruct((n,) + x.shape, x.dtype),
+        in_specs=[ANY],
+        out_specs=ANY,
+        scratch_shapes=[pltpu.SemaphoreType.DMA] + [pltpu.SemaphoreType.DMA((n - 1,))] * 4,
+        compiler_params=params_of(number),
+        name="gather_dp",
+    )(x)
+    return out.reshape((n * x.shape[0],) + x.shape[1:])
+
+
+def gather_ctx_kernel(n, x_ref, o_ref, local, ss, rs, fs, fr):
+    dp, me = lax.axis_index("dp"), lax.axis_index("ctx")
+    half, parity, pair, partner, ahead, behind = pairs_of(n, me)
+    greet([(dp, partner)] + [(dp, a) for a in ahead])
+    own = pltpu.make_async_copy(x_ref, o_ref.at[me], local)
+    sends = [
+        remote(x_ref, o_ref.at[me], ss.at[k], rs.at[k], (dp, a))
+        for k, a in enumerate(ahead + [partner])
+    ]
+    for copy in sends:
+        copy.start()
+    own.start()
+    forwards = []
+    for k, b in enumerate(behind):
+        remote(x_ref, o_ref.at[b], ss.at[k], rs.at[k], (dp, b)).wait_recv()
+        forward = remote(o_ref.at[b], o_ref.at[b], fs.at[k], fr.at[k], (dp, partner))
+        forward.start()
+        forwards.append(forward)
+    sends[-1].wait_recv()
+    for forward in forwards:
+        forward.wait()
+    for copy in sends:
+        copy.wait_send()
+    own.wait()
+
+
+def gather_ctx(x, number):
+    n = lax.axis_size("ctx")
+    half = n // 2
+    out = pl.pallas_call(
+        functools.partial(gather_ctx_kernel, n),
+        out_shape=jax.ShapeDtypeStruct((n,) + x.shape, x.dtype),
+        in_specs=[ANY],
+        out_specs=ANY,
+        scratch_shapes=[pltpu.SemaphoreType.DMA]
+        + [pltpu.SemaphoreType.DMA((half,))] * 2
+        + [pltpu.SemaphoreType.DMA((half - 1,))] * 2,
+        compiler_params=params_of(number),
+        name="gather_ctx",
+    )(x)
+    return out.reshape((n * x.shape[0],) + x.shape[1:])
+
+
+def reduce_ctx(n, dp, me, a_ref, w_ref, o_ref, sa, ra, sb, rb, s1, r1, s2, r2):
+    half, parity, pair, partner, ahead, behind = pairs_of(n, me)
+    length, width = o_ref.shape
+    tile = width // 4
+
+    def product(block, store):
+        rows = pl.ds(pl.multiple_of(block * length, length), length)
+
+        @pl.loop(0, 4)
+        def _(j):
+            part = pl.ds(pl.multiple_of(j * tile, tile), tile)
+            store(part, dot_t(a_ref[rows, :], w_ref[part, :]))
+
+    first, second = [], []
+    for k in range(half):
+
+        def store(part, value, k=k):
+            sa[k, :, part] = value.astype(BF)
+
+        product(2 * ((pair + k + 1) % half) + 1 - parity, store)
+        copy = remote(sa.at[k], ra.at[k], s1.at[k], r1.at[k], (dp, partner))
+        copy.start()
+        first.append(copy)
+    for k in range(half):
+        target = 2 * ((pair + k + 1) % half) + parity
+        first[k].wait_recv()
+
+        def store(part, value, k=k):
+            value = value + ra[k, :, part].astype(F32)
+            if k < half - 1:
+                sb[k, :, part] = value.astype(BF)
+            else:
+                o_ref[:, part] = value
+
+        product(target, store)
+        if k < half - 1:
+            copy = remote(sb.at[k], rb.at[k], s2.at[k], r2.at[k], (dp, target))
+            copy.start()
+            second.append(copy)
+    for k in range(half - 1):
+        second[k].wait_recv()
+        o_ref[...] += rb[k].astype(F32)
+    return first + second
+
+
+def scatter_ctx_kernel(n, a_ref, w_ref, o_ref, sa, ra, sb, rb, s1, r1, s2, r2):
+    dp, me = lax.axis_index("dp"), lax.axis_index("ctx")
+    half, parity, pair, partner, ahead, behind = pairs_of(n, me)
+    greet([(dp, partner)] + [(dp, a) for a in ahead])
+    for copy in reduce_ctx(n, dp, me, a_ref, w_ref, o_ref, sa, ra, sb, rb, s1, r1, s2, r2):
+        copy.wait_send()
+
+
+def scatter_ctx(a, w, number):
+    n = lax.axis_size("ctx")
+    half, length, width = n // 2, a.shape[0] // n, w.shape[0]
+    dma = pltpu.SemaphoreType.DMA
+    return pl.pallas_call(
+        functools.partial(scatter_ctx_kernel, n),
+        out_shape=jax.ShapeDtypeStruct((length, width), F32),
+        in_specs=[VMEM, VMEM],
+        out_specs=VMEM,
+        scratch_shapes=[
+            pltpu.VMEM((half, length, width), BF),
+            pltpu.VMEM((half, length, width), BF),
+            pltpu.VMEM((half - 1, length, width), BF),
+            pltpu.VMEM((half - 1, length, width), BF),
+            dma((half,)),
+            dma((half,)),
+            dma((half - 1,)),
+            dma((half - 1,)),
+        ],
+        compiler_params=params_of(number),
+        name="scatter_ctx",
+    )(a, w)
+
+
+def scatter_dp_kernel(n, a_ref, w_ref, o_ref, sa, ra, ss, rs):
+    me, ctx = lax.axis_index("dp"), lax.axis_index("ctx")
+    length, width = o_ref.shape
+    tile = width // 4
+
+    def product(block, out):
+        rows = pl.ds(pl.multiple_of(block * length, length), length)
+
+        @pl.loop(0, 4)
+        def _(j):
+            part = pl.ds(pl.multiple_of(j * tile, tile), tile)
+            out[:, part] = dot_t(a_ref[rows, :], w_ref[part, :]).astype(out.dtype)
+
+    greet([((me + k) % n, ctx) for k in range(1, n)])
+    copies = []
+    for k in range(1, n):
+        target = (me + k) % n
+        product(target, sa.at[k - 1])
+        copy = remote(sa.at[k - 1], ra.at[k - 1], ss.at[k - 1], rs.at[k - 1], (target, ctx))
+        copy.start()
+        copies.append(copy)
+    product(me, o_ref)
+    for k in range(n - 1):
+        copies[k].wait_recv()
+        o_ref[...] += ra[k].astype(F32)
+    for copy in copies:
+        copy.wait_send()
+
+
+def scatter_dp(a, w, number):
+    n = lax.axis_size("dp")
+    length, width = a.shape[0] // n, w.shape[0]
+    dma = pltpu.SemaphoreType.DMA
+    return pl.pallas_call(
+        functools.partial(scatter_dp_kernel, n),
+        out_shape=jax.ShapeDtypeStruct((length, width), F32),
+        in_specs=[VMEM, VMEM],
+        out_specs=VMEM,
+        scratch_shapes=[
+            pltpu.VMEM((n - 1, length, width), BF),
+            pltpu.VMEM((n - 1, length, width), BF),
+            dma((n - 1,)),
+            dma((n - 1,)),
+        ],
+        compiler_params=params_of(number, 56),
+        name="scatter_dp",
+    )(a, w)
+
+
+def swap_dp_kernel(n, x_ref, o_ref, local, ss, rs):
+    me, ctx = lax.axis_index("dp"), lax.axis_index("ctx")
+    greet([((me + k) % n, ctx) for k in range(1, n)])
+    own = pltpu.make_async_copy(x_ref.at[me], o_ref.at[me], local)
+    copies = []
+    for k in range(1, n):
+        to = (me + k) % n
+        copy = remote(x_ref.at[to], o_ref.at[me], ss.at[k - 1], rs.at[k - 1], (to, ctx))
+        copy.start()
+        copies.append(copy)
+    own.start()
+    for k in range(1, n):
+        source = (me + n - k) % n
+        remote(x_ref.at[me], o_ref.at[source], ss.at[k - 1], rs.at[k - 1], (source, ctx)).wait_recv()
+    for copy in copies:
+        copy.wait_send()
+    own.wait()
+
+
+def swap_dp(x, number):
+    n = lax.axis_size("dp")
+    dma = pltpu.SemaphoreType.DMA
+    return pl.pallas_call(
+        functools.partial(swap_dp_kernel, n),
+        out_shape=jax.ShapeDtypeStruct(x.shape, x.dtype),
+        in_specs=[ANY],
+        out_specs=ANY,
+        scratch_shapes=[dma, dma((n - 1,)), dma((n - 1,))],
+        compiler_params=params_of(number),
+        name="swap_dp",
+    )(x)
+
+
+def spread_kernel(n_dp, n, w_ref, x_ref, o_ref, y_ref, local, sa, ra, ss, rs, fs, fr, sr, rr, sl, rl):
+    dp, me = lax.axis_index("dp"), lax.axis_index("ctx")
+    half, parity, pair, partner, ahead, behind = pairs_of(n, me)
+    greet(
+        [((dp + 1) % n_dp, me), ((dp + n_dp - 1) % n_dp, me)]
+        + [(dp, (me + k) % n) for k in range(1, n)]
+    )
+    own_w = pltpu.make_async_copy(w_ref.at[me], o_ref.at[dp, me], local.at[0])
+    own_x = pltpu.make_async_copy(x_ref, y_ref.at[me], local.at[1])
+    own_w.start()
+    swaps = []
+    for k in range(1, n):
+        to = (me + k) % n
+        copy = remote(w_ref.at[to], o_ref.at[dp, me], sa.at[k - 1], ra.at[k - 1], (dp, to))
+        copy.start()
+        swaps.append(copy)
+    sends = [
+        remote(x_ref, y_ref.at[me], ss.at[k], rs.at[k], (dp, a))
+        for k, a in enumerate(ahead + [partner])
+    ]
+    for copy in sends:
+        copy.start()
+    own_x.start()
+
+    def right(s, k, b):
+        c = (me + n - k) % n
+        return remote(o_ref.at[b, c], o_ref.at[b, c], sr.at[s, k], rr.at[s, k], (dp + 1, me))
+
+    def left(s, k, b):
+        c = (me + n - k) % n
+        return remote(o_ref.at[b, c], o_ref.at[b, c], sl.at[s, k], rl.at[s, k], (dp - 1, me))
+
+    for s in range(n_dp):
+        for k in range(n):
+            if s == 0 and k == 0:
+                own_w.wait()
+            elif s == 0:
+                source = (me + n - k) % n
+                remote(
+                    w_ref.at[me], o_ref.at[dp, source], sa.at[k - 1], ra.at[k - 1], (dp, source)
+                ).wait_recv()
+            else:
+
+                @pl.when(dp >= s)
+                def _():
+                    right(s - 1, k, dp - s).wait_recv()
+
+                @pl.when(dp + s < n_dp)
+                def _():
+                    left(s - 1, k, dp + s).wait_recv()
+
+            if s < n_dp - 1:
+
+                @pl.when((dp < n_dp - 1) & (dp >= s))
+                def _():
+                    right(s, k, dp - s).start()
+
+                @pl.when((dp > 0) & (dp + s < n_dp))
+                def _():
+                    left(s, k, dp + s).start()
+
+        if s == 0:
+            forwards = []
+            for k, b in enumerate(behind):
+                remote(x_ref, y_ref.at[b], ss.at[k], rs.at[k], (dp, b)).wait_recv()
+                forward = remote(y_ref.at[b], y_ref.at[b], fs.at[k], fr.at[k], (dp, partner))
+                forward.start()
+                forwards.append(forward)
+    for s in range(n_dp - 1):
+        for k in range(n):
+
+            @pl.when((dp < n_dp - 1) & (dp >= s))
+            def _():
+                right(s, k, dp - s).wait_send()
+
+            @pl.when((dp > 0) & (dp + s < n_dp))
+            def _():
+                left(s, k, dp + s).wait_send()
+
+    sends[-1].wait_recv()
+    for forward in forwards:
+        forward.wait()
+    for copy in sends + swaps:
+        copy.wait_send()
+    own_x.wait()
+
+
+def spread(w, x, number):
+    n_dp, n = lax.axis_size("dp"), lax.axis_size("ctx")
+    half = n // 2
+    dma = pltpu.SemaphoreType.DMA
+    out, x_all = pl.pallas_call(
+        functools.partial(spread_kernel, n_dp, n),
+        out_shape=(
+            jax.ShapeDtypeStruct((n_dp,) + w.shape, w.dtype),
+            jax.ShapeDtypeStruct((n,) + x.shape, x.dtype),
+        ),
+        in_specs=[ANY, ANY],
+        out_specs=(ANY, ANY),
+        scratch_shapes=[dma((2,)), dma((n - 1,)), dma((n - 1,)), dma((half,)), dma((half,))]
+        + [dma((half - 1,))] * 2
+        + [dma((n_dp - 1, n))] * 4,
+        compiler_params=params_of(number),
+        name="spread",
+    )(w, x)
+    return out.reshape(-1, w.shape[-1]), x_all.reshape(-1, x.shape[-1])
+
+
+def collect_kernel(
+    n_dp, n, g_ref, a_ref, w_ref, o_ref, y_ref,
+    own, ra, rc, sb, pa, qa, pb, qb,
+    local, sa, rs, sc, rd, s1, r1, s2, r2,
+):
+    dp, me = lax.axis_index("dp"), lax.axis_index("ctx")
+    greet(
+        [((dp + k) % n_dp, me) for k in range(1, n_dp)] + [(dp, (me + k) % n) for k in range(1, n)]
+    )
+    mine = pltpu.make_async_copy(g_ref.at[dp], own, local)
+    mine.start()
+    first = []
+    for c in range(n):
+        row = []
+        for k in range(1, n_dp):
+            to = (dp + k) % n_dp
+            copy = remote(
+                g_ref.at[to, (me + 1 + c) % n],
+                ra.at[c, k - 1],
+                sa.at[c, k - 1],
+                rs.at[c, k - 1],
+                (to, me),
+            )
+            copy.start()
+            row.append(copy)
+        first.append(row)
+    sums = reduce_ctx(n, dp, me, a_ref, w_ref, y_ref, pa, qa, pb, qb, s1, r1, s2, r2)
+    mine.wait()
+    second = []
+    for c in range(n):
+        to = (me + 1 + c) % n
+        total = own[to].astype(F32)
+        for k in range(n_dp - 1):
+            first[c][k].wait_recv()
+            total = total + ra[c, k].astype(F32)
+        if c < n - 1:
+            sb[c] = total.astype(BF)
+            copy = remote(sb.at[c], rc.at[c], sc.at[c], rd.at[c], (dp, to))
+            copy.start()
+            second.append(copy)
+        else:
+            o_ref[me] = total.astype(BF)
+    for c in range(n - 1):
+        second[c].wait_recv()
+        o_ref[(me + n - 1 - c) % n] = rc[c]
+    for row in first:
+        for copy in row:
+            copy.wait_send()
+    for copy in second + sums:
+        copy.wait_send()
+
+
+def collect(g, a, w, number):
+    n_dp, n = lax.axis_size("dp"), lax.axis_size("ctx")
+    rows, width = g.shape[0] // (n_dp * n), g.shape[1]
+    half, length, features = n // 2, a.shape[0] // n, w.shape[0]
+    dma = pltpu.SemaphoreType.DMA
+    return pl.pallas_call(
+        functools.partial(collect_kernel, n_dp, n),
+        out_shape=(
+            jax.ShapeDtypeStruct((n, rows, width), BF),
+            jax.ShapeDtypeStruct((length, features), F32),
+        ),
+        in_specs=[ANY, VMEM, VMEM],
+        out_specs=(VMEM, VMEM),
+        scratch_shapes=[
+            pltpu.VMEM((n, rows, width), BF),
+            pltpu.VMEM((n, n_dp - 1, rows, width), BF),
+            pltpu.VMEM((n - 1, rows, width), BF),
+            pltpu.VMEM((n - 1, rows, width), BF),
+            pltpu.VMEM((half, length, features), BF),
+            pltpu.VMEM((half, length, features), BF),
+            pltpu.VMEM((half - 1, length, features), BF),
+            pltpu.VMEM((half - 1, length, features), BF),
+            dma,
+            dma((n, n_dp - 1)),
+            dma((n, n_dp - 1)),
+            dma((n - 1,)),
+            dma((n - 1,)),
+            dma((half,)),
+            dma((half,)),
+            dma((half - 1,)),
+            dma((half - 1,)),
+        ],
+        compiler_params=params_of(number),
+        name="collect",
+    )(g.reshape(n_dp, n, rows, width), a, w)
+
+
+def total_kernel(n_dp, n, ga_ref, gu_ref, gd_ref, gain_ref, o_ref, mine, buf, part, all_parts, ss, rs, st, rt):
+    dp, me = lax.axis_index("dp"), lax.axis_index("ctx")
+    gain_rows = gain_ref.shape[0]
+
+    def squares(ref):
+        acc = jnp.zeros((ref.shape[1], ref.shape[2]), F32)
+        for i in range(ref.shape[0]):
+            block = ref[i].astype(F32)
+            acc += block * block
+        return jnp.sum(acc, axis=0, keepdims=True)
+
+    total = (
+        jnp.sum(squares(ga_ref), axis=1, keepdims=True)
+        + jnp.sum(squares(gu_ref), axis=1, keepdims=True)
+        + jnp.sum(squares(gd_ref), axis=1, keepdims=True)
+    )
+    mine[0:gain_rows, :] = gain_ref[...]
+    mine[gain_rows:, :] = jnp.broadcast_to(total, (8, 128))
+    greet(
+        [((dp + k) % n_dp, me) for k in range(1, n_dp)] + [(dp, (me + k) % n) for k in range(1, n)]
+    )
+    copies = []
+    for k in range(1, n):
+        copy = remote(mine, buf.at[me], ss.at[k - 1], rs.at[k - 1], (dp, (me + k) % n))
+        copy.start()
+        copies.append(copy)
+    buf[me] = mine[...]
+    for k in range(1, n):
+        source = (me + n - k) % n
+        remote(mine, buf.at[source], ss.at[k - 1], rs.at[k - 1], (dp, source)).wait_recv()
+    acc = buf[0]
+    for j in range(1, n):
+        acc = acc + buf[j]
+    part[...] = acc
+    all_parts[dp] = acc
+    for k in range(1, n_dp):
+        copy = remote(part, all_parts.at[dp], st.at[k - 1], rt.at[k - 1], ((dp + k) % n_dp, me))
+        copy.start()
+        copies.append(copy)
+    for k in range(1, n_dp):
+        source = (dp + n_dp - k) % n_dp
+        remote(part, all_parts.at[source], st.at[k - 1], rt.at[k - 1], (source, me)).wait_recv()
+    acc = all_parts[0]
+    for j in range(1, n_dp):
+        acc = acc + all_parts[j]
+    o_ref[...] = acc
+    for copy in copies:
+        copy.wait_send()
+
+
+def total_over(ga, gu, gd, gain_part, number):
+    n_dp, n = lax.axis_size("dp"), lax.axis_size("ctx")
+    gain_rows = gain_part.size // 128
+    shape = (gain_rows + 8, 128)
+    dma = pltpu.SemaphoreType.DMA
+    out = pl.pallas_call(
+        functools.partial(total_kernel, n_dp, n),
+        out_shape=jax.ShapeDtypeStruct(shape, F32),
+        in_specs=[VMEM] * 4,
+        out_specs=VMEM,
+        scratch_shapes=[
+            pltpu.VMEM(shape, F32),
+            pltpu.VMEM((n,) + shape, F32),
+            pltpu.VMEM(shape, F32),
+            pltpu.VMEM((n_dp,) + shape, F32),
+            dma((n - 1,)),
+            dma((n - 1,)),
+            dma((n_dp - 1,)),
+            dma((n_dp - 1,)),
+        ],
+        compiler_params=params_of(number),
+        name="total",
+    )(ga, gu, gd, gain_part.reshape(gain_rows, 128))
+    return out[gain_rows, 0], out[:gain_rows].reshape(gain_part.shape)
+
+
+def adam_kernel(factor_ref, p_ref, m_ref, v_ref, ga_ref, gu_ref, gd_ref, po_ref, mo_ref, vo_ref, g_ref):
+    part = pl.program_id(0)
+    n, _, four = ga_ref.shape
+    hc = four // 4
+    fs = gd_ref.shape[2]
+
+    @pl.when(part == 0)
+    def _():
+        for matrix in range(4):
+            for c in range(n):
+                start = (matrix * n + c) * hc
+                g_ref[:, start : start + hc] = ga_ref[c, :, matrix * hc : (matrix + 1) * hc].astype(F32)
+
+    @pl.when((part == 1) | (part == 2))
+    def _():
+        for d in range(gu_ref.shape[0]):
+            g_ref[:, d * fs : (d + 1) * fs] = gu_ref[d].astype(F32)
+
+    @pl.when(part == 3)
+    def _():
+        for d in range(gd_ref.shape[0]):
+            g_ref[:, d * fs : (d + 1) * fs] = gd_ref[d].astype(F32)
+
+    clipped = g_ref[...] * factor_ref[0, 0]
+    new_p, new_m, new_v = adam_update(p_ref[...], m_ref[...], v_ref[...], clipped, RATE, DECAY)
+    po_ref[...] = new_p
+    mo_ref[...] = new_m
+    vo_ref[...] = new_v
+
+
+def adam(factor, params, first, second, ga, gu, gd):
+    rows, columns = params.shape
+    n, n_dp, fs = ga.shape[0], gd.shape[0], gd.shape[2]
+    block = min(rows, 16)
+    steps = rows // block
+    wide = pl.BlockSpec((block, columns // 4), lambda i, r: (r, i))
+    return pl.pallas_call(
+        adam_kernel,
+        grid=(4, steps),
+        out_shape=(jax.ShapeDtypeStruct(params.shape, F32),) * 3,
+        in_specs=[
+            pl.BlockSpec(memory_space=pltpu.SMEM),
+            wide,
+            wide,
+            wide,
+            pl.BlockSpec((n, block, ga.shape[2]), lambda i, r: (0, jnp.where(i == 0, r, steps - 1), 0)),
+            pl.BlockSpec(
+                (n_dp, block, fs),
+                lambda i, r: (
+                    0,
+                    jnp.where(i == 0, 0, jnp.where(i == 3, steps - 1, r)),
+                    jnp.clip(i - 1, 0, 1),
+                ),
+            ),
+            pl.BlockSpec((n_dp, block, fs), lambda i, r: (0, jnp.where(i == 3, r, 0), 0)),
+        ],
+        out_specs=(wide, wide, wide),
+        scratch_shapes=[pltpu.VMEM((block, columns // 4), F32)],
+        compiler_params=pltpu.CompilerParams(vmem_limit_bytes=48 * 1024 * 1024),
+        name="adam",
+    )(factor.reshape(1, 1), params, first, second, ga, gu, gd)
+
+
+def arrange_kernel(n, n_dp, p_ref, a_ref, g_ref, u_ref, d_ref):
+    part = pl.program_id(0)
+    hc = a_ref.shape[2] // 4
+    fs = g_ref.shape[2]
+
+    @pl.when(part == 0)
+    def _():
+        for matrix in range(4):
+            for c in range(n):
+                start = (matrix * n + c) * hc
+                a_ref[c, :, matrix * hc : (matrix + 1) * hc] = p_ref[:, start : start + hc].astype(BF)
+
+    for index, ref in ((1, g_ref), (2, u_ref), (3, d_ref)):
+
+        @pl.when(part == index)
+        def _():
+            for d in range(n_dp):
+                ref[d] = p_ref[:, d * fs : (d + 1) * fs].astype(BF)
+
+
+def arrange(params, width):
+    n_dp, n = lax.axis_size("dp"), lax.axis_size("ctx")
+    rows, columns = params.shape
+    fs, hc = columns // 4 // n_dp, width // n
+    whole = lambda shape: pl.BlockSpec(shape, lambda i: (0,) * len(shape))
+    shapes = [(n, rows, 4 * hc)] + [(n_dp, rows, fs)] * 3
+    return pl.pallas_call(
+        functools.partial(arrange_kernel, n, n_dp),
+        grid=(4,),
+        out_shape=tuple(jax.ShapeDtypeStruct(s, BF) for s in shapes),
+        in_specs=[pl.BlockSpec((rows, columns // 4), lambda i: (0, i))],
+        out_specs=tuple(whole(s) for s in shapes),
+        compiler_params=pltpu.CompilerParams(vmem_limit_bytes=48 * 1024 * 1024),
+        name="arrange",
+    )(params)
 
 
 def shards(
@@ -107,16 +783,15 @@
             values.reshape(t, n_ctx, n_dp, rows).transpose(0, 2, 1, 3).reshape(t, width)
         )
 
-    low = params.astype(BF)
-    wa = low[:, : 4 * width].reshape(rows, 4, n_ctx, hc).transpose(2, 0, 1, 3)
-    wa = lax.all_to_all(wa.reshape(n_ctx * rows, 4 * hc), "ctx", 0, 0, tiled=True)
-    wa = lax.all_gather(wa, "dp", axis=0, tiled=True)
+    wa, wg, wu, wd = arrange(params, width)
+    wgu = swap_dp(jnp.concatenate([wg, wu], axis=2), 10)
+    w_gu = lax.all_gather(wgu.reshape(n_dp * rows, 2 * fs), "ctx", axis=0, tiled=True)
+    wa, wgu = lax.optimization_barrier((wa, wgu))
+    wa, x_all = spread(wa, tokens, 1)
     w_qkv, w_o = wa[:, : 3 * hc], wa[:, 3 * hc :]
-    x_all = lax.all_gather(tokens, "ctx", axis=0, tiled=True)
-    wf = low[:, 4 * width :].reshape(rows, 3, n_dp, fs).transpose(2, 0, 1, 3)
-    wf = lax.all_to_all(wf.reshape(n_dp * rows, 3 * fs), "dp", 0, 0, tiled=True)
-    wf = lax.all_gather(wf, "ctx", axis=0, tiled=True)
-    w_gu, w_d = wf[:, : 2 * fs], wf[:, 2 * fs :]
+    wd, x_all = lax.optimization_barrier((wd, x_all))
+    w_d = lax.all_to_all(wd.reshape(n_dp * rows, fs), "dp", 0, 0, tiled=True)
+    w_d = lax.all_gather(w_d, "ctx", axis=0, tiled=True)
 
     indices = jnp.arange(seq, dtype=jnp.int32)
     owners = indices // length
@@ -158,45 +833,37 @@
     probs_low = probs.astype(BF)
     attn = jnp.einsum("hqk,hkd->hqd", probs_low, vh, preferred_element_type=F32)
     attn_low = join(attn).astype(BF)
-    branch = lax.psum_scatter(
-        dot_t(attn_low, w_o).astype(BF), "ctx", scatter_dimension=0, tiled=True
-    ).astype(F32)
+    attn_low, w_gu = lax.optimization_barrier((attn_low, w_gu))
+    branch = scatter_ctx(attn_low, w_o, 2)
     a_scale = rms_scale(branch)
     hidden1 = tokens.astype(F32) + branch * a_scale * gains[2]
 
-    h1_all = lax.all_gather(mix(hidden1.astype(BF)), "dp", axis=0, tiled=True)
+    h1_all = gather_dp(mix(hidden1.astype(BF)), 3)
     gate_up = dot(h1_all, w_gu)
     gate_pre, up_pre = gate_up[:, :fs], gate_up[:, fs:]
     gate_sig = jax.nn.sigmoid(gate_pre)
     silu_val = gate_pre * gate_sig
     inner = (silu_val * up_pre).astype(BF)
-    mlp_out = unmix(
-        lax.psum_scatter(
-            dot_t(inner, w_d).astype(BF), "dp", scatter_dimension=0, tiled=True
-        ).astype(F32)
-    )
+    mlp_out = unmix(scatter_dp(inner, w_d, 4))
     m_scale = rms_scale(mlp_out)
     result = hidden1 + mlp_out * m_scale * gains[3]
 
     g_ff_part = jnp.sum(upstream * mlp_out * m_scale, axis=0)
     d_mlp = norm_back(upstream * gains[3], mlp_out, m_scale).astype(BF)
-    d_mlp_all = lax.all_gather(mix(d_mlp), "dp", axis=0, tiled=True)
+    d_mlp_all = gather_dp(mix(d_mlp), 5)
+    d_grad = lax.psum_scatter(
+        t_dot(d_mlp_all, inner).astype(BF), "ctx", scatter_dimension=0, tiled=True
+    )
     d_inner = dot(d_mlp_all, w_d)
     d_gate = d_inner * up_pre * gate_sig * (1.0 + gate_pre * (1.0 - gate_sig))
     d_upper = d_inner * silu_val
     d_gu = jnp.concatenate([d_gate, d_upper], axis=1).astype(BF)
-    d_h1 = upstream + unmix(
-        lax.psum_scatter(
-            dot_t(d_gu, w_gu).astype(BF), "dp", scatter_dimension=0, tiled=True
-        ).astype(F32)
-    )
-    ff_grad = jnp.concatenate([t_dot(h1_all, d_gu), t_dot(d_mlp_all, inner)], axis=1).astype(BF)
+    d_h1 = upstream + unmix(scatter_dp(d_gu, w_gu, 6))
+    gu_grad = t_dot(h1_all, d_gu).astype(BF)
 
     g_attn_part = jnp.sum(d_h1 * branch * a_scale, axis=0)
     d_branch = norm_back(d_h1 * gains[2], branch, a_scale).astype(BF)
-    d_branch_all = lax.all_gather(d_branch, "ctx", axis=0, tiled=True)
-    ff_grad = lax.psum_scatter(ff_grad, "ctx", scatter_dimension=0, tiled=True)
-    ff_grad = lax.all_to_all(ff_grad, "dp", 0, 0, tiled=True)
+    d_branch_all = gather_ctx(d_branch, 7)
     d_attn = dot(d_branch_all, w_o).astype(BF)
     dh = split(d_attn)
     delta = jnp.sum(dh.astype(F32) * attn, axis=-1, keepdims=True)
@@ -217,19 +884,12 @@
     d_k_pre = k_scale * (e_k - k_pre * k_scale * k_scale * means[:, 1:])
     d_qkv = jnp.concatenate([d_q_pre, d_k_pre, d_value], axis=1).astype(BF)
     attn_grad = jnp.concatenate([t_dot(x_all, d_qkv), t_dot(d_branch_all, attn_low)], axis=1)
-    attn_grad = lax.psum_scatter(attn_grad.astype(BF), "dp", scatter_dimension=0, tiled=True)
-    attn_grad = lax.all_to_all(attn_grad, "ctx", 0, 0, tiled=True)
-    d_input = d_h1 + lax.psum_scatter(
-        dot_t(d_qkv, w_qkv).astype(BF), "ctx", scatter_dimension=0, tiled=True
-    ).astype(F32)
-
-    grad = jnp.concatenate(
-        [
-            attn_grad.reshape(n_ctx, rows, 4, hc).transpose(1, 2, 0, 3).reshape(rows, 4 * width),
-            ff_grad.reshape(n_dp, rows, 3, fs).transpose(1, 2, 0, 3).reshape(rows, 3 * ff),
-        ],
-        axis=1,
-    ).astype(F32)
+    d_grad = lax.all_to_all(d_grad, "dp", 0, 0, tiled=True).reshape(n_dp, rows, fs)
+    gu_grad = lax.psum_scatter(gu_grad, "ctx", scatter_dimension=0, tiled=True)
+    gu_grad = lax.all_to_all(gu_grad, "dp", 0, 0, tiled=True).reshape(n_dp, rows, 2 * fs)
+    attn_grad, d_x = collect(attn_grad.astype(BF), d_qkv, w_qkv, 9)
+    d_input = d_h1 + d_x
+
     gain_part = jnp.stack(
         [
             lax.dynamic_update_slice(jnp.zeros(width, F32), g_q_part, (me_ctx * hc,)),
@@ -239,11 +899,11 @@
         ],
         axis=0,
     )
-    square_total, gain_total = lax.psum((jnp.sum(grad * grad), gain_part), ("dp", "ctx"))
+    square_total, gain_total = total_over(attn_grad, gu_grad, d_grad, gain_part, 11)
     grad_norm = jnp.sqrt(square_total + jnp.sum(gain_total * gain_total))
     factor = CLIP / (grad_norm + 1e-06)
-    new_params, new_first, new_second = adam_update(
-        params, first_moment, second_moment, grad * factor, RATE, DECAY
+    new_params, new_first, new_second = adam(
+        factor, params, first_moment, second_moment, attn_grad, gu_grad, d_grad
     )
     new_gains, new_gains_first, new_gains_second = adam_update(
         gains, gains_first, gains_second, gain_total * factor, GAIN_RATE, 0.0

time: 1180 us -> 868 us (0.74)
  waiting for transfers between devices: 734 us -> 2.26 us
  Pallas kernels: 0 us -> 566 us
  blocking collectives: 104 us -> 54.4 us
  other arithmetic: 94.9 us -> 53.3 us
  matrix products: 111 us -> 77.6 us
  local copies, waits for them, and re-layouts: 94.3 us -> 64.1 us
  starting transfers between devices: 10.6 us -> 26 us
    pallas_call x0 -> x12, Pallas kernels: none -> 566 us  [the longest x1 119 us: spread(): pl.pallas_call(functools.partial(spread_kernel, n_dp, n), out_shape=(jax....]
    all_gather x6 -> x2, waiting for transfers between devices: 318 us -> 0.01 us  [the longest x1 0.01 us: shards(): lax.all_gather(wgu.reshape(n_dp * rows, 2 * fs), 'ctx', axis=0, tiled=True)]
    reduce_scatter x6 -> x2, waiting for transfers between devices: 271 us -> 2.18 us  [the longest x1 2.18 us: shards(): gu_grad = lax.psum_scatter(gu_grad, 'ctx', scatter_dimension=0, tiled=True)]
    all_to_all x2, waiting for transfers between devices: 145 us -> 0.01 us  [the longest x1 0.01 us: shards(): lax.all_to_all(d_grad, 'dp', 0, 0, tiled=True).reshape(n_dp, rows, fs)]
    psum x1 -> x0, blocking collectives: 37.6 us -> none  [shards(): lax.psum((jnp.sum(grad * grad), gain_part), ('dp', 'ctx'))]
    dot_general x4 -> x0, matrix products: 35.1 us -> none  [dot_t(): lax.dot_general(a, b, (((1,), (1,)), ((), ())), preferred_element_type=F32)]
    reshape x6 -> x4, local copies, waits for them, and re-layouts: 30 us -> 3.53 us  [the longest x1 2.06 us: join(): return v.transpose(1, 0, 2).reshape(seq, hc)]
    sub x2 -> x1, other arithmetic: 20.7 us -> 0.69 us  [adam_update(): weight - rate * (first_hat / (jnp.sqrt(second_hat) + ADAM_EPS) + decay *...]
  transfers between devices with their start and end apart: 14 -> 6, of which waited for: 12 -> 1; matrix products, arithmetic and copies ran while one was open for 10% -> 19% of each run, Pallas kernels for 0% -> 45%
where the time goes in v2:
time: 868 us; the launch traced here: 861 us
  Pallas kernels  566 us (65%)
  matrix products  77.6 us (9%)
  local copies, waits for them, and re-layouts  64.1 us (7%)
  blocking collectives  54.4 us (6%)
  other arithmetic  53.3 us (6%)
  starting transfers between devices  26 us (3%)
  between operations  17.9 us (2%)
    pallas_call x1, Pallas kernels, spread(): pl.pallas_call(functools.partial(spread_kernel, n_dp, n), out_shape=(jax....  119 us
    pallas_call x1, Pallas kernels, collect(): pl.pallas_call(functools.partial(collect_kernel, n_dp, n), out_shape=(jax...  111 us
    pallas_call x2, Pallas kernels, scatter_dp(): pl.pallas_call(functools.partial(scatter_dp_kernel, n), out_shape=jax.Sha...  96.2 us
    pallas_call x2, Pallas kernels, gather_dp(): pl.pallas_call(functools.partial(gather_dp_kernel, n), out_shape=jax.Shap...  88 us
    pallas_call x1, Pallas kernels, swap_dp(): pl.pallas_call(functools.partial(swap_dp_kernel, n), out_shape=jax.ShapeD...  39.9 us
    pallas_call x1, Pallas kernels, gather_ctx(): pl.pallas_call(functools.partial(gather_ctx_kernel, n), out_shape=jax.Sha...  39.3 us
    dot_general x4, matrix products, dot(): return jnp.dot(a, b, preferred_element_type=F32)  36.4 us
    pallas_call x1, Pallas kernels, scatter_ctx(): pl.pallas_call(functools.partial(scatter_ctx_kernel, n), out_shape=jax.Sh...  30.3 us
  transfers between devices with their start and end apart: 6, of which 1 were waited for; matrix products, arithmetic and copies ran while one was open for 19% of the time, Pallas kernels for 45%

profile of v2, /device:TPU:0, one launch (start us, length us, event | category | flops | bytes accessed | tf_op | source)
XLA Modules:
  0.0 861.5 jit_solution(5641140926987778476)
XLA Ops:
  7.2 4.2 arrange.1
  11.7 39.9 %swap_dp.1 = bf16[4,64,4096]{2,1,0:T(8,128)(2,1)} custom-call(bf16[4,64,4096]{2,1,0:T(8,128)(2,1)S(1)} %pad_maximum_fusion.2.x_ref), custom_call_target="tpu_custom_call" | custom-call | tf_op jit(solution)/shard_map/swap_dp/pallas_call | solution.py:365
  51.7 118.8 %spread.1 = (bf16[4,8,64,1024]{3,2,1,0:T(8,128)(2,1)S(1)}, bf16[8,128,2048]{2,1,0:T(8,128)(2,1)}) custom-call(bf16[8,64,1024]{2,1,0:T(8,128)(2,1)S(1)} %get-tuple-element.29.w_ref, bf16[128,2048]{1,0:T(8,128)(2,1)S(1)} %bitcast.174), custom_call_target="tpu_custom_call" | custom-call | tf_op jit(solution)/shard_map/spread/pallas_call | solution.py:467
  170.6 1.9 copy-done.5
  172.5 28.4 %all_to_all.27 = bf16[4,64,2048]{2,1,0:T(8,128)(2,1)} all-to-all(bf16[4,64,2048]{2,1,0:T(8,128)(2,1)S(1)} %get-tuple-element.35), channel_id=1, replica_groups=mesh['dp'=4,'ctx'=8] {'dp'}, dimensions={0} | all-to-all | bytes 2097152 | tf_op jit(solution)/shard_map/all_to_all | solution.py:793
  201.0 6.2 fusion.45
  207.5 2.2 slice.120.w_ref
  209.7 1.5 fusion.48
  211.2 1.6 copy.203
  212.8 1.5 squeeze.18
  214.3 1.6 copy.204
  215.8 1.5 squeeze.19
  217.3 1.8 multiply_reduce_fusion
  219.1 13.1 %psum.14 = f32[1024,2]{0,1:T(2,128)S(1)} all-reduce(f32[1024,2]{0,1:T(2,128)S(1)} %multiply_reduce_fusion), channel_id=1, replica_groups=mesh['dp'=4,'ctx'=8] {'ctx'}, use_global_device_ids=true, to_apply=%region_2.3 | all-reduce | flops 2048 | bytes 16384 | tf_op jit(solution)/shard_map/psum | solution.py:813
  232.4 3.0 fusion.29
  235.4 2.1 fusion.22
  238.7 2.0 compare_and_fusion
  242.0 7.5 fusion.52
  249.5 4.7 fusion.7
  254.2 2.2 fusion.53
  258.0 30.3 %scatter_ctx.1 = f32[128,2048]{1,0:T(8,128)S(1)} custom-call(bf16[1024,256]{1,0:T(8,128)(2,1)S(1)} %copy.201.a_ref, bf16[2048,256]{1,0:T(8,128)(2,1)S(1)} %slice.120.w_ref), custom_call_target="tpu_custom_call" | custom-call | tf_op jit(solution)/shard_map/scatter_ctx/pallas_call | solution.py:274
  289.3 38.8 %gather_dp.2 = bf16[4,128,2048]{2,1,0:T(8,128)(2,1)S(1)} custom-call(bf16[128,2048]{1,0:T(8,128)(2,1)S(1)} %copy.160.x_ref), custom_call_target="tpu_custom_call" | custom-call | tf_op jit(solution)/shard_map/gather_dp/pallas_call | solution.py:162
  328.1 12.8 %fusion.54 = f32[512,4096]{1,0:T(8,128)S(1)} fusion(bf16[512,2048]{1,0:T(8,128)(2,1)S(1)} %bitcast.179, bf16[2048,4096]{1,0:T(8,128)(2,1)} %all-gather.3.cloned.1.call-done.w_ref), kind=kOutput, calls=%fused_computation.136 | convolution fusion | flops 8589934592 | bytes 27262976 | tf_op jit(solution)/shard_map/dot_general | solution.py:69
  340.9 3.4 copy-done.25
  344.3 2.6 multiply_convert_fusion.3.a_ref
  346.9 44.7 %scatter_dp.2 = f32[128,2048]{1,0:T(8,128)} custom-call(bf16[512,2048]{1,0:T(8,128)(2,1)} %multiply_convert_fusion.3.a_ref, bf16[2048,2048]{1,0:T(8,128)(2,1)} %all-gather.5.cloned.1.call-done.w_ref), custom_call_target="tpu_custom_call" | custom-call | tf_op jit(solution)/shard_map/scatter_dp/pallas_call | solution.py:327
  391.6 1.5 copy.161
  393.5 1.9 multiply_reduce_fusion.1
  397.8 49.2 %gather_dp.3 = bf16[4,128,2048]{2,1,0:T(8,128)(2,1)} custom-call(bf16[128,2048]{1,0:T(8,128)(2,1)S(1)} %copy.167.x_ref), custom_call_target="tpu_custom_call" | custom-call | tf_op jit(solution)/shard_map/gather_dp/pallas_call | solution.py:162
  447.0 10.2 %convolution_convert_fusion.1 = bf16[2048,2048]{1,0:T(8,128)(2,1)} fusion(bf16[512,2048]{1,0:T(8,128)(2,1)} %bitcast.32, bf16[512,2048]{1,0:T(8,128)(2,1)} %multiply_convert_fusion.3.a_ref), kind=kOutput, calls=%fused_computation.4 | convolution fusion | flops 4299161600 | bytes 12582912 | tf_op jit(solution)/shard_map/dot_general | solution.py:77
  457.2 13.8 %multiply_convert_fusion.2 = (bf16[512,2048]{1,0:T(8,128)(2,1)S(1)}, bf16[512,2048]{1,0:T(8,128)(2,1)S(1)}) fusion(f32[512,4096]{1,0:T(8,128)} %copy-done.25, bf16[512,2048]{1,0:T(8,128)(2,1)} %bitcast.32, bf16[2048,2048]{1,0:T(8,128)(2,1)} %all-gather.5.cloned.1.call-done.w_ref), kind=kOutput, calls=%fused_computation.10 | convolution fusion | flops 4308598784 | bytes 23068672 | tf_op jit(solution)/shard_map/dot_general | solution.py:69
  473.1 12.9 %convolution_convert_fusion = bf16[2048,4096]{1,0:T(8,128)(2,1)} fusion(bf16[512,2048]{1,0:T(8,128)(2,1)S(1)} %bitcast.180, bf16[512,2048]{1,0:T(8,128)(2,1)S(1)} %get-tuple-element.49, bf16[512,2048]{1,0:T(8,128)(2,1)S(1)} %get-tuple-element.48), kind=kOutput, calls=%fused_computation.1 | convolution fusion | flops 8606711808 | bytes 23068672 | tf_op jit(solution)/shard_map/dot_general | solution.py:77
  486.0 4.1 slice.109.w_ref
  491.2 2.5 pad_maximum_fusion.a_ref
  493.7 51.5 %scatter_dp.3 = f32[128,2048]{1,0:T(8,128)} custom-call(bf16[512,4096]{1,0:T(8,128)(2,1)} %pad_maximum_fusion.a_ref, bf16[2048,4096]{1,0:T(8,128)(2,1)} %all-gather.3.cloned.1.call-done.w_ref), custom_call_target="tpu_custom_call" | custom-call | tf_op jit(solution)/shard_map/scatter_dp/pallas_call | solution.py:327
  545.2 1.8 copy.168
  548.1 1.8 copy.170
  549.9 3.1 copy.163
  553.3 2.7 multiply_convert_fusion.4
  556.0 39.3 %gather_ctx.1 = bf16[8,128,2048]{2,1,0:T(8,128)(2,1)S(1)} custom-call(bf16[128,2048]{1,0:T(8,128)(2,1)S(1)} %get-tuple-element.60.x_ref), custom_call_target="tpu_custom_call" | custom-call | tf_op jit(solution)/shard_map/gather_ctx/pallas_call | solution.py:203
  595.3 3.5 multiply_reduce_fusion.5
  599.8 1.4 multiply_convert_fusion
  601.2 2.0 fusion.8
  608.2 21.2 %all-to-all-start.2 = ((bf16[4,64,2048]{2,1,0:T(8,128)(2,1)}), bf16[4,64,2048]{2,1,0:T(8,128)(2,1)S(1)}, u32[]{:S(2)}, u32[]{:S(2)}) async-start(bf16[4,64,2048]{2,1,0:T(8,128)(2,1)} %bitcast.202), calls=%async_computation.4 | async-start | bytes 2097152 | tf_op jit(solution)/shard_map/all_to_all | solution.py:887
  630.8 3.1 copy.177
  633.8 3.1 concatenate.44
  637.0 3.0 copy.181
  640.0 3.1 concatenate.45
  643.1 1.4 multiply_reduce_fusion.4
  644.6 1.4 multiply_reduce_fusion.3
  646.2 4.6 convolution_convert_fusion.4
  650.8 2.1 copy.202
  652.8 6.4 copy.184
  659.3 2.1 fusion.21
  661.4 2.1 fusion.10
  663.5 2.2 reduce-scatter.3.cloned.1.call-done
  665.7 4.6 all-to-all-start.1
  670.3 12.9 %psum.15 = f32[1024,2]{0,1:T(2,128)S(1)} all-reduce(f32[1024,2]{0,1:T(2,128)S(1)} %pad_maximum_fusion.7), channel_id=1, replica_groups=mesh['dp'=4,'ctx'=8] {'ctx'}, use_global_device_ids=true, to_apply=%region_12.13 | all-reduce | flops 2048 | bytes 16384 | tf_op jit(solution)/shard_map/psum | solution.py:881
  683.3 2.6 fusion.20
  689.7 4.0 convolution_convert_fusion.2
  693.7 2.6 pad_maximum_fusion.1.g_ref
  696.3 111.2 %collect.1 = (bf16[8,64,1024]{2,1,0:T(8,128)(2,1)S(1)}, f32[128,2048]{1,0:T(8,128)S(1)}) custom-call(bf16[4,8,64,1024]{3,2,1,0:T(8,128)(2,1)} %pad_maximum_fusion.1.g_ref, bf16[1024,768]{1,0:T(8,128)(2,1)S(1)} %pad_maximum_fusion.3.a_ref, bf16[2048,768]{1,0:T(8,128)(2,1)} %slice.109.w_ref), custom_call_target="tpu_custom_call" | custom-call | tf_op jit(solution)/shard_map/collect/pallas_call | solution.py:541
  810.6 13.9 %total.1 = f32[72,128]{1,0:T(8,128)S(1)} custom-call(bf16[8,64,1024]{2,1,0:T(8,128)(2,1)S(1)} %copy-done.3, bf16[4,64,4096]{2,1,0:T(8,128)(2,1)S(1)} %all-to-all-done.1.gu_ref, bf16[4,64,2048]{2,1,0:T(8,128)(2,1)S(1)} %all-to-all-done.2.gd_ref, f32[64,128]{1,0:T(8,128)S(1)} %reshape.430.gain_ref), custom_call_target="tpu_custom_call" | custom-call | tf_op jit(solution)/shard_map/total/pallas_call | solution.py:628
  829.1 24.3 %adam.1 = (f32[64,32768]{1,0:T(8,128)}, f32[64,32768]{1,0:T(8,128)}, f32[64,32768]{1,0:T(8,128)}) custom-call(f32[1,1]{1,0:T(1,128)} %bitcast.65.factor_ref, f32[64,32768]{1,0:T(8,128)} %p_ref.3, f32[64,32768]{1,0:T(8,128)} %m_ref.1, f32[64,32768]{1,0:T(8,128)} %v_ref.1, bf16[8,64,1024]{2,1,0:T(8,128)(2,1)S(1)} %copy-done.4, ...), custom_call_target="tpu_custom_call" | custom-call | tf_op jit(solution)/shard_map/adam/pallas_call | solution.py:685
  (183 shorter events, 30.3 us)
Async XLA Ops:
  7.2 250.9 %all-gather.3.cloned.1.call-start = ((), (), s32[]{:S(2)}) async-start(), calls=%async_computation.5 | async-start | bytes 18874368 | tf_op jit(solution)/shard_map/all_gather | solution.py:788
  11.7 40.0 %copy-start.1 = (bf16[1,128,2048]{2,1,0:T(8,128)(2,1)S(1)}, bf16[1,128,2048]{2,1,0:T(8,128)(2,1)}, u32[]{:S(2)}) copy-start(bf16[1,128,2048]{2,1,0:T(8,128)(2,1)} %param.10) | copy-start | bytes 1572868
  51.7 295.2 %all-gather.5.cloned.1.call-start = ((), (), s32[]{:S(2)}) async-start(), calls=%async_computation.6 | async-start | bytes 9437184 | tf_op jit(solution)/shard_map/all_gather | solution.py:794
  170.6 1.9 copy-start.5
  201.0 407.2 %reduce-scatter.5.cloned.1.call-start = ((), (), s32[]{:S(2)}) async-start(), calls=%async_computation.8 | async-start | bytes 9437184 | tf_op jit(solution)/shard_map/reduce_scatter | solution.py:854
  207.3 3.9 copy-start.29
  207.5 46.7 %copy-start.39 = (bf16[1024,256]{0,1:T(8,128)(2,1)}, bf16[1024,256]{0,1:T(8,128)(2,1)S(1)}, u32[]{:S(2)}) copy-start(bf16[1024,256]{0,1:T(8,128)(2,1)S(1)} %slice.162) | copy-start | bytes 1572868
  212.7 1.5 copy-start.14
  212.7 19.5 %copy-start.49 = (f32[4,2048]{1,0:T(4,128)S(1)}, f32[4,2048]{1,0:T(4,128)}, u32[]{:S(2)}) copy-start(f32[4,2048]{1,0:T(4,128)} %param.17) | copy-start | bytes 98308
  212.7 19.5 %copy-start.53 = (s32[8]{0:T(128)S(1)}, s32[8]{0:T(128)}, u32[]{:S(2)}) copy-start(s32[8]{0:T(128)} %param.13) | copy-start | bytes 100
  215.8 21.7 %copy-start.11 = (f32[1024,1,256]{2,0,1:T(8,128)}, f32[1024,1,256]{2,0,1:T(8,128)S(1)}, u32[]{:S(2)}) copy-start(f32[1024,1,256]{2,0,1:T(8,128)S(1)} %copy.204) | copy-start | bytes 3145732
  235.4 2.9 copy-start.34
  237.5 1.2 copy-start.52
  238.3 2.4 copy-start.32
  238.3 3.7 copy-start.30
  238.7 2.0 copy-start.36
  254.2 2.3 copy-start.10
  254.2 2.7 copy-start.26
  256.7 32.3 %copy-start.8 = (bf16[1024,256]{1,0:T(8,128)(2,1)}, bf16[1024,256]{1,0:T(8,128)(2,1)S(1)}, u32[]{:S(2)}) copy-start(bf16[1024,256]{1,0:T(8,128)(2,1)S(1)} %copy.201.a_ref) | copy-start | bytes 1572868
  328.1 12.8 %copy-start.6 = (bf16[4,128,2048]{2,1,0:T(8,128)(2,1)}, bf16[4,128,2048]{2,1,0:T(8,128)(2,1)S(1)}, u32[]{:S(2)}) copy-start(bf16[4,128,2048]{2,1,0:T(8,128)(2,1)S(1)} %gather_dp.2) | copy-start | bytes 6291460
  340.9 3.4 copy-start.25
  393.1 2.2 copy-start.24
  457.2 208.5 %reduce-scatter.3.cloned.1.call-start = ((), (), s32[]{:S(2)}) async-start(), calls=%async_computation.7 | async-start | bytes 18874368 | tf_op jit(solution)/shard_map/reduce_scatter | solution.py:888
  457.2 15.9 %copy-start.7 = (bf16[4,128,2048]{2,1,0:T(8,128)(2,1)S(1)}, bf16[4,128,2048]{2,1,0:T(8,128)(2,1)}, u32[]{:S(2)}) copy-start(bf16[4,128,2048]{2,1,0:T(8,128)(2,1)} %copy-done.6) | copy-start | bytes 6291460
  471.1 1.3 copy-start.43
  471.1 2.0 copy-start.45
  486.0 5.2 copy-start.44
  486.0 5.2 copy-start.46
  545.2 7.8 copy-start.27
  549.8 6.2 copy-start.22
  556.0 39.3 %copy-start.47 = (f32[2,1024,128]{1,2,0:T(8,128)S(1)}, f32[2,1024,128]{1,2,0:T(8,128)}, u32[]{:S(2)}) copy-start(f32[2,1024,128]{1,2,0:T(8,128)} %get-tuple-element.83) | copy-start | bytes 3145732
  556.0 42.9 %slice-start = ((s8[8388608]{0:T(1024)(128)(4,1)}), s8[4194304]{0:T(1024)(128)(4,1)S(1)}, s32[]{:S(2)}) async-start(s8[8388608]{0:T(1024)(128)(4,1)} %bitcast.185), calls=%async_computation.9 | async-start | bytes 8388608
  595.3 3.6 copy-start
  595.3 4.3 slice-start.1
  595.3 4.4 copy-start.40
  598.9 2.2 copy-start.48
  599.8 1.4 copy-start.31
  599.8 1.4 copy-start.33
  601.2 2.0 copy-start.37
  603.2 1.3 copy-start.35
  603.2 1.3 copy-start.41
  605.5 0.9 copy-start.20
  605.5 1.3 copy-start.21
  605.5 23.9 %copy-start.18 = (f32[1024,2,64]{2,0,1:T(8,128)}, f32[1024,2,64]{2,0,1:T(8,128)S(1)}, u32[]{:S(2)}) copy-start(f32[1024,2,64]{2,0,1:T(8,128)S(1)} %get-tuple-element.63) | copy-start | bytes 1572868
  605.5 25.2 %copy-start.16 = (f32[1024,2,64]{2,0,1:T(8,128)}, f32[1024,2,64]{2,0,1:T(8,128)S(1)}, u32[]{:S(2)}) copy-start(f32[1024,2,64]{2,0,1:T(8,128)S(1)} %get-tuple-element.62) | copy-start | bytes 1572868
  608.2 55.3 %all-to-all-start.2 = ((bf16[4,64,2048]{2,1,0:T(8,128)(2,1)}), bf16[4,64,2048]{2,1,0:T(8,128)(2,1)S(1)}, u32[]{:S(2)}, u32[]{:S(2)}) async-start(bf16[4,64,2048]{2,1,0:T(8,128)(2,1)} %bitcast.202), calls=%async_computation.4 | async-start | bytes 2097152 | tf_op jit(solution)/shard_map/all_to_all | solution.py:887
  630.7 12.4 %copy-start.15 = (f32[1024,1,256]{2,0,1:T(8,128)S(1)}, f32[1024,1,256]{2,0,1:T(8,128)}, u32[]{:S(2)}) copy-start(f32[1024,1,256]{2,0,1:T(8,128)} %copy-done.14) | copy-start | bytes 3145732
  633.8 10.8 %copy-start.12 = (f32[1024,1,256]{2,0,1:T(8,128)S(1)}, f32[1024,1,256]{2,0,1:T(8,128)}, u32[]{:S(2)}) copy-start(f32[1024,1,256]{2,0,1:T(8,128)} %copy-done.11) | copy-start | bytes 3145732
  665.7 143.7 %all-to-all-start.1 = ((bf16[4,64,4096]{2,1,0:T(8,128)(2,1)}), bf16[4,64,4096]{2,1,0:T(8,128)(2,1)S(1)}, u32[]{:S(2)}, u32[]{:S(2)}) async-start(bf16[4,64,4096]{2,1,0:T(8,128)(2,1)} %bitcast.199), calls=%async_computation.2 | async-start | bytes 4194304 | tf_op jit(solution)/shard_map/all_to_all | solution.py:889
  683.2 2.7 copy-start.13
  683.2 2.7 copy-start.17
  683.2 2.8 copy-start.19
  683.3 3.4 copy-start.42
  685.9 1.1 copy-start.9
  685.9 2.4 copy-start.38
  686.8 2.9 copy-start.54
  696.3 112.1 %copy-start.23 = (f32[128,2048]{1,0:T(8,128)S(1)}, f32[128,2048]{1,0:T(8,128)}, u32[]{:S(2)}) copy-start(f32[128,2048]{1,0:T(8,128)} %copy-done.22) | copy-start | bytes 3145732
  696.3 112.1 %copy-start.28 = (bf16[1,128,2048]{2,1,0:T(8,128)(2,1)S(1)}, bf16[1,128,2048]{2,1,0:T(8,128)(2,1)}, u32[]{:S(2)}) copy-start(bf16[1,128,2048]{2,1,0:T(8,128)(2,1)} %param.11) | copy-start | bytes 1572868
  807.4 1.0 copy-start.2
  808.4 18.7 %copy-start.50 = (f32[4,2048]{1,0:T(4,128)S(1)}, f32[4,2048]{1,0:T(4,128)}, u32[]{:S(2)}) copy-start(f32[4,2048]{1,0:T(4,128)} %param.18) | copy-start | bytes 98308
  808.4 18.7 %copy-start.51 = (f32[4,2048]{1,0:T(4,128)S(1)}, f32[4,2048]{1,0:T(4,128)}, u32[]{:S(2)}) copy-start(f32[4,2048]{1,0:T(4,128)} %param.19) | copy-start | bytes 98308
  809.4 1.2 copy-start.3
  827.8 1.2 copy-start.4
Sparse Core Ops, SparseCore 0:
  51.8 125.6 all-gather.2
  201.1 53.5 all-gather.4
  457.3 69.0 reduce-scatter.4
  530.3 135.3 reduce-scatter.2

commit v3 on v2

--- a/solution.py
+++ b/solution.py
@@ -42,20 +42,6 @@
     return (jnp.cos(angles), jnp.sin(angles))
 
 
-def rotate(values, cos_tab, sine_tab):
-    shape = values.shape
-    values = values.reshape(shape[0], shape[1] // HD, HD)
-    half_size = HD // 2
-    first_half = values[..., :half_size]
-    second_half = values[..., half_size:]
-    cos_b = cos_tab[:, None, :]
-    sine_b = sine_tab[:, None, :]
-    return jnp.concatenate(
-        [first_half * cos_b - second_half * sine_b, second_half * cos_b + first_half * sine_b],
-        axis=-1,
-    ).reshape(shape)
-
-
 def adam_update(weight, first_in, second_in, clipped, rate, decay):
     new_first = BETA1 * first_in + (1.0 - BETA1) * clipped
     new_second = BETA2 * second_in + (1.0 - BETA2) * clipped * clipped
@@ -171,50 +157,7 @@
     return out.reshape((n * x.shape[0],) + x.shape[1:])
 
 
-def gather_ctx_kernel(n, x_ref, o_ref, local, ss, rs, fs, fr):
-    dp, me = lax.axis_index("dp"), lax.axis_index("ctx")
-    half, parity, pair, partner, ahead, behind = pairs_of(n, me)
-    greet([(dp, partner)] + [(dp, a) for a in ahead])
-    own = pltpu.make_async_copy(x_ref, o_ref.at[me], local)
-    sends = [
-        remote(x_ref, o_ref.at[me], ss.at[k], rs.at[k], (dp, a))
-        for k, a in enumerate(ahead + [partner])
-    ]
-    for copy in sends:
-        copy.start()
-    own.start()
-    forwards = []
-    for k, b in enumerate(behind):
-        remote(x_ref, o_ref.at[b], ss.at[k], rs.at[k], (dp, b)).wait_recv()
-        forward = remote(o_ref.at[b], o_ref.at[b], fs.at[k], fr.at[k], (dp, partner))
-        forward.start()
-        forwards.append(forward)
-    sends[-1].wait_recv()
-    for forward in forwards:
-        forward.wait()
-    for copy in sends:
-        copy.wait_send()
-    own.wait()
-
-
-def gather_ctx(x, number):
-    n = lax.axis_size("ctx")
-    half = n // 2
-    out = pl.pallas_call(
-        functools.partial(gather_ctx_kernel, n),
-        out_shape=jax.ShapeDtypeStruct((n,) + x.shape, x.dtype),
-        in_specs=[ANY],
-        out_specs=ANY,
-        scratch_shapes=[pltpu.SemaphoreType.DMA]
-        + [pltpu.SemaphoreType.DMA((half,))] * 2
-        + [pltpu.SemaphoreType.DMA((half - 1,))] * 2,
-        compiler_params=params_of(number),
-        name="gather_ctx",
-    )(x)
-    return out.reshape((n * x.shape[0],) + x.shape[1:])
-
-
-def reduce_ctx(n, dp, me, a_ref, w_ref, o_ref, sa, ra, sb, rb, s1, r1, s2, r2):
+def reduce_ctx(n, dp, me, a_ref, w_ref, cols, o_ref, sa, ra, sb, rb, s1, r1, s2, r2):
     half, parity, pair, partner, ahead, behind = pairs_of(n, me)
     length, width = o_ref.shape
     tile = width // 4
@@ -225,7 +168,7 @@
         @pl.loop(0, 4)
         def _(j):
             part = pl.ds(pl.multiple_of(j * tile, tile), tile)
-            store(part, dot_t(a_ref[rows, :], w_ref[part, :]))
+            store(part, dot_t(a_ref[rows, :], w_ref[part, cols]))
 
     first, second = [], []
     for k in range(half):
@@ -259,39 +202,8 @@
     return first + second
 
 
-def scatter_ctx_kernel(n, a_ref, w_ref, o_ref, sa, ra, sb, rb, s1, r1, s2, r2):
-    dp, me = lax.axis_index("dp"), lax.axis_index("ctx")
-    half, parity, pair, partner, ahead, behind = pairs_of(n, me)
-    greet([(dp, partner)] + [(dp, a) for a in ahead])
-    for copy in reduce_ctx(n, dp, me, a_ref, w_ref, o_ref, sa, ra, sb, rb, s1, r1, s2, r2):
-        copy.wait_send()
-
-
-def scatter_ctx(a, w, number):
-    n = lax.axis_size("ctx")
-    half, length, width = n // 2, a.shape[0] // n, w.shape[0]
-    dma = pltpu.SemaphoreType.DMA
-    return pl.pallas_call(
-        functools.partial(scatter_ctx_kernel, n),
-        out_shape=jax.ShapeDtypeStruct((length, width), F32),
-        in_specs=[VMEM, VMEM],
-        out_specs=VMEM,
-        scratch_shapes=[
-            pltpu.VMEM((half, length, width), BF),
-            pltpu.VMEM((half, length, width), BF),
-            pltpu.VMEM((half - 1, length, width), BF),
-            pltpu.VMEM((half - 1, length, width), BF),
-            dma((half,)),
-            dma((half,)),
-            dma((half - 1,)),
-            dma((half - 1,)),
-        ],
-        compiler_params=params_of(number),
-        name="scatter_ctx",
-    )(a, w)
-
-
-def scatter_dp_kernel(n, a_ref, w_ref, o_ref, sa, ra, ss, rs):
+def scatter_dp_kernel(n, pairs, *refs):
+    operands, (o_ref, sa, ra, ss, rs) = refs[: 2 * pairs], refs[2 * pairs :]
     me, ctx = lax.axis_index("dp"), lax.axis_index("ctx")
     length, width = o_ref.shape
     tile = width // 4
@@ -302,7 +214,10 @@
         @pl.loop(0, 4)
         def _(j):
             part = pl.ds(pl.multiple_of(j * tile, tile), tile)
-            out[:, part] = dot_t(a_ref[rows, :], w_ref[part, :]).astype(out.dtype)
+            value = dot_t(operands[0][rows, :], operands[1][part, :])
+            for i in range(1, pairs):
+                value += dot_t(operands[2 * i][rows, :], operands[2 * i + 1][part, :])
+            out[:, part] = value.astype(out.dtype)
 
     greet([((me + k) % n, ctx) for k in range(1, n)])
     copies = []
@@ -320,14 +235,14 @@
         copy.wait_send()
 
 
-def scatter_dp(a, w, number):
+def scatter_dp(operands, number):
     n = lax.axis_size("dp")
-    length, width = a.shape[0] // n, w.shape[0]
+    length, width = operands[0].shape[0] // n, operands[1].shape[0]
     dma = pltpu.SemaphoreType.DMA
     return pl.pallas_call(
-        functools.partial(scatter_dp_kernel, n),
+        functools.partial(scatter_dp_kernel, n, len(operands) // 2),
         out_shape=jax.ShapeDtypeStruct((length, width), F32),
-        in_specs=[VMEM, VMEM],
+        in_specs=[VMEM] * len(operands),
         out_specs=VMEM,
         scratch_shapes=[
             pltpu.VMEM((n - 1, length, width), BF),
@@ -337,148 +252,87 @@
         ],
         compiler_params=params_of(number, 56),
         name="scatter_dp",
-    )(a, w)
-
-
-def swap_dp_kernel(n, x_ref, o_ref, local, ss, rs):
-    me, ctx = lax.axis_index("dp"), lax.axis_index("ctx")
-    greet([((me + k) % n, ctx) for k in range(1, n)])
-    own = pltpu.make_async_copy(x_ref.at[me], o_ref.at[me], local)
-    copies = []
-    for k in range(1, n):
-        to = (me + k) % n
-        copy = remote(x_ref.at[to], o_ref.at[me], ss.at[k - 1], rs.at[k - 1], (to, ctx))
-        copy.start()
-        copies.append(copy)
-    own.start()
-    for k in range(1, n):
-        source = (me + n - k) % n
-        remote(x_ref.at[me], o_ref.at[source], ss.at[k - 1], rs.at[k - 1], (source, ctx)).wait_recv()
-    for copy in copies:
-        copy.wait_send()
-    own.wait()
-
-
-def swap_dp(x, number):
-    n = lax.axis_size("dp")
-    dma = pltpu.SemaphoreType.DMA
-    return pl.pallas_call(
-        functools.partial(swap_dp_kernel, n),
-        out_shape=jax.ShapeDtypeStruct(x.shape, x.dtype),
-        in_specs=[ANY],
-        out_specs=ANY,
-        scratch_shapes=[dma, dma((n - 1,)), dma((n - 1,))],
-        compiler_params=params_of(number),
-        name="swap_dp",
-    )(x)
-
-
-def spread_kernel(n_dp, n, w_ref, x_ref, o_ref, y_ref, local, sa, ra, ss, rs, fs, fr, sr, rr, sl, rl):
+    )(*operands)
+
+
+def start_kernel(
+    n_dp, n, g_ref, w_ref, x_ref, h_ref, o_ref, y_ref, local, sg, rg, sa, ra, ss, rs, fs, fr
+):
     dp, me = lax.axis_index("dp"), lax.axis_index("ctx")
     half, parity, pair, partner, ahead, behind = pairs_of(n, me)
     greet(
-        [((dp + 1) % n_dp, me), ((dp + n_dp - 1) % n_dp, me)]
-        + [(dp, (me + k) % n) for k in range(1, n)]
-    )
-    own_w = pltpu.make_async_copy(w_ref.at[me], o_ref.at[dp, me], local.at[0])
-    own_x = pltpu.make_async_copy(x_ref, y_ref.at[me], local.at[1])
-    own_w.start()
-    swaps = []
+        [((dp + k) % n_dp, me) for k in range(1, n_dp)] + [(dp, (me + k) % n) for k in range(1, n)]
+    )
+    owns = [
+        pltpu.make_async_copy(g_ref.at[dp], h_ref.at[dp], local.at[0]),
+        pltpu.make_async_copy(w_ref.at[me], o_ref.at[me], local.at[1]),
+        pltpu.make_async_copy(x_ref, y_ref.at[me], local.at[2]),
+    ]
+    sends = []
+    for k in range(1, n_dp):
+        to = (dp + k) % n_dp
+        sends.append(remote(g_ref.at[to], h_ref.at[dp], sg.at[k - 1], rg.at[k - 1], (to, me)))
     for k in range(1, n):
         to = (me + k) % n
-        copy = remote(w_ref.at[to], o_ref.at[dp, me], sa.at[k - 1], ra.at[k - 1], (dp, to))
+        sends.append(remote(w_ref.at[to], o_ref.at[me], sa.at[k - 1], ra.at[k - 1], (dp, to)))
+    for k, a in enumerate(ahead + [partner]):
+        sends.append(remote(x_ref, y_ref.at[me], ss.at[k], rs.at[k], (dp, a)))
+    for copy in sends + owns:
         copy.start()
-        swaps.append(copy)
-    sends = [
-        remote(x_ref, y_ref.at[me], ss.at[k], rs.at[k], (dp, a))
-        for k, a in enumerate(ahead + [partner])
-    ]
-    for copy in sends:
-        copy.start()
-    own_x.start()
-
-    def right(s, k, b):
-        c = (me + n - k) % n
-        return remote(o_ref.at[b, c], o_ref.at[b, c], sr.at[s, k], rr.at[s, k], (dp + 1, me))
-
-    def left(s, k, b):
-        c = (me + n - k) % n
-        return remote(o_ref.at[b, c], o_ref.at[b, c], sl.at[s, k], rl.at[s, k], (dp - 1, me))
-
-    for s in range(n_dp):
-        for k in range(n):
-            if s == 0 and k == 0:
-                own_w.wait()
-            elif s == 0:
-                source = (me + n - k) % n
-                remote(
-                    w_ref.at[me], o_ref.at[dp, source], sa.at[k - 1], ra.at[k - 1], (dp, source)
-                ).wait_recv()
-            else:
-
-                @pl.when(dp >= s)
-                def _():
-                    right(s - 1, k, dp - s).wait_recv()
-
-                @pl.when(dp + s < n_dp)
-                def _():
-                    left(s - 1, k, dp + s).wait_recv()
-
-            if s < n_dp - 1:
-
-                @pl.when((dp < n_dp - 1) & (dp >= s))
-                def _():
-                    right(s, k, dp - s).start()
-
-                @pl.when((dp > 0) & (dp + s < n_dp))
-                def _():
-                    left(s, k, dp + s).start()
-
-        if s == 0:
-            forwards = []
-            for k, b in enumerate(behind):
-                remote(x_ref, y_ref.at[b], ss.at[k], rs.at[k], (dp, b)).wait_recv()
-                forward = remote(y_ref.at[b], y_ref.at[b], fs.at[k], fr.at[k], (dp, partner))
-                forward.start()
-                forwards.append(forward)
-    for s in range(n_dp - 1):
-        for k in range(n):
-
-            @pl.when((dp < n_dp - 1) & (dp >= s))
-            def _():
-                right(s, k, dp - s).wait_send()
-
-            @pl.when((dp > 0) & (dp + s < n_dp))
-            def _():
-                left(s, k, dp + s).wait_send()
-
+    forwards = []
+    for k, b in enumerate(behind):
+        remote(x_ref, y_ref.at[b], ss.at[k], rs.at[k], (dp, b)).wait_recv()
+        forward = remote(y_ref.at[b], y_ref.at[b], fs.at[k], fr.at[k], (dp, partner))
+        forward.start()
+        forwards.append(forward)
     sends[-1].wait_recv()
+    for k in range(1, n):
+        source = (me + n - k) % n
+        remote(w_ref.at[me], o_ref.at[source], sa.at[k - 1], ra.at[k - 1], (dp, source)).wait_recv()
+    for k in range(1, n_dp):
+        source = (dp + n_dp - k) % n_dp
+        remote(g_ref.at[dp], h_ref.at[source], sg.at[k - 1], rg.at[k - 1], (source, me)).wait_recv()
     for forward in forwards:
         forward.wait()
-    for copy in sends + swaps:
+    for copy in sends:
         copy.wait_send()
-    own_x.wait()
-
-
-def spread(w, x, number):
+    for copy in owns:
+        copy.wait()
+
+
+def start(g, w, x, number):
     n_dp, n = lax.axis_size("dp"), lax.axis_size("ctx")
     half = n // 2
     dma = pltpu.SemaphoreType.DMA
-    out, x_all = pl.pallas_call(
-        functools.partial(spread_kernel, n_dp, n),
+    g_out, w_out, x_all = pl.pallas_call(
+        functools.partial(start_kernel, n_dp, n),
         out_shape=(
-            jax.ShapeDtypeStruct((n_dp,) + w.shape, w.dtype),
+            jax.ShapeDtypeStruct(g.shape, g.dtype),
+            jax.ShapeDtypeStruct(w.shape, w.dtype),
             jax.ShapeDtypeStruct((n,) + x.shape, x.dtype),
         ),
-        in_specs=[ANY, ANY],
-        out_specs=(ANY, ANY),
-        scratch_shapes=[dma((2,)), dma((n - 1,)), dma((n - 1,)), dma((half,)), dma((half,))]
-        + [dma((half - 1,))] * 2
-        + [dma((n_dp - 1, n))] * 4,
+        in_specs=[ANY] * 3,
+        out_specs=(ANY,) * 3,
+        scratch_shapes=[dma((3,))]
+        + [dma((n_dp - 1,))] * 2
+        + [dma((n - 1,))] * 2
+        + [dma((half,))] * 2
+        + [dma((half - 1,))] * 2,
         compiler_params=params_of(number),
-        name="spread",
-    )(w, x)
-    return out.reshape(-1, w.shape[-1]), x_all.reshape(-1, x.shape[-1])
+        name="start",
+    )(g, w, x)
+    return g_out, w_out, x_all.reshape(-1, x.shape[-1])
+
+
+def swap_behind(x):
+    n, me = lax.axis_size("dp"), lax.axis_index("dp")
+    out = jnp.zeros_like(x)
+    for k in range(n):
+        piece = lax.dynamic_index_in_dim(x, (me + k) % n, keepdims=True)
+        if k:
+            piece = lax.ppermute(piece, "dp", [(i, (i + k) % n) for i in range(n)])
+        out = lax.dynamic_update_index_in_dim(out, piece, (me + n - k) % n, 0)
+    return out
 
 
 def collect_kernel(
@@ -507,7 +361,7 @@
             copy.start()
             row.append(copy)
         first.append(row)
-    sums = reduce_ctx(n, dp, me, a_ref, w_ref, y_ref, pa, qa, pb, qb, s1, r1, s2, r2)
+    sums = reduce_ctx(n, dp, me, a_ref, w_ref, slice(0, a_ref.shape[1]), y_ref, pa, qa, pb, qb, s1, r1, s2, r2)
     mine.wait()
     second = []
     for c in range(n):
@@ -746,6 +600,260 @@
     )(params)
 
 
+def row_sums(value, row):
+    pick = lax.broadcasted_iota(jnp.int32, (8, value.shape[1]), 0) == row
+    return lax.dot_general(
+        pick.astype(F32),
+        value,
+        (((1,), (1,)), ((), ())),
+        preferred_element_type=F32,
+        precision=lax.Precision.HIGHEST,
+    )
+
+
+def exchange(n, dp, me, buf, ss, rs):
+    copies = []
+    for k in range(1, n):
+        copy = remote(buf.at[me], buf.at[me], ss.at[k - 1], rs.at[k - 1], (dp, (me + k) % n))
+        copy.start()
+        copies.append(copy)
+    for k in range(1, n):
+        source = (me + n - k) % n
+        remote(buf.at[me], buf.at[source], ss.at[k - 1], rs.at[k - 1], (dp, source)).wait_recv()
+    total = buf[0]
+    for j in range(1, n):
+        total = total + buf[j]
+    for copy in copies:
+        copy.wait_send()
+    return total
+
+
+def turn(value, cos, sine):
+    return value * cos + pltpu.roll(value, HD // 2, 1) * sine
+
+
+def mask_of(rows, info_col, info_row):
+    pos_i, doc_i = info_col[rows, 0:1], info_col[rows, 1:2]
+    return (info_row[1:2, :] == doc_i) & (info_row[0:1, :] <= pos_i)
+
+
+def attend_kernel(
+    n, x_ref, w_ref, gain_ref, cos_ref, sin_ref, col_ref, row_ref,
+    y_ref, q_ref, k_ref, v_ref, o_ref, pre_ref, scale_ref, lse_ref,
+    buf, pa, qa, pb, qb, ss, rs, s1, r1, s2, r2,
+):
+    dp, me = lax.axis_index("dp"), lax.axis_index("ctx")
+    seq, width = x_ref.shape
+    hc = o_ref.shape[1]
+    block = min(seq, 256)
+    greet([(dp, (me + k) % n) for k in range(1, n)])
+
+    @pl.loop(0, seq // block)
+    def _(i):
+        rows = pl.ds(pl.multiple_of(i * block, block), block)
+        value = dot(x_ref[rows, :], w_ref[:, : 3 * hc])
+        pre_ref[rows, :] = value[:, : 2 * hc]
+        v_ref[rows, :] = value[:, 2 * hc :].astype(BF)
+        squares = value[:, : 2 * hc] * value[:, : 2 * hc]
+        buf[me, :, rows] = row_sums(squares[:, :hc], 0) + row_sums(squares[:, hc:], 1)
+
+    scale_ref[...] = jnp.transpose(lax.rsqrt(exchange(n, dp, me, buf, ss, rs) / width + EPS))
+
+    @pl.loop(0, seq // block)
+    def _(i):
+        rows = pl.ds(pl.multiple_of(i * block, block), block)
+        cos, sine = cos_ref[rows, :], sin_ref[rows, :]
+        for which, ref, factor in ((0, q_ref, HD ** (-0.5)), (1, k_ref, 1.0)):
+            scale = scale_ref[rows, which : which + 1]
+            for start in range(0, hc, HD):
+                part = slice(start, start + HD)
+                value = pre_ref[rows, which * hc + start : which * hc + start + HD] * scale
+                ref[rows, part] = (
+                    turn(value * gain_ref[which : which + 1, part], cos, sine) * factor
+                ).astype(BF)
+
+    @pl.loop(0, seq // block)
+    def _(i):
+        rows = pl.ds(pl.multiple_of(i * block, block), block)
+        visible = mask_of(rows, col_ref, row_ref)
+        for head in range(hc // HD):
+            part = slice(head * HD, (head + 1) * HD)
+            scores = jnp.where(visible, dot_t(q_ref[rows, part], k_ref[:, part]), -jnp.inf)
+            top = jnp.max(scores, axis=1, keepdims=True)
+            weights = jnp.exp(scores - top)
+            total = jnp.sum(weights, axis=1, keepdims=True)
+            o_ref[rows, part] = (dot(weights.astype(BF), v_ref[:, part]) / total).astype(BF)
+            lse_ref[rows, head : head + 1] = top + jnp.log(total)
+
+    cols = slice(3 * hc, 4 * hc)
+    for copy in reduce_ctx(n, dp, me, o_ref, w_ref, cols, y_ref, pa, qa, pb, qb, s1, r1, s2, r2):
+        copy.wait_send()
+
+
+def attend(x_all, w, gain, cos, sine, info_col, info_row, number):
+    n = lax.axis_size("ctx")
+    seq, width = x_all.shape
+    half, length, hc = n // 2, seq // n, w.shape[1] // 4
+    dma = pltpu.SemaphoreType.DMA
+    low = jax.ShapeDtypeStruct((seq, hc), BF)
+    return pl.pallas_call(
+        functools.partial(attend_kernel, n),
+        out_shape=(
+            jax.ShapeDtypeStruct((length, width), F32),
+            low,
+            low,
+            low,
+            low,
+            jax.ShapeDtypeStruct((seq, 2 * hc), F32),
+            jax.ShapeDtypeStruct((seq, 8), F32),
+            jax.ShapeDtypeStruct((seq, 8), F32),
+        ),
+        in_specs=[VMEM] * 7,
+        out_specs=(VMEM,) * 8,
+        scratch_shapes=[
+            pltpu.VMEM((n, 8, seq), F32),
+            pltpu.VMEM((half, length, width), BF),
+            pltpu.VMEM((half, length, width), BF),
+            pltpu.VMEM((half - 1, length, width), BF),
+            pltpu.VMEM((half - 1, length, width), BF),
+            dma((n - 1,)),
+            dma((n - 1,)),
+            dma((half,)),
+            dma((half,)),
+            dma((half - 1,)),
+            dma((half - 1,)),
+        ],
+        compiler_params=params_of(number),
+        name="attend",
+    )(x_all, w, gain, cos, sine, info_col, info_row)
+
+
+def attend_back_kernel(
+    n, e_ref, w_ref, gain_ref, cos_ref, sin_ref, col_ref, row_ref,
+    q_ref, k_ref, v_ref, pre_ref, scale_ref, lse_ref,
+    all_ref, d_ref, gain_out,
+    do_ref, dq_ref, dk_ref, dv_ref, mean_ref, buf, ss, rs, s1, r1, s2, r2,
+):
+    dp, me = lax.axis_index("dp"), lax.axis_index("ctx")
+    half, parity, pair, partner, ahead, behind = pairs_of(n, me)
+    seq, hc = q_ref.shape
+    length, width = e_ref.shape
+    block = min(seq, 256)
+    greet([(dp, (me + k) % n) for k in range(1, n)])
+    sends = [
+        remote(e_ref, all_ref.at[me], s1.at[k], r1.at[k], (dp, a))
+        for k, a in enumerate(ahead + [partner])
+    ]
+    for copy in sends:
+        copy.start()
+    all_ref[me] = e_ref[...]
+    dk_ref[...] = jnp.zeros_like(dk_ref)
+    dv_ref[...] = jnp.zeros_like(dv_ref)
+
+    def project(b):
+        rows = pl.ds(pl.multiple_of(b * length, length), length)
+        do_ref[rows, :] = dot(all_ref[b], w_ref[:, 3 * hc : 4 * hc]).astype(BF)
+
+    project(me)
+    sends[-1].wait_recv()
+    project(partner)
+    forwards = []
+    for k, b in enumerate(behind):
+        remote(e_ref, all_ref.at[b], s1.at[k], r1.at[k], (dp, b)).wait_recv()
+        forward = remote(all_ref.at[b], all_ref.at[b], s2.at[k], r2.at[k], (dp, partner))
+        forward.start()
+        forwards.append(forward)
+        project(b)
+    for k, b in enumerate(behind):
+        forwards[k].wait_recv()
+        project(b + 1 - 2 * parity)
+
+    @pl.loop(0, seq // block)
+    def _(i):
+        rows = pl.ds(pl.multiple_of(i * block, block), block)
+        visible = mask_of(rows, col_ref, row_ref)
+        for head in range(hc // HD):
+            part = slice(head * HD, (head + 1) * HD)
+            query, key, value, back = q_ref[rows, part], k_ref[:, part], v_ref[:, part], do_ref[rows, part]
+            scores = jnp.where(visible, dot_t(query, key), -jnp.inf)
+            probs = jnp.exp(scores - lse_ref[rows, head : head + 1])
+            d_probs = dot_t(back, value)
+            delta = jnp.sum(probs * d_probs, axis=1, keepdims=True)
+            d_scores = (probs * (d_probs - delta)).astype(BF)
+            dq_ref[rows, part] = dot(d_scores, key)
+            dk_ref[:, part] += t_dot(d_scores, query)
+            dv_ref[:, part] += t_dot(probs.astype(BF), back)
+
+    gain_out[...] = jnp.zeros_like(gain_out)
+
+    @pl.loop(0, seq // block)
+    def _(i):
+        rows = pl.ds(pl.multiple_of(i * block, block), block)
+        cos, sine = cos_ref[rows, :], sin_ref[rows, :]
+        sums = jnp.zeros((8, block), F32)
+        for which, ref, factor in ((0, dq_ref, HD ** (-0.5)), (1, dk_ref, 1.0)):
+            scale = scale_ref[rows, which : which + 1]
+            for start in range(0, hc, HD):
+                part = slice(start, start + HD)
+                pre = pre_ref[rows, which * hc + start : which * hc + start + HD]
+                value = turn(ref[rows, part] * factor, cos, -sine)
+                gain_out[which : which + 1, part] += jnp.sum(value * pre * scale, axis=0, keepdims=True)
+                value = value * gain_ref[which : which + 1, part]
+                ref[rows, part] = value
+                sums += row_sums(value * pre, which)
+        buf[me, :, rows] = sums
+
+    mean_ref[...] = jnp.transpose(exchange(n, dp, me, buf, ss, rs) / width)
+
+    @pl.loop(0, seq // block)
+    def _(i):
+        rows = pl.ds(pl.multiple_of(i * block, block), block)
+        for which, ref in ((0, dq_ref), (1, dk_ref)):
+            scale = scale_ref[rows, which : which + 1]
+            mean = mean_ref[rows, which : which + 1]
+            cols = slice(which * hc, (which + 1) * hc)
+            value = scale * (ref[rows, :] - pre_ref[rows, cols] * (scale * scale * mean))
+            d_ref[rows, cols] = value.astype(BF)
+        d_ref[rows, 2 * hc :] = dv_ref[rows, :].astype(BF)
+
+    for copy in sends + forwards:
+        copy.wait_send()
+
+
+def attend_back(e, w, gain, cos, sine, info_col, info_row, q, k, v, pre, scale, lse, number):
+    n = lax.axis_size("ctx")
+    seq, hc = q.shape
+    half, (length, width) = n // 2, e.shape
+    dma = pltpu.SemaphoreType.DMA
+    all_e, d_qkv, d_gain = pl.pallas_call(
+        functools.partial(attend_back_kernel, n),
+        out_shape=(
+            jax.ShapeDtypeStruct((n, length, width), BF),
+            jax.ShapeDtypeStruct((seq, 3 * hc), BF),
+            jax.ShapeDtypeStruct((2, hc), F32),
+        ),
+        in_specs=[VMEM] * 13,
+        out_specs=(VMEM,) * 3,
+        scratch_shapes=[
+            pltpu.VMEM((seq, hc), BF),
+            pltpu.VMEM((seq, hc), F32),
+            pltpu.VMEM((seq, hc), F32),
+            pltpu.VMEM((seq, hc), F32),
+            pltpu.VMEM((seq, 8), F32),
+            pltpu.VMEM((n, 8, seq), F32),
+            dma((n - 1,)),
+            dma((n - 1,)),
+            dma((half,)),
+            dma((half,)),
+            dma((half - 1,)),
+            dma((half - 1,)),
+        ],
+        compiler_params=params_of(number),
+        name="attend_back",
+    )(e, w, gain, cos, sine, info_col, info_row, q, k, v, pre, scale, lse)
+    return all_e.reshape(seq, width), d_qkv, d_gain
+
+
 def shards(
     inputs,
     cotangent,
@@ -784,14 +892,14 @@
         )
 
     wa, wg, wu, wd = arrange(params, width)
-    wgu = swap_dp(jnp.concatenate([wg, wu], axis=2), 10)
-    w_gu = lax.all_gather(wgu.reshape(n_dp * rows, 2 * fs), "ctx", axis=0, tiled=True)
-    wa, wgu = lax.optimization_barrier((wa, wgu))
-    wa, x_all = spread(wa, tokens, 1)
-    w_qkv, w_o = wa[:, : 3 * hc], wa[:, 3 * hc :]
-    wd, x_all = lax.optimization_barrier((wd, x_all))
-    w_d = lax.all_to_all(wd.reshape(n_dp * rows, fs), "dp", 0, 0, tiled=True)
-    w_d = lax.all_gather(w_d, "ctx", axis=0, tiled=True)
+    wg, wa, x_all = start(wg, wa, tokens, 1)
+    w_g = lax.all_gather(wg.reshape(n_dp * rows, fs), "ctx", axis=0, tiled=True)
+    wa = gather_dp(wa.reshape(n_ctx * rows, 4 * hc), 2)
+    wu, wd, wa = lax.optimization_barrier((wu, wd, wa))
+    w_u, w_d = [
+        lax.all_gather(swap_behind(w).reshape(n_dp * rows, fs), "ctx", axis=0, tiled=True)
+        for w in (wu, wd)
+    ]
 
     indices = jnp.arange(seq, dtype=jnp.int32)
     owners = indices // length
@@ -803,97 +911,54 @@
     )
     pos = placed * length + indices % length
     docs = documents[0]
-    visible = (docs[None, :] == docs[:, None]) & (pos[None, :] <= pos[:, None])
+    info_row = jnp.concatenate([pos[None], docs[None], jnp.zeros((6, seq), jnp.int32)])
+    info_col = info_row.T
     cos_tab, sine_tab = rope_tables(pos, HD)
-
-    my_gains = lax.dynamic_slice_in_dim(gains, me_ctx * hc, hc, axis=1)
-    projected = dot(x_all, w_qkv)
-    qk_pre = projected[:, : 2 * hc].reshape(seq, 2, hc)
-    values = projected[:, 2 * hc :].astype(BF)
-    squares = lax.psum(jnp.sum(qk_pre * qk_pre, axis=-1), "ctx")
-    scales = lax.rsqrt(squares / width + EPS)
-    q_pre, k_pre = qk_pre[:, 0], qk_pre[:, 1]
-    q_scale, k_scale = scales[:, :1], scales[:, 1:]
-    queries = (rotate(q_pre * q_scale * my_gains[0], cos_tab, sine_tab) * HD ** (-0.5)).astype(BF)
-    keys = rotate(k_pre * k_scale * my_gains[1], cos_tab, sine_tab).astype(BF)
-
-    def split(v):
-        return v.reshape(seq, heads, HD).transpose(1, 0, 2)
-
-    def join(v):
-        return v.transpose(1, 0, 2).reshape(seq, hc)
-
-    qh, kh, vh = split(queries), split(keys), split(values)
-    scores = jnp.einsum("hqd,hkd->hqk", qh, kh, preferred_element_type=F32)
-    scores = jnp.where(visible[None], scores, -jnp.inf)
-    top = jnp.max(scores, axis=-1, keepdims=True)
-    weights = jnp.exp(scores - top)
-    total = jnp.sum(weights, axis=-1, keepdims=True)
-    probs = weights / total
-    probs_low = probs.astype(BF)
-    attn = jnp.einsum("hqk,hkd->hqd", probs_low, vh, preferred_element_type=F32)
-    attn_low = join(attn).astype(BF)
-    attn_low, w_gu = lax.optimization_barrier((attn_low, w_gu))
-    branch = scatter_ctx(attn_low, w_o, 2)
+    cos_tab = jnp.concatenate([cos_tab, cos_tab], axis=1)
+    sine_tab = jnp.concatenate([-sine_tab, sine_tab], axis=1)
+    my_gains = lax.dynamic_slice_in_dim(gains[:2], me_ctx * hc, hc, axis=1)
+    tables = (my_gains, cos_tab, sine_tab, info_col, info_row)
+
+    branch, queries, keys, values, attn_low, qk_pre, scales, lse = attend(x_all, wa, *tables, 3)
     a_scale = rms_scale(branch)
     hidden1 = tokens.astype(F32) + branch * a_scale * gains[2]
 
-    h1_all = gather_dp(mix(hidden1.astype(BF)), 3)
-    gate_up = dot(h1_all, w_gu)
-    gate_pre, up_pre = gate_up[:, :fs], gate_up[:, fs:]
+    h1_all = gather_dp(mix(hidden1.astype(BF)), 4)
+    gate_pre, up_pre = dot(h1_all, w_g), dot(h1_all, w_u)
     gate_sig = jax.nn.sigmoid(gate_pre)
     silu_val = gate_pre * gate_sig
     inner = (silu_val * up_pre).astype(BF)
-    mlp_out = unmix(scatter_dp(inner, w_d, 4))
+    mlp_out = unmix(scatter_dp((inner, w_d), 5))
     m_scale = rms_scale(mlp_out)
     result = hidden1 + mlp_out * m_scale * gains[3]
 
     g_ff_part = jnp.sum(upstream * mlp_out * m_scale, axis=0)
     d_mlp = norm_back(upstream * gains[3], mlp_out, m_scale).astype(BF)
-    d_mlp_all = gather_dp(mix(d_mlp), 5)
+    d_mlp_all = gather_dp(mix(d_mlp), 6)
     d_grad = lax.psum_scatter(
         t_dot(d_mlp_all, inner).astype(BF), "ctx", scatter_dimension=0, tiled=True
     )
     d_inner = dot(d_mlp_all, w_d)
-    d_gate = d_inner * up_pre * gate_sig * (1.0 + gate_pre * (1.0 - gate_sig))
-    d_upper = d_inner * silu_val
-    d_gu = jnp.concatenate([d_gate, d_upper], axis=1).astype(BF)
-    d_h1 = upstream + unmix(scatter_dp(d_gu, w_gu, 6))
-    gu_grad = t_dot(h1_all, d_gu).astype(BF)
+    d_gate = (d_inner * up_pre * gate_sig * (1.0 + gate_pre * (1.0 - gate_sig))).astype(BF)
+    d_upper = (d_inner * silu_val).astype(BF)
+    d_h1 = upstream + unmix(scatter_dp((d_gate, w_g, d_upper, w_u), 7))
+    gu_grad = t_dot(h1_all, jnp.concatenate([d_gate, d_upper], axis=1)).astype(BF)
 
     g_attn_part = jnp.sum(d_h1 * branch * a_scale, axis=0)
     d_branch = norm_back(d_h1 * gains[2], branch, a_scale).astype(BF)
-    d_branch_all = gather_ctx(d_branch, 7)
-    d_attn = dot(d_branch_all, w_o).astype(BF)
-    dh = split(d_attn)
-    delta = jnp.sum(dh.astype(F32) * attn, axis=-1, keepdims=True)
-    d_probs = jnp.einsum("hqd,hkd->hqk", dh, vh, preferred_element_type=F32)
-    d_scores = (probs * (d_probs - delta)).astype(BF)
-    d_query = join(jnp.einsum("hqk,hkd->hqd", d_scores, kh, preferred_element_type=F32))
-    d_key = join(jnp.einsum("hqk,hqd->hkd", d_scores, qh, preferred_element_type=F32))
-    d_value = join(jnp.einsum("hqk,hqd->hkd", probs_low, dh, preferred_element_type=F32))
-    d_qn = rotate(d_query * HD ** (-0.5), cos_tab, -sine_tab)
-    d_kn = rotate(d_key, cos_tab, -sine_tab)
-    g_q_part = jnp.sum(d_qn * q_pre * q_scale, axis=0)
-    g_k_part = jnp.sum(d_kn * k_pre * k_scale, axis=0)
-    e_q, e_k = d_qn * my_gains[0], d_kn * my_gains[1]
-    means = (
-        lax.psum(jnp.stack([jnp.sum(e_q * q_pre, -1), jnp.sum(e_k * k_pre, -1)], -1), "ctx") / width
-    )
-    d_q_pre = q_scale * (e_q - q_pre * q_scale * q_scale * means[:, :1])
-    d_k_pre = k_scale * (e_k - k_pre * k_scale * k_scale * means[:, 1:])
-    d_qkv = jnp.concatenate([d_q_pre, d_k_pre, d_value], axis=1).astype(BF)
+    d_branch_all, d_qkv, d_gain = attend_back(
+        d_branch, wa, *tables, queries, keys, values, qk_pre, scales, lse, 8
+    )
     attn_grad = jnp.concatenate([t_dot(x_all, d_qkv), t_dot(d_branch_all, attn_low)], axis=1)
     d_grad = lax.all_to_all(d_grad, "dp", 0, 0, tiled=True).reshape(n_dp, rows, fs)
     gu_grad = lax.psum_scatter(gu_grad, "ctx", scatter_dimension=0, tiled=True)
     gu_grad = lax.all_to_all(gu_grad, "dp", 0, 0, tiled=True).reshape(n_dp, rows, 2 * fs)
-    attn_grad, d_x = collect(attn_grad.astype(BF), d_qkv, w_qkv, 9)
+    attn_grad, d_x = collect(attn_grad.astype(BF), d_qkv, wa, 9)
     d_input = d_h1 + d_x
 
     gain_part = jnp.stack(
         [
-            lax.dynamic_update_slice(jnp.zeros(width, F32), g_q_part, (me_ctx * hc,)),
-            lax.dynamic_update_slice(jnp.zeros(width, F32), g_k_part, (me_ctx * hc,)),
+            *lax.dynamic_update_slice(jnp.zeros((2, width), F32), d_gain, (0, me_ctx * hc)),
             g_attn_part,
             g_ff_part,
         ],

time: 868 us -> 871 us (level)
  waiting for transfers between devices: 2.26 us -> 114 us
  blocking collectives: 54.4 us -> 0 us
  other arithmetic: 53.3 us -> 18.1 us
  matrix products: 77.6 us -> 64.7 us
  local copies, waits for them, and re-layouts: 64.1 us -> 52.7 us
  Pallas kernels: 566 us -> 577 us
    pallas_call x2 -> x3, Pallas kernels: 88 us -> 171 us  [gather_dp(): pl.pallas_call(functools.partial(gather_dp_kernel, n), out_shape=jax.Shap...]
    pallas_call x6 -> x5, Pallas kernels: 324 us -> 266 us  [the longest x2 103 us: scatter_dp(): pl.pallas_call(functools.partial(scatter_dp_kernel, n, len(operands) // 2...]
    reduce_scatter x1, waiting for transfers between devices: 2.18 us -> 45.3 us  [shards(): gu_grad = lax.psum_scatter(gu_grad, 'ctx', scatter_dimension=0, tiled=True)]
    reduce_scatter x1, waiting for transfers between devices: 0.01 us -> 39.2 us  [shards(): lax.psum_scatter(t_dot(d_mlp_all, inner).astype(BF), 'ctx', scatter_dimen...]
    ppermute x0 -> x6, waiting for transfers between devices: none -> 29.7 us  [swap_behind(): piece = lax.ppermute(piece, 'dp', [(i, (i + k) % n) for i in range(n)])]
    all_to_all x1 -> x0, blocking collectives: 28.4 us -> none  [shards(): w_d = lax.all_to_all(wd.reshape(n_dp * rows, fs), 'dp', 0, 0, tiled=True)]
    psum x2 -> x0, blocking collectives: 26 us -> none  [the longest x1 13.1 us: shards(): squares = lax.psum(jnp.sum(qk_pre * qk_pre, axis=-1), 'ctx')]
    all_to_all x1, starting transfers between devices: 21.2 us -> 4.61 us  [shards(): lax.all_to_all(d_grad, 'dp', 0, 0, tiled=True).reshape(n_dp, rows, fs)]
  transfers between devices with their start and end apart: 6 -> 13, of which waited for: 1 -> 7; matrix products, arithmetic and copies ran while one was open for 19% -> 11% of each run, Pallas kernels for 45% -> 46%
where the time goes in v3:
time: 871 us; the launch traced here: 866 us
  Pallas kernels  577 us (66%)
  waiting for transfers between devices  114 us (13%)
  matrix products  64.7 us (7%)
  local copies, waits for them, and re-layouts  52.7 us (6%)
  starting transfers between devices  21.3 us (2%)
  other arithmetic  18.1 us (2%)
  between operations  17.2 us (2%)
    pallas_call x3, Pallas kernels, gather_dp(): pl.pallas_call(functools.partial(gather_dp_kernel, n), out_shape=jax.Shap...  171 us
    pallas_call x2, Pallas kernels, scatter_dp(): pl.pallas_call(functools.partial(scatter_dp_kernel, n, len(operands) // 2...  103 us
    pallas_call x1, Pallas kernels, collect(): pl.pallas_call(functools.partial(collect_kernel, n_dp, n), out_shape=(jax...  97.3 us
    pallas_call x1, Pallas kernels, attend(): pl.pallas_call(functools.partial(attend_kernel, n), out_shape=(jax.ShapeD...  67.5 us
    pallas_call x1, Pallas kernels, attend_back(): pl.pallas_call(functools.partial(attend_back_kernel, n), out_shape=(jax.S...  51.3 us
    reduce_scatter x1, waiting for transfers between devices, shards(): gu_grad = lax.psum_scatter(gu_grad, 'ctx', scatter_dimension=0, tiled=True)  45.3 us
    pallas_call x1, Pallas kernels, start(): pl.pallas_call(functools.partial(start_kernel, n_dp, n), out_shape=(jax.S...  43.8 us
    reduce_scatter x1, waiting for transfers between devices, shards(): lax.psum_scatter(t_dot(d_mlp_all, inner).astype(BF), 'ctx', scatter_dimen...  39.2 us
  transfers between devices with their start and end apart: 13, of which 7 were waited for; matrix products, arithmetic and copies ran while one was open for 11% of the time, Pallas kernels for 46%

profile of v3, /device:TPU:0, one launch (start us, length us, event | category | flops | bytes accessed | tf_op | source)
XLA Modules:
  0.0 865.6 jit_solution(4201072581904128610)
XLA Ops:
  7.2 4.3 arrange.1
  11.5 1.0 copy-done.16
  12.5 43.8 %start.1 = (bf16[4,64,2048]{2,1,0:T(8,128)(2,1)}, bf16[8,64,1024]{2,1,0:T(8,128)(2,1)S(1)}, bf16[8,128,2048]{2,1,0:T(8,128)(2,1)}) custom-call(bf16[4,64,2048]{2,1,0:T(8,128)(2,1)S(1)} %get-tuple-element.35.g_ref, bf16[8,64,1024]{2,1,0:T(8,128)(2,1)S(1)} %get-tuple-element.36.w_ref, bf16[128,2048]{1,0:T(8,128)(2,1)S(1)} %bitcast.85), custom_call_target="tpu_custom_call" | custom-call | tf_op jit(solution)/shard_map/start/pallas_call | solution.py:307
  56.4 73.8 %gather_dp.3 = bf16[4,512,1024]{2,1,0:T(8,128)(2,1)S(1)} custom-call(bf16[512,1024]{1,0:T(8,128)(2,1)S(1)} %bitcast.89), custom_call_target="tpu_custom_call" | custom-call | tf_op jit(solution)/shard_map/gather_dp/pallas_call | solution.py:148
  130.3 2.0 copy-done
  132.4 1.3 constant_dynamic-slice_fusion.3
  133.8 2.6 collective-permute-start.1
  136.4 1.2 collective-permute-start.2
  137.6 7.3 collective-permute-done
  144.9 8.7 %collective-permute-done.1 = bf16[1,64,2048]{2,1,0:T(8,128)(2,1)S(1)} collective-permute-done((bf16[1,64,2048]{2,1,0:T(8,128)(2,1)S(1)}, bf16[1,64,2048]{2,1,0:T(8,128)(2,1)S(1)}, u32[]{:S(2)}, u32[]{:S(2)}) %collective-permute-start.1) | collective-permute-done | bytes 262176 | tf_op jit(solution)/shard_map/ppermute | solution.py:333
  153.7 1.0 copy-done.35
  155.0 5.2 collective-permute-start.3
  160.2 2.4 collective-permute-start.5
  162.6 4.3 collective-permute-done.3
  167.0 8.4 collective-permute-done.4
  175.4 0.9 collective-permute-done.5
  176.4 1.0 copy-done.34
  178.0 1.9 fusion.9
  180.3 67.5 %attend.1 = (f32[128,2048]{1,0:T(8,128)S(1)}, bf16[1024,256]{1,0:T(8,128)(2,1)S(1)}, bf16[1024,256]{1,0:T(8,128)(2,1)S(1)}, bf16[1024,256]{1,0:T(8,128)(2,1)S(1)...) custom-call(bf16[1024,2048]{1,0:T(8,128)(2,1)} %bitcast.92, ...), custom_call_target="tpu_custom_call" | custom-call | tf_op jit(solution)/shard_map/attend/pallas_call | solution.py:699
  249.4 0.8 copy-done.21
  253.4 1.0 copy.85.x_ref
  254.4 1.0 copy-done.13
  255.5 48.2 %gather_dp.4 = bf16[4,128,2048]{2,1,0:T(8,128)(2,1)S(1)} custom-call(bf16[128,2048]{1,0:T(8,128)(2,1)S(1)} %copy-done.13), custom_call_target="tpu_custom_call" | custom-call | tf_op jit(solution)/shard_map/gather_dp/pallas_call | solution.py:148
  303.8 2.2 copy.89
  306.0 9.4 %fusion.24 = f32[512,2048]{1,0:T(8,128)} fusion(bf16[512,2048]{1,0:T(8,128)(2,1)S(1)} %bitcast.86, bf16[2048,2048]{1,0:T(8,128)(2,1)} %all-gather.4.cloned.1.call-done.refs_1_), kind=kOutput, calls=%fused_computation.86 | convolution fusion | flops 4294967296 | bytes 14680064 | tf_op jit(solution)/shard_map/dot_general | solution.py:55
  315.4 10.9 %multiply_convert_fusion.2 = (bf16[512,2048]{1,0:T(8,128)(2,1)}, f32[512,2048]{1,0:T(8,128)}) fusion(f32[512,2048]{1,0:T(8,128)} %fusion.24, bf16[512,2048]{1,0:T(8,128)(2,1)S(1)} %bitcast.87, bf16[2048,2048]{1,0:T(8,128)(2,1)} %all-gather.6.cloned.1.call-done.refs_3_), kind=kOutput, calls=%fused_computation.8 | convolution fusion | flops 4301258752 | bytes 20971520 | tf_op jit(solution)/shard_map/dot_general | solution.py:55
  326.2 46.3 %scatter_dp.2 = f32[128,2048]{1,0:T(8,128)} custom-call(bf16[512,2048]{1,0:T(8,128)(2,1)} %get-tuple-element.90.refs_0_, bf16[2048,2048]{1,0:T(8,128)(2,1)} %all-gather.8.cloned.1.call-done.refs_1_), custom_call_target="tpu_custom_call" | custom-call | tf_op jit(solution)/shard_map/scatter_dp/pallas_call | solution.py:242
  372.6 2.6 copy.86
  375.2 1.7 multiply_reduce_fusion.4
  376.8 2.5 multiply_reduce_fusion
  379.4 1.2 multiply_convert_fusion.4
  380.5 2.0 copy.92.x_ref
  382.6 1.0 copy-done.14
  383.6 49.1 %gather_dp.5 = bf16[4,128,2048]{2,1,0:T(8,128)(2,1)} custom-call(bf16[128,2048]{1,0:T(8,128)(2,1)S(1)} %copy-done.14), custom_call_target="tpu_custom_call" | custom-call | tf_op jit(solution)/shard_map/gather_dp/pallas_call | solution.py:148
  432.8 10.2 %convolution_convert_fusion.1 = bf16[2048,2048]{1,0:T(8,128)(2,1)} fusion(bf16[512,2048]{1,0:T(8,128)(2,1)} %bitcast.24, bf16[512,2048]{1,0:T(8,128)(2,1)} %get-tuple-element.90.refs_0_), kind=kOutput, calls=%fused_computation.1 | convolution fusion | flops 4299161600 | bytes 12582912 | tf_op jit(solution)/shard_map/dot_general | solution.py:63
  443.0 14.2 %multiply_convert_fusion = (bf16[512,2048]{1,0:T(8,128)(2,1)S(1)}, bf16[512,2048]{1,0:T(8,128)(2,1)S(1)}) fusion(f32[512,2048]{1,0:T(8,128)} %fusion.24, f32[512,2048]{1,0:T(8,128)} %get-tuple-element.91, bf16[512,2048]{1,0:T(8,128)(2,1)} %bitcast.24, bf16[2048,2048]{1,0:T(8,128)(2,1)} %all-gather.8.cloned.1.call-done.refs_1_), kind=kOutput, calls=%fused_computation.6 | convolution fusion | flops 4308598784 | bytes 23068672 | tf_op jit(solution)/shard_map/dot_general | solution.py:55
  457.2 1.4 copy-done.36
  459.2 12.9 %convolution_convert_fusion = bf16[2048,4096]{1,0:T(8,128)(2,1)} fusion(bf16[512,2048]{1,0:T(8,128)(2,1)S(1)} %bitcast.88, bf16[512,2048]{1,0:T(8,128)(2,1)S(1)} %get-tuple-element.68.refs_2_, bf16[512,2048]{1,0:T(8,128)(2,1)S(1)} %get-tuple-element.69.refs_0_), kind=kOutput, calls=%fused_computation | convolution fusion | flops 8606711808 | bytes 23068672 | tf_op jit(solution)/shard_map/dot_general | solution.py:63
  472.1 39.2 %reduce-scatter.5.cloned.1.call-done = bf16[256,2048]{1,0:T(8,128)(2,1)} async-done(((bf16[2048,2048]{1,0:T(8,128)(2,1)}), bf16[256,2048]{1,0:T(8,128)(2,1)}) %reduce-scatter.5.cloned.1.call-update) | async-done | bytes 1048592 | tf_op jit(solution)/shard_map/reduce_scatter | solution.py:938
  511.3 4.6 all-to-all-start.1
  515.9 6.4 copy.96
  522.4 57.1 %scatter_dp.3 = f32[128,2048]{1,0:T(8,128)} custom-call(bf16[512,2048]{1,0:T(8,128)(2,1)} %copy-done.37, bf16[2048,2048]{1,0:T(8,128)(2,1)} %all-gather.4.cloned.1.call-done.refs_1_, bf16[512,2048]{1,0:T(8,128)(2,1)} %copy-done.36, bf16[2048,2048]{1,0:T(8,128)(2,1)} %all-gather.6.cloned.1.call-done.refs_3_), custom_call_target="tpu_custom_call" | custom-call | tf_op jit(solution)/shard_map/scatter_dp/pallas_call | solution.py:242
  579.5 1.7 copy.93
  581.1 1.0 copy.94
  582.2 2.7 copy.95
  584.9 1.0 copy-done.1
  585.8 45.3 %reduce-scatter.3.cloned.1.call-done = bf16[256,4096]{1,0:T(8,128)(2,1)} async-done(((bf16[2048,4096]{1,0:T(8,128)(2,1)}), bf16[256,4096]{1,0:T(8,128)(2,1)}) %reduce-scatter.3.cloned.1.call-update) | async-done | bytes 2097168 | tf_op jit(solution)/shard_map/reduce_scatter | solution.py:954
  631.1 5.0 all-to-all-start
  636.1 1.7 multiply_reduce_fusion.1
  637.8 2.3 copy.87
  640.1 2.6 copy.88
  642.9 3.4 multiply_convert_fusion.3
  646.3 51.3 %attend_back.1 = (bf16[8,128,2048]{2,1,0:T(8,128)(2,1)}, bf16[1024,768]{1,0:T(8,128)(2,1)}, f32[2,256]{1,0:T(2,128)S(1)}) custom-call(bf16[128,2048]{1,0:T(8,128)(2,1)S(1)} %get-tuple-element.70.e_ref, bf16[2048,1024]{1,0:T(8,128)(2,1)} %bitcast.83, f32[2,256]{1,0:T(2,128)S(1)} %constant_dynamic-slice_fusion.6.gain_ref, f32[1024,128]{1,0:T(8,128)S(1)} %copy-done.5, ...), custom_call_target="tpu_custom_call" | custom-call | tf_op jit(solution)/shard_map/attend_back/pallas_call | solution.py:828
  697.7 6.5 copy.98
  704.1 3.6 convolution_convert_fusion.3
  708.1 3.6 convolution_convert_fusion.2
  711.7 2.6 pad_maximum_fusion.g_ref
  714.2 97.3 %collect.1 = (bf16[8,64,1024]{2,1,0:T(8,128)(2,1)S(1)}, f32[128,2048]{1,0:T(8,128)S(1)}) custom-call(bf16[4,8,64,1024]{3,2,1,0:T(8,128)(2,1)} %pad_maximum_fusion.g_ref, bf16[1024,768]{1,0:T(8,128)(2,1)S(1)} %copy-done.15, bf16[2048,1024]{1,0:T(8,128)(2,1)} %bitcast.84), custom_call_target="tpu_custom_call" | custom-call | tf_op jit(solution)/shard_map/collect/pallas_call | solution.py:395
  811.5 1.0 copy-done.10
  812.5 1.0 fusion.7
  813.5 1.2 copy-done.11
  814.7 14.3 %total.1 = f32[72,128]{1,0:T(8,128)S(1)} custom-call(bf16[8,64,1024]{2,1,0:T(8,128)(2,1)S(1)} %copy-done.11, bf16[4,64,4096]{2,1,0:T(8,128)(2,1)S(1)} %all-to-all-done.gu_ref, bf16[4,64,2048]{2,1,0:T(8,128)(2,1)S(1)} %copy-done.2, f32[64,128]{1,0:T(8,128)S(1)} %reshape.241.gain_ref), custom_call_target="tpu_custom_call" | custom-call | tf_op jit(solution)/shard_map/total/pallas_call | solution.py:482
  832.2 1.2 copy-done.12
  833.5 24.3 %adam.1 = (f32[64,32768]{1,0:T(8,128)}, f32[64,32768]{1,0:T(8,128)}, f32[64,32768]{1,0:T(8,128)}) custom-call(f32[1,1]{1,0:T(1,128)} %bitcast.42.factor_ref, f32[64,32768]{1,0:T(8,128)} %p_ref.3, f32[64,32768]{1,0:T(8,128)} %m_ref.1, f32[64,32768]{1,0:T(8,128)} %v_ref.1, bf16[8,64,1024]{2,1,0:T(8,128)(2,1)S(1)} %copy-done.12, ...), custom_call_target="tpu_custom_call" | custom-call | tf_op jit(solution)/shard_map/adam/pallas_call | solution.py:539
  (136 shorter events, 9.6 us)
Async XLA Ops:
  7.2 5.3 copy-start.3
  7.2 298.8 %all-gather.4.cloned.1.call-start = ((), (), s32[]{:S(2)}) async-start(), calls=%async_computation.4 | async-start | bytes 9437184 | tf_op jit(solution)/shard_map/all_gather | solution.py:896
  11.5 1.0 copy-start.16
  56.3 259.1 %all-gather.6.cloned.1.call-start = ((), (), s32[]{:S(2)}) async-start(), calls=%async_computation.5 | async-start | bytes 9437184 | tf_op jit(solution)/shard_map/all_gather | solution.py:900
  130.3 2.0 copy-start
  133.7 11.2 %collective-permute-start = (bf16[1,64,2048]{2,1,0:T(8,128)(2,1)S(1)}, bf16[1,64,2048]{2,1,0:T(8,128)(2,1)S(1)}, u32[]{:S(2)}, u32[]{:S(2)}) collective-permute-start(bf16[1,64,2048]{2,1,0:T(8,128)(2,1)S(1)} %get-tuple-element.78), channel_id=1, source_target_pairs={{0,8},{8,16},{16,24},{24,0},{1,9},{9,17},{17,25},{25,1},{2,10},{10... | collective-permute-start | bytes 786440 | tf_op jit(solution)/shard_map/ppermute | solution.py:333
  133.8 19.9 %collective-permute-start.1 = (bf16[1,64,2048]{2,1,0:T(8,128)(2,1)S(1)}, bf16[1,64,2048]{2,1,0:T(8,128)(2,1)S(1)}, u32[]{:S(2)}, u32[]{:S(2)}) collective-permute-start(bf16[1,64,2048]{2,1,0:T(8,128)(2,1)S(1)} %get-tuple-element.77), channel_id=1, source_target_pairs={{0,16},{8,24},{16,0},{24,8},{1,17},{9,25},{17,1},{25,9},{2,18},{10... | collective-permute-start | bytes 786440 | tf_op jit(solution)/shard_map/ppermute | solution.py:333
  136.4 17.3 %collective-permute-start.2 = (bf16[1,64,2048]{2,1,0:T(8,128)(2,1)S(1)}, bf16[1,64,2048]{2,1,0:T(8,128)(2,1)S(1)}, u32[]{:S(2)}, u32[]{:S(2)}) collective-permute-start(bf16[1,64,2048]{2,1,0:T(8,128)(2,1)S(1)} %get-tuple-element.76), channel_id=1, source_target_pairs={{0,24},{8,0},{16,8},{24,16},{1,25},{9,1},{17,9},{25,17},{2,26},{10... | collective-permute-start | bytes 786440 | tf_op jit(solution)/shard_map/ppermute | solution.py:333
  144.9 32.6 %copy-start.42 = (s32[8]{0:T(128)S(1)}, s32[8]{0:T(128)}, u32[]{:S(2)}) copy-start(s32[8]{0:T(128)} %param.13) | copy-start | bytes 100
  144.9 32.7 %copy-start.41 = (s32[1,1024]{1,0:T(1,128)S(1)}, s32[1,1024]{1,0:T(1,128)}, u32[]{:S(2)}) copy-start(s32[1,1024]{1,0:T(1,128)} %param.12) | copy-start | bytes 12292
  144.9 33.0 %slice-start = ((f32[4,2048]{1,0:T(4,128)}), f32[2,2048]{1,0:T(2,128)S(1)}, s32[]{:S(2)}) async-start(f32[4,2048]{1,0:T(4,128)} %param.17), calls=%async_computation.9 | async-start | bytes 32768 | tf_op jit(solution)/shard_map/slice | solution.py:919
  153.7 1.0 copy-start.35
  154.7 171.5 %all-gather.8.cloned.1.call-start = ((), (), s32[]{:S(2)}) async-start(), calls=%async_computation.6 | async-start | bytes 9437184 | tf_op jit(solution)/shard_map/all_gather | solution.py:900
  155.0 12.0 %collective-permute-start.3 = (bf16[1,64,2048]{2,1,0:T(8,128)(2,1)S(1)}, bf16[1,64,2048]{2,1,0:T(8,128)(2,1)S(1)}, u32[]{:S(2)}, u32[]{:S(2)}) collective-permute-start(bf16[1,64,2048]{2,1,0:T(8,128)(2,1)S(1)} %get-tuple-element.74), channel_id=1, source_target_pairs={{0,8},{8,16},{16,24},{24,0},{1,9},{9,17},{17,25},{25,1},{2,10},{10... | collective-permute-start | bytes 786440 | tf_op jit(solution)/shard_map/ppermute | solution.py:333
  160.2 15.2 %collective-permute-start.4 = (bf16[1,64,2048]{2,1,0:T(8,128)(2,1)S(1)}, bf16[1,64,2048]{2,1,0:T(8,128)(2,1)S(1)}, u32[]{:S(2)}, u32[]{:S(2)}) collective-permute-start(bf16[1,64,2048]{2,1,0:T(8,128)(2,1)S(1)} %get-tuple-element.73), channel_id=1, source_target_pairs={{0,16},{8,24},{16,0},{24,8},{1,17},{9,25},{17,1},{25,9},{2,18},{10... | collective-permute-start | bytes 786440 | tf_op jit(solution)/shard_map/ppermute | solution.py:333
  160.2 16.1 %collective-permute-start.5 = (bf16[1,64,2048]{2,1,0:T(8,128)(2,1)S(1)}, bf16[1,64,2048]{2,1,0:T(8,128)(2,1)S(1)}, u32[]{:S(2)}, u32[]{:S(2)}) collective-permute-start(bf16[1,64,2048]{2,1,0:T(8,128)(2,1)S(1)} %get-tuple-element.72), channel_id=1, source_target_pairs={{0,24},{8,0},{16,8},{24,16},{1,25},{9,1},{17,9},{25,17},{2,26},{10... | collective-permute-start | bytes 786440 | tf_op jit(solution)/shard_map/ppermute | solution.py:333
  176.4 1.0 copy-start.34
  177.4 333.9 %reduce-scatter.5.cloned.1.call-start = ((), (), s32[]{:S(2)}) async-start(), calls=%async_computation.8 | async-start | bytes 9437184 | tf_op jit(solution)/shard_map/reduce_scatter | solution.py:938
  177.9 69.9 %copy-start.8 = (s32[1024,8]{1,0:T(8,128)}, s32[1024,8]{1,0:T(8,128)S(1)}, u32[]{:S(2)}) copy-start(s32[1024,8]{1,0:T(8,128)S(1)} %copy.82.col_ref) | copy-start | bytes 98308
  180.2 67.6 %copy-start.4 = (f32[1024,128]{1,0:T(8,128)}, f32[1024,128]{1,0:T(8,128)S(1)}, u32[]{:S(2)}) copy-start(f32[1024,128]{1,0:T(8,128)S(1)} %get-tuple-element.92.cos_ref) | copy-start | bytes 1572868
  180.2 67.6 %copy-start.6 = (f32[1024,128]{1,0:T(8,128)}, f32[1024,128]{1,0:T(8,128)S(1)}, u32[]{:S(2)}) copy-start(f32[1024,128]{1,0:T(8,128)S(1)} %get-tuple-element.93.sin_ref) | copy-start | bytes 1572868
  180.2 72.6 %copy-start.38 = (f32[4,2048]{1,0:T(4,128)S(1)}, f32[4,2048]{1,0:T(4,128)}, u32[]{:S(2)}) copy-start(f32[4,2048]{1,0:T(4,128)} %param.17) | copy-start | bytes 98308
  247.8 0.8 copy-start.17
  248.7 0.8 copy-start.19
  249.4 0.8 copy-start.21
  250.3 0.8 copy-start.23
  251.0 0.8 copy-start.25
  251.9 0.8 copy-start.27
  254.4 1.0 copy-start.13
  375.2 4.2 copy-start.29
  375.2 4.2 copy-start.31
  382.6 1.0 copy-start.14
  443.0 188.2 %reduce-scatter.3.cloned.1.call-start = ((), (), s32[]{:S(2)}) async-start(), calls=%async_computation.7 | async-start | bytes 18874368 | tf_op jit(solution)/shard_map/reduce_scatter | solution.py:954
  457.2 1.4 copy-start.36
  457.2 2.0 copy-start.37
  511.3 73.6 %all-to-all-start.1 = ((bf16[4,64,2048]{2,1,0:T(8,128)(2,1)}), bf16[4,64,2048]{2,1,0:T(8,128)(2,1)S(1)}, u32[]{:S(2)}, u32[]{:S(2)}) async-start(bf16[4,64,2048]{2,1,0:T(8,128)(2,1)} %bitcast.108), calls=%async_computation.3 | async-start | bytes 2097152 | tf_op jit(solution)/shard_map/all_to_all | solution.py:953
  584.9 1.0 copy-start.1
  631.1 182.3 %all-to-all-start = ((bf16[4,64,4096]{2,1,0:T(8,128)(2,1)}), bf16[4,64,4096]{2,1,0:T(8,128)(2,1)S(1)}, u32[]{:S(2)}, u32[]{:S(2)}) async-start(bf16[4,64,4096]{2,1,0:T(8,128)(2,1)} %bitcast.105), calls=%async_computation.1 | async-start | bytes 4194304 | tf_op jit(solution)/shard_map/all_to_all | solution.py:955
  642.8 3.5 copy-start.5
  642.8 3.5 copy-start.7
  642.8 3.5 copy-start.9
  642.8 3.4 copy-start.18
  642.8 3.4 copy-start.20
  642.8 3.4 copy-start.22
  642.8 3.4 copy-start.24
  642.9 3.4 copy-start.26
  697.7 6.5 copy-start.28
  704.1 3.6 copy-start.15
  704.1 3.9 copy-start.33
  714.2 98.3 %copy-start.30 = (f32[128,2048]{1,0:T(8,128)S(1)}, f32[128,2048]{1,0:T(8,128)}, u32[]{:S(2)}) copy-start(f32[128,2048]{1,0:T(8,128)} %copy.95) | copy-start | bytes 3145732
  714.2 98.3 %copy-start.32 = (bf16[1,128,2048]{2,1,0:T(8,128)(2,1)S(1)}, bf16[1,128,2048]{2,1,0:T(8,128)(2,1)}, u32[]{:S(2)}) copy-start(bf16[1,128,2048]{2,1,0:T(8,128)(2,1)} %param.11) | copy-start | bytes 1572868
  714.2 99.3 %copy-start.2 = (bf16[4,64,2048]{2,1,0:T(8,128)(2,1)S(1)}, bf16[4,64,2048]{2,1,0:T(8,128)(2,1)}, u32[]{:S(2)}) copy-start(bf16[4,64,2048]{2,1,0:T(8,128)(2,1)} %copy-done.1) | copy-start | bytes 3145732
  811.5 1.0 copy-start.10
  812.5 19.0 %copy-start.39 = (f32[4,2048]{1,0:T(4,128)S(1)}, f32[4,2048]{1,0:T(4,128)}, u32[]{:S(2)}) copy-start(f32[4,2048]{1,0:T(4,128)} %param.18) | copy-start | bytes 98308
  812.5 19.1 %copy-start.40 = (f32[4,2048]{1,0:T(4,128)S(1)}, f32[4,2048]{1,0:T(4,128)}, u32[]{:S(2)}) copy-start(f32[4,2048]{1,0:T(4,128)} %param.19) | copy-start | bytes 98308
  813.5 1.2 copy-start.11
  832.2 1.2 copy-start.12
Sparse Core Ops, SparseCore 0:
  56.4 53.3 all-gather.3
  154.8 58.8 all-gather.5
  215.7 70.0 all-gather.7
  443.1 68.1 reduce-scatter.4
  515.1 115.9 reduce-scatter.2

commit v4 on v3

--- a/solution.py
+++ b/solution.py
@@ -256,7 +256,8 @@
 
 
 def start_kernel(
-    n_dp, n, g_ref, w_ref, x_ref, h_ref, o_ref, y_ref, local, sg, rg, sa, ra, ss, rs, fs, fr
+    n_dp, n, g_ref, w_ref, v_ref, x_ref, h_ref, o_ref, p_ref, y_ref,
+    local, sg, rg, sa, ra, sv, rv, ss, rs, fs, fr,
 ):
     dp, me = lax.axis_index("dp"), lax.axis_index("ctx")
     half, parity, pair, partner, ahead, behind = pairs_of(n, me)
@@ -267,6 +268,7 @@
         pltpu.make_async_copy(g_ref.at[dp], h_ref.at[dp], local.at[0]),
         pltpu.make_async_copy(w_ref.at[me], o_ref.at[me], local.at[1]),
         pltpu.make_async_copy(x_ref, y_ref.at[me], local.at[2]),
+        pltpu.make_async_copy(v_ref.at[me], p_ref.at[me], local.at[3]),
     ]
     sends = []
     for k in range(1, n_dp):
@@ -275,6 +277,7 @@
     for k in range(1, n):
         to = (me + k) % n
         sends.append(remote(w_ref.at[to], o_ref.at[me], sa.at[k - 1], ra.at[k - 1], (dp, to)))
+        sends.append(remote(v_ref.at[to], p_ref.at[me], sv.at[k - 1], rv.at[k - 1], (dp, to)))
     for k, a in enumerate(ahead + [partner]):
         sends.append(remote(x_ref, y_ref.at[me], ss.at[k], rs.at[k], (dp, a)))
     for copy in sends + owns:
@@ -288,7 +291,9 @@
     sends[-1].wait_recv()
     for k in range(1, n):
         source = (me + n - k) % n
-        remote(w_ref.at[me], o_ref.at[source], sa.at[k - 1], ra.at[k - 1], (dp, source)).wait_recv()
+        peer = (dp, source)
+        remote(w_ref.at[me], o_ref.at[source], sa.at[k - 1], ra.at[k - 1], peer).wait_recv()
+        remote(v_ref.at[me], p_ref.at[source], sv.at[k - 1], rv.at[k - 1], peer).wait_recv()
     for k in range(1, n_dp):
         source = (dp + n_dp - k) % n_dp
         remote(g_ref.at[dp], h_ref.at[source], sg.at[k - 1], rg.at[k - 1], (source, me)).wait_recv()
@@ -300,52 +305,44 @@
         copy.wait()
 
 
-def start(g, w, x, number):
+def start(g, w, v, x, number):
     n_dp, n = lax.axis_size("dp"), lax.axis_size("ctx")
     half = n // 2
     dma = pltpu.SemaphoreType.DMA
-    g_out, w_out, x_all = pl.pallas_call(
+    g_out, w_out, v_out, x_all = pl.pallas_call(
         functools.partial(start_kernel, n_dp, n),
         out_shape=(
             jax.ShapeDtypeStruct(g.shape, g.dtype),
             jax.ShapeDtypeStruct(w.shape, w.dtype),
+            jax.ShapeDtypeStruct(v.shape, v.dtype),
             jax.ShapeDtypeStruct((n,) + x.shape, x.dtype),
         ),
-        in_specs=[ANY] * 3,
-        out_specs=(ANY,) * 3,
-        scratch_shapes=[dma((3,))]
+        in_specs=[ANY] * 4,
+        out_specs=(ANY,) * 4,
+        scratch_shapes=[dma((4,))]
         + [dma((n_dp - 1,))] * 2
-        + [dma((n - 1,))] * 2
+        + [dma((n - 1,))] * 4
         + [dma((half,))] * 2
         + [dma((half - 1,))] * 2,
         compiler_params=params_of(number),
         name="start",
-    )(g, w, x)
-    return g_out, w_out, x_all.reshape(-1, x.shape[-1])
-
-
-def swap_behind(x):
-    n, me = lax.axis_size("dp"), lax.axis_index("dp")
-    out = jnp.zeros_like(x)
-    for k in range(n):
-        piece = lax.dynamic_index_in_dim(x, (me + k) % n, keepdims=True)
-        if k:
-            piece = lax.ppermute(piece, "dp", [(i, (i + k) % n) for i in range(n)])
-        out = lax.dynamic_update_index_in_dim(out, piece, (me + n - k) % n, 0)
-    return out
+    )(g, w, v, x)
+    return g_out, w_out, v_out, x_all.reshape(-1, x.shape[-1])
 
 
 def collect_kernel(
-    n_dp, n, g_ref, a_ref, w_ref, o_ref, y_ref,
+    n_dp, n, g_ref, h_ref, a_ref, w_ref, o_ref, h_out, y_ref,
     own, ra, rc, sb, pa, qa, pb, qb,
-    local, sa, rs, sc, rd, s1, r1, s2, r2,
+    local, sa, rs, sc, rd, s1, r1, s2, r2, sh, rh,
 ):
     dp, me = lax.axis_index("dp"), lax.axis_index("ctx")
     greet(
         [((dp + k) % n_dp, me) for k in range(1, n_dp)] + [(dp, (me + k) % n) for k in range(1, n)]
     )
-    mine = pltpu.make_async_copy(g_ref.at[dp], own, local)
+    mine = pltpu.make_async_copy(g_ref.at[dp], own, local.at[0])
     mine.start()
+    stay = pltpu.make_async_copy(h_ref.at[dp], h_out.at[dp], local.at[1])
+    stay.start()
     first = []
     for c in range(n):
         row = []
@@ -361,6 +358,12 @@
             copy.start()
             row.append(copy)
         first.append(row)
+    swaps = []
+    for k in range(1, n_dp):
+        to = (dp + k) % n_dp
+        copy = remote(h_ref.at[to], h_out.at[dp], sh.at[k - 1], rh.at[k - 1], (to, me))
+        copy.start()
+        swaps.append(copy)
     sums = reduce_ctx(n, dp, me, a_ref, w_ref, slice(0, a_ref.shape[1]), y_ref, pa, qa, pb, qb, s1, r1, s2, r2)
     mine.wait()
     second = []
@@ -380,14 +383,18 @@
     for c in range(n - 1):
         second[c].wait_recv()
         o_ref[(me + n - 1 - c) % n] = rc[c]
+    for k in range(1, n_dp):
+        source = (dp + n_dp - k) % n_dp
+        remote(h_ref.at[dp], h_out.at[source], sh.at[k - 1], rh.at[k - 1], (source, me)).wait_recv()
+    stay.wait()
     for row in first:
         for copy in row:
             copy.wait_send()
-    for copy in second + sums:
+    for copy in second + sums + swaps:
         copy.wait_send()
 
 
-def collect(g, a, w, number):
+def collect(g, h, a, w, number):
     n_dp, n = lax.axis_size("dp"), lax.axis_size("ctx")
     rows, width = g.shape[0] // (n_dp * n), g.shape[1]
     half, length, features = n // 2, a.shape[0] // n, w.shape[0]
@@ -396,10 +403,11 @@
         functools.partial(collect_kernel, n_dp, n),
         out_shape=(
             jax.ShapeDtypeStruct((n, rows, width), BF),
+            jax.ShapeDtypeStruct(h.shape, BF),
             jax.ShapeDtypeStruct((length, features), F32),
         ),
-        in_specs=[ANY, VMEM, VMEM],
-        out_specs=(VMEM, VMEM),
+        in_specs=[ANY, ANY, VMEM, VMEM],
+        out_specs=(VMEM, ANY, VMEM),
         scratch_shapes=[
             pltpu.VMEM((n, rows, width), BF),
             pltpu.VMEM((n, n_dp - 1, rows, width), BF),
@@ -409,7 +417,7 @@
             pltpu.VMEM((half, length, features), BF),
             pltpu.VMEM((half - 1, length, features), BF),
             pltpu.VMEM((half - 1, length, features), BF),
-            dma,
+            dma((2,)),
             dma((n, n_dp - 1)),
             dma((n, n_dp - 1)),
             dma((n - 1,)),
@@ -418,10 +426,12 @@
             dma((half,)),
             dma((half - 1,)),
             dma((half - 1,)),
+            dma((n_dp - 1,)),
+            dma((n_dp - 1,)),
         ],
         compiler_params=params_of(number),
         name="collect",
-    )(g.reshape(n_dp, n, rows, width), a, w)
+    )(g.reshape(n_dp, n, rows, width), h, a, w)
 
 
 def total_kernel(n_dp, n, ga_ref, gu_ref, gd_ref, gain_ref, o_ref, mine, buf, part, all_parts, ss, rs, st, rt):
@@ -563,24 +573,28 @@
     )(factor.reshape(1, 1), params, first, second, ga, gu, gd)
 
 
-def arrange_kernel(n, n_dp, p_ref, a_ref, g_ref, u_ref, d_ref):
+def arrange_kernel(n, n_dp, p_ref, a_ref, o_ref, g_ref, d_ref):
     part = pl.program_id(0)
-    hc = a_ref.shape[2] // 4
-    fs = g_ref.shape[2]
+    hc = o_ref.shape[2]
+    fs = d_ref.shape[2]
 
     @pl.when(part == 0)
     def _():
         for matrix in range(4):
             for c in range(n):
                 start = (matrix * n + c) * hc
-                a_ref[c, :, matrix * hc : (matrix + 1) * hc] = p_ref[:, start : start + hc].astype(BF)
-
-    for index, ref in ((1, g_ref), (2, u_ref), (3, d_ref)):
+                value = p_ref[:, start : start + hc].astype(BF)
+                if matrix < 3:
+                    a_ref[c, :, matrix * hc : (matrix + 1) * hc] = value
+                else:
+                    o_ref[c] = value
+
+    for index, ref, first in ((1, g_ref, 0), (2, g_ref, fs), (3, d_ref, 0)):
 
         @pl.when(part == index)
         def _():
             for d in range(n_dp):
-                ref[d] = p_ref[:, d * fs : (d + 1) * fs].astype(BF)
+                ref[d, :, first : first + fs] = p_ref[:, d * fs : (d + 1) * fs].astype(BF)
 
 
 def arrange(params, width):
@@ -588,7 +602,7 @@
     rows, columns = params.shape
     fs, hc = columns // 4 // n_dp, width // n
     whole = lambda shape: pl.BlockSpec(shape, lambda i: (0,) * len(shape))
-    shapes = [(n, rows, 4 * hc)] + [(n_dp, rows, fs)] * 3
+    shapes = [(n, rows, 3 * hc), (n, rows, hc), (n_dp, rows, 2 * fs), (n_dp, rows, fs)]
     return pl.pallas_call(
         functools.partial(arrange_kernel, n, n_dp),
         grid=(4,),
@@ -638,20 +652,38 @@
 
 
 def attend_kernel(
-    n, x_ref, w_ref, gain_ref, cos_ref, sin_ref, col_ref, row_ref,
-    y_ref, q_ref, k_ref, v_ref, o_ref, pre_ref, scale_ref, lse_ref,
-    buf, pa, qa, pb, qb, ss, rs, s1, r1, s2, r2,
+    n_dp, n, x_ref, w_ref, wo_ref, d_ref, gain_ref, cos_ref, sin_ref, col_ref, row_ref,
+    y_ref, q_ref, k_ref, v_ref, o_ref, pre_ref, scale_ref, lse_ref, wo_all, d_out,
+    buf, pa, qa, pb, qb, ss, rs, s1, r1, s2, r2, sw, rw, sd, rd, local,
 ):
     dp, me = lax.axis_index("dp"), lax.axis_index("ctx")
     seq, width = x_ref.shape
     hc = o_ref.shape[1]
     block = min(seq, 256)
-    greet([(dp, (me + k) % n) for k in range(1, n)])
+    greet(
+        [((dp + k) % n_dp, me) for k in range(1, n_dp)] + [(dp, (me + k) % n) for k in range(1, n)]
+    )
+    piece = wo_ref.shape[0]
+
+    def part_of(d):
+        return wo_all.at[pl.ds(pl.multiple_of(d * piece, piece), piece), :]
+
+    owns = [
+        pltpu.make_async_copy(wo_ref, part_of(dp), local.at[0]),
+        pltpu.make_async_copy(d_ref.at[dp], d_out.at[dp], local.at[1]),
+    ]
+    behind_wo, behind_d = [], []
+    for k in range(1, n_dp):
+        to = (dp + k) % n_dp
+        behind_wo.append(remote(wo_ref, part_of(dp), sw.at[k - 1], rw.at[k - 1], (to, me)))
+        behind_d.append(remote(d_ref.at[to], d_out.at[dp], sd.at[k - 1], rd.at[k - 1], (to, me)))
+    for copy in behind_wo + behind_d + owns:
+        copy.start()
 
     @pl.loop(0, seq // block)
     def _(i):
         rows = pl.ds(pl.multiple_of(i * block, block), block)
-        value = dot(x_ref[rows, :], w_ref[:, : 3 * hc])
+        value = dot(x_ref[rows, :], w_ref[...])
         pre_ref[rows, :] = value[:, : 2 * hc]
         v_ref[rows, :] = value[:, 2 * hc :].astype(BF)
         squares = value[:, : 2 * hc] * value[:, : 2 * hc]
@@ -685,19 +717,28 @@
             o_ref[rows, part] = (dot(weights.astype(BF), v_ref[:, part]) / total).astype(BF)
             lse_ref[rows, head : head + 1] = top + jnp.log(total)
 
-    cols = slice(3 * hc, 4 * hc)
-    for copy in reduce_ctx(n, dp, me, o_ref, w_ref, cols, y_ref, pa, qa, pb, qb, s1, r1, s2, r2):
+    owns[0].wait()
+    for k in range(1, n_dp):
+        source = (dp + n_dp - k) % n_dp
+        remote(wo_ref, part_of(source), sw.at[k - 1], rw.at[k - 1], (source, me)).wait_recv()
+    cols = slice(0, hc)
+    sums = reduce_ctx(n, dp, me, o_ref, wo_all, cols, y_ref, pa, qa, pb, qb, s1, r1, s2, r2)
+    for k in range(1, n_dp):
+        source = (dp + n_dp - k) % n_dp
+        remote(d_ref.at[dp], d_out.at[source], sd.at[k - 1], rd.at[k - 1], (source, me)).wait_recv()
+    for copy in sums + behind_wo + behind_d:
         copy.wait_send()
-
-
-def attend(x_all, w, gain, cos, sine, info_col, info_row, number):
-    n = lax.axis_size("ctx")
+    owns[1].wait()
+
+
+def attend(x_all, w, wo, d, gain, cos, sine, info_col, info_row, number):
+    n_dp, n = lax.axis_size("dp"), lax.axis_size("ctx")
     seq, width = x_all.shape
-    half, length, hc = n // 2, seq // n, w.shape[1] // 4
+    half, length, hc = n // 2, seq // n, w.shape[1] // 3
     dma = pltpu.SemaphoreType.DMA
     low = jax.ShapeDtypeStruct((seq, hc), BF)
     return pl.pallas_call(
-        functools.partial(attend_kernel, n),
+        functools.partial(attend_kernel, n_dp, n),
         out_shape=(
             jax.ShapeDtypeStruct((length, width), F32),
             low,
@@ -707,9 +748,11 @@
             jax.ShapeDtypeStruct((seq, 2 * hc), F32),
             jax.ShapeDtypeStruct((seq, 8), F32),
             jax.ShapeDtypeStruct((seq, 8), F32),
+            jax.ShapeDtypeStruct((width, hc), BF),
+            jax.ShapeDtypeStruct(d.shape, BF),
         ),
-        in_specs=[VMEM] * 7,
-        out_specs=(VMEM,) * 8,
+        in_specs=[VMEM] * 2 + [ANY] * 2 + [VMEM] * 5,
+        out_specs=(VMEM,) * 9 + (ANY,),
         scratch_shapes=[
             pltpu.VMEM((n, 8, seq), F32),
             pltpu.VMEM((half, length, width), BF),
@@ -722,10 +765,15 @@
             dma((half,)),
             dma((half - 1,)),
             dma((half - 1,)),
+            dma((n_dp - 1,)),
+            dma((n_dp - 1,)),
+            dma((n_dp - 1,)),
+            dma((n_dp - 1,)),
+            dma((2,)),
         ],
         compiler_params=params_of(number),
         name="attend",
-    )(x_all, w, gain, cos, sine, info_col, info_row)
+    )(x_all, w, wo, d, gain, cos, sine, info_col, info_row)
 
 
 def attend_back_kernel(
@@ -752,7 +800,7 @@
 
     def project(b):
         rows = pl.ds(pl.multiple_of(b * length, length), length)
-        do_ref[rows, :] = dot(all_ref[b], w_ref[:, 3 * hc : 4 * hc]).astype(BF)
+        do_ref[rows, :] = dot(all_ref[b], w_ref[...]).astype(BF)
 
     project(me)
     sends[-1].wait_recv()
@@ -891,15 +939,10 @@
             values.reshape(t, n_ctx, n_dp, rows).transpose(0, 2, 1, 3).reshape(t, width)
         )
 
-    wa, wg, wu, wd = arrange(params, width)
-    wg, wa, x_all = start(wg, wa, tokens, 1)
-    w_g = lax.all_gather(wg.reshape(n_dp * rows, fs), "ctx", axis=0, tiled=True)
-    wa = gather_dp(wa.reshape(n_ctx * rows, 4 * hc), 2)
-    wu, wd, wa = lax.optimization_barrier((wu, wd, wa))
-    w_u, w_d = [
-        lax.all_gather(swap_behind(w).reshape(n_dp * rows, fs), "ctx", axis=0, tiled=True)
-        for w in (wu, wd)
-    ]
+    w_qkv, w_o, w_gu, w_d = arrange(params, width)
+    w_gu, w_qkv, w_o, x_all = start(w_gu, w_qkv, w_o, tokens, 1)
+    w_gu = lax.all_gather(w_gu.reshape(n_dp * rows, 2 * fs), "ctx", axis=0, tiled=True)
+    w_qkv = gather_dp(w_qkv.reshape(n_ctx * rows, 3 * hc), 2)
 
     indices = jnp.arange(seq, dtype=jnp.int32)
     owners = indices // length
@@ -919,12 +962,16 @@
     my_gains = lax.dynamic_slice_in_dim(gains[:2], me_ctx * hc, hc, axis=1)
     tables = (my_gains, cos_tab, sine_tab, info_col, info_row)
 
-    branch, queries, keys, values, attn_low, qk_pre, scales, lse = attend(x_all, wa, *tables, 3)
+    branch, queries, keys, values, attn_low, qk_pre, scales, lse, w_o, w_d = attend(
+        x_all, w_qkv, w_o.reshape(n_ctx * rows, hc), w_d, *tables, 3
+    )
+    w_d = lax.all_gather(w_d.reshape(n_dp * rows, fs), "ctx", axis=0, tiled=True)
     a_scale = rms_scale(branch)
     hidden1 = tokens.astype(F32) + branch * a_scale * gains[2]
 
     h1_all = gather_dp(mix(hidden1.astype(BF)), 4)
-    gate_pre, up_pre = dot(h1_all, w_g), dot(h1_all, w_u)
+    gate_up = dot(h1_all, w_gu)
+    gate_pre, up_pre = gate_up[:, :fs], gate_up[:, fs:]
     gate_sig = jax.nn.sigmoid(gate_pre)
     silu_val = gate_pre * gate_sig
     inner = (silu_val * up_pre).astype(BF)
@@ -941,19 +988,21 @@
     d_inner = dot(d_mlp_all, w_d)
     d_gate = (d_inner * up_pre * gate_sig * (1.0 + gate_pre * (1.0 - gate_sig))).astype(BF)
     d_upper = (d_inner * silu_val).astype(BF)
-    d_h1 = upstream + unmix(scatter_dp((d_gate, w_g, d_upper, w_u), 7))
-    gu_grad = t_dot(h1_all, jnp.concatenate([d_gate, d_upper], axis=1)).astype(BF)
+    d_gu = jnp.concatenate([d_gate, d_upper], axis=1)
+    gu_grad = lax.psum_scatter(
+        t_dot(h1_all, d_gu).astype(BF), "ctx", scatter_dimension=0, tiled=True
+    ).reshape(n_dp, rows, 2 * fs)
+    d_h1 = upstream + unmix(scatter_dp((d_gu, w_gu), 7))
 
     g_attn_part = jnp.sum(d_h1 * branch * a_scale, axis=0)
     d_branch = norm_back(d_h1 * gains[2], branch, a_scale).astype(BF)
+    d_grad, d_branch = lax.optimization_barrier((d_grad, d_branch))
     d_branch_all, d_qkv, d_gain = attend_back(
-        d_branch, wa, *tables, queries, keys, values, qk_pre, scales, lse, 8
+        d_branch, w_o, *tables, queries, keys, values, qk_pre, scales, lse, 8
     )
     attn_grad = jnp.concatenate([t_dot(x_all, d_qkv), t_dot(d_branch_all, attn_low)], axis=1)
     d_grad = lax.all_to_all(d_grad, "dp", 0, 0, tiled=True).reshape(n_dp, rows, fs)
-    gu_grad = lax.psum_scatter(gu_grad, "ctx", scatter_dimension=0, tiled=True)
-    gu_grad = lax.all_to_all(gu_grad, "dp", 0, 0, tiled=True).reshape(n_dp, rows, 2 * fs)
-    attn_grad, d_x = collect(attn_grad.astype(BF), d_qkv, wa, 9)
+    attn_grad, gu_grad, d_x = collect(attn_grad.astype(BF), gu_grad, d_qkv, w_qkv, 9)
     d_input = d_h1 + d_x
 
     gain_part = jnp.stack(

time: 871 us -> 818 us (0.939)
  waiting for transfers between devices: 114 us -> 0.07 us
  Pallas kernels: 577 us -> 626 us
  local copies, waits for them, and re-layouts: 52.7 us -> 71.5 us
  matrix products: 64.7 us -> 54.7 us
    reduce_scatter x1, waiting for transfers between devices: 45.3 us -> 0.01 us  [shards(): lax.psum_scatter(t_dot(h1_all, d_gu).astype(BF), 'ctx', scatter_dimension...]
    pallas_call x1, Pallas kernels: 97.3 us -> 140 us  [collect(): pl.pallas_call(functools.partial(collect_kernel, n_dp, n), out_shape=(jax...]
    reduce_scatter x1, waiting for transfers between devices: 39.2 us -> 0.01 us  [shards(): lax.psum_scatter(t_dot(d_mlp_all, inner).astype(BF), 'ctx', scatter_dimen...]
    ppermute x6 -> x0, waiting for transfers between devices: 29.7 us -> none  [swap_behind(): piece = lax.ppermute(piece, 'dp', [(i, (i + k) % n) for i in range(n)])]
    pallas_call x1, Pallas kernels: 51.3 us -> 71.9 us  [attend_back(): pl.pallas_call(functools.partial(attend_back_kernel, n), out_shape=(jax.S...]
    unnamed x86, local copies, waits for them, and re-layouts: 18.6 us -> 32.3 us
    ppermute x6 -> x0, starting transfers between devices: 11.5 us -> none  [swap_behind(): piece = lax.ppermute(piece, 'dp', [(i, (i + k) % n) for i in range(n)])]
    pallas_call x3, Pallas kernels: 171 us -> 160 us  [gather_dp(): pl.pallas_call(functools.partial(gather_dp_kernel, n), out_shape=jax.Shap...]
  transfers between devices with their start and end apart: 13 -> 5, of which waited for: 7 -> 0; matrix products, arithmetic and copies ran while one was open for 11% -> 12% of each run, Pallas kernels for 46% -> 54%
where the time goes in v4:
time: 818 us; the launch traced here: 810 us
  Pallas kernels  626 us (77%)
  local copies, waits for them, and re-layouts  71.5 us (9%)
  matrix products  54.7 us (7%)
  other arithmetic  26.1 us (3%)
  between operations  17 us (2%)
  starting transfers between devices  14.9 us (2%)
    pallas_call x3, Pallas kernels, gather_dp(): pl.pallas_call(functools.partial(gather_dp_kernel, n), out_shape=jax.Shap...  160 us
    pallas_call x1, Pallas kernels, collect(): pl.pallas_call(functools.partial(collect_kernel, n_dp, n), out_shape=(jax...  140 us
    pallas_call x2, Pallas kernels, scatter_dp(): pl.pallas_call(functools.partial(scatter_dp_kernel, n, len(operands) // 2...  96.5 us
    pallas_call x1, Pallas kernels, attend_back(): pl.pallas_call(functools.partial(attend_back_kernel, n), out_shape=(jax.S...  71.9 us
    pallas_call x1, Pallas kernels, attend(): pl.pallas_call(functools.partial(attend_kernel, n_dp, n), out_shape=(jax....  61.3 us
    pallas_call x1, Pallas kernels, start(): pl.pallas_call(functools.partial(start_kernel, n_dp, n), out_shape=(jax.S...  43.9 us
    unnamed x86, local copies, waits for them, and re-layouts  32.3 us
    dot_general x4, matrix products, t_dot(): lax.dot_general(a, b, (((0,), (0,)), ((), ())), preferred_element_type=F32)  28.4 us
  transfers between devices with their start and end apart: 5, of which 0 were waited for; matrix products, arithmetic and copies ran while one was open for 12% of the time, Pallas kernels for 54%

profile of v4, /device:TPU:0, one launch (start us, length us, event | category | flops | bytes accessed | tf_op | source)
XLA Modules:
  0.0 810.0 jit_solution(2494585986358513859)
XLA Ops:
  7.2 4.2 arrange.1
  11.5 1.3 copy-done.9
  12.8 1.0 copy-done.17
  13.8 43.9 %start.1 = (bf16[4,64,4096]{2,1,0:T(8,128)(2,1)}, bf16[8,64,768]{2,1,0:T(8,128)(2,1)S(1)}, bf16[8,64,256]{2,1,0:T(8,128)(2,1)S(1)}, bf16[8,128,2048]{2,1,0:T(8,128)(2,1)}) custom-call(bf16[4,64,4096]{2,1,0:T(8,128)(2,1)} %copy-done.9, bf16[8,64,768]{2,1,0:T(8,128)(2,1)S(1)} %get-tuple-element.39.w_ref, bf16[8,64,256]{2,1,0:T(8,128)(2,1)S(1)} %get-tuple-element.40.v_ref, ...), custom_call_target="tpu_custom_call" | custom-call | tf_op jit(solution)/shard_map/start/pallas_call | solution.py:312
  57.8 63.0 %gather_dp.3 = bf16[4,512,768]{2,1,0:T(8,128)(2,1)S(1)} custom-call(bf16[512,768]{1,0:T(8,128)(2,1)S(1)} %bitcast.87), custom_call_target="tpu_custom_call" | custom-call | tf_op jit(solution)/shard_map/gather_dp/pallas_call | solution.py:148
  120.8 1.6 copy-done
  123.0 1.9 fusion.6
  125.3 61.3 %attend.1 = (f32[128,2048]{1,0:T(8,128)S(1)}, bf16[1024,256]{1,0:T(8,128)(2,1)S(1)}, bf16[1024,256]{1,0:T(8,128)(2,1)S(1)}, bf16[1024,256]{1,0:T(8,128)(2,1)S(1)...) custom-call(bf16[1024,2048]{1,0:T(8,128)(2,1)} %bitcast.91, ...), custom_call_target="tpu_custom_call" | custom-call | tf_op jit(solution)/shard_map/attend/pallas_call | solution.py:740
  191.9 1.0 fusion.2
  192.9 2.0 copy.83
  195.0 1.9 copy.84
  196.8 2.0 copy.85.x_ref
  198.9 1.0 copy-done.10
  199.9 48.3 %gather_dp.4 = bf16[4,128,2048]{2,1,0:T(8,128)(2,1)S(1)} custom-call(bf16[128,2048]{1,0:T(8,128)(2,1)S(1)} %copy-done.10), custom_call_target="tpu_custom_call" | custom-call | tf_op jit(solution)/shard_map/gather_dp/pallas_call | solution.py:148
  248.2 1.3 copy-done.6
  249.5 2.2 copy.89
  251.8 12.3 %fusion.20 = f32[512,4096]{1,0:T(8,128)S(1)} fusion(bf16[512,2048]{1,0:T(8,128)(2,1)} %bitcast.83, bf16[2048,4096]{1,0:T(8,128)(2,1)} %all-gather.3.cloned.1.call-done.refs_1_), kind=kOutput, calls=%fused_computation.69 | convolution fusion | flops 8589934592 | bytes 27262976 | tf_op jit(solution)/shard_map/dot_general | solution.py:55
  264.1 3.4 copy-done.33
  267.5 2.6 multiply_convert_fusion.2.refs_0_
  270.1 45.4 %scatter_dp.2 = f32[128,2048]{1,0:T(8,128)} custom-call(bf16[512,2048]{1,0:T(8,128)(2,1)} %multiply_convert_fusion.2.refs_0_, bf16[2048,2048]{1,0:T(8,128)(2,1)} %all-gather.5.cloned.1.call-done.refs_1_), custom_call_target="tpu_custom_call" | custom-call | tf_op jit(solution)/shard_map/scatter_dp/pallas_call | solution.py:242
  315.5 2.5 copy.86
  318.1 1.7 multiply_reduce_fusion.4
  319.7 2.5 multiply_reduce_fusion
  322.3 1.2 multiply_convert_fusion.4
  323.4 2.0 copy.92.x_ref
  325.5 1.0 copy-done.11
  326.5 48.4 %gather_dp.5 = bf16[4,128,2048]{2,1,0:T(8,128)(2,1)S(1)} custom-call(bf16[128,2048]{1,0:T(8,128)(2,1)S(1)} %copy-done.11), custom_call_target="tpu_custom_call" | custom-call | tf_op jit(solution)/shard_map/gather_dp/pallas_call | solution.py:148
  375.0 1.4 copy-done.8
  376.4 8.4 %convolution_convert_fusion.1 = bf16[2048,2048]{1,0:T(8,128)(2,1)} fusion(bf16[512,2048]{1,0:T(8,128)(2,1)S(1)} %bitcast.85, bf16[512,2048]{1,0:T(8,128)(2,1)} %multiply_convert_fusion.2.refs_0_), kind=kOutput, calls=%fused_computation.1 | convolution fusion | flops 4299161600 | bytes 12582912 | tf_op jit(solution)/shard_map/dot_general | solution.py:63
  385.2 14.1 %multiply_convert_fusion.1 = (bf16[512,2048]{1,0:T(8,128)(2,1)S(1)}, bf16[512,2048]{1,0:T(8,128)(2,1)S(1)}) fusion(f32[512,4096]{1,0:T(8,128)} %copy-done.33, bf16[512,2048]{1,0:T(8,128)(2,1)} %bitcast.86, bf16[2048,2048]{1,0:T(8,128)(2,1)} %all-gather.5.cloned.1.call-done.refs_1_), kind=kOutput, calls=%fused_computation.5 | convolution fusion | flops 4308598784 | bytes 23068672 | tf_op jit(solution)/shard_map/dot_general | solution.py:55
  399.4 1.3 copy-done.36
  401.4 12.7 %convolution_convert_fusion = bf16[2048,4096]{1,0:T(8,128)(2,1)} fusion(bf16[512,2048]{1,0:T(8,128)(2,1)S(1)} %bitcast.84, bf16[512,2048]{1,0:T(8,128)(2,1)S(1)} %get-tuple-element.75, bf16[512,2048]{1,0:T(8,128)(2,1)S(1)} %get-tuple-element.74), kind=kOutput, calls=%fused_computation | convolution fusion | flops 8606711808 | bytes 23068672 | tf_op jit(solution)/shard_map/dot_general | solution.py:63
  414.1 6.4 copy.96
  420.5 2.3 copy.87
  422.9 4.7 pad_maximum_fusion.refs_0_
  427.6 51.1 %scatter_dp.3 = f32[128,2048]{1,0:T(8,128)} custom-call(bf16[512,4096]{1,0:T(8,128)(2,1)} %pad_maximum_fusion.refs_0_, bf16[2048,4096]{1,0:T(8,128)(2,1)} %all-gather.3.cloned.1.call-done.refs_1_), custom_call_target="tpu_custom_call" | custom-call | tf_op jit(solution)/shard_map/scatter_dp/pallas_call | solution.py:242
  478.7 2.7 copy.93
  481.3 2.5 copy.94
  483.8 2.6 copy.95
  486.4 2.5 copy.88
  489.0 1.7 multiply_reduce_fusion.1
  490.8 3.3 multiply_convert_fusion.3
  494.0 1.1 copy-done.5
  495.1 1.2 copy-done.14
  496.3 1.0 copy-done.19
  497.4 1.0 copy-done.21
  498.4 1.0 copy-done.23
  499.4 1.1 copy-done.25
  500.5 1.0 copy-done.27
  501.5 71.9 %attend_back.1 = (bf16[8,128,2048]{2,1,0:T(8,128)(2,1)}, bf16[1024,768]{1,0:T(8,128)(2,1)}, f32[2,256]{1,0:T(2,128)S(1)}) custom-call(bf16[128,2048]{1,0:T(8,128)(2,1)S(1)} %copy-done.5, bf16[2048,256]{1,0:T(8,128)(2,1)S(1)} %copy-done.14, f32[2,256]{1,0:T(2,128)S(1)} %constant_dynamic-slice_fusion.gain_ref, f32[1024,128]{1,0:T(8,128)S(1)} %get-tuple-element.88.cos_ref, ...), custom_call_target="tpu_custom_call" | custom-call | tf_op jit(solution)/shard_map/attend_back/pallas_call | solution.py:876
  573.5 6.4 copy.98
  579.9 14.1 %all-to-all-start = ((bf16[4,64,2048]{2,1,0:T(8,128)(2,1)}), bf16[4,64,2048]{2,1,0:T(8,128)(2,1)S(1)}, u32[]{:S(2)}, u32[]{:S(2)}) async-start(bf16[4,64,2048]{2,1,0:T(8,128)(2,1)} %bitcast.105), calls=%async_computation.2 | async-start | bytes 2097152 | tf_op jit(solution)/shard_map/all_to_all | solution.py:1004
  594.2 3.6 convolution_convert_fusion.3
  597.8 3.6 convolution_convert_fusion.2
  601.5 2.6 pad_maximum_fusion.1.g_ref
  604.0 1.4 copy-done.13
  605.4 140.2 %collect.1 = (bf16[8,64,1024]{2,1,0:T(8,128)(2,1)S(1)}, bf16[4,64,4096]{2,1,0:T(8,128)(2,1)S(1)}, f32[128,2048]{1,0:T(8,128)S(1)}) custom-call(bf16[4,8,64,1024]{3,2,1,0:T(8,128)(2,1)} %pad_maximum_fusion.1.g_ref, bf16[4,64,4096]{2,1,0:T(8,128)(2,1)} %bitcast.104, bf16[1024,768]{1,0:T(8,128)(2,1)S(1)} %copy-done.13, bf16[2048,768]{1,0:T(8,128)(2,1)} %bitcast.81), custom_call_target="tpu_custom_call" | custom-call | tf_op jit(solution)/shard_map/collect/pallas_call | solution.py:402
  745.6 1.0 copy-done.2
  746.6 1.0 copy-done.15
  747.6 1.2 copy-done.3
  748.8 23.6 %total.1 = f32[72,128]{1,0:T(8,128)S(1)} custom-call(bf16[8,64,1024]{2,1,0:T(8,128)(2,1)S(1)} %copy-done.3, bf16[4,64,4096]{2,1,0:T(8,128)(2,1)S(1)} %get-tuple-element.61.gu_ref, bf16[4,64,2048]{2,1,0:T(8,128)(2,1)S(1)} %all-to-all-done.gd_ref, f32[64,128]{1,0:T(8,128)S(1)} %reshape.241.gain_ref), custom_call_target="tpu_custom_call" | custom-call | tf_op jit(solution)/shard_map/total/pallas_call | solution.py:492
  773.5 1.0 fusion.4
  776.6 1.2 copy-done.4
  777.8 24.3 %adam.1 = (f32[64,32768]{1,0:T(8,128)}, f32[64,32768]{1,0:T(8,128)}, f32[64,32768]{1,0:T(8,128)}) custom-call(f32[1,1]{1,0:T(1,128)} %bitcast.42.factor_ref, f32[64,32768]{1,0:T(8,128)} %p_ref.3, f32[64,32768]{1,0:T(8,128)} %m_ref.1, f32[64,32768]{1,0:T(8,128)} %v_ref.1, bf16[8,64,1024]{2,1,0:T(8,128)(2,1)S(1)} %copy-done.4, ...), custom_call_target="tpu_custom_call" | custom-call | tf_op jit(solution)/shard_map/adam/pallas_call | solution.py:549
  (110 shorter events, 9.6 us)
Async XLA Ops:
  7.2 6.6 copy-start.1
  7.2 244.6 %all-gather.3.cloned.1.call-start = ((), (), s32[]{:S(2)}) async-start(), calls=%async_computation.3 | async-start | bytes 18874368 | tf_op jit(solution)/shard_map/all_gather | solution.py:944
  11.5 1.3 copy-start.9
  12.8 1.0 copy-start.17
  13.8 108.8 %copy-start.42 = (s32[8]{0:T(128)S(1)}, s32[8]{0:T(128)}, u32[]{:S(2)}) copy-start(s32[8]{0:T(128)} %param.13) | copy-start | bytes 100
  13.8 108.9 %copy-start.41 = (s32[1,1024]{1,0:T(1,128)S(1)}, s32[1,1024]{1,0:T(1,128)}, u32[]{:S(2)}) copy-start(s32[1,1024]{1,0:T(1,128)} %param.12) | copy-start | bytes 12292
  57.7 65.3 %slice-start = ((f32[4,2048]{1,0:T(4,128)}), f32[2,2048]{1,0:T(2,128)S(1)}, s32[]{:S(2)}) async-start(f32[4,2048]{1,0:T(4,128)} %param.17), calls=%async_computation.7 | async-start | bytes 32768 | tf_op jit(solution)/shard_map/slice | solution.py:962
  57.7 212.4 %all-gather.5.cloned.1.call-start = ((), (), s32[]{:S(2)}) async-start(), calls=%async_computation.4 | async-start | bytes 9437184 | tf_op jit(solution)/shard_map/all_gather | solution.py:968
  120.8 1.6 copy-start
  125.2 66.6 %copy-start.38 = (f32[4,2048]{1,0:T(4,128)S(1)}, f32[4,2048]{1,0:T(4,128)}, u32[]{:S(2)}) copy-start(f32[4,2048]{1,0:T(4,128)} %param.17) | copy-start | bytes 98308
  186.6 0.8 copy-start.18
  187.4 0.8 copy-start.20
  188.2 0.8 copy-start.22
  189.0 0.8 copy-start.24
  189.8 0.8 copy-start.26
  190.6 0.8 copy-start.28
  191.4 302.6 %reduce-scatter.3.cloned.1.call-start = ((), (), s32[]{:S(2)}) async-start(), calls=%async_computation.5 | async-start | bytes 9437184 | tf_op jit(solution)/shard_map/reduce_scatter | solution.py:985
  198.9 1.0 copy-start.10
  248.2 1.3 copy-start.6
  264.1 3.4 copy-start.33
  318.1 4.2 copy-start.30
  318.1 4.2 copy-start.32
  325.5 1.0 copy-start.11
  375.0 1.4 copy-start.8
  384.8 219.2 %reduce-scatter.5.cloned.1.call-start = ((), (), s32[]{:S(2)}) async-start(), calls=%async_computation.6 | async-start | bytes 18874368 | tf_op jit(solution)/shard_map/reduce_scatter | solution.py:992
  385.2 16.2 %copy-start.7 = (bf16[4,128,2048]{2,1,0:T(8,128)(2,1)S(1)}, bf16[4,128,2048]{2,1,0:T(8,128)(2,1)}, u32[]{:S(2)}) copy-start(bf16[4,128,2048]{2,1,0:T(8,128)(2,1)} %copy-done.6) | copy-start | bytes 6291460
  399.3 1.3 copy-start.36
  399.4 2.0 copy-start.37
  494.0 1.1 copy-start.5
  495.1 1.2 copy-start.14
  496.3 1.0 copy-start.19
  497.4 1.0 copy-start.21
  498.4 1.0 copy-start.23
  499.4 1.1 copy-start.25
  500.5 1.0 copy-start.27
  573.4 20.7 %copy-start.29 = (bf16[1024,256]{1,0:T(8,128)(2,1)S(1)}, bf16[1024,256]{1,0:T(8,128)(2,1)}, u32[]{:S(2)}) copy-start(bf16[1024,256]{1,0:T(8,128)(2,1)} %copy-done.28) | copy-start | bytes 1572868
  579.9 17.9 %copy-start.12 = (bf16[1024,768]{1,0:T(8,128)(2,1)S(1)}, bf16[1024,768]{1,0:T(8,128)(2,1)}, u32[]{:S(2)}) copy-start(bf16[1024,768]{1,0:T(8,128)(2,1)} %get-tuple-element.56.a_ref) | copy-start | bytes 4718596
  579.9 167.7 %all-to-all-start = ((bf16[4,64,2048]{2,1,0:T(8,128)(2,1)}), bf16[4,64,2048]{2,1,0:T(8,128)(2,1)S(1)}, u32[]{:S(2)}, u32[]{:S(2)}) async-start(bf16[4,64,2048]{2,1,0:T(8,128)(2,1)} %bitcast.105), calls=%async_computation.2 | async-start | bytes 2097152 | tf_op jit(solution)/shard_map/all_to_all | solution.py:1004
  594.2 3.7 copy-start.35
  604.0 1.4 copy-start.13
  605.4 170.5 %copy-start.39 = (f32[4,2048]{1,0:T(4,128)S(1)}, f32[4,2048]{1,0:T(4,128)}, u32[]{:S(2)}) copy-start(f32[4,2048]{1,0:T(4,128)} %param.18) | copy-start | bytes 98308
  605.4 170.5 %copy-start.40 = (f32[4,2048]{1,0:T(4,128)S(1)}, f32[4,2048]{1,0:T(4,128)}, u32[]{:S(2)}) copy-start(f32[4,2048]{1,0:T(4,128)} %param.19) | copy-start | bytes 98308
  745.6 1.0 copy-start.2
  746.6 1.0 copy-start.15
  747.6 1.2 copy-start.3
  748.8 24.7 %copy-start.16 = (f32[128,2048]{1,0:T(8,128)S(1)}, f32[128,2048]{1,0:T(8,128)}, u32[]{:S(2)}) copy-start(f32[128,2048]{1,0:T(8,128)} %copy-done.15) | copy-start | bytes 3145732
  748.8 24.7 %copy-start.31 = (f32[128,2048]{1,0:T(8,128)S(1)}, f32[128,2048]{1,0:T(8,128)}, u32[]{:S(2)}) copy-start(f32[128,2048]{1,0:T(8,128)} %copy.95) | copy-start | bytes 3145732
  748.8 24.7 %copy-start.34 = (bf16[1,128,2048]{2,1,0:T(8,128)(2,1)S(1)}, bf16[1,128,2048]{2,1,0:T(8,128)(2,1)}, u32[]{:S(2)}) copy-start(bf16[1,128,2048]{2,1,0:T(8,128)(2,1)} %param.11) | copy-start | bytes 1572868
  776.6 1.2 copy-start.4
Sparse Core Ops, SparseCore 0:
  57.9 100.5 all-gather.2
  191.5 63.7 all-gather.4
  384.9 69.0 reduce-scatter.2
  457.8 138.4 reduce-scatter.4

commit v5 on v4

--- a/solution.py
+++ b/solution.py
@@ -157,43 +157,70 @@
     return out.reshape((n * x.shape[0],) + x.shape[1:])
 
 
+def group_of(n_dp, n, dp, me):
+    pair, parity = me // 2, me % 2
+    return 2 * n_dp, 2 * dp + parity, lambda j: (j // 2, 2 * pair + j % 2)
+
+
+def greet_all(n_dp, n, dp, me):
+    partner = me + 1 - 2 * (me % 2)
+    others = [(dp + k) % n_dp for k in range(1, n_dp)]
+    greet([(dp, (me + k) % n) for k in range(1, n)] + [(d, c) for d in others for c in (me, partner)])
+
+
+def swap(src, dst, send, recv, count, mine, place):
+    sends, receives = [], []
+    for k in range(1, count):
+        to, source = (mine + k) % count, (mine + count - k) % count
+        sends.append(remote(src.at[to], dst.at[mine], send.at[k - 1], recv.at[k - 1], place(to)))
+        receives.append(
+            remote(src.at[mine], dst.at[source], send.at[k - 1], recv.at[k - 1], place(source))
+        )
+    for copy in sends:
+        copy.start()
+    return sends, receives
+
+
+def tiles(total, tile, body):
+    tile = min(total, tile)
+
+    @pl.loop(0, total // tile)
+    def _(j):
+        body(pl.ds(pl.multiple_of(j * tile, tile), tile))
+
+
 def reduce_ctx(n, dp, me, a_ref, w_ref, cols, o_ref, sa, ra, sb, rb, s1, r1, s2, r2):
     half, parity, pair, partner, ahead, behind = pairs_of(n, me)
     length, width = o_ref.shape
-    tile = width // 4
-
-    def product(block, store):
-        rows = pl.ds(pl.multiple_of(block * length, length), length)
-
-        @pl.loop(0, 4)
-        def _(j):
-            part = pl.ds(pl.multiple_of(j * tile, tile), tile)
-            store(part, dot_t(a_ref[rows, :], w_ref[part, cols]))
+
+    def rows(block):
+        return pl.ds(pl.multiple_of(block * length, length), length)
 
     first, second = [], []
     for k in range(half):
-
-        def store(part, value, k=k):
+        target = (pair + k + 1) % half
+
+        def give(part):
+            value = dot_t(a_ref[rows(2 * target + 1 - parity), :], w_ref[part, cols])
             sa[k, :, part] = value.astype(BF)
 
-        product(2 * ((pair + k + 1) % half) + 1 - parity, store)
+        tiles(width, 512, give)
         copy = remote(sa.at[k], ra.at[k], s1.at[k], r1.at[k], (dp, partner))
         copy.start()
         first.append(copy)
-    for k in range(half):
-        target = 2 * ((pair + k + 1) % half) + parity
-        first[k].wait_recv()
-
-        def store(part, value, k=k):
+        copy.wait_recv()
+
+        def keep(part):
+            value = dot_t(a_ref[rows(2 * target + parity), :], w_ref[part, cols])
             value = value + ra[k, :, part].astype(F32)
             if k < half - 1:
                 sb[k, :, part] = value.astype(BF)
             else:
                 o_ref[:, part] = value
 
-        product(target, store)
+        tiles(width, 512, keep)
         if k < half - 1:
-            copy = remote(sb.at[k], rb.at[k], s2.at[k], r2.at[k], (dp, target))
+            copy = remote(sb.at[k], rb.at[k], s2.at[k], r2.at[k], (dp, 2 * target + parity))
             copy.start()
             second.append(copy)
     for k in range(half - 1):
@@ -202,57 +229,371 @@
     return first + second
 
 
-def scatter_dp_kernel(n, pairs, *refs):
-    operands, (o_ref, sa, ra, ss, rs) = refs[: 2 * pairs], refs[2 * pairs :]
-    me, ctx = lax.axis_index("dp"), lax.axis_index("ctx")
+def load_rows(hbm, vmem, sems):
+    half, n_dp, rows, _ = hbm.shape
+    copies = []
+    for d in range(n_dp):
+        for p in range(half):
+            part = pl.ds((d * half + p) * rows, rows)
+            copies.append(pltpu.make_async_copy(hbm.at[p, d], vmem.at[part, :], sems.at[d * half + p]))
+    for copy in copies:
+        copy.start()
+    return copies
+
+
+def gather_group(n, dp, me, all_ref, length, sr, rr, sl, rl, sf, rf, process):
+    parity = me % 2
+    partner = me + 1 - 2 * parity
+
+    def block(b, side):
+        start = (2 * b + side) * length
+        return all_ref.at[pl.ds(pl.multiple_of(start, length), length), :]
+
+    def right(s, b):
+        return remote(block(b, parity), block(b, parity), sr.at[s], rr.at[s], (dp + 1, me))
+
+    def left(s, b):
+        return remote(block(b, parity), block(b, parity), sl.at[s], rl.at[s], (dp - 1, me))
+
+    def aside(b):
+        return remote(block(b, parity), block(b, parity), sf.at[b], rf.at[b], (dp, partner))
+
+    def from_aside(b):
+        return remote(block(b, 1 - parity), block(b, 1 - parity), sf.at[b], rf.at[b], (dp, partner))
+
+    for s in range(n):
+        if s == 0:
+            aside(dp).start()
+        else:
+
+            @pl.when(dp >= s)
+            def _():
+                right(s - 1, dp - s).wait_recv()
+
+            @pl.when(dp + s < n)
+            def _():
+                left(s - 1, dp + s).wait_recv()
+
+        @pl.when((dp < n - 1) & (dp >= s))
+        def _():
+            right(s, dp - s).start()
+
+        @pl.when((dp > 0) & (dp + s < n))
+        def _():
+            left(s, dp + s).start()
+
+        if s == 0:
+            from_aside(dp).wait_recv()
+            process(dp, True)
+        else:
+
+            @pl.when(dp >= s)
+            def _():
+                aside(dp - s).start()
+
+            @pl.when(dp + s < n)
+            def _():
+                aside(dp + s).start()
+
+            below = jnp.where(dp >= s, 1, 0)
+            above = jnp.where(dp + s < n, 1, 0)
+
+            @pl.loop(0, below + above)
+            def _(j):
+                b = jnp.where(j < below, dp - s, dp + s)
+                from_aside(b).wait_recv()
+                process(b, False)
+
+    for s in range(n):
+
+        @pl.when((dp < n - 1) & (dp >= s))
+        def _():
+            right(s, dp - s).wait_send()
+
+        @pl.when((dp > 0) & (dp + s < n))
+        def _():
+            left(s, dp + s).wait_send()
+
+        aside(s).wait_send()
+
+
+def gather_sems(n_dp):
+    return [pltpu.SemaphoreType.DMA((n_dp,))] * 6
+
+
+def give_block(dp, me, b, own, a_ref, w_ref, o_ref, sa, ra, sb, rb, s1, r1, s2, r2):
     length, width = o_ref.shape
-    tile = width // 4
-
-    def product(block, out):
-        rows = pl.ds(pl.multiple_of(block * length, length), length)
-
-        @pl.loop(0, 4)
-        def _(j):
-            part = pl.ds(pl.multiple_of(j * tile, tile), tile)
-            value = dot_t(operands[0][rows, :], operands[1][part, :])
-            for i in range(1, pairs):
-                value += dot_t(operands[2 * i][rows, :], operands[2 * i + 1][part, :])
-            out[:, part] = value.astype(out.dtype)
-
-    greet([((me + k) % n, ctx) for k in range(1, n)])
-    copies = []
+    parity = me % 2
+    partner = me + 1 - 2 * parity
+
+    def rows(side):
+        return pl.ds(pl.multiple_of((2 * b + side) * length, length), length)
+
+    def give(part):
+        sa[b, :, part] = dot_t(a_ref[rows(1 - parity), :], w_ref[part, :]).astype(BF)
+
+    tiles(width, 512, give)
+    copy = remote(sa.at[b], ra.at[b], s1.at[b], r1.at[b], (dp, partner))
+    copy.start()
+    copy.wait_recv()
+
+    def keep(part):
+        value = dot_t(a_ref[rows(parity), :], w_ref[part, :]) + ra[b, :, part].astype(F32)
+        if own:
+            o_ref[:, part] = value
+        else:
+            sb[b, :, part] = value.astype(BF)
+
+    tiles(width, 512, keep)
+    if not own:
+        remote(sb.at[b], rb.at[dp], s2.at[b], r2.at[dp], (b, me)).start()
+
+
+def give_end(n, dp, me, o_ref, sa, ra, sb, rb, s1, r1, s2, r2):
+    partner = me + 1 - 2 * (me % 2)
     for k in range(1, n):
-        target = (me + k) % n
-        product(target, sa.at[k - 1])
-        copy = remote(sa.at[k - 1], ra.at[k - 1], ss.at[k - 1], rs.at[k - 1], (target, ctx))
-        copy.start()
-        copies.append(copy)
-    product(me, o_ref)
-    for k in range(n - 1):
-        copies[k].wait_recv()
-        o_ref[...] += ra[k].astype(F32)
-    for copy in copies:
-        copy.wait_send()
-
-
-def scatter_dp(operands, number):
-    n = lax.axis_size("dp")
-    length, width = operands[0].shape[0] // n, operands[1].shape[0]
-    dma = pltpu.SemaphoreType.DMA
+        b = (dp + k) % n
+        remote(sb.at[b], rb.at[b], s2.at[b], r2.at[b], (b, me)).wait_recv()
+        o_ref[...] += rb[b].astype(F32)
+    for k in range(1, n):
+        b = (dp + k) % n
+        remote(sb.at[b], rb.at[b], s2.at[b], r2.at[b], (b, me)).wait_send()
+    for b in range(n):
+        remote(sa.at[b], ra.at[b], s1.at[b], r1.at[b], (dp, partner)).wait_send()
+
+
+def give_scratch(n_dp, length, width):
+    return [pltpu.VMEM((n_dp, length, width), BF)] * 4 + [pltpu.SemaphoreType.DMA((n_dp,))] * 4
+
+
+def greet_group(n_dp, dp, me):
+    partner = me + 1 - 2 * (me % 2)
+    greet([(dp, partner)] + [((dp + k) % n_dp, me) for k in range(1, n_dp)])
+
+
+def ff_forward_kernel(
+    n_dp, h_ref, up_ref, gain_ref, gu_hbm, d_hbm,
+    res_ref, dm_ref, gp_ref, all_ref, pre_ref, hid_ref,
+    gu_ref, d_ref, acc, sem_gu, sem_d, *rest,
+):
+    gather, give = rest[:6], rest[6:]
+    dp, me = lax.axis_index("dp"), lax.axis_index("ctx")
+    length, width = h_ref.shape
+    fh = hid_ref.shape[1]
+    loads_gu, loads_d = load_rows(gu_hbm, gu_ref, sem_gu), load_rows(d_hbm, d_ref, sem_d)
+    mine = pl.ds(pl.multiple_of((2 * dp + me % 2) * length, length), length)
+    all_ref[mine, :] = h_ref[...].astype(BF)
+    greet_group(n_dp, dp, me)
+
+    def process(b, own):
+        rows = pl.ds(pl.multiple_of(2 * b * length, 2 * length), 2 * length)
+        if own:
+            for copy in loads_gu:
+                copy.wait()
+
+        def hidden(part):
+            second = pl.ds(pl.multiple_of(fh + part.start, part.size), part.size)
+            gate = dot(all_ref[rows, :], gu_ref[:, part])
+            upper = dot(all_ref[rows, :], gu_ref[:, second])
+            pre_ref[rows, part] = gate
+            pre_ref[rows, second] = upper
+            hid_ref[rows, part] = (gate * jax.nn.sigmoid(gate) * upper).astype(BF)
+
+        tiles(fh, 256, hidden)
+        if own:
+            for copy in loads_d:
+                copy.wait()
+        give_block(dp, me, b, own, hid_ref, d_ref, acc, *give)
+
+    gather_group(n_dp, dp, me, all_ref, length, *gather, process)
+    give_end(n_dp, dp, me, acc, *give)
+    gp_ref[...] = jnp.zeros_like(gp_ref)
+
+    def finish(rows):
+        out, up, gain = acc[rows, :], up_ref[rows, :].astype(F32), gain_ref[...]
+        scale = rms_scale(out)
+        res_ref[rows, :] = (h_ref[rows, :] + out * scale * gain).astype(BF)
+        gp_ref[...] += jnp.sum(up * out * scale, axis=0, keepdims=True)
+        dm_ref[rows, :] = norm_back(up * gain, out, scale).astype(BF)
+
+    tiles(length, 16, finish)
+
+
+def ff_forward(h1, up, gain, w_gu, w_d, number):
+    n_dp = lax.axis_size("dp")
+    (length, width), fh = h1.shape, w_d.shape[3]
+    tokens = 2 * n_dp * length
+    blocks = w_d.shape[0] * n_dp
+    low = jax.ShapeDtypeStruct((length, width), BF)
     return pl.pallas_call(
-        functools.partial(scatter_dp_kernel, n, len(operands) // 2),
-        out_shape=jax.ShapeDtypeStruct((length, width), F32),
-        in_specs=[VMEM] * len(operands),
-        out_specs=VMEM,
+        functools.partial(ff_forward_kernel, n_dp),
+        out_shape=(
+            low,
+            low,
+            jax.ShapeDtypeStruct((1, width), F32),
+            jax.ShapeDtypeStruct((tokens, width), BF),
+            jax.ShapeDtypeStruct((tokens, 2 * fh), F32),
+            jax.ShapeDtypeStruct((tokens, fh), BF),
+        ),
+        in_specs=[VMEM] * 3 + [ANY] * 2,
+        out_specs=(VMEM,) * 6,
         scratch_shapes=[
-            pltpu.VMEM((n - 1, length, width), BF),
-            pltpu.VMEM((n - 1, length, width), BF),
-            dma((n - 1,)),
-            dma((n - 1,)),
+            pltpu.VMEM((width, 2 * fh), BF),
+            pltpu.VMEM((width, fh), BF),
+            pltpu.VMEM((length, width), F32),
+            pltpu.SemaphoreType.DMA((blocks,)),
+            pltpu.SemaphoreType.DMA((blocks,)),
+        ]
+        + gather_sems(n_dp)
+        + give_scratch(n_dp, length, width),
+        compiler_params=params_of(number, 58),
+        name="ff_forward",
+    )(h1, up, gain, w_gu, w_d)
+
+
+def ff_back_kernel(n_dp, dm_ref, d_hbm, pre_hbm, all_ref, dgu_ref, d_ref, pre_ref, sem_d, sem_p, *gather):
+    dp, me = lax.axis_index("dp"), lax.axis_index("ctx")
+    length, width = dm_ref.shape
+    fh = d_ref.shape[1]
+    loads = load_rows(d_hbm, d_ref, sem_d)
+
+    def rows_of(b):
+        return pl.ds(pl.multiple_of(2 * b * length, 2 * length), 2 * length)
+
+    def load_pre(b):
+        return pltpu.make_async_copy(pre_hbm.at[rows_of(b), :], pre_ref.at[rows_of(b), :], sem_p.at[b])
+
+    for k in range(n_dp):
+        load_pre((dp + k) % n_dp).start()
+    mine = pl.ds(pl.multiple_of((2 * dp + me % 2) * length, length), length)
+    all_ref[mine, :] = dm_ref[...]
+    greet_group(n_dp, dp, me)
+
+    def process(b, own):
+        rows = rows_of(b)
+        if own:
+            for copy in loads:
+                copy.wait()
+        load_pre(b).wait()
+
+        def hidden(part):
+            second = pl.ds(pl.multiple_of(fh + part.start, part.size), part.size)
+            back = dot(all_ref[rows, :], d_ref[:, part])
+            gate, upper = pre_ref[rows, part], pre_ref[rows, second]
+            sig = jax.nn.sigmoid(gate)
+            dgu_ref[rows, part] = (back * upper * sig * (1.0 + gate * (1.0 - sig))).astype(BF)
+            dgu_ref[rows, second] = (back * gate * sig).astype(BF)
+
+        tiles(fh, 256, hidden)
+
+    gather_group(n_dp, dp, me, all_ref, length, *gather, process)
+
+
+def ff_back(dm, w_d, pre, number):
+    n_dp = lax.axis_size("dp")
+    (length, width), fh = dm.shape, w_d.shape[3]
+    tokens = 2 * n_dp * length
+    return pl.pallas_call(
+        functools.partial(ff_back_kernel, n_dp),
+        out_shape=(
+            jax.ShapeDtypeStruct((tokens, width), BF),
+            jax.ShapeDtypeStruct((tokens, 2 * fh), BF),
+        ),
+        in_specs=[VMEM, ANY, ANY],
+        out_specs=(VMEM,) * 2,
+        scratch_shapes=[
+            pltpu.VMEM((width, fh), BF),
+            pltpu.VMEM((tokens, 2 * fh), F32),
+            pltpu.SemaphoreType.DMA((w_d.shape[0] * n_dp,)),
+            pltpu.SemaphoreType.DMA((n_dp,)),
+        ]
+        + gather_sems(n_dp),
+        compiler_params=params_of(number, 58),
+        name="ff_back",
+    )(dm, w_d, pre)
+
+
+def ff_scatter_kernel(
+    n_dp, dgu_ref, gu_hbm, up_ref, branch_ref, gain_ref, dh_ref, db_ref, gp_ref, gu_ref, sem_gu, *give
+):
+    dp, me = lax.axis_index("dp"), lax.axis_index("ctx")
+    length, width = dh_ref.shape
+    loads = load_rows(gu_hbm, gu_ref, sem_gu)
+    greet_group(n_dp, dp, me)
+    for copy in loads:
+        copy.wait()
+
+    @pl.loop(1, n_dp)
+    def _(k):
+        give_block(dp, me, (dp + k) % n_dp, False, dgu_ref, gu_ref, dh_ref, *give)
+
+    give_block(dp, me, dp, True, dgu_ref, gu_ref, dh_ref, *give)
+    give_end(n_dp, dp, me, dh_ref, *give)
+    gp_ref[...] = jnp.zeros_like(gp_ref)
+
+    def finish(rows):
+        grad, branch = dh_ref[rows, :] + up_ref[rows, :].astype(F32), branch_ref[rows, :]
+        scale = rms_scale(branch)
+        dh_ref[rows, :] = grad
+        gp_ref[...] += jnp.sum(grad * branch * scale, axis=0, keepdims=True)
+        db_ref[rows, :] = norm_back(grad * gain_ref[...], branch, scale).astype(BF)
+
+    tiles(length, 16, finish)
+
+
+def ff_scatter(dgu, w_gu, up, branch, gain, number):
+    n_dp = lax.axis_size("dp")
+    length, width = up.shape
+    return pl.pallas_call(
+        functools.partial(ff_scatter_kernel, n_dp),
+        out_shape=(
+            jax.ShapeDtypeStruct((length, width), F32),
+            jax.ShapeDtypeStruct((length, width), BF),
+            jax.ShapeDtypeStruct((1, width), F32),
+        ),
+        in_specs=[VMEM, ANY] + [VMEM] * 3,
+        out_specs=(VMEM,) * 3,
+        scratch_shapes=[
+            pltpu.VMEM((width, w_gu.shape[3]), BF),
+            pltpu.SemaphoreType.DMA((w_gu.shape[0] * n_dp,)),
+        ]
+        + give_scratch(n_dp, length, width),
+        compiler_params=params_of(number, 56),
+        name="ff_scatter",
+    )(dgu, w_gu, up, branch, gain)
+
+
+def ff_grad_kernel(x_ref, d_ref, o_ref):
+    value = t_dot(x_ref[...], d_ref[...]).astype(BF)
+    rows = o_ref.shape[2]
+    for s in range(o_ref.shape[0]):
+        o_ref[s, 0] = value[s * rows : (s + 1) * rows]
+
+
+def ff_grad(x, d, rows):
+    n_dp, half = lax.axis_size("dp"), lax.axis_size("ctx") // 2
+    (tokens, width), columns = x.shape, d.shape[1]
+    block = 256
+    many = block // (2 * rows)
+    return pl.pallas_call(
+        ff_grad_kernel,
+        grid=(width // block,),
+        out_shape=jax.ShapeDtypeStruct((half, n_dp, 2 * rows, columns), BF),
+        in_specs=[
+            pl.BlockSpec((tokens, block), lambda i: (0, i)),
+            pl.BlockSpec((tokens, columns), lambda i: (0, 0)),
         ],
-        compiler_params=params_of(number, 56),
-        name="scatter_dp",
-    )(*operands)
+        out_specs=pl.BlockSpec(
+            (many, 1, 2 * rows, columns), lambda i: (i % (half // many), i // (half // many), 0, 0)
+        ),
+        compiler_params=pltpu.CompilerParams(vmem_limit_bytes=48 * 1024 * 1024),
+        cost_estimate=pl.CostEstimate(
+            flops=2 * tokens * width * columns,
+            bytes_accessed=2 * (tokens * width + tokens * columns + width * columns),
+            transcendentals=0,
+        ),
+        name="ff_grad",
+    )(x, d)
 
 
 def start_kernel(
@@ -261,26 +602,24 @@
 ):
     dp, me = lax.axis_index("dp"), lax.axis_index("ctx")
     half, parity, pair, partner, ahead, behind = pairs_of(n, me)
-    greet(
-        [((dp + k) % n_dp, me) for k in range(1, n_dp)] + [(dp, (me + k) % n) for k in range(1, n)]
-    )
+    count, mine, place = group_of(n_dp, n, dp, me)
+    greet_all(n_dp, n, dp, me)
     owns = [
-        pltpu.make_async_copy(g_ref.at[dp], h_ref.at[dp], local.at[0]),
+        pltpu.make_async_copy(g_ref.at[mine], h_ref.at[mine], local.at[0]),
         pltpu.make_async_copy(w_ref.at[me], o_ref.at[me], local.at[1]),
         pltpu.make_async_copy(x_ref, y_ref.at[me], local.at[2]),
         pltpu.make_async_copy(v_ref.at[me], p_ref.at[me], local.at[3]),
     ]
-    sends = []
-    for k in range(1, n_dp):
-        to = (dp + k) % n_dp
-        sends.append(remote(g_ref.at[to], h_ref.at[dp], sg.at[k - 1], rg.at[k - 1], (to, me)))
-    for k in range(1, n):
-        to = (me + k) % n
-        sends.append(remote(w_ref.at[to], o_ref.at[me], sa.at[k - 1], ra.at[k - 1], (dp, to)))
-        sends.append(remote(v_ref.at[to], p_ref.at[me], sv.at[k - 1], rv.at[k - 1], (dp, to)))
-    for k, a in enumerate(ahead + [partner]):
-        sends.append(remote(x_ref, y_ref.at[me], ss.at[k], rs.at[k], (dp, a)))
-    for copy in sends + owns:
+    sends, receives = swap(g_ref, h_ref, sg, rg, count, mine, place)
+    for src, dst, send, recv in ((w_ref, o_ref, sa, ra), (v_ref, p_ref, sv, rv)):
+        more, waits = swap(src, dst, send, recv, n, me, lambda c: (dp, c))
+        sends += more
+        receives += waits
+    gathers = [
+        remote(x_ref, y_ref.at[me], ss.at[k], rs.at[k], (dp, a))
+        for k, a in enumerate(ahead + [partner])
+    ]
+    for copy in gathers + owns:
         copy.start()
     forwards = []
     for k, b in enumerate(behind):
@@ -288,18 +627,12 @@
         forward = remote(y_ref.at[b], y_ref.at[b], fs.at[k], fr.at[k], (dp, partner))
         forward.start()
         forwards.append(forward)
-    sends[-1].wait_recv()
-    for k in range(1, n):
-        source = (me + n - k) % n
-        peer = (dp, source)
-        remote(w_ref.at[me], o_ref.at[source], sa.at[k - 1], ra.at[k - 1], peer).wait_recv()
-        remote(v_ref.at[me], p_ref.at[source], sv.at[k - 1], rv.at[k - 1], peer).wait_recv()
-    for k in range(1, n_dp):
-        source = (dp + n_dp - k) % n_dp
-        remote(g_ref.at[dp], h_ref.at[source], sg.at[k - 1], rg.at[k - 1], (source, me)).wait_recv()
+    gathers[-1].wait_recv()
+    for copy in receives:
+        copy.wait_recv()
     for forward in forwards:
         forward.wait()
-    for copy in sends:
+    for copy in sends + gathers:
         copy.wait_send()
     for copy in owns:
         copy.wait()
@@ -320,7 +653,7 @@
         in_specs=[ANY] * 4,
         out_specs=(ANY,) * 4,
         scratch_shapes=[dma((4,))]
-        + [dma((n_dp - 1,))] * 2
+        + [dma((2 * n_dp - 1,))] * 2
         + [dma((n - 1,))] * 4
         + [dma((half,))] * 2
         + [dma((half - 1,))] * 2,
@@ -336,12 +669,11 @@
     local, sa, rs, sc, rd, s1, r1, s2, r2, sh, rh,
 ):
     dp, me = lax.axis_index("dp"), lax.axis_index("ctx")
-    greet(
-        [((dp + k) % n_dp, me) for k in range(1, n_dp)] + [(dp, (me + k) % n) for k in range(1, n)]
-    )
+    count, index, place = group_of(n_dp, n, dp, me)
+    greet_all(n_dp, n, dp, me)
     mine = pltpu.make_async_copy(g_ref.at[dp], own, local.at[0])
     mine.start()
-    stay = pltpu.make_async_copy(h_ref.at[dp], h_out.at[dp], local.at[1])
+    stay = pltpu.make_async_copy(h_ref.at[index], h_out.at[index], local.at[1])
     stay.start()
     first = []
     for c in range(n):
@@ -358,12 +690,7 @@
             copy.start()
             row.append(copy)
         first.append(row)
-    swaps = []
-    for k in range(1, n_dp):
-        to = (dp + k) % n_dp
-        copy = remote(h_ref.at[to], h_out.at[dp], sh.at[k - 1], rh.at[k - 1], (to, me))
-        copy.start()
-        swaps.append(copy)
+    swaps, receives = swap(h_ref, h_out, sh, rh, count, index, place)
     sums = reduce_ctx(n, dp, me, a_ref, w_ref, slice(0, a_ref.shape[1]), y_ref, pa, qa, pb, qb, s1, r1, s2, r2)
     mine.wait()
     second = []
@@ -383,9 +710,8 @@
     for c in range(n - 1):
         second[c].wait_recv()
         o_ref[(me + n - 1 - c) % n] = rc[c]
-    for k in range(1, n_dp):
-        source = (dp + n_dp - k) % n_dp
-        remote(h_ref.at[dp], h_out.at[source], sh.at[k - 1], rh.at[k - 1], (source, me)).wait_recv()
+    for copy in receives:
+        copy.wait_recv()
     stay.wait()
     for row in first:
         for copy in row:
@@ -426,8 +752,8 @@
             dma((half,)),
             dma((half - 1,)),
             dma((half - 1,)),
-            dma((n_dp - 1,)),
-            dma((n_dp - 1,)),
+            dma((2 * n_dp - 1,)),
+            dma((2 * n_dp - 1,)),
         ],
         compiler_params=params_of(number),
         name="collect",
@@ -573,7 +899,7 @@
     )(factor.reshape(1, 1), params, first, second, ga, gu, gd)
 
 
-def arrange_kernel(n, n_dp, p_ref, a_ref, o_ref, g_ref, d_ref):
+def arrange_kernel(n, count, p_ref, a_ref, o_ref, g_ref, d_ref):
     part = pl.program_id(0)
     hc = o_ref.shape[2]
     fs = d_ref.shape[2]
@@ -593,18 +919,18 @@
 
         @pl.when(part == index)
         def _():
-            for d in range(n_dp):
+            for d in range(count):
                 ref[d, :, first : first + fs] = p_ref[:, d * fs : (d + 1) * fs].astype(BF)
 
 
 def arrange(params, width):
-    n_dp, n = lax.axis_size("dp"), lax.axis_size("ctx")
+    count, n = 2 * lax.axis_size("dp"), lax.axis_size("ctx")
     rows, columns = params.shape
-    fs, hc = columns // 4 // n_dp, width // n
+    fs, hc = columns // 4 // count, width // n
     whole = lambda shape: pl.BlockSpec(shape, lambda i: (0,) * len(shape))
-    shapes = [(n, rows, 3 * hc), (n, rows, hc), (n_dp, rows, 2 * fs), (n_dp, rows, fs)]
+    shapes = [(n, rows, 3 * hc), (n, rows, hc), (count, rows, 2 * fs), (count, rows, fs)]
     return pl.pallas_call(
-        functools.partial(arrange_kernel, n, n_dp),
+        functools.partial(arrange_kernel, n, count),
         grid=(4,),
         out_shape=tuple(jax.ShapeDtypeStruct(s, BF) for s in shapes),
         in_specs=[pl.BlockSpec((rows, columns // 4), lambda i: (0, i))],
@@ -652,17 +978,16 @@
 
 
 def attend_kernel(
-    n_dp, n, x_ref, w_ref, wo_ref, d_ref, gain_ref, cos_ref, sin_ref, col_ref, row_ref,
-    y_ref, q_ref, k_ref, v_ref, o_ref, pre_ref, scale_ref, lse_ref, wo_all, d_out,
+    n_dp, n, x_ref, w_ref, wo_ref, d_ref, t_ref, norm_ref, gain_ref, cos_ref, sin_ref, col_ref, row_ref,
+    y_ref, h_ref, q_ref, k_ref, v_ref, o_ref, pre_ref, scale_ref, lse_ref, wo_all, d_out,
     buf, pa, qa, pb, qb, ss, rs, s1, r1, s2, r2, sw, rw, sd, rd, local,
 ):
     dp, me = lax.axis_index("dp"), lax.axis_index("ctx")
     seq, width = x_ref.shape
     hc = o_ref.shape[1]
     block = min(seq, 256)
-    greet(
-        [((dp + k) % n_dp, me) for k in range(1, n_dp)] + [(dp, (me + k) % n) for k in range(1, n)]
-    )
+    count, mine, place = group_of(n_dp, n, dp, me)
+    greet_all(n_dp, n, dp, me)
     piece = wo_ref.shape[0]
 
     def part_of(d):
@@ -670,15 +995,15 @@
 
     owns = [
         pltpu.make_async_copy(wo_ref, part_of(dp), local.at[0]),
-        pltpu.make_async_copy(d_ref.at[dp], d_out.at[dp], local.at[1]),
+        pltpu.make_async_copy(d_ref.at[mine], d_out.at[mine], local.at[1]),
     ]
-    behind_wo, behind_d = [], []
-    for k in range(1, n_dp):
-        to = (dp + k) % n_dp
-        behind_wo.append(remote(wo_ref, part_of(dp), sw.at[k - 1], rw.at[k - 1], (to, me)))
-        behind_d.append(remote(d_ref.at[to], d_out.at[dp], sd.at[k - 1], rd.at[k - 1], (to, me)))
-    for copy in behind_wo + behind_d + owns:
+    behind_wo = [
+        remote(wo_ref, part_of(dp), sw.at[k - 1], rw.at[k - 1], ((dp + k) % n_dp, me))
+        for k in range(1, n_dp)
+    ]
+    for copy in behind_wo + owns:
         copy.start()
+    behind_d, receives = swap(d_ref, d_out, sd, rd, count, mine, place)
 
     @pl.loop(0, seq // block)
     def _(i):
@@ -723,15 +1048,20 @@
         remote(wo_ref, part_of(source), sw.at[k - 1], rw.at[k - 1], (source, me)).wait_recv()
     cols = slice(0, hc)
     sums = reduce_ctx(n, dp, me, o_ref, wo_all, cols, y_ref, pa, qa, pb, qb, s1, r1, s2, r2)
-    for k in range(1, n_dp):
-        source = (dp + n_dp - k) % n_dp
-        remote(d_ref.at[dp], d_out.at[source], sd.at[k - 1], rd.at[k - 1], (source, me)).wait_recv()
+
+    def finish(rows):
+        branch = y_ref[rows, :]
+        h_ref[rows, :] = t_ref[rows, :].astype(F32) + branch * rms_scale(branch) * norm_ref[...]
+
+    tiles(y_ref.shape[0], 16, finish)
+    for copy in receives:
+        copy.wait_recv()
     for copy in sums + behind_wo + behind_d:
         copy.wait_send()
     owns[1].wait()
 
 
-def attend(x_all, w, wo, d, gain, cos, sine, info_col, info_row, number):
+def attend(x_all, w, wo, d, tokens, norm, gain, cos, sine, info_col, info_row, number):
     n_dp, n = lax.axis_size("dp"), lax.axis_size("ctx")
     seq, width = x_all.shape
     half, length, hc = n // 2, seq // n, w.shape[1] // 3
@@ -740,6 +1070,7 @@
     return pl.pallas_call(
         functools.partial(attend_kernel, n_dp, n),
         out_shape=(
+            jax.ShapeDtypeStruct((length, width), F32),
             jax.ShapeDtypeStruct((length, width), F32),
             low,
             low,
@@ -751,8 +1082,8 @@
             jax.ShapeDtypeStruct((width, hc), BF),
             jax.ShapeDtypeStruct(d.shape, BF),
         ),
-        in_specs=[VMEM] * 2 + [ANY] * 2 + [VMEM] * 5,
-        out_specs=(VMEM,) * 9 + (ANY,),
+        in_specs=[VMEM] * 2 + [ANY] * 2 + [VMEM] * 7,
+        out_specs=(VMEM,) * 10 + (ANY,),
         scratch_shapes=[
             pltpu.VMEM((n, 8, seq), F32),
             pltpu.VMEM((half, length, width), BF),
@@ -767,33 +1098,37 @@
             dma((half - 1,)),
             dma((n_dp - 1,)),
             dma((n_dp - 1,)),
-            dma((n_dp - 1,)),
-            dma((n_dp - 1,)),
+            dma((2 * n_dp - 1,)),
+            dma((2 * n_dp - 1,)),
             dma((2,)),
         ],
         compiler_params=params_of(number),
         name="attend",
-    )(x_all, w, wo, d, gain, cos, sine, info_col, info_row)
+    )(x_all, w, wo, d, tokens, norm, gain, cos, sine, info_col, info_row)
 
 
 def attend_back_kernel(
-    n, e_ref, w_ref, gain_ref, cos_ref, sin_ref, col_ref, row_ref,
+    n_dp, n, e_ref, w_ref, h_ref, gain_ref, cos_ref, sin_ref, col_ref, row_ref,
     q_ref, k_ref, v_ref, pre_ref, scale_ref, lse_ref,
-    all_ref, d_ref, gain_out,
-    do_ref, dq_ref, dk_ref, dv_ref, mean_ref, buf, ss, rs, s1, r1, s2, r2,
+    all_ref, d_ref, gain_out, h_out,
+    do_ref, dq_ref, dk_ref, dv_ref, mean_ref, buf, ss, rs, s1, r1, s2, r2, sh, rh, local,
 ):
     dp, me = lax.axis_index("dp"), lax.axis_index("ctx")
     half, parity, pair, partner, ahead, behind = pairs_of(n, me)
     seq, hc = q_ref.shape
     length, width = e_ref.shape
     block = min(seq, 256)
-    greet([(dp, (me + k) % n) for k in range(1, n)])
+    count, index, place = group_of(n_dp, n, dp, me)
+    greet_all(n_dp, n, dp, me)
     sends = [
         remote(e_ref, all_ref.at[me], s1.at[k], r1.at[k], (dp, a))
         for k, a in enumerate(ahead + [partner])
     ]
     for copy in sends:
         copy.start()
+    swaps, receives = swap(h_ref, h_out, sh, rh, count, index, place)
+    stay = pltpu.make_async_copy(h_ref.at[index], h_out.at[index], local)
+    stay.start()
     all_ref[me] = e_ref[...]
     dk_ref[...] = jnp.zeros_like(dk_ref)
     dv_ref[...] = jnp.zeros_like(dv_ref)
@@ -864,24 +1199,28 @@
             d_ref[rows, cols] = value.astype(BF)
         d_ref[rows, 2 * hc :] = dv_ref[rows, :].astype(BF)
 
-    for copy in sends + forwards:
+    for copy in receives:
+        copy.wait_recv()
+    for copy in sends + forwards + swaps:
         copy.wait_send()
-
-
-def attend_back(e, w, gain, cos, sine, info_col, info_row, q, k, v, pre, scale, lse, number):
-    n = lax.axis_size("ctx")
+    stay.wait()
+
+
+def attend_back(e, w, h, gain, cos, sine, info_col, info_row, q, k, v, pre, scale, lse, number):
+    n_dp, n = lax.axis_size("dp"), lax.axis_size("ctx")
     seq, hc = q.shape
     half, (length, width) = n // 2, e.shape
     dma = pltpu.SemaphoreType.DMA
-    all_e, d_qkv, d_gain = pl.pallas_call(
-        functools.partial(attend_back_kernel, n),
+    all_e, d_qkv, d_gain, h = pl.pallas_call(
+        functools.partial(attend_back_kernel, n_dp, n),
         out_shape=(
             jax.ShapeDtypeStruct((n, length, width), BF),
             jax.ShapeDtypeStruct((seq, 3 * hc), BF),
             jax.ShapeDtypeStruct((2, hc), F32),
+            jax.ShapeDtypeStruct(h.shape, BF),
         ),
-        in_specs=[VMEM] * 13,
-        out_specs=(VMEM,) * 3,
+        in_specs=[VMEM, VMEM, ANY] + [VMEM] * 11,
+        out_specs=(VMEM,) * 3 + (ANY,),
         scratch_shapes=[
             pltpu.VMEM((seq, hc), BF),
             pltpu.VMEM((seq, hc), F32),
@@ -895,11 +1234,14 @@
             dma((half,)),
             dma((half - 1,)),
             dma((half - 1,)),
+            dma((2 * n_dp - 1,)),
+            dma((2 * n_dp - 1,)),
+            dma,
         ],
         compiler_params=params_of(number),
         name="attend_back",
-    )(e, w, gain, cos, sine, info_col, info_row, q, k, v, pre, scale, lse)
-    return all_e.reshape(seq, width), d_qkv, d_gain
+    )(e, w, h, gain, cos, sine, info_col, info_row, q, k, v, pre, scale, lse)
+    return all_e.reshape(seq, width), d_qkv, d_gain, h
 
 
 def shards(
@@ -915,7 +1257,7 @@
     gains_second,
 ):
     tokens = inputs[0]
-    upstream = cotangent[0].astype(F32)
+    upstream = cotangent[0]
     length, width = tokens.shape
     n_ctx = lax.axis_size("ctx")
     n_dp = lax.axis_size("dp")
@@ -924,24 +1266,29 @@
     rows = params.shape[0]
     ff = (params.shape[1] - 4 * width) // 3
     hc = width // n_ctx
-    heads = hc // HD
-    fs = ff // n_dp
-
-    def mix(values):
-        t = values.shape[0]
-        return (
-            values.reshape(t, n_dp, n_ctx, rows).transpose(0, 2, 1, 3).reshape(t, width)
+    half, group = n_ctx // 2, 2 * n_dp
+    fh = ff // group
+    parities = [[2 * p + side for p in range(half)] for side in range(2)]
+
+    def gather_pairs(w):
+        w = lax.all_gather(
+            w.reshape(group * rows, w.shape[2]), "ctx", axis=0, tiled=True, axis_index_groups=parities
         )
-
-    def unmix(values):
-        t = values.shape[0]
-        return (
-            values.reshape(t, n_ctx, n_dp, rows).transpose(0, 2, 1, 3).reshape(t, width)
+        return w.reshape(half, n_dp, 2 * rows, w.shape[1])
+
+    def scatter_pairs(g):
+        g = lax.psum_scatter(
+            g.reshape(width, g.shape[3]),
+            "ctx",
+            scatter_dimension=0,
+            tiled=True,
+            axis_index_groups=parities,
         )
+        return g.reshape(group, rows, g.shape[1])
 
     w_qkv, w_o, w_gu, w_d = arrange(params, width)
     w_gu, w_qkv, w_o, x_all = start(w_gu, w_qkv, w_o, tokens, 1)
-    w_gu = lax.all_gather(w_gu.reshape(n_dp * rows, 2 * fs), "ctx", axis=0, tiled=True)
+    w_gu = gather_pairs(w_gu)
     w_qkv = gather_dp(w_qkv.reshape(n_ctx * rows, 3 * hc), 2)
 
     indices = jnp.arange(seq, dtype=jnp.int32)
@@ -962,52 +1309,30 @@
     my_gains = lax.dynamic_slice_in_dim(gains[:2], me_ctx * hc, hc, axis=1)
     tables = (my_gains, cos_tab, sine_tab, info_col, info_row)
 
-    branch, queries, keys, values, attn_low, qk_pre, scales, lse, w_o, w_d = attend(
-        x_all, w_qkv, w_o.reshape(n_ctx * rows, hc), w_d, *tables, 3
-    )
-    w_d = lax.all_gather(w_d.reshape(n_dp * rows, fs), "ctx", axis=0, tiled=True)
-    a_scale = rms_scale(branch)
-    hidden1 = tokens.astype(F32) + branch * a_scale * gains[2]
-
-    h1_all = gather_dp(mix(hidden1.astype(BF)), 4)
-    gate_up = dot(h1_all, w_gu)
-    gate_pre, up_pre = gate_up[:, :fs], gate_up[:, fs:]
-    gate_sig = jax.nn.sigmoid(gate_pre)
-    silu_val = gate_pre * gate_sig
-    inner = (silu_val * up_pre).astype(BF)
-    mlp_out = unmix(scatter_dp((inner, w_d), 5))
-    m_scale = rms_scale(mlp_out)
-    result = hidden1 + mlp_out * m_scale * gains[3]
-
-    g_ff_part = jnp.sum(upstream * mlp_out * m_scale, axis=0)
-    d_mlp = norm_back(upstream * gains[3], mlp_out, m_scale).astype(BF)
-    d_mlp_all = gather_dp(mix(d_mlp), 6)
-    d_grad = lax.psum_scatter(
-        t_dot(d_mlp_all, inner).astype(BF), "ctx", scatter_dimension=0, tiled=True
-    )
-    d_inner = dot(d_mlp_all, w_d)
-    d_gate = (d_inner * up_pre * gate_sig * (1.0 + gate_pre * (1.0 - gate_sig))).astype(BF)
-    d_upper = (d_inner * silu_val).astype(BF)
-    d_gu = jnp.concatenate([d_gate, d_upper], axis=1)
-    gu_grad = lax.psum_scatter(
-        t_dot(h1_all, d_gu).astype(BF), "ctx", scatter_dimension=0, tiled=True
-    ).reshape(n_dp, rows, 2 * fs)
-    d_h1 = upstream + unmix(scatter_dp((d_gu, w_gu), 7))
-
-    g_attn_part = jnp.sum(d_h1 * branch * a_scale, axis=0)
-    d_branch = norm_back(d_h1 * gains[2], branch, a_scale).astype(BF)
-    d_grad, d_branch = lax.optimization_barrier((d_grad, d_branch))
-    d_branch_all, d_qkv, d_gain = attend_back(
-        d_branch, w_o, *tables, queries, keys, values, qk_pre, scales, lse, 8
+    branch, hidden1, queries, keys, values, attn_low, qk_pre, scales, lse, w_o, w_d = attend(
+        x_all, w_qkv, w_o.reshape(n_ctx * rows, hc), w_d, tokens, gains[2:3], *tables, 3
+    )
+    w_d = gather_pairs(w_d)
+
+    result, d_mlp, g_ff_part, h1_all, gate_up, inner = ff_forward(
+        hidden1, upstream, gains[3:4], w_gu, w_d, 4
+    )
+    d_mlp_all, d_gu = ff_back(d_mlp, w_d, gate_up, 5)
+    d_grad, gu_grad = ff_grad(d_mlp_all, inner, rows), ff_grad(h1_all, d_gu, rows)
+    d_grad, gu_grad, d_gu = lax.optimization_barrier((d_grad, gu_grad, d_gu))
+    d_grad, gu_grad = scatter_pairs(d_grad), scatter_pairs(gu_grad)
+    d_h1, d_branch, g_attn_part = ff_scatter(d_gu, w_gu, upstream, branch, gains[2:3], 6)
+
+    d_branch_all, d_qkv, d_gain, d_grad = attend_back(
+        d_branch, w_o, d_grad, *tables, queries, keys, values, qk_pre, scales, lse, 8
     )
     attn_grad = jnp.concatenate([t_dot(x_all, d_qkv), t_dot(d_branch_all, attn_low)], axis=1)
-    d_grad = lax.all_to_all(d_grad, "dp", 0, 0, tiled=True).reshape(n_dp, rows, fs)
     attn_grad, gu_grad, d_x = collect(attn_grad.astype(BF), gu_grad, d_qkv, w_qkv, 9)
     d_input = d_h1 + d_x
 
-    gain_part = jnp.stack(
+    gain_part = jnp.concatenate(
         [
-            *lax.dynamic_update_slice(jnp.zeros((2, width), F32), d_gain, (0, me_ctx * hc)),
+            lax.dynamic_update_slice(jnp.zeros((2, width), F32), d_gain, (0, me_ctx * hc)),
             g_attn_part,
             g_ff_part,
         ],
@@ -1023,7 +1348,7 @@
         gains, gains_first, gains_second, gain_total * factor, GAIN_RATE, 0.0
     )
     return (
-        result.astype(BF)[None],
+        result[None],
         d_input.astype(BF)[None],
         grad_norm,
         new_params,

time: 818 us -> 883 us (1.079)
  waiting for transfers between devices: 0.07 us -> 160 us
  matrix products: 54.7 us -> 7.21 us
  local copies, waits for them, and re-layouts: 71.5 us -> 36.7 us
  Pallas kernels: 626 us -> 650 us
  other arithmetic: 26.1 us -> 11.3 us
  starting transfers between devices: 14.9 us -> 0.16 us
    all_gather x2, waiting for transfers between devices: 0.01 us -> 158 us  [gather_pairs(): lax.all_gather(w.reshape(group * rows, w.shape[2]), 'ctx', axis=0, tiled=...]
    pallas_call x4 -> x7, Pallas kernels: 173 us -> 306 us  [the longest x1 91.2 us: ff_forward(): pl.pallas_call(functools.partial(ff_forward_kernel, n_dp), out_shape=(low...]
    pallas_call x3 -> x1, Pallas kernels: 160 us -> 63.3 us  [gather_dp(): pl.pallas_call(functools.partial(gather_dp_kernel, n), out_shape=jax.Shap...]
    dot_general x2 -> x0, matrix products: 26.4 us -> none  [dot(): return jnp.dot(a, b, preferred_element_type=F32)]
    dot_general x4 -> x2, matrix products: 28.4 us -> 7.21 us  [t_dot(): lax.dot_general(a, b, (((0,), (0,)), ((), ())), preferred_element_type=F32)]
    all_to_all x1 -> x0, starting transfers between devices: 14.1 us -> none  [shards(): lax.all_to_all(d_grad, 'dp', 0, 0, tiled=True).reshape(n_dp, rows, fs)]
    pallas_call x1, Pallas kernels: 140 us -> 127 us  [collect(): pl.pallas_call(functools.partial(collect_kernel, n_dp, n), out_shape=(jax...]
    unnamed x86 -> x71, local copies, waits for them, and re-layouts: 32.3 us -> 21.5 us
  transfers between devices with their start and end apart: 5 -> 4, of which waited for: 0 -> 2; matrix products, arithmetic and copies ran while one was open for 12% -> 3% of each run, Pallas kernels for 54% -> 16%
where the time goes in v5:
time: 883 us; the launch traced here: 882 us
  Pallas kernels  650 us (74%)
  waiting for transfers between devices  160 us (18%)
  local copies, waits for them, and re-layouts  36.7 us (4%)
  between operations  16.7 us (2%)
  other arithmetic  11.3 us (1%)
    all_gather x2, waiting for transfers between devices, gather_pairs(): lax.all_gather(w.reshape(group * rows, w.shape[2]), 'ctx', axis=0, tiled=...  158 us
    pallas_call x1, Pallas kernels, collect(): pl.pallas_call(functools.partial(collect_kernel, n_dp, n), out_shape=(jax...  127 us
    pallas_call x1, Pallas kernels, ff_forward(): pl.pallas_call(functools.partial(ff_forward_kernel, n_dp), out_shape=(low...  91.2 us
    pallas_call x1, Pallas kernels, attend_back(): pl.pallas_call(functools.partial(attend_back_kernel, n_dp, n), out_shape=...  83.8 us
    pallas_call x1, Pallas kernels, gather_dp(): pl.pallas_call(functools.partial(gather_dp_kernel, n), out_shape=jax.Shap...  63.3 us
    pallas_call x1, Pallas kernels, attend(): pl.pallas_call(functools.partial(attend_kernel, n_dp, n), out_shape=(jax....  57.7 us
    pallas_call x1, Pallas kernels, ff_scatter(): pl.pallas_call(functools.partial(ff_scatter_kernel, n_dp), out_shape=(jax...  56.9 us
    pallas_call x1, Pallas kernels, ff_back(): pl.pallas_call(functools.partial(ff_back_kernel, n_dp), out_shape=(jax.Sh...  45.8 us
  transfers between devices with their start and end apart: 4, of which 2 were waited for; matrix products, arithmetic and copies ran while one was open for 3% of the time, Pallas kernels for 16%

profile of v5, /device:TPU:0, one launch (start us, length us, event | category | flops | bytes accessed | tf_op | source)
XLA Modules:
  0.0 881.8 jit_solution(12484072211920375573)
XLA Ops:
  7.2 0.0 all-gather.5.cloned.1.call-start
  7.2 1.5 fusion.17
  8.7 4.2 arrange.1
  13.0 0.0 copy-start.4
  13.0 1.3 copy-done.4
  14.3 1.0 copy-done.8
  15.3 44.7 %start.1 = (bf16[8,64,2048]{2,1,0:T(8,128)(2,1)S(1)}, bf16[8,64,768]{2,1,0:T(8,128)(2,1)S(1)}, bf16[8,64,256]{2,1,0:T(8,128)(2,1)S(1)}, bf16[8,128,2048]{2,1,0:T(8,128)(2,1)}) custom-call(bf16[8,64,2048]{2,1,0:T(8,128)(2,1)} %copy-done.4, bf16[8,64,768]{2,1,0:T(8,128)(2,1)S(1)} %get-tuple-element.53.w_ref, bf16[8,64,256]{2,1,0:T(8,128)(2,1)S(1)} %get-tuple-element.54.v_ref, ...), custom_call_target="tpu_custom_call" | custom-call | tf_op jit(solution)/shard_map/start/pallas_call | solution.py:645
  59.9 0.0 copy-start.5
  60.0 1.3 copy-done.5
  61.3 63.3 %gather_dp.1 = bf16[4,512,768]{2,1,0:T(8,128)(2,1)S(1)} custom-call(bf16[512,768]{1,0:T(8,128)(2,1)S(1)} %bitcast.46), custom_call_target="tpu_custom_call" | custom-call | tf_op jit(solution)/shard_map/gather_dp/pallas_call | solution.py:148
  124.6 1.6 copy-done
  126.2 0.1 select_reduce_fusion
  126.3 0.1 pad.7.clone
  126.4 0.1 add_add_fusion
  126.4 0.2 copy.27.col_ref
  126.7 3.1 fusion.3
  129.7 1.7 pad_maximum_fusion.1
  131.4 57.7 %attend.1 = (f32[128,2048]{1,0:T(8,128)}, f32[128,2048]{1,0:T(8,128)}, bf16[1024,256]{1,0:T(8,128)(2,1)S(1)}, bf16[1024,256]{1,0:T(8,128)(2,1)S(1)}, bf16[1024,2...) custom-call(bf16[1024,2048]{1,0:T(8,128)(2,1)} %bitcast.52, ...), custom_call_target="tpu_custom_call" | custom-call | tf_op jit(solution)/shard_map/attend/pallas_call | solution.py:1070
  189.1 0.8 copy-done.10
  189.9 0.8 copy-done.12
  190.7 0.8 copy-done.14
  191.5 0.9 copy-done.16
  192.4 0.8 copy-done.18
  193.2 0.0 all-gather.5.cloned.1.call-update
  193.2 0.0 all-gather.3.cloned.1.call-start
  193.2 0.7 all-gather.3.cloned.1.call-update
  194.0 0.0 reduce-scatter.3.cloned.1.call-start
  194.0 68.3 %all-gather.5.cloned.1.call-done = bf16[2048,1024]{1,0:T(8,128)(2,1)} async-done(((bf16[512,1024]{1,0:T(8,128)(2,1)}), bf16[2048,1024]{1,0:T(8,128)(2,1)}) %all-gather.5.cloned.1.call-update) | async-done | bytes 4194320 | tf_op jit(solution)/shard_map/all_gather | solution.py:1274
  262.3 90.1 %all-gather.3.cloned.1.call-done = bf16[2048,2048]{1,0:T(8,128)(2,1)} async-done(((bf16[512,2048]{1,0:T(8,128)(2,1)}), bf16[2048,2048]{1,0:T(8,128)(2,1)}) %all-gather.3.cloned.1.call-update) | async-done | bytes 8388624 | tf_op jit(solution)/shard_map/all_gather | solution.py:1274
  352.3 91.2 %ff_forward.1 = (bf16[128,2048]{1,0:T(8,128)(2,1)}, bf16[128,2048]{1,0:T(8,128)(2,1)}, f32[1,2048]{1,0:T(1,128)}, bf16[1024,2048]{1,0:T(8,128)(2,1)}, f32[1024,2048]{1,0:T(8,128)}, /*index=5*/bf16[1024,1024]{1,0:T(8,128)(2,1)}) custom-call(f32[128,2048]{1,0:T(8,128)} %get-tuple-element.59.h_ref, bf16[128,2048]{1,0:T(8,128)(2,1)} %bitcast.59, ...), custom_call_target="tpu_custom_call" | custom-call | tf_op jit(solution)/shard_map/ff_forward/pallas_call | solution.py:428
  443.5 45.8 %ff_back.1 = (bf16[1024,2048]{1,0:T(8,128)(2,1)}, bf16[1024,2048]{1,0:T(8,128)(2,1)}) custom-call(bf16[128,2048]{1,0:T(8,128)(2,1)} %get-tuple-element.63.dm_ref, bf16[4,4,128,1024]{3,2,1,0:T(8,128)(2,1)} %bitcast.51, f32[1024,2048]{1,0:T(8,128)} %get-tuple-element.64.pre_hbm), custom_call_target="tpu_custom_call" | custom-call | tf_op jit(solution)/shard_map/ff_back/pallas_call | solution.py:496
  489.4 2.2 copy-done.22
  491.6 14.3 %ff_grad.3 = bf16[4,4,128,2048]{3,2,1,0:T(8,128)(2,1)} custom-call(bf16[1024,2048]{1,0:T(8,128)(2,1)S(1)} %copy-done.22, bf16[1024,2048]{1,0:T(8,128)(2,1)} %get-tuple-element.69.d_ref.dgu_ref), custom_call_target="tpu_custom_call" | custom-call | flops 8589934592 | bytes 16777216 | tf_op jit(solution)/shard_map/ff_grad/pallas_call | solution.py:578
  505.9 9.4 %ff_grad.2 = bf16[4,4,128,1024]{3,2,1,0:T(8,128)(2,1)} custom-call(bf16[1024,2048]{1,0:T(8,128)(2,1)} %get-tuple-element.65.x_ref, bf16[1024,1024]{1,0:T(8,128)(2,1)S(1)} %copy-done.23), custom_call_target="tpu_custom_call" | custom-call | flops 4294967296 | bytes 10485760 | tf_op jit(solution)/shard_map/ff_grad/pallas_call | solution.py:578
  515.3 0.0 reduce-scatter.3.cloned.1.call-update
  515.3 0.0 reduce-scatter.5.cloned.1.call-start
  515.4 0.5 reduce-scatter.5.cloned.1.call-update
  515.9 6.4 copy.28
  522.3 56.9 %ff_scatter.1 = (f32[128,2048]{1,0:T(8,128)}, bf16[128,2048]{1,0:T(8,128)(2,1)}, f32[1,2048]{1,0:T(1,128)}) custom-call(bf16[1024,2048]{1,0:T(8,128)(2,1)} %get-tuple-element.69.d_ref.dgu_ref, bf16[4,4,128,2048]{3,2,1,0:T(8,128)(2,1)} %bitcast.49, bf16[128,2048]{1,0:T(8,128)(2,1)} %bitcast.60, f32[128,2048]{1,0:T(8,128)} %get-tuple-element.70.branch_ref, ...), custom_call_target="tpu_custom_call" | custom-call | tf_op jit(solution)/shard_map/ff_scatter/pallas_call | solution.py:547
  579.2 0.0 reduce-scatter.3.cloned.1.call-done
  579.2 1.0 copy-done.13
  580.3 1.0 copy-done.15
  581.3 1.0 copy-done.17
  582.4 1.0 copy-done.19
  583.4 1.0 copy-done.20
  584.5 83.8 %attend_back.1 = (bf16[8,128,2048]{2,1,0:T(8,128)(2,1)}, bf16[1024,768]{1,0:T(8,128)(2,1)}, f32[2,256]{1,0:T(2,128)S(1)}, bf16[8,64,1024]{2,1,0:T(8,128)(2,1)S(1)}) custom-call(bf16[128,2048]{1,0:T(8,128)(2,1)S(1)} %copy-done.20, bf16[2048,256]{1,0:T(8,128)(2,1)} %get-tuple-element.73.w_ref, bf16[8,64,1024]{2,1,0:T(8,128)(2,1)} %bitcast.62, ...), custom_call_target="tpu_custom_call" | custom-call | tf_op jit(solution)/shard_map/attend_back/pallas_call | solution.py:1214
  668.3 6.5 copy.30
  674.9 3.6 convolution_convert_fusion.1
  678.5 0.4 copy-done.26
  678.9 3.6 convolution_convert_fusion
  682.5 2.6 pad_maximum_fusion.g_ref
  685.1 1.4 copy-done.7
  686.5 126.7 %collect.1 = (bf16[8,64,1024]{2,1,0:T(8,128)(2,1)S(1)}, bf16[8,64,2048]{2,1,0:T(8,128)(2,1)S(1)}, f32[128,2048]{1,0:T(8,128)S(1)}) custom-call(bf16[4,8,64,1024]{3,2,1,0:T(8,128)(2,1)} %pad_maximum_fusion.g_ref, bf16[8,64,2048]{2,1,0:T(8,128)(2,1)} %bitcast.61, bf16[1024,768]{1,0:T(8,128)(2,1)S(1)} %copy-done.7, bf16[2048,768]{1,0:T(8,128)(2,1)} %bitcast.42), custom_call_target="tpu_custom_call" | custom-call | tf_op jit(solution)/shard_map/collect/pallas_call | solution.py:728
  813.2 0.0 copy-start.29
  813.2 0.0 copy-start.30
  813.3 27.9 %total.1 = f32[72,128]{1,0:T(8,128)S(1)} custom-call(bf16[8,64,1024]{2,1,0:T(8,128)(2,1)S(1)} %get-tuple-element.86.ga_ref, bf16[8,64,2048]{2,1,0:T(8,128)(2,1)S(1)} %get-tuple-element.87.gu_ref, bf16[8,64,1024]{2,1,0:T(8,128)(2,1)S(1)} %get-tuple-element.88.gd_ref, f32[64,128]{1,0:T(8,128)S(1)} %reshape.152.gain_ref), custom_call_target="tpu_custom_call" | custom-call | tf_op jit(solution)/shard_map/total/pallas_call | solution.py:818
  841.2 1.0 copy-done.1
  842.1 0.5 slice.19
  842.6 0.6 multiply_reduce_fusion
  844.7 2.5 fusion.1
  847.1 0.7 multiply_subtract_fusion
  847.8 1.2 copy-done.2
  849.0 24.3 %adam.1 = (f32[64,32768]{1,0:T(8,128)}, f32[64,32768]{1,0:T(8,128)}, f32[64,32768]{1,0:T(8,128)}) custom-call(f32[1,1]{1,0:T(1,128)} %bitcast.28.factor_ref, f32[64,32768]{1,0:T(8,128)} %p_ref.3, f32[64,32768]{1,0:T(8,128)} %m_ref.1, f32[64,32768]{1,0:T(8,128)} %v_ref.1, bf16[8,64,1024]{2,1,0:T(8,128)(2,1)S(1)} %copy-done.2, ...), custom_call_target="tpu_custom_call" | custom-call | tf_op jit(solution)/shard_map/adam/pallas_call | solution.py:875
  873.4 0.8 copy.35
  (62 shorter events, 0.2 us)
Async XLA Ops:
  7.2 255.1 %all-gather.5.cloned.1.call-start = ((), (), s32[]{:S(2)}) async-start(), calls=%async_computation.3 | async-start | bytes 5242880 | tf_op jit(solution)/shard_map/all_gather | solution.py:1274
  8.7 122.7 %copy-start.21 = (f32[1,2048]{1,0:T(1,128)}, f32[1,2048]{1,0:T(1,128)S(1)}, u32[]{:S(2)}) copy-start(f32[1,2048]{1,0:T(1,128)S(1)} %get-tuple-element.99.norm_ref.gain_ref) | copy-start | bytes 24580
  8.7 6.5 copy-start.3
  13.0 1.3 copy-start.4
  14.3 1.0 copy-start.8
  15.2 110.9 %copy-start.34 = (s32[8]{0:T(128)S(1)}, s32[8]{0:T(128)}, u32[]{:S(2)}) copy-start(s32[8]{0:T(128)} %param.13) | copy-start | bytes 100
  15.2 111.1 %copy-start.33 = (s32[1,1024]{1,0:T(1,128)S(1)}, s32[1,1024]{1,0:T(1,128)}, u32[]{:S(2)}) copy-start(s32[1,1024]{1,0:T(1,128)} %param.12) | copy-start | bytes 12292
  15.3 114.5 %slice-start = ((f32[4,2048]{1,0:T(4,128)}), f32[2,2048]{1,0:T(2,128)S(1)}, s32[]{:S(2)}) async-start(f32[4,2048]{1,0:T(4,128)} %param.17), calls=%async_computation.6 | async-start | bytes 32768 | tf_op jit(solution)/shard_map/slice | solution.py:1309
  59.9 1.3 copy-start.5
  124.6 1.6 copy-start
  189.1 0.8 copy-start.10
  189.9 0.8 copy-start.12
  190.7 0.8 copy-start.14
  191.5 0.9 copy-start.16
  192.4 0.8 copy-start.18
  193.2 250.3 %copy-start.24 = (bf16[1024,256]{1,0:T(8,128)(2,1)}, bf16[1024,256]{1,0:T(8,128)(2,1)S(1)}, u32[]{:S(2)}) copy-start(bf16[1024,256]{1,0:T(8,128)(2,1)S(1)} %get-tuple-element.83) | copy-start | bytes 1572868
  193.2 159.1 %all-gather.3.cloned.1.call-start = ((), (), s32[]{:S(2)}) async-start(), calls=%async_computation.2 | async-start | bytes 10485760 | tf_op jit(solution)/shard_map/all_gather | solution.py:1274
  194.0 385.3 %reduce-scatter.3.cloned.1.call-start = ((), (), s32[]{:S(2)}) async-start(), calls=%async_computation.4 | async-start | bytes 5242880 | tf_op jit(solution)/shard_map/reduce_scatter | solution.py:1280
  489.4 2.2 copy-start.22
  491.6 14.3 %copy-start.23 = (bf16[1024,1024]{1,0:T(8,128)(2,1)S(1)}, bf16[1024,1024]{1,0:T(8,128)(2,1)}, u32[]{:S(2)}) copy-start(bf16[1024,1024]{1,0:T(8,128)(2,1)} %get-tuple-element.66.d_ref) | copy-start | bytes 6291460
  515.3 169.7 %reduce-scatter.5.cloned.1.call-start = ((), (), s32[]{:S(2)}) async-start(), calls=%async_computation.5 | async-start | bytes 10485760 | tf_op jit(solution)/shard_map/reduce_scatter | solution.py:1280
  522.3 56.9 %copy-start.11 = (bf16[1024,256]{1,0:T(8,128)(2,1)S(1)}, bf16[1024,256]{1,0:T(8,128)(2,1)}, u32[]{:S(2)}) copy-start(bf16[1024,256]{1,0:T(8,128)(2,1)} %copy-done.10) | copy-start | bytes 1572868
  579.2 1.0 copy-start.13
  580.3 1.0 copy-start.15
  581.3 1.0 copy-start.17
  582.4 1.0 copy-start.19
  583.4 1.0 copy-start.20
  584.4 83.8 %copy-start.31 = (f32[1,2048]{1,0:T(1,128)S(1)}, f32[1,2048]{1,0:T(1,128)}, u32[]{:S(2)}) copy-start(f32[1,2048]{1,0:T(1,128)} %get-tuple-element.91) | copy-start | bytes 24580
  584.4 83.8 %copy-start.32 = (f32[1,2048]{1,0:T(1,128)S(1)}, f32[1,2048]{1,0:T(1,128)}, u32[]{:S(2)}) copy-start(f32[1,2048]{1,0:T(1,128)} %get-tuple-element.90) | copy-start | bytes 24580
  668.3 6.5 copy-start.25
  674.9 3.6 copy-start.6
  674.9 4.1 copy-start.26
  685.1 1.4 copy-start.7
  813.2 27.9 %copy-start.9 = (f32[128,2048]{1,0:T(8,128)}, f32[128,2048]{1,0:T(8,128)S(1)}, u32[]{:S(2)}) copy-start(f32[128,2048]{1,0:T(8,128)S(1)} %get-tuple-element.85) | copy-start | bytes 3145732
  813.2 33.9 %copy-start.28 = (f32[4,2048]{1,0:T(4,128)S(1)}, f32[4,2048]{1,0:T(4,128)}, u32[]{:S(2)}) copy-start(f32[4,2048]{1,0:T(4,128)} %param.17) | copy-start | bytes 98308
  813.2 33.9 %copy-start.29 = (f32[4,2048]{1,0:T(4,128)S(1)}, f32[4,2048]{1,0:T(4,128)}, u32[]{:S(2)}) copy-start(f32[4,2048]{1,0:T(4,128)} %param.18) | copy-start | bytes 98308
  813.2 33.9 %copy-start.30 = (f32[4,2048]{1,0:T(4,128)S(1)}, f32[4,2048]{1,0:T(4,128)}, u32[]{:S(2)}) copy-start(f32[4,2048]{1,0:T(4,128)} %param.19) | copy-start | bytes 98308
  841.2 1.0 copy-start.1
  847.8 1.2 copy-start.2
  849.0 24.3 %copy-start.27 = (bf16[128,2048]{1,0:T(8,128)(2,1)S(1)}, bf16[128,2048]{1,0:T(8,128)(2,1)}, u32[]{:S(2)}) copy-start(bf16[128,2048]{1,0:T(8,128)(2,1)} %get-tuple-element.62) | copy-start | bytes 1572868
Sparse Core Ops, SparseCore 0:
  193.3 68.9 all-gather.4
  264.7 87.5 all-gather.2
  515.5 52.6 reduce-scatter.2
  571.9 111.6 reduce-scatter.4

commit v6 on v5

--- a/solution.py
+++ b/solution.py
@@ -76,6 +76,10 @@
     )
 
 
+def cost(us):
+    return pl.CostEstimate(flops=0, bytes_accessed=us * 3_600_000, transcendentals=0)
+
+
 def params_of(number, vmem=48):
     return pltpu.CompilerParams(
         collective_id=number, has_side_effects=True, vmem_limit_bytes=vmem * 1024 * 1024
@@ -152,6 +156,7 @@
         out_specs=ANY,
         scratch_shapes=[pltpu.SemaphoreType.DMA] + [pltpu.SemaphoreType.DMA((n - 1,))] * 4,
         compiler_params=params_of(number),
+        cost_estimate=cost(60),
         name="gather_dp",
     )(x)
     return out.reshape((n * x.shape[0],) + x.shape[1:])
@@ -372,18 +377,36 @@
 
 
 def ff_forward_kernel(
-    n_dp, h_ref, up_ref, gain_ref, gu_hbm, d_hbm,
-    res_ref, dm_ref, gp_ref, all_ref, pre_ref, hid_ref,
-    gu_ref, d_ref, acc, sem_gu, sem_d, *rest,
+    n_dp, n, h_ref, up_ref, gain_ref, gu_hbm, d_hbm,
+    res_ref, dm_ref, gp_ref, all_ref, pre_ref, hid_ref, d_ref,
+    gu_ref, acc, sem_gu, sem_d, sd, rd, *rest,
 ):
     gather, give = rest[:6], rest[6:]
     dp, me = lax.axis_index("dp"), lax.axis_index("ctx")
     length, width = h_ref.shape
     fh = hid_ref.shape[1]
-    loads_gu, loads_d = load_rows(gu_hbm, gu_ref, sem_gu), load_rows(d_hbm, d_ref, sem_d)
+    half, parity, pair, partner, ahead, behind = pairs_of(n, me)
+    loads_gu = load_rows(gu_hbm, gu_ref, sem_gu)
     mine = pl.ds(pl.multiple_of((2 * dp + me % 2) * length, length), length)
     all_ref[mine, :] = h_ref[...].astype(BF)
-    greet_group(n_dp, dp, me)
+    greet(
+        [(dp, partner)]
+        + [((dp + k) % n_dp, me) for k in range(1, n_dp)]
+        + [(dp, a) for a in ahead]
+    )
+    tall = d_hbm.shape[1]
+
+    def down(d, p):
+        return d_ref.at[pl.ds(pl.multiple_of((d * half + p) * tall, tall), tall), :]
+
+    loads_d = [pltpu.make_async_copy(d_hbm.at[d], down(d, pair), sem_d.at[d]) for d in range(n_dp)]
+    spreads = [
+        remote(d_hbm.at[d], down(d, pair), sd.at[k, d], rd.at[k, d], (dp, a))
+        for k, a in enumerate(ahead)
+        for d in range(n_dp)
+    ]
+    for copy in spreads + loads_d:
+        copy.start()
 
     def process(b, own):
         rows = pl.ds(pl.multiple_of(2 * b * length, 2 * length), 2 * length)
@@ -400,12 +423,19 @@
             hid_ref[rows, part] = (gate * jax.nn.sigmoid(gate) * upper).astype(BF)
 
         tiles(fh, 256, hidden)
-        if own:
-            for copy in loads_d:
-                copy.wait()
-        give_block(dp, me, b, own, hid_ref, d_ref, acc, *give)
 
     gather_group(n_dp, dp, me, all_ref, length, *gather, process)
+    for copy in loads_d:
+        copy.wait()
+    for k, b in enumerate(behind):
+        for d in range(n_dp):
+            remote(d_hbm.at[d], down(d, b // 2), sd.at[k, d], rd.at[k, d], (dp, b)).wait_recv()
+
+    @pl.loop(1, n_dp)
+    def _(k):
+        give_block(dp, me, (dp + k) % n_dp, False, hid_ref, d_ref, acc, *give)
+
+    give_block(dp, me, dp, True, hid_ref, d_ref, acc, *give)
     give_end(n_dp, dp, me, acc, *give)
     gp_ref[...] = jnp.zeros_like(gp_ref)
 
@@ -417,16 +447,18 @@
         dm_ref[rows, :] = norm_back(up * gain, out, scale).astype(BF)
 
     tiles(length, 16, finish)
+    for copy in spreads:
+        copy.wait_send()
 
 
 def ff_forward(h1, up, gain, w_gu, w_d, number):
-    n_dp = lax.axis_size("dp")
-    (length, width), fh = h1.shape, w_d.shape[3]
+    n_dp, n = lax.axis_size("dp"), lax.axis_size("ctx")
+    (length, width), fh = h1.shape, w_d.shape[2]
     tokens = 2 * n_dp * length
-    blocks = w_d.shape[0] * n_dp
+    half = n // 2
     low = jax.ShapeDtypeStruct((length, width), BF)
     return pl.pallas_call(
-        functools.partial(ff_forward_kernel, n_dp),
+        functools.partial(ff_forward_kernel, n_dp, n),
         out_shape=(
             low,
             low,
@@ -434,28 +466,43 @@
             jax.ShapeDtypeStruct((tokens, width), BF),
             jax.ShapeDtypeStruct((tokens, 2 * fh), F32),
             jax.ShapeDtypeStruct((tokens, fh), BF),
+            jax.ShapeDtypeStruct((width, fh), BF),
         ),
         in_specs=[VMEM] * 3 + [ANY] * 2,
-        out_specs=(VMEM,) * 6,
+        out_specs=(VMEM,) * 7,
         scratch_shapes=[
             pltpu.VMEM((width, 2 * fh), BF),
-            pltpu.VMEM((width, fh), BF),
             pltpu.VMEM((length, width), F32),
-            pltpu.SemaphoreType.DMA((blocks,)),
-            pltpu.SemaphoreType.DMA((blocks,)),
+            pltpu.SemaphoreType.DMA((half * n_dp,)),
+            pltpu.SemaphoreType.DMA((n_dp,)),
+            pltpu.SemaphoreType.DMA((half - 1, n_dp)),
+            pltpu.SemaphoreType.DMA((half - 1, n_dp)),
         ]
         + gather_sems(n_dp)
         + give_scratch(n_dp, length, width),
         compiler_params=params_of(number, 58),
+        cost_estimate=cost(90),
         name="ff_forward",
     )(h1, up, gain, w_gu, w_d)
 
 
-def ff_back_kernel(n_dp, dm_ref, d_hbm, pre_hbm, all_ref, dgu_ref, d_ref, pre_ref, sem_d, sem_p, *gather):
+def store_rows(n_dp, value_of, out):
+    half, _, rows, _ = out.shape
+
+    @pl.loop(0, n_dp * half)
+    def _(r):
+        out[r % half, r // half] = value_of(pl.ds(pl.multiple_of(r * rows, rows), rows)).astype(BF)
+
+
+def ff_back_kernel(
+    n_dp, dm_ref, hid_ref, d_hbm, pre_hbm, dgu_ref, gd_ref,
+    all_ref, d_ref, pre_ref, acc, sem_d, sem_p, *gather,
+):
     dp, me = lax.axis_index("dp"), lax.axis_index("ctx")
     length, width = dm_ref.shape
     fh = d_ref.shape[1]
-    loads = load_rows(d_hbm, d_ref, sem_d)
+    load = pltpu.make_async_copy(d_hbm, d_ref, sem_d)
+    load.start()
 
     def rows_of(b):
         return pl.ds(pl.multiple_of(2 * b * length, 2 * length), 2 * length)
@@ -472,8 +519,7 @@
     def process(b, own):
         rows = rows_of(b)
         if own:
-            for copy in loads:
-                copy.wait()
+            load.wait()
         load_pre(b).wait()
 
         def hidden(part):
@@ -486,40 +532,59 @@
 
         tiles(fh, 256, hidden)
 
+        def product(part):
+            value = t_dot(all_ref[rows, part], hid_ref[rows, :])
+            acc[part, :] = value if own else acc[part, :] + value
+
+        tiles(width, 256, product)
+
     gather_group(n_dp, dp, me, all_ref, length, *gather, process)
-
-
-def ff_back(dm, w_d, pre, number):
-    n_dp = lax.axis_size("dp")
-    (length, width), fh = dm.shape, w_d.shape[3]
+    store_rows(n_dp, lambda part: acc[part, :], gd_ref)
+
+
+def ff_back(dm, hid, w_d, pre, rows, number):
+    n_dp, half = lax.axis_size("dp"), lax.axis_size("ctx") // 2
+    (length, width), fh = dm.shape, w_d.shape[1]
     tokens = 2 * n_dp * length
     return pl.pallas_call(
         functools.partial(ff_back_kernel, n_dp),
         out_shape=(
-            jax.ShapeDtypeStruct((tokens, width), BF),
             jax.ShapeDtypeStruct((tokens, 2 * fh), BF),
+            jax.ShapeDtypeStruct((half, n_dp, 2 * rows, fh), BF),
         ),
-        in_specs=[VMEM, ANY, ANY],
+        in_specs=[VMEM, VMEM, ANY, ANY],
         out_specs=(VMEM,) * 2,
         scratch_shapes=[
+            pltpu.VMEM((tokens, width), BF),
             pltpu.VMEM((width, fh), BF),
             pltpu.VMEM((tokens, 2 * fh), F32),
-            pltpu.SemaphoreType.DMA((w_d.shape[0] * n_dp,)),
+            pltpu.VMEM((width, fh), F32),
+            pltpu.SemaphoreType.DMA,
             pltpu.SemaphoreType.DMA((n_dp,)),
         ]
         + gather_sems(n_dp),
         compiler_params=params_of(number, 58),
+        cost_estimate=cost(45),
         name="ff_back",
-    )(dm, w_d, pre)
+    )(dm, hid, w_d, pre)
 
 
 def ff_scatter_kernel(
-    n_dp, dgu_ref, gu_hbm, up_ref, branch_ref, gain_ref, dh_ref, db_ref, gp_ref, gu_ref, sem_gu, *give
+    n_dp, n, dgu_ref, gu_hbm, all_hbm, up_ref, branch_ref, gain_ref, dh_ref, db_ref, gp_ref, gg_ref, gv_ref,
+    gu_ref, all_ref, acc, sem_gu, sem_all, ss, rs, fs, fr, *give,
 ):
     dp, me = lax.axis_index("dp"), lax.axis_index("ctx")
     length, width = dh_ref.shape
+    half, parity, pair, partner, ahead, behind = pairs_of(n, me)
+    _, _, rows, fh = gg_ref.shape
     loads = load_rows(gu_hbm, gu_ref, sem_gu)
-    greet_group(n_dp, dp, me)
+    load = pltpu.make_async_copy(all_hbm, all_ref, sem_all)
+    load.start()
+    greet(
+        [(dp, partner)]
+        + [((dp + k) % n_dp, me) for k in range(1, n_dp)]
+        + [(dp, a) for a in ahead]
+    )
     for copy in loads:
         copy.wait()
 
@@ -528,72 +593,84 @@
         give_block(dp, me, (dp + k) % n_dp, False, dgu_ref, gu_ref, dh_ref, *give)
 
     give_block(dp, me, dp, True, dgu_ref, gu_ref, dh_ref, *give)
+    load.wait()
+    block = acc.shape[0]
+
+    @pl.loop(0, width // block)
+    def _(j):
+        acc[...] = t_dot(all_ref[:, pl.ds(pl.multiple_of(j * block, block), block)], dgu_ref[...])
+        for s in range(block // rows):
+            r = j * (block // rows) + s
+            part = slice(s * rows, (s + 1) * rows)
+            gg_ref[r % half, r // half] = acc[part, :fh].astype(BF)
+            gv_ref[r % half, r // half] = acc[part, fh:].astype(BF)
+
     give_end(n_dp, dp, me, dh_ref, *give)
     gp_ref[...] = jnp.zeros_like(gp_ref)
+
+    def block(b):
+        return db_ref.at[pl.ds(pl.multiple_of(b * length, length), length), :]
 
     def finish(rows):
         grad, branch = dh_ref[rows, :] + up_ref[rows, :].astype(F32), branch_ref[rows, :]
         scale = rms_scale(branch)
         dh_ref[rows, :] = grad
         gp_ref[...] += jnp.sum(grad * branch * scale, axis=0, keepdims=True)
-        db_ref[rows, :] = norm_back(grad * gain_ref[...], branch, scale).astype(BF)
+        mine = pl.ds(pl.multiple_of(me * length + rows.start, rows.size), rows.size)
+        db_ref[mine, :] = norm_back(grad * gain_ref[...], branch, scale).astype(BF)
 
     tiles(length, 16, finish)
-
-
-def ff_scatter(dgu, w_gu, up, branch, gain, number):
-    n_dp = lax.axis_size("dp")
+    sends = [
+        remote(block(me), block(me), ss.at[k], rs.at[k], (dp, a)) for k, a in enumerate(ahead + [partner])
+    ]
+    for copy in sends:
+        copy.start()
+    forwards = []
+    for k, b in enumerate(behind):
+        remote(block(b), block(b), ss.at[k], rs.at[k], (dp, b)).wait_recv()
+        forward = remote(block(b), block(b), fs.at[k], fr.at[k], (dp, partner))
+        forward.start()
+        forwards.append(forward)
+    remote(block(partner), block(partner), ss.at[half - 1], rs.at[half - 1], (dp, partner)).wait_recv()
+    for k, b in enumerate(behind):
+        other = b + 1 - 2 * parity
+        remote(block(other), block(other), fs.at[k], fr.at[k], (dp, partner)).wait_recv()
+    for copy in sends + forwards:
+        copy.wait_send()
+
+
+def ff_scatter(dgu, w_gu, h1_all, up, branch, gain, number):
+    n_dp, n = lax.axis_size("dp"), lax.axis_size("ctx")
     length, width = up.shape
+    half = n // 2
+    grad = jax.ShapeDtypeStruct(w_gu.shape[:3] + (w_gu.shape[3] // 2,), BF)
     return pl.pallas_call(
-        functools.partial(ff_scatter_kernel, n_dp),
+        functools.partial(ff_scatter_kernel, n_dp, n),
         out_shape=(
             jax.ShapeDtypeStruct((length, width), F32),
-            jax.ShapeDtypeStruct((length, width), BF),
+            jax.ShapeDtypeStruct((n * length, width), BF),
             jax.ShapeDtypeStruct((1, width), F32),
+            grad,
+            grad,
         ),
-        in_specs=[VMEM, ANY] + [VMEM] * 3,
-        out_specs=(VMEM,) * 3,
+        in_specs=[VMEM, ANY, ANY] + [VMEM] * 3,
+        out_specs=(VMEM,) * 5,
         scratch_shapes=[
             pltpu.VMEM((width, w_gu.shape[3]), BF),
+            pltpu.VMEM(h1_all.shape, BF),
+            pltpu.VMEM((256, w_gu.shape[3]), F32),
             pltpu.SemaphoreType.DMA((w_gu.shape[0] * n_dp,)),
+            pltpu.SemaphoreType.DMA,
+            pltpu.SemaphoreType.DMA((half,)),
+            pltpu.SemaphoreType.DMA((half,)),
+            pltpu.SemaphoreType.DMA((half - 1,)),
+            pltpu.SemaphoreType.DMA((half - 1,)),
         ]
         + give_scratch(n_dp, length, width),
         compiler_params=params_of(number, 56),
+        cost_estimate=cost(50),
         name="ff_scatter",
-    )(dgu, w_gu, up, branch, gain)
-
-
-def ff_grad_kernel(x_ref, d_ref, o_ref):
-    value = t_dot(x_ref[...], d_ref[...]).astype(BF)
-    rows = o_ref.shape[2]
-    for s in range(o_ref.shape[0]):
-        o_ref[s, 0] = value[s * rows : (s + 1) * rows]
-
-
-def ff_grad(x, d, rows):
-    n_dp, half = lax.axis_size("dp"), lax.axis_size("ctx") // 2
-    (tokens, width), columns = x.shape, d.shape[1]
-    block = 256
-    many = block // (2 * rows)
-    return pl.pallas_call(
-        ff_grad_kernel,
-        grid=(width // block,),
-        out_shape=jax.ShapeDtypeStruct((half, n_dp, 2 * rows, columns), BF),
-        in_specs=[
-            pl.BlockSpec((tokens, block), lambda i: (0, i)),
-            pl.BlockSpec((tokens, columns), lambda i: (0, 0)),
-        ],
-        out_specs=pl.BlockSpec(
-            (many, 1, 2 * rows, columns), lambda i: (i % (half // many), i // (half // many), 0, 0)
-        ),
-        compiler_params=pltpu.CompilerParams(vmem_limit_bytes=48 * 1024 * 1024),
-        cost_estimate=pl.CostEstimate(
-            flops=2 * tokens * width * columns,
-            bytes_accessed=2 * (tokens * width + tokens * columns + width * columns),
-            transcendentals=0,
-        ),
-        name="ff_grad",
-    )(x, d)
+    )(dgu, w_gu, h1_all, up, branch, gain)
 
 
 def start_kernel(
@@ -658,6 +735,7 @@
         + [dma((half,))] * 2
         + [dma((half - 1,))] * 2,
         compiler_params=params_of(number),
+        cost_estimate=cost(45),
         name="start",
     )(g, w, v, x)
     return g_out, w_out, v_out, x_all.reshape(-1, x.shape[-1])
@@ -665,89 +743,65 @@
 
 def collect_kernel(
     n_dp, n, g_ref, h_ref, a_ref, w_ref, o_ref, h_out, y_ref,
-    own, ra, rc, sb, pa, qa, pb, qb,
-    local, sa, rs, sc, rd, s1, r1, s2, r2, sh, rh,
+    own, co_ref, pa, qa, pb, qb, local, sw, rw, s1, r1, s2, r2, sh, rh,
 ):
     dp, me = lax.axis_index("dp"), lax.axis_index("ctx")
+    tall = own.shape[0]
     count, index, place = group_of(n_dp, n, dp, me)
     greet_all(n_dp, n, dp, me)
-    mine = pltpu.make_async_copy(g_ref.at[dp], own, local.at[0])
-    mine.start()
-    stay = pltpu.make_async_copy(h_ref.at[index], h_out.at[index], local.at[1])
-    stay.start()
-    first = []
-    for c in range(n):
-        row = []
-        for k in range(1, n_dp):
-            to = (dp + k) % n_dp
-            copy = remote(
-                g_ref.at[to, (me + 1 + c) % n],
-                ra.at[c, k - 1],
-                sa.at[c, k - 1],
-                rs.at[c, k - 1],
-                (to, me),
-            )
-            copy.start()
-            row.append(copy)
-        first.append(row)
+    gives = slab_give(n_dp, dp, me, g_ref, co_ref, sw, rw)
     swaps, receives = swap(h_ref, h_out, sh, rh, count, index, place)
-    sums = reduce_ctx(n, dp, me, a_ref, w_ref, slice(0, a_ref.shape[1]), y_ref, pa, qa, pb, qb, s1, r1, s2, r2)
-    mine.wait()
-    second = []
-    for c in range(n):
-        to = (me + 1 + c) % n
-        total = own[to].astype(F32)
+    mine = g_ref.at[pl.ds(pl.multiple_of(dp * tall, tall), tall), :]
+    stays = [
+        pltpu.make_async_copy(mine, own, local.at[0]),
+        pltpu.make_async_copy(h_ref.at[index], h_out.at[index], local.at[1]),
+    ]
+    for copy in stays:
+        copy.start()
+    cols = slice(0, a_ref.shape[1])
+    sums = reduce_ctx(n, dp, me, a_ref, w_ref, cols, y_ref, pa, qa, pb, qb, s1, r1, s2, r2)
+    for copy in stays:
+        copy.wait()
+    for copy in gives:
+        copy.wait_recv()
+
+    def add(part):
+        total = own[part, :].astype(F32)
         for k in range(n_dp - 1):
-            first[c][k].wait_recv()
-            total = total + ra[c, k].astype(F32)
-        if c < n - 1:
-            sb[c] = total.astype(BF)
-            copy = remote(sb.at[c], rc.at[c], sc.at[c], rd.at[c], (dp, to))
-            copy.start()
-            second.append(copy)
-        else:
-            o_ref[me] = total.astype(BF)
-    for c in range(n - 1):
-        second[c].wait_recv()
-        o_ref[(me + n - 1 - c) % n] = rc[c]
+            total = total + co_ref[k, part, :].astype(F32)
+        o_ref[part, :] = total.astype(BF)
+
+    tiles(tall, 64, add)
     for copy in receives:
         copy.wait_recv()
-    stay.wait()
-    for row in first:
-        for copy in row:
-            copy.wait_send()
-    for copy in second + sums + swaps:
+    for copy in gives + swaps + sums:
         copy.wait_send()
 
 
 def collect(g, h, a, w, number):
     n_dp, n = lax.axis_size("dp"), lax.axis_size("ctx")
-    rows, width = g.shape[0] // (n_dp * n), g.shape[1]
+    tall, width = g.shape[0] // n_dp, g.shape[1]
     half, length, features = n // 2, a.shape[0] // n, w.shape[0]
     dma = pltpu.SemaphoreType.DMA
     return pl.pallas_call(
         functools.partial(collect_kernel, n_dp, n),
         out_shape=(
-            jax.ShapeDtypeStruct((n, rows, width), BF),
+            jax.ShapeDtypeStruct((tall, width), BF),
             jax.ShapeDtypeStruct(h.shape, BF),
             jax.ShapeDtypeStruct((length, features), F32),
         ),
         in_specs=[ANY, ANY, VMEM, VMEM],
         out_specs=(VMEM, ANY, VMEM),
         scratch_shapes=[
-            pltpu.VMEM((n, rows, width), BF),
-            pltpu.VMEM((n, n_dp - 1, rows, width), BF),
-            pltpu.VMEM((n - 1, rows, width), BF),
-            pltpu.VMEM((n - 1, rows, width), BF),
+            pltpu.VMEM((tall, width), BF),
+            pltpu.VMEM((n_dp - 1, tall, width), BF),
             pltpu.VMEM((half, length, features), BF),
             pltpu.VMEM((half, length, features), BF),
             pltpu.VMEM((half - 1, length, features), BF),
             pltpu.VMEM((half - 1, length, features), BF),
             dma((2,)),
-            dma((n, n_dp - 1)),
-            dma((n, n_dp - 1)),
-            dma((n - 1,)),
-            dma((n - 1,)),
+            dma((n_dp - 1,)),
+            dma((n_dp - 1,)),
             dma((half,)),
             dma((half,)),
             dma((half - 1,)),
@@ -756,32 +810,47 @@
             dma((2 * n_dp - 1,)),
         ],
         compiler_params=params_of(number),
+        cost_estimate=cost(70),
         name="collect",
-    )(g.reshape(n_dp, n, rows, width), h, a, w)
-
-
-def total_kernel(n_dp, n, ga_ref, gu_ref, gd_ref, gain_ref, o_ref, mine, buf, part, all_parts, ss, rs, st, rt):
+    )(g, h, a, w)
+
+
+def total_kernel(
+    n_dp, n, qk_ref, wv_ref, wo_ref, u_ref, gg_ref, gd_ref, gain_ref, ga_ref, gu_ref, o_ref,
+    sb, mine, buf, part, all_parts, local, sx, rx, sh, rh, ss, rs, st, rt,
+):
     dp, me = lax.axis_index("dp"), lax.axis_index("ctx")
     gain_rows = gain_ref.shape[0]
+    hc = wv_ref.shape[2]
+    count, index, place = group_of(n_dp, n, dp, me)
+    greet_all(n_dp, n, dp, me)
+    swaps, receives = swap(u_ref, gu_ref, sh, rh, count, index, place)
+    stay = pltpu.make_async_copy(u_ref.at[index], gu_ref.at[index], local)
+    stay.start()
+    sb[:, :, : 2 * hc] = qk_ref[...]
+    sb[:, :, 2 * hc : 3 * hc] = wv_ref[...]
+    sb[:, :, 3 * hc :] = wo_ref[...]
+    more, waits = swap(sb, ga_ref, sx, rx, n, me, lambda c: (dp, c))
+    ga_ref[me] = sb[me]
 
     def squares(ref):
         acc = jnp.zeros((ref.shape[1], ref.shape[2]), F32)
         for i in range(ref.shape[0]):
             block = ref[i].astype(F32)
             acc += block * block
-        return jnp.sum(acc, axis=0, keepdims=True)
-
-    total = (
-        jnp.sum(squares(ga_ref), axis=1, keepdims=True)
-        + jnp.sum(squares(gu_ref), axis=1, keepdims=True)
-        + jnp.sum(squares(gd_ref), axis=1, keepdims=True)
-    )
+        return jnp.sum(jnp.sum(acc, axis=0, keepdims=True), axis=1, keepdims=True)
+
+    total = squares(gg_ref) + squares(gd_ref)
+    for copy in waits:
+        copy.wait_recv()
+    total += squares(ga_ref)
+    for copy in receives:
+        copy.wait_recv()
+    stay.wait()
+    total += squares(gu_ref)
     mine[0:gain_rows, :] = gain_ref[...]
     mine[gain_rows:, :] = jnp.broadcast_to(total, (8, 128))
-    greet(
-        [((dp + k) % n_dp, me) for k in range(1, n_dp)] + [(dp, (me + k) % n) for k in range(1, n)]
-    )
-    copies = []
+    copies = swaps + more
     for k in range(1, n):
         copy = remote(mine, buf.at[me], ss.at[k - 1], rs.at[k - 1], (dp, (me + k) % n))
         copy.start()
@@ -810,33 +879,53 @@
         copy.wait_send()
 
 
-def total_over(ga, gu, gd, gain_part, number):
+def total_over(qk, wv, wo, u, gg, gd, gain_part, number):
     n_dp, n = lax.axis_size("dp"), lax.axis_size("ctx")
+    rows, hc = qk.shape[0] // n, wv.shape[1]
     gain_rows = gain_part.size // 128
     shape = (gain_rows + 8, 128)
     dma = pltpu.SemaphoreType.DMA
-    out = pl.pallas_call(
+    ga, gu, out = pl.pallas_call(
         functools.partial(total_kernel, n_dp, n),
-        out_shape=jax.ShapeDtypeStruct(shape, F32),
-        in_specs=[VMEM] * 4,
-        out_specs=VMEM,
+        out_shape=(
+            jax.ShapeDtypeStruct((n, rows, 4 * hc), BF),
+            jax.ShapeDtypeStruct(u.shape, BF),
+            jax.ShapeDtypeStruct(shape, F32),
+        ),
+        in_specs=[VMEM] * 3 + [ANY] + [VMEM] * 3,
+        out_specs=(VMEM,) * 3,
         scratch_shapes=[
+            pltpu.VMEM((n, rows, 4 * hc), BF),
             pltpu.VMEM(shape, F32),
             pltpu.VMEM((n,) + shape, F32),
             pltpu.VMEM(shape, F32),
             pltpu.VMEM((n_dp,) + shape, F32),
+            dma,
+            dma((n - 1,)),
+            dma((n - 1,)),
+            dma((2 * n_dp - 1,)),
+            dma((2 * n_dp - 1,)),
             dma((n - 1,)),
             dma((n - 1,)),
             dma((n_dp - 1,)),
             dma((n_dp - 1,)),
         ],
         compiler_params=params_of(number),
+        cost_estimate=cost(35),
         name="total",
-    )(ga, gu, gd, gain_part.reshape(gain_rows, 128))
-    return out[gain_rows, 0], out[:gain_rows].reshape(gain_part.shape)
-
-
-def adam_kernel(factor_ref, p_ref, m_ref, v_ref, ga_ref, gu_ref, gd_ref, po_ref, mo_ref, vo_ref, g_ref):
+    )(
+        qk.reshape(n, rows, 2 * hc),
+        wv.reshape(n, rows, hc),
+        wo.reshape(n, rows, hc),
+        u,
+        gg,
+        gd,
+        gain_part.reshape(gain_rows, 128),
+    )
+    return ga, gu, out[gain_rows, 0], out[:gain_rows].reshape(gain_part.shape)
+
+
+def adam_kernel(factor_ref, p_ref, m_ref, v_ref, ga_ref, gg_ref, gu_ref, gd_ref, po_ref, mo_ref, vo_ref, g_ref):
     part = pl.program_id(0)
     n, _, four = ga_ref.shape
     hc = four // 4
@@ -849,24 +938,23 @@
                 start = (matrix * n + c) * hc
                 g_ref[:, start : start + hc] = ga_ref[c, :, matrix * hc : (matrix + 1) * hc].astype(F32)
 
-    @pl.when((part == 1) | (part == 2))
-    def _():
-        for d in range(gu_ref.shape[0]):
-            g_ref[:, d * fs : (d + 1) * fs] = gu_ref[d].astype(F32)
-
-    @pl.when(part == 3)
-    def _():
-        for d in range(gd_ref.shape[0]):
-            g_ref[:, d * fs : (d + 1) * fs] = gd_ref[d].astype(F32)
+    for index, ref in ((1, gg_ref), (2, gu_ref), (3, gd_ref)):
+
+        @pl.when(part == index)
+        def _():
+            for d in range(ref.shape[0]):
+                g_ref[:, d * fs : (d + 1) * fs] = ref[d].astype(F32)
 
     clipped = g_ref[...] * factor_ref[0, 0]
-    new_p, new_m, new_v = adam_update(p_ref[...], m_ref[...], v_ref[...], clipped, RATE, DECAY)
-    po_ref[...] = new_p
+    new_m = BETA1 * m_ref[...] + (1.0 - BETA1) * clipped
+    new_v = BETA2 * v_ref[...] + (1.0 - BETA2) * (clipped * clipped)
+    root = jnp.sqrt(new_v * (1.0 / (1.0 - BETA2**STEP))) + ADAM_EPS
+    po_ref[...] = p_ref[...] * (1.0 - RATE * DECAY) - (new_m * (RATE / (1.0 - BETA1**STEP))) / root
     mo_ref[...] = new_m
     vo_ref[...] = new_v
 
 
-def adam(factor, params, first, second, ga, gu, gd):
+def adam(factor, params, first, second, ga, gg, gu, gd):
     rows, columns = params.shape
     n, n_dp, fs = ga.shape[0], gd.shape[0], gd.shape[2]
     block = min(rows, 16)
@@ -882,21 +970,23 @@
             wide,
             wide,
             pl.BlockSpec((n, block, ga.shape[2]), lambda i, r: (0, jnp.where(i == 0, r, steps - 1), 0)),
-            pl.BlockSpec(
-                (n_dp, block, fs),
-                lambda i, r: (
-                    0,
-                    jnp.where(i == 0, 0, jnp.where(i == 3, steps - 1, r)),
-                    jnp.clip(i - 1, 0, 1),
-                ),
-            ),
-            pl.BlockSpec((n_dp, block, fs), lambda i, r: (0, jnp.where(i == 3, r, 0), 0)),
+            *[
+                pl.BlockSpec(
+                    (n_dp, block, fs),
+                    lambda i, r, part=part: (
+                        0,
+                        jnp.where(i < part, 0, jnp.where(i == part, r, steps - 1)),
+                        0,
+                    ),
+                )
+                for part in (1, 2, 3)
+            ],
         ],
         out_specs=(wide, wide, wide),
         scratch_shapes=[pltpu.VMEM((block, columns // 4), F32)],
         compiler_params=pltpu.CompilerParams(vmem_limit_bytes=48 * 1024 * 1024),
         name="adam",
-    )(factor.reshape(1, 1), params, first, second, ga, gu, gd)
+    )(factor.reshape(1, 1), params, first, second, ga, gg, gu, gd)
 
 
 def arrange_kernel(n, count, p_ref, a_ref, o_ref, g_ref, d_ref):
@@ -1103,53 +1193,65 @@
             dma((2,)),
         ],
         compiler_params=params_of(number),
+        cost_estimate=cost(60),
         name="attend",
     )(x_all, w, wo, d, tokens, norm, gain, cos, sine, info_col, info_row)
 
 
+def slab_give(n_dp, dp, me, g_ref, co_ref, sw, rw):
+    tall = co_ref.shape[1]
+    gives = []
+    for k in range(1, n_dp):
+        to = (dp + k) % n_dp
+        part = pl.ds(pl.multiple_of(to * tall, tall), tall)
+        copy = remote(g_ref.at[part, :], co_ref.at[k - 1], sw.at[k - 1], rw.at[k - 1], (to, me))
+        copy.start()
+        gives.append(copy)
+    return gives
+
+
+def slab_sum(dp, gives, g_ref, co_ref, out_ref):
+    tall = co_ref.shape[1]
+    total = g_ref[pl.ds(pl.multiple_of(dp * tall, tall), tall), :].astype(F32)
+    for k, copy in enumerate(gives):
+        copy.wait_recv()
+        total = total + co_ref[k].astype(F32)
+    out_ref[...] = total.astype(BF)
+
+
+def greet_wide_group(n_dp, dp, me):
+    partner = me + 1 - 2 * (me % 2)
+    others = [(dp + k) % n_dp for k in range(1, n_dp)]
+    greet([(dp, partner)] + [(d, c) for d in others for c in (me, partner)])
+
+
 def attend_back_kernel(
-    n_dp, n, e_ref, w_ref, h_ref, gain_ref, cos_ref, sin_ref, col_ref, row_ref,
-    q_ref, k_ref, v_ref, pre_ref, scale_ref, lse_ref,
-    all_ref, d_ref, gain_out, h_out,
-    do_ref, dq_ref, dk_ref, dv_ref, mean_ref, buf, ss, rs, s1, r1, s2, r2, sh, rh, local,
+    n_dp, n, e_ref, w_ref, h_ref, o_ref, col_ref, row_ref, q_ref, k_ref, v_ref, lse_ref,
+    dq_ref, dk_ref, dv_ref, h_out, wo_ref,
+    go_ref, co_ref, do_ref, sh, rh, local, sw, rw,
 ):
     dp, me = lax.axis_index("dp"), lax.axis_index("ctx")
-    half, parity, pair, partner, ahead, behind = pairs_of(n, me)
     seq, hc = q_ref.shape
-    length, width = e_ref.shape
+    width = e_ref.shape[1]
     block = min(seq, 256)
     count, index, place = group_of(n_dp, n, dp, me)
-    greet_all(n_dp, n, dp, me)
-    sends = [
-        remote(e_ref, all_ref.at[me], s1.at[k], r1.at[k], (dp, a))
-        for k, a in enumerate(ahead + [partner])
-    ]
-    for copy in sends:
-        copy.start()
+    greet_wide_group(n_dp, dp, me)
     swaps, receives = swap(h_ref, h_out, sh, rh, count, index, place)
     stay = pltpu.make_async_copy(h_ref.at[index], h_out.at[index], local)
     stay.start()
-    all_ref[me] = e_ref[...]
+
+    def product(part):
+        go_ref[part, :] = t_dot(e_ref[:, part], o_ref[...]).astype(BF)
+
+    tiles(width, 256, product)
+    gives = slab_give(n_dp, dp, me, go_ref, co_ref, sw, rw)
+
+    def project(rows):
+        do_ref[rows, :] = dot(e_ref[rows, :], w_ref[...]).astype(BF)
+
+    tiles(seq, block, project)
     dk_ref[...] = jnp.zeros_like(dk_ref)
     dv_ref[...] = jnp.zeros_like(dv_ref)
-
-    def project(b):
-        rows = pl.ds(pl.multiple_of(b * length, length), length)
-        do_ref[rows, :] = dot(all_ref[b], w_ref[...]).astype(BF)
-
-    project(me)
-    sends[-1].wait_recv()
-    project(partner)
-    forwards = []
-    for k, b in enumerate(behind):
-        remote(e_ref, all_ref.at[b], s1.at[k], r1.at[k], (dp, b)).wait_recv()
-        forward = remote(all_ref.at[b], all_ref.at[b], s2.at[k], r2.at[k], (dp, partner))
-        forward.start()
-        forwards.append(forward)
-        project(b)
-    for k, b in enumerate(behind):
-        forwards[k].wait_recv()
-        project(b + 1 - 2 * parity)
 
     @pl.loop(0, seq // block)
     def _(i):
@@ -1167,6 +1269,62 @@
             dk_ref[:, part] += t_dot(d_scores, query)
             dv_ref[:, part] += t_dot(probs.astype(BF), back)
 
+    slab_sum(dp, gives, go_ref, co_ref, wo_ref)
+    for copy in receives:
+        copy.wait_recv()
+    for copy in swaps + gives:
+        copy.wait_send()
+    stay.wait()
+
+
+def attend_back(e, w, h, o, info_col, info_row, q, k, v, lse, number):
+    n_dp, n = lax.axis_size("dp"), lax.axis_size("ctx")
+    (seq, hc), width = q.shape, e.shape[1]
+    dma = pltpu.SemaphoreType.DMA
+    return pl.pallas_call(
+        functools.partial(attend_back_kernel, n_dp, n),
+        out_shape=(
+            *[jax.ShapeDtypeStruct((seq, hc), F32)] * 3,
+            jax.ShapeDtypeStruct(h.shape, BF),
+            jax.ShapeDtypeStruct((width // n_dp, hc), BF),
+        ),
+        in_specs=[VMEM, VMEM, ANY] + [VMEM] * 7,
+        out_specs=(VMEM, VMEM, VMEM, ANY, VMEM),
+        scratch_shapes=[
+            pltpu.VMEM((width, hc), BF),
+            pltpu.VMEM((n_dp - 1, width // n_dp, hc), BF),
+            pltpu.VMEM((seq, hc), BF),
+            dma((2 * n_dp - 1,)),
+            dma((2 * n_dp - 1,)),
+            dma,
+            dma((n_dp - 1,)),
+            dma((n_dp - 1,)),
+        ],
+        compiler_params=params_of(number),
+        cost_estimate=cost(45),
+        name="attend_back",
+    )(e, w, h, o, info_col, info_row, q, k, v, lse)
+
+
+def project_back_kernel(
+    n_dp, n, dq_in, dk_in, dv_ref, x_ref, gain_ref, cos_ref, sin_ref, pre_ref, scale_ref,
+    d_ref, gain_out, g_ref, wv_ref,
+    dq_ref, dk_ref, mean_ref, buf, go_ref, co_ref, ss, rs, sw, rw,
+):
+    dp, me = lax.axis_index("dp"), lax.axis_index("ctx")
+    seq, hc = dv_ref.shape
+    width = x_ref.shape[1]
+    block = min(seq, 256)
+    greet(
+        [(dp, (me + k) % n) for k in range(1, n)] + [((dp + k) % n_dp, me) for k in range(1, n_dp)]
+    )
+    d_ref[:, 2 * hc :] = dv_ref[...].astype(BF)
+
+    def values(part):
+        go_ref[part, :] = t_dot(x_ref[:, part], d_ref[:, 2 * hc :]).astype(BF)
+
+    tiles(width, 256, values)
+    gives = slab_give(n_dp, dp, me, go_ref, co_ref, sw, rw)
     gain_out[...] = jnp.zeros_like(gain_out)
 
     @pl.loop(0, seq // block)
@@ -1174,12 +1332,15 @@
         rows = pl.ds(pl.multiple_of(i * block, block), block)
         cos, sine = cos_ref[rows, :], sin_ref[rows, :]
         sums = jnp.zeros((8, block), F32)
-        for which, ref, factor in ((0, dq_ref, HD ** (-0.5)), (1, dk_ref, 1.0)):
+        for which, source, ref, factor in (
+            (0, dq_in, dq_ref, HD ** (-0.5)),
+            (1, dk_in, dk_ref, 1.0),
+        ):
             scale = scale_ref[rows, which : which + 1]
             for start in range(0, hc, HD):
                 part = slice(start, start + HD)
                 pre = pre_ref[rows, which * hc + start : which * hc + start + HD]
-                value = turn(ref[rows, part] * factor, cos, -sine)
+                value = turn(source[rows, part] * factor, cos, -sine)
                 gain_out[which : which + 1, part] += jnp.sum(value * pre * scale, axis=0, keepdims=True)
                 value = value * gain_ref[which : which + 1, part]
                 ref[rows, part] = value
@@ -1197,51 +1358,46 @@
             cols = slice(which * hc, (which + 1) * hc)
             value = scale * (ref[rows, :] - pre_ref[rows, cols] * (scale * scale * mean))
             d_ref[rows, cols] = value.astype(BF)
-        d_ref[rows, 2 * hc :] = dv_ref[rows, :].astype(BF)
-
-    for copy in receives:
-        copy.wait_recv()
-    for copy in sends + forwards + swaps:
+
+    def product(part):
+        g_ref[part, :] = t_dot(x_ref[:, part], d_ref[:, : 2 * hc]).astype(BF)
+
+    tiles(width, 256, product)
+    slab_sum(dp, gives, go_ref, co_ref, wv_ref)
+    for copy in gives:
         copy.wait_send()
-    stay.wait()
-
-
-def attend_back(e, w, h, gain, cos, sine, info_col, info_row, q, k, v, pre, scale, lse, number):
+
+
+def project_back(dq, dk, dv, x, gain, cos, sine, pre, scale, number):
     n_dp, n = lax.axis_size("dp"), lax.axis_size("ctx")
-    seq, hc = q.shape
-    half, (length, width) = n // 2, e.shape
+    (seq, hc), width = dq.shape, x.shape[1]
     dma = pltpu.SemaphoreType.DMA
-    all_e, d_qkv, d_gain, h = pl.pallas_call(
-        functools.partial(attend_back_kernel, n_dp, n),
+    return pl.pallas_call(
+        functools.partial(project_back_kernel, n_dp, n),
         out_shape=(
-            jax.ShapeDtypeStruct((n, length, width), BF),
             jax.ShapeDtypeStruct((seq, 3 * hc), BF),
             jax.ShapeDtypeStruct((2, hc), F32),
-            jax.ShapeDtypeStruct(h.shape, BF),
+            jax.ShapeDtypeStruct((width, 2 * hc), BF),
+            jax.ShapeDtypeStruct((width // n_dp, hc), BF),
         ),
-        in_specs=[VMEM, VMEM, ANY] + [VMEM] * 11,
-        out_specs=(VMEM,) * 3 + (ANY,),
+        in_specs=[VMEM] * 9,
+        out_specs=(VMEM,) * 4,
         scratch_shapes=[
-            pltpu.VMEM((seq, hc), BF),
-            pltpu.VMEM((seq, hc), F32),
             pltpu.VMEM((seq, hc), F32),
             pltpu.VMEM((seq, hc), F32),
             pltpu.VMEM((seq, 8), F32),
             pltpu.VMEM((n, 8, seq), F32),
+            pltpu.VMEM((width, hc), BF),
+            pltpu.VMEM((n_dp - 1, width // n_dp, hc), BF),
             dma((n - 1,)),
             dma((n - 1,)),
-            dma((half,)),
-            dma((half,)),
-            dma((half - 1,)),
-            dma((half - 1,)),
-            dma((2 * n_dp - 1,)),
-            dma((2 * n_dp - 1,)),
-            dma,
+            dma((n_dp - 1,)),
+            dma((n_dp - 1,)),
         ],
         compiler_params=params_of(number),
-        name="attend_back",
-    )(e, w, h, gain, cos, sine, info_col, info_row, q, k, v, pre, scale, lse)
-    return all_e.reshape(seq, width), d_qkv, d_gain, h
+        cost_estimate=cost(30),
+        name="project_back",
+    )(dq, dk, dv, x, gain, cos, sine, pre, scale)
 
 
 def shards(
@@ -1312,22 +1468,24 @@
     branch, hidden1, queries, keys, values, attn_low, qk_pre, scales, lse, w_o, w_d = attend(
         x_all, w_qkv, w_o.reshape(n_ctx * rows, hc), w_d, tokens, gains[2:3], *tables, 3
     )
-    w_d = gather_pairs(w_d)
-
-    result, d_mlp, g_ff_part, h1_all, gate_up, inner = ff_forward(
-        hidden1, upstream, gains[3:4], w_gu, w_d, 4
-    )
-    d_mlp_all, d_gu = ff_back(d_mlp, w_d, gate_up, 5)
-    d_grad, gu_grad = ff_grad(d_mlp_all, inner, rows), ff_grad(h1_all, d_gu, rows)
-    d_grad, gu_grad, d_gu = lax.optimization_barrier((d_grad, gu_grad, d_gu))
-    d_grad, gu_grad = scatter_pairs(d_grad), scatter_pairs(gu_grad)
-    d_h1, d_branch, g_attn_part = ff_scatter(d_gu, w_gu, upstream, branch, gains[2:3], 6)
-
-    d_branch_all, d_qkv, d_gain, d_grad = attend_back(
-        d_branch, w_o, d_grad, *tables, queries, keys, values, qk_pre, scales, lse, 8
-    )
-    attn_grad = jnp.concatenate([t_dot(x_all, d_qkv), t_dot(d_branch_all, attn_low)], axis=1)
-    attn_grad, gu_grad, d_x = collect(attn_grad.astype(BF), gu_grad, d_qkv, w_qkv, 9)
+
+    result, d_mlp, g_ff_part, h1_all, gate_up, inner, w_d = ff_forward(
+        hidden1, upstream, gains[3:4], w_gu, w_d.reshape(n_dp, 2 * rows, fh), 4
+    )
+    d_gu, d_grad = ff_back(d_mlp, inner, w_d, gate_up, rows, 5)
+    d_grad = scatter_pairs(d_grad)
+    d_h1, d_branch_all, g_attn_part, g_grad, u_grad = ff_scatter(
+        d_gu, w_gu, h1_all, upstream, branch, gains[2:3], 6
+    )
+    g_grad, u_grad = scatter_pairs(g_grad), scatter_pairs(u_grad)
+
+    d_query, d_key, d_value, d_grad, wo_grad = attend_back(
+        d_branch_all, w_o, d_grad, attn_low, info_col, info_row, queries, keys, values, lse, 8
+    )
+    d_qkv, d_gain, qk_grad, wv_grad = project_back(
+        d_query, d_key, d_value, x_all, my_gains, cos_tab, sine_tab, qk_pre, scales, 10
+    )
+    qk_grad, g_grad, d_x = collect(qk_grad, g_grad, d_qkv, w_qkv, 9)
     d_input = d_h1 + d_x
 
     gain_part = jnp.concatenate(
@@ -1338,11 +1496,13 @@
         ],
         axis=0,
     )
-    square_total, gain_total = total_over(attn_grad, gu_grad, d_grad, gain_part, 11)
+    attn_grad, u_grad, square_total, gain_total = total_over(
+        qk_grad, wv_grad, wo_grad, u_grad, g_grad, d_grad, gain_part, 11
+    )
     grad_norm = jnp.sqrt(square_total + jnp.sum(gain_total * gain_total))
     factor = CLIP / (grad_norm + 1e-06)
     new_params, new_first, new_second = adam(
-        factor, params, first_moment, second_moment, attn_grad, gu_grad, d_grad
+        factor, params, first_moment, second_moment, attn_grad, g_grad, u_grad, d_grad
     )
     new_gains, new_gains_first, new_gains_second = adam_update(
         gains, gains_first, gains_second, gain_total * factor, GAIN_RATE, 0.0

time: 883 us -> 716 us (0.81)
  waiting for transfers between devices: 160 us -> 0.39 us
  Pallas kernels: 650 us -> 664 us
  local copies, waits for them, and re-layouts: 36.7 us -> 26.1 us
    all_gather x2 -> x1, waiting for transfers between devices: 158 us -> 0.01 us  [gather_pairs(): lax.all_gather(w.reshape(group * rows, w.shape[2]), 'ctx', axis=0, tiled=...]
    pallas_call x5 -> x4, Pallas kernels: 200 us -> 279 us  [the longest x1 117 us: ff_forward(): pl.pallas_call(functools.partial(ff_forward_kernel, n_dp, n), out_shape=(...]
    pallas_call x1, Pallas kernels: 127 us -> 71.2 us  [collect(): pl.pallas_call(functools.partial(collect_kernel, n_dp, n), out_shape=(jax...]
    pallas_call x1, Pallas kernels: 83.8 us -> 57.7 us  [attend_back(): pl.pallas_call(functools.partial(attend_back_kernel, n_dp, n), out_shape=...]
    pallas_call x1, Pallas kernels: 45.8 us -> 61.7 us  [ff_back(): pl.pallas_call(functools.partial(ff_back_kernel, n_dp), out_shape=(jax.Sh...]
    dot_general x2 -> x0, local copies, waits for them, and re-layouts: 12.9 us -> none  [t_dot(): lax.dot_general(a, b, (((0,), (0,)), ((), ())), preferred_element_type=F32)]
    unnamed x71 -> x65, local copies, waits for them, and re-layouts: 21.5 us -> 24.6 us
  transfers between devices with their start and end apart: 4 -> 4, of which waited for: 2 -> 0; matrix products, arithmetic and copies ran while one was open for 3% -> 0% of each run, Pallas kernels for 16% -> 52%
where the time goes in v6:
time: 716 us; the launch traced here: 715 us
  Pallas kernels  664 us (93%)
  local copies, waits for them, and re-layouts  26.1 us (4%)
  between operations  16.6 us (2%)
    pallas_call x1, Pallas kernels, ff_forward(): pl.pallas_call(functools.partial(ff_forward_kernel, n_dp, n), out_shape=(...  117 us
    pallas_call x1, Pallas kernels, ff_scatter(): pl.pallas_call(functools.partial(ff_scatter_kernel, n_dp, n), out_shape=(...  85.5 us
    pallas_call x1, Pallas kernels, collect(): pl.pallas_call(functools.partial(collect_kernel, n_dp, n), out_shape=(jax...  71.2 us
    pallas_call x1, Pallas kernels, gather_dp(): pl.pallas_call(functools.partial(gather_dp_kernel, n), out_shape=jax.Shap...  63.5 us
    pallas_call x1, Pallas kernels, ff_back(): pl.pallas_call(functools.partial(ff_back_kernel, n_dp), out_shape=(jax.Sh...  61.7 us
    pallas_call x1, Pallas kernels, attend(): pl.pallas_call(functools.partial(attend_kernel, n_dp, n), out_shape=(jax....  59.4 us
    pallas_call x1, Pallas kernels, attend_back(): pl.pallas_call(functools.partial(attend_back_kernel, n_dp, n), out_shape=...  57.7 us
    pallas_call x1, Pallas kernels, start(): pl.pallas_call(functools.partial(start_kernel, n_dp, n), out_shape=(jax.S...  44.6 us
  transfers between devices with their start and end apart: 4, of which 0 were waited for; matrix products, arithmetic and copies ran while one was open for 0% of the time, Pallas kernels for 52%

profile of v6, /device:TPU:0, one launch (start us, length us, event | category | flops | bytes accessed | tf_op | source)
XLA Modules:
  0.0 714.7 jit_solution(18328257079549827481)
XLA Ops:
  7.2 0.0 all-gather.2.cloned.1.call-start
  7.2 4.2 arrange.1
  11.5 0.0 copy-start.3
  11.5 1.3 copy-done.3
  12.8 1.0 copy-done.6
  13.8 44.6 %start.1 = (bf16[8,64,2048]{2,1,0:T(8,128)(2,1)S(1)}, bf16[8,64,768]{2,1,0:T(8,128)(2,1)S(1)}, bf16[8,64,256]{2,1,0:T(8,128)(2,1)S(1)}, bf16[8,128,2048]{2,1,0:T(8,128)(2,1)}) custom-call(bf16[8,64,2048]{2,1,0:T(8,128)(2,1)} %copy-done.3, bf16[8,64,768]{2,1,0:T(8,128)(2,1)S(1)} %get-tuple-element.61.w_ref, bf16[8,64,256]{2,1,0:T(8,128)(2,1)S(1)} %get-tuple-element.62.v_ref, ...), custom_call_target="tpu_custom_call" | custom-call | bytes 162000000 | tf_op jit(solution)/shard_map/start/pallas_call | solution.py:722
  58.4 0.0 copy-start.4
  58.4 1.3 copy-done.4
  59.7 0.0 all-gather.2.cloned.1.call-update
  59.7 0.0 reduce-scatter.4.cloned.1.call-start
  59.8 0.0 copy-start.27
  59.8 63.5 %gather_dp.1 = bf16[4,512,768]{2,1,0:T(8,128)(2,1)S(1)} custom-call(bf16[512,768]{1,0:T(8,128)(2,1)S(1)} %bitcast.33), custom_call_target="tpu_custom_call" | custom-call | bytes 216000000 | tf_op jit(solution)/shard_map/gather_dp/pallas_call | solution.py:152
  123.4 0.0 copy-start
  123.4 1.7 copy-done
  125.0 0.1 pad.5.clone
  125.1 0.1 select_reduce_fusion
  125.2 0.1 add_add_fusion
  125.3 0.2 copy.21.col_ref
  125.6 1.9 fusion.1
  127.5 0.3 pad_maximum_fusion
  127.8 0.6 fusion.15
  128.4 59.4 %attend.1 = (f32[128,2048]{1,0:T(8,128)}, f32[128,2048]{1,0:T(8,128)}, bf16[1024,256]{1,0:T(8,128)(2,1)S(1)}, bf16[1024,256]{1,0:T(8,128)(2,1)S(1)}, bf16[1024,2...) custom-call(bf16[1024,2048]{1,0:T(8,128)(2,1)} %bitcast.40, ...), custom_call_target="tpu_custom_call" | custom-call | bytes 216000000 | tf_op jit(solution)/shard_map/attend/pallas_call | solution.py:1160
  187.9 0.0 copy-start.13
  187.9 0.8 copy-done.13
  188.7 0.8 copy-done.15
  189.5 0.8 copy-done.17
  190.3 0.8 copy-done.19
  191.1 116.7 %ff_forward.1 = (bf16[128,2048]{1,0:T(8,128)(2,1)}, bf16[128,2048]{1,0:T(8,128)(2,1)}, f32[1,2048]{1,0:T(1,128)}, bf16[1024,2048]{1,0:T(8,128)(2,1)}, f32[1024,2...) custom-call(f32[128,2048]{1,0:T(8,128)} %get-tuple-element.67.h_ref, ...), custom_call_target="tpu_custom_call" | custom-call | bytes 324000000 | tf_op jit(solution)/shard_map/ff_forward/pallas_call | solution.py:460
  307.8 61.7 %ff_back.1 = (bf16[1024,2048]{1,0:T(8,128)(2,1)}, bf16[4,4,128,1024]{3,2,1,0:T(8,128)(2,1)}) custom-call(bf16[128,2048]{1,0:T(8,128)(2,1)} %get-tuple-element.71.dm_ref, bf16[1024,1024]{1,0:T(8,128)(2,1)} %get-tuple-element.72.hid_ref, bf16[2048,1024]{1,0:T(8,128)(2,1)} %get-tuple-element.73.d_hbm, f32[1024,2048]{1,0:T(8,128)} %get-tuple-element.74.pre_hbm), custom_call_target="tpu_custom_call" | custom-call | bytes 162000000 | tf_op jit(solution)/shard_map/ff_back/pallas_call | solution.py:549
  369.5 0.0 reduce-scatter.4.cloned.1.call-update
  369.5 0.0 reduce-scatter.6.cloned.1.call-start
  369.6 85.5 %ff_scatter.1 = (f32[128,2048]{1,0:T(8,128)}, bf16[1024,2048]{1,0:T(8,128)(2,1)}, f32[1,2048]{1,0:T(1,128)}, bf16[4,4,128,1024]{3,2,1,0:T(8,128)(2,1)}, bf16[4,4,128,1024]{3,2,1,0:T(8,128)(2,1)}) custom-call(bf16[1024,2048]{1,0:T(8,128)(2,1)} %get-tuple-element.75.dgu_ref, bf16[4,4,128,2048]{3,2,1,0:T(8,128)(2,1)} %bitcast.39, ...), custom_call_target="tpu_custom_call" | custom-call | bytes 180000000 | tf_op jit(solution)/shard_map/ff_scatter/pallas_call | solution.py:647
  455.1 0.0 copy-start.14
  455.1 0.0 reduce-scatter.6.cloned.1.call-update
  455.1 0.3 reduce-scatter.8.cloned.1.call-start
  455.4 0.3 reduce-scatter.8.cloned.1.call-update
  455.7 0.0 reduce-scatter.4.cloned.1.call-done
  455.7 0.4 copy-done.14
  456.1 1.0 copy-done.16
  457.1 1.0 copy-done.18
  458.2 1.0 copy-done.20
  459.2 57.7 %attend_back.1 = (f32[1024,256]{1,0:T(8,128)S(1)}, f32[1024,256]{1,0:T(8,128)S(1)}, f32[1024,256]{1,0:T(8,128)}, bf16[8,64,1024]{2,1,0:T(8,128)(2,1)}, bf16[512,256]{1,0:T(8,128)(2,1)S(1)}) custom-call(bf16[1024,2048]{1,0:T(8,128)(2,1)} %get-tuple-element.79.e_ref, bf16[2048,256]{1,0:T(8,128)(2,1)} %get-tuple-element.80.w_ref, ...), custom_call_target="tpu_custom_call" | custom-call | bytes 162000000 | tf_op jit(solution)/shard_map/attend_back/pallas_call | solution.py:1284
  517.0 1.2 copy-done.10
  518.2 33.7 %project_back.1 = (bf16[1024,768]{1,0:T(8,128)(2,1)}, f32[2,256]{1,0:T(2,128)S(1)}, bf16[2048,512]{1,0:T(8,128)(2,1)}, bf16[512,256]{1,0:T(8,128)(2,1)S(1)}) custom-call(f32[1024,256]{1,0:T(8,128)S(1)} %get-tuple-element.87.dq_in, f32[1024,256]{1,0:T(8,128)S(1)} %get-tuple-element.88.dk_in, f32[1024,256]{1,0:T(8,128)S(1)} %copy-done.10, ...), custom_call_target="tpu_custom_call" | custom-call | bytes 108000000 | tf_op jit(solution)/shard_map/project_back/pallas_call | solution.py:1375
  551.9 0.0 copy-start.23
  551.9 0.7 copy-done.23
  552.7 0.0 reduce-scatter.6.cloned.1.call-done
  552.7 1.5 copy-done.5
  554.2 1.2 copy-done.7
  555.4 71.2 %collect.1 = (bf16[512,512]{1,0:T(8,128)(2,1)S(1)}, bf16[8,64,1024]{2,1,0:T(8,128)(2,1)S(1)}, f32[128,2048]{1,0:T(8,128)S(1)}) custom-call(bf16[2048,512]{1,0:T(8,128)(2,1)} %get-tuple-element.92.g_ref, bf16[8,64,1024]{2,1,0:T(8,128)(2,1)S(1)} %bitcast.31, bf16[1024,768]{1,0:T(8,128)(2,1)S(1)} %copy-done.5, bf16[2048,768]{1,0:T(8,128)(2,1)} %bitcast.27), custom_call_target="tpu_custom_call" | custom-call | bytes 252000000 | tf_op jit(solution)/shard_map/collect/pallas_call | solution.py:786
  626.6 1.0 copy-done.11
  627.6 0.8 copy-done.21
  628.4 1.3 copy-done.12
  629.7 1.0 copy-done.22
  630.7 0.9 copy-done.24
  631.7 43.4 %total.1 = (bf16[8,64,1024]{2,1,0:T(8,128)(2,1)S(1)}, bf16[8,64,1024]{2,1,0:T(8,128)(2,1)S(1)}, f32[72,128]{1,0:T(8,128)S(1)}) custom-call(bf16[8,64,512]{2,1,0:T(8,128)(2,1)S(1)} %bitcast.34, bf16[8,64,256]{2,1,0:T(8,128)(2,1)S(1)} %bitcast.37, bf16[8,64,256]{2,1,0:T(8,128)(2,1)S(1)} %bitcast.36, bf16[8,64,1024]{2,1,0:T(8,128)(2,1)S(1)} %bitcast.32, ...), custom_call_target="tpu_custom_call" | custom-call | bytes 126000000 | tf_op jit(solution)/shard_map/total/pallas_call | solution.py:888
  675.1 1.0 copy-done.8
  676.1 0.5 slice.19
  676.6 0.6 multiply_reduce_fusion
  678.6 2.5 fusion
  681.0 1.5 multiply_subtract_fusion
  682.5 1.2 copy-done.9
  683.7 22.5 %adam.1 = (f32[64,32768]{1,0:T(8,128)}, f32[64,32768]{1,0:T(8,128)}, f32[64,32768]{1,0:T(8,128)}) custom-call(f32[1,1]{1,0:T(1,128)} %bitcast.23.factor_ref, f32[64,32768]{1,0:T(8,128)} %p_ref.3, f32[64,32768]{1,0:T(8,128)} %m_ref.1, f32[64,32768]{1,0:T(8,128)} %v_ref.1, bf16[8,64,1024]{2,1,0:T(8,128)(2,1)S(1)} %get-tuple-element.106.ga_ref, ...), custom_call_target="tpu_custom_call" | custom-call | tf_op jit(solution)/shard_map/adam/pallas_call | solution.py:963
  706.2 0.8 copy.25
  (50 shorter events, 0.2 us)
Async XLA Ops:
  7.2 6.6 copy-start.2
  7.2 183.9 %all-gather.2.cloned.1.call-start = ((), (), s32[]{:S(2)}) async-start(), calls=%async_computation.3 | async-start | bytes 10485760 | tf_op jit(solution)/shard_map/all_gather | solution.py:1430
  11.5 1.3 copy-start.3
  12.8 1.0 copy-start.6
  13.8 111.3 %copy-start.31 = (s32[8]{0:T(128)S(1)}, s32[8]{0:T(128)}, u32[]{:S(2)}) copy-start(s32[8]{0:T(128)} %param.13) | copy-start | bytes 100
  13.8 111.5 %copy-start.30 = (s32[1,1024]{1,0:T(1,128)S(1)}, s32[1,1024]{1,0:T(1,128)}, u32[]{:S(2)}) copy-start(s32[1,1024]{1,0:T(1,128)} %param.12) | copy-start | bytes 12292
  58.4 1.3 copy-start.4
  59.7 65.8 %slice-start = ((f32[4,2048]{1,0:T(4,128)}), f32[2,2048]{1,0:T(2,128)S(1)}, s32[]{:S(2)}) async-start(f32[4,2048]{1,0:T(4,128)} %param.17), calls=%async_computation.7 | async-start | bytes 32768 | tf_op jit(solution)/shard_map/slice | solution.py:1465
  59.7 395.9 %reduce-scatter.4.cloned.1.call-start = ((), (), s32[]{:S(2)}) async-start(), calls=%async_computation.4 | async-start | bytes 5242880 | tf_op jit(solution)/shard_map/reduce_scatter | solution.py:1436
  59.8 68.0 %copy-start.27 = (f32[4,2048]{1,0:T(4,128)S(1)}, f32[4,2048]{1,0:T(4,128)}, u32[]{:S(2)}) copy-start(f32[4,2048]{1,0:T(4,128)} %param.17) | copy-start | bytes 98308
  123.4 1.7 copy-start
  128.4 59.5 %copy-start.25 = (f32[1,2048]{1,0:T(1,128)}, f32[1,2048]{1,0:T(1,128)S(1)}, u32[]{:S(2)}) copy-start(f32[1,2048]{1,0:T(1,128)S(1)} %get-tuple-element.115.norm_ref.gain_ref) | copy-start | bytes 24580
  187.9 0.8 copy-start.13
  188.7 0.8 copy-start.15
  189.5 0.8 copy-start.17
  190.3 0.8 copy-start.19
  369.5 183.2 %reduce-scatter.6.cloned.1.call-start = ((), (), s32[]{:S(2)}) async-start(), calls=%async_computation.5 | async-start | bytes 5242880 | tf_op jit(solution)/shard_map/reduce_scatter | solution.py:1436
  455.1 1.0 copy-start.14
  455.1 173.3 %reduce-scatter.8.cloned.1.call-start = ((), (), s32[]{:S(2)}) async-start(), calls=%async_computation.6 | async-start | bytes 5242880 | tf_op jit(solution)/shard_map/reduce_scatter | solution.py:1436
  456.1 1.0 copy-start.16
  457.1 1.0 copy-start.18
  458.2 1.0 copy-start.20
  516.9 1.2 copy-start.10
  518.2 34.5 %copy-start.28 = (f32[1,2048]{1,0:T(1,128)S(1)}, f32[1,2048]{1,0:T(1,128)}, u32[]{:S(2)}) copy-start(f32[1,2048]{1,0:T(1,128)} %get-tuple-element.104) | copy-start | bytes 24580
  518.2 34.5 %copy-start.29 = (f32[1,2048]{1,0:T(1,128)S(1)}, f32[1,2048]{1,0:T(1,128)}, u32[]{:S(2)}) copy-start(f32[1,2048]{1,0:T(1,128)} %get-tuple-element.103) | copy-start | bytes 24580
  551.9 0.7 copy-start.23
  552.7 1.5 copy-start.5
  554.2 1.2 copy-start.7
  626.6 1.0 copy-start.11
  627.6 0.8 copy-start.21
  628.4 54.1 %copy-start.1 = (bf16[8,64,1024]{2,1,0:T(8,128)(2,1)S(1)}, bf16[8,64,1024]{2,1,0:T(8,128)(2,1)}, u32[]{:S(2)}) copy-start(bf16[8,64,1024]{2,1,0:T(8,128)(2,1)} %get-tuple-element.101.gd_ref) | copy-start | bytes 3145732
  628.4 1.3 copy-start.12
  629.7 1.0 copy-start.22
  630.7 0.9 copy-start.24
  675.1 1.0 copy-start.8
  682.5 1.2 copy-start.9
  683.7 22.5 %copy-start.26 = (bf16[128,2048]{1,0:T(8,128)(2,1)S(1)}, bf16[128,2048]{1,0:T(8,128)(2,1)}, u32[]{:S(2)}) copy-start(bf16[128,2048]{1,0:T(8,128)(2,1)} %get-tuple-element.70) | copy-start | bytes 1572868
Sparse Core Ops, SparseCore 0:
  59.9 97.6 all-gather.1
  369.7 52.1 reduce-scatter.3
  455.2 60.3 reduce-scatter.5
  518.4 55.7 reduce-scatter.7

commit v7 on v6

--- a/solution.py
+++ b/solution.py
@@ -326,49 +326,112 @@
     return [pltpu.SemaphoreType.DMA((n_dp,))] * 6
 
 
-def give_block(dp, me, b, own, a_ref, w_ref, o_ref, sa, ra, sb, rb, s1, r1, s2, r2):
-    length, width = o_ref.shape
+def line_sum(n, dp, me, make, val, o_ref, buf, send, recv, sync, between=None):
+    rows_of = lambda ref, body: tiles(ref.shape[0], 32, body)
+
+    def move(way, d):
+        to = jnp.where(way == 1, dp + 1, dp - 1)
+        return remote(buf.at[way, d], buf.at[way, d], send.at[way, d], recv.at[way, d], (to, me))
+
+    for j in range(1, n):
+
+        @pl.loop(0, 2)
+        def _(phase):
+            way = jnp.where(2 * dp < n, 1 - phase, phase)
+            d = jnp.where(way == 1, n - j, j - 1)
+            first = jnp.where(way == 1, 0, n - 1)
+            ahead = jnp.where(way == 1, d - dp, dp - d)
+
+            @pl.when(ahead > 0)
+            def _():
+                make(d, val)
+
+                @pl.when(dp == first)
+                def _():
+                    def begin(part):
+                        buf[way, d, part, :] = val[part, :].astype(BF)
+
+                    rows_of(val, begin)
+
+                @pl.when(dp != first)
+                def _():
+                    move(way, d).wait_recv()
+
+                    def add(part):
+                        buf[way, d, part, :] = (val[part, :] + buf[way, d, part, :].astype(F32)).astype(BF)
+
+                    rows_of(val, add)
+
+                move(way, d).start()
+
+        if between is not None:
+            between(j - 1)
+
+    make(dp, o_ref)
+    for way, first in ((1, 0), (0, n - 1)):
+
+        @pl.when(dp != first)
+        def _():
+            move(way, dp).wait_recv()
+
+            def add(part):
+                o_ref[part, :] += buf[way, dp, part, :].astype(F32)
+
+            rows_of(val, add)
+
+    sync()
+    for j in range(1, n):
+        for way, d in ((1, n - j), (0, j - 1)):
+
+            @pl.when((d - dp if way == 1 else dp - d) > 0)
+            def _():
+                move(way, d).wait_send()
+
+
+def line_scratch(n_dp, length, width):
+    return [
+        pltpu.VMEM((length, width), F32),
+        pltpu.VMEM((2, n_dp, length, width), BF),
+        pltpu.SemaphoreType.DMA((2, n_dp)),
+        pltpu.SemaphoreType.DMA((2, n_dp)),
+    ]
+
+
+def part_of_pair(dp, me, a_ref, w_ref, length, sa, ra, s1, r1):
     parity = me % 2
     partner = me + 1 - 2 * parity
 
-    def rows(side):
-        return pl.ds(pl.multiple_of((2 * b + side) * length, length), length)
-
-    def give(part):
-        sa[b, :, part] = dot_t(a_ref[rows(1 - parity), :], w_ref[part, :]).astype(BF)
-
-    tiles(width, 512, give)
-    copy = remote(sa.at[b], ra.at[b], s1.at[b], r1.at[b], (dp, partner))
-    copy.start()
-    copy.wait_recv()
-
-    def keep(part):
-        value = dot_t(a_ref[rows(parity), :], w_ref[part, :]) + ra[b, :, part].astype(F32)
-        if own:
-            o_ref[:, part] = value
-        else:
-            sb[b, :, part] = value.astype(BF)
-
-    tiles(width, 512, keep)
-    if not own:
-        remote(sb.at[b], rb.at[dp], s2.at[b], r2.at[dp], (b, me)).start()
-
-
-def give_end(n, dp, me, o_ref, sa, ra, sb, rb, s1, r1, s2, r2):
-    partner = me + 1 - 2 * (me % 2)
-    for k in range(1, n):
-        b = (dp + k) % n
-        remote(sb.at[b], rb.at[b], s2.at[b], r2.at[b], (b, me)).wait_recv()
-        o_ref[...] += rb[b].astype(F32)
-    for k in range(1, n):
-        b = (dp + k) % n
-        remote(sb.at[b], rb.at[b], s2.at[b], r2.at[b], (b, me)).wait_send()
-    for b in range(n):
-        remote(sa.at[b], ra.at[b], s1.at[b], r1.at[b], (dp, partner)).wait_send()
-
-
-def give_scratch(n_dp, length, width):
-    return [pltpu.VMEM((n_dp, length, width), BF)] * 4 + [pltpu.SemaphoreType.DMA((n_dp,))] * 4
+    def make(d, out):
+        def rows(side):
+            return pl.ds(pl.multiple_of((2 * d + side) * length, length), length)
+
+        def give(part):
+            sa[d, :, part] = dot_t(a_ref[rows(1 - parity), :], w_ref[part, :]).astype(BF)
+
+        tiles(out.shape[1], 512, give)
+        copy = remote(sa.at[d], ra.at[d], s1.at[d], r1.at[d], (dp, partner))
+        copy.start()
+
+        def keep(part):
+            out[:, part] = dot_t(a_ref[rows(parity), :], w_ref[part, :])
+
+        tiles(out.shape[1], 512, keep)
+        copy.wait_recv()
+
+        def add(part):
+            out[part, :] += ra[d, part, :].astype(F32)
+
+        tiles(length, 32, add)
+
+    def done(n):
+        for d in range(n):
+            remote(sa.at[d], ra.at[d], s1.at[d], r1.at[d], (dp, partner)).wait_send()
+
+    return make, done
+
+
+def pair_scratch(n_dp, length, width):
+    return [pltpu.VMEM((n_dp, length, width), BF)] * 2 + [pltpu.SemaphoreType.DMA((n_dp,))] * 2
 
 
 def greet_group(n_dp, dp, me):
@@ -377,11 +440,11 @@
 
 
 def ff_forward_kernel(
-    n_dp, n, h_ref, up_ref, gain_ref, gu_hbm, d_hbm,
-    res_ref, dm_ref, gp_ref, all_ref, pre_ref, hid_ref, d_ref,
-    gu_ref, acc, sem_gu, sem_d, sd, rd, *rest,
+    n_dp, n, h_ref, up_ref, gain_ref, gu_hbm, d_hbm, wo_hbm,
+    res_ref, dm_ref, gp_ref, all_out, pre_out, hid_out, d_out, wo_out,
+    all_ref, pre_ref, hid_ref, d_ref, gu_ref, acc, sem_gu, sem_d, sem_out, sd, rd, so, ro, fo, go, *rest,
 ):
-    gather, give = rest[:6], rest[6:]
+    gather, pair_refs, line_refs = rest[:6], rest[6:10], rest[10:]
     dp, me = lax.axis_index("dp"), lax.axis_index("ctx")
     length, width = h_ref.shape
     fh = hid_ref.shape[1]
@@ -431,12 +494,20 @@
         for d in range(n_dp):
             remote(d_hbm.at[d], down(d, b // 2), sd.at[k, d], rd.at[k, d], (dp, b)).wait_recv()
 
-    @pl.loop(1, n_dp)
-    def _(k):
-        give_block(dp, me, (dp + k) % n_dp, False, hid_ref, d_ref, acc, *give)
-
-    give_block(dp, me, dp, True, hid_ref, d_ref, acc, *give)
-    give_end(n_dp, dp, me, acc, *give)
+    outs = [
+        pltpu.make_async_copy(ref, out, sem_out.at[i])
+        for i, (ref, out) in enumerate(
+            ((all_ref, all_out), (pre_ref, pre_out), (hid_ref, hid_out), (d_ref, d_out))
+        )
+    ]
+    outs.append(pltpu.make_async_copy(wo_hbm, wo_out.at[me], sem_out.at[4]))
+    spreads_wo = [
+        remote(wo_hbm, wo_out.at[me], so.at[k], ro.at[k], (dp, a)) for k, a in enumerate(ahead + [partner])
+    ]
+    for copy in outs + spreads_wo:
+        copy.start()
+    make, done = part_of_pair(dp, me, hid_ref, d_ref, length, *pair_refs)
+
     gp_ref[...] = jnp.zeros_like(gp_ref)
 
     def finish(rows):
@@ -446,12 +517,28 @@
         gp_ref[...] += jnp.sum(up * out * scale, axis=0, keepdims=True)
         dm_ref[rows, :] = norm_back(up * gain, out, scale).astype(BF)
 
-    tiles(length, 16, finish)
-    for copy in spreads:
+    forwards = []
+
+    def last():
+        for k, b in enumerate(behind):
+            remote(wo_hbm, wo_out.at[b], so.at[k], ro.at[k], (dp, b)).wait_recv()
+            forward = remote(wo_out.at[b], wo_out.at[b], fo.at[k], go.at[k], (dp, partner))
+            forward.start()
+            forwards.append(forward)
+        tiles(length, 16, finish)
+
+    line_sum(n_dp, dp, me, make, line_refs[0], acc, *line_refs[1:], last)
+    done(n_dp)
+    spreads_wo[-1].wait_recv()
+    for copy in forwards:
+        copy.wait_recv()
+    for copy in spreads + spreads_wo + forwards:
         copy.wait_send()
-
-
-def ff_forward(h1, up, gain, w_gu, w_d, number):
+    for copy in outs:
+        copy.wait()
+
+
+def ff_forward(h1, up, gain, w_gu, w_d, w_o, number):
     n_dp, n = lax.axis_size("dp"), lax.axis_size("ctx")
     (length, width), fh = h1.shape, w_d.shape[2]
     tokens = 2 * n_dp * length
@@ -467,23 +554,34 @@
             jax.ShapeDtypeStruct((tokens, 2 * fh), F32),
             jax.ShapeDtypeStruct((tokens, fh), BF),
             jax.ShapeDtypeStruct((width, fh), BF),
+            jax.ShapeDtypeStruct((n,) + w_o.shape, BF),
         ),
-        in_specs=[VMEM] * 3 + [ANY] * 2,
-        out_specs=(VMEM,) * 7,
+        in_specs=[VMEM] * 3 + [ANY] * 3,
+        out_specs=(VMEM,) * 3 + (ANY,) * 5,
         scratch_shapes=[
+            pltpu.VMEM((tokens, width), BF),
+            pltpu.VMEM((tokens, 2 * fh), F32),
+            pltpu.VMEM((tokens, fh), BF),
+            pltpu.VMEM((width, fh), BF),
             pltpu.VMEM((width, 2 * fh), BF),
             pltpu.VMEM((length, width), F32),
             pltpu.SemaphoreType.DMA((half * n_dp,)),
             pltpu.SemaphoreType.DMA((n_dp,)),
+            pltpu.SemaphoreType.DMA((5,)),
             pltpu.SemaphoreType.DMA((half - 1, n_dp)),
             pltpu.SemaphoreType.DMA((half - 1, n_dp)),
+            pltpu.SemaphoreType.DMA((half,)),
+            pltpu.SemaphoreType.DMA((half,)),
+            pltpu.SemaphoreType.DMA((half - 1,)),
+            pltpu.SemaphoreType.DMA((half - 1,)),
         ]
         + gather_sems(n_dp)
-        + give_scratch(n_dp, length, width),
+        + pair_scratch(n_dp, length, width)
+        + line_scratch(n_dp, length, width),
         compiler_params=params_of(number, 58),
         cost_estimate=cost(90),
         name="ff_forward",
-    )(h1, up, gain, w_gu, w_d)
+    )(h1, up, gain, w_gu, w_d, w_o)
 
 
 def store_rows(n_dp, value_of, out):
@@ -570,107 +668,153 @@
 
 
 def ff_scatter_kernel(
-    n_dp, n, dgu_ref, gu_hbm, all_hbm, up_ref, branch_ref, gain_ref, dh_ref, db_ref, gp_ref, gg_ref, gv_ref,
-    gu_ref, all_ref, acc, sem_gu, sem_all, ss, rs, fs, fr, *give,
+    n_dp, n, dgu_ref, gu_hbm, all_hbm, wo_hbm, up_ref, branch_ref, gain_ref, dh_ref, dc_ref, do_ref, gp_ref, gg_out, gv_out,
+    gg_ref, gv_ref, gu_ref, all_ref, wo_ref, give_ref, db_ref, mix_ref, acc, sem_gu, sem_all, sem_out, ss, rs, sc, rc, *rest,
 ):
     dp, me = lax.axis_index("dp"), lax.axis_index("ctx")
     length, width = dh_ref.shape
+    pair_refs, line_refs = rest[:4], rest[4:]
     half, parity, pair, partner, ahead, behind = pairs_of(n, me)
     _, _, rows, fh = gg_ref.shape
     loads = load_rows(gu_hbm, gu_ref, sem_gu)
     load = pltpu.make_async_copy(all_hbm, all_ref, sem_all)
     load.start()
+    load_wo = pltpu.make_async_copy(wo_hbm, wo_ref, sem_out.at[2])
+    load_wo.start()
     greet(
-        [(dp, partner)]
-        + [((dp + k) % n_dp, me) for k in range(1, n_dp)]
-        + [(dp, a) for a in ahead]
+        [(dp, (me + k) % n) for k in range(1, n)] + [((dp + k) % n_dp, me) for k in range(1, n_dp)]
     )
     for copy in loads:
         copy.wait()
 
-    @pl.loop(1, n_dp)
-    def _(k):
-        give_block(dp, me, (dp + k) % n_dp, False, dgu_ref, gu_ref, dh_ref, *give)
-
-    give_block(dp, me, dp, True, dgu_ref, gu_ref, dh_ref, *give)
-    load.wait()
-    block = acc.shape[0]
-
-    @pl.loop(0, width // block)
-    def _(j):
-        acc[...] = t_dot(all_ref[:, pl.ds(pl.multiple_of(j * block, block), block)], dgu_ref[...])
-        for s in range(block // rows):
-            r = j * (block // rows) + s
-            part = slice(s * rows, (s + 1) * rows)
-            gg_ref[r % half, r // half] = acc[part, :fh].astype(BF)
-            gv_ref[r % half, r // half] = acc[part, fh:].astype(BF)
-
-    give_end(n_dp, dp, me, dh_ref, *give)
+    make, done = part_of_pair(dp, me, dgu_ref, gu_ref, length, *pair_refs)
     gp_ref[...] = jnp.zeros_like(gp_ref)
-
-    def block(b):
-        return db_ref.at[pl.ds(pl.multiple_of(b * length, length), length), :]
 
     def finish(rows):
         grad, branch = dh_ref[rows, :] + up_ref[rows, :].astype(F32), branch_ref[rows, :]
         scale = rms_scale(branch)
         dh_ref[rows, :] = grad
         gp_ref[...] += jnp.sum(grad * branch * scale, axis=0, keepdims=True)
-        mine = pl.ds(pl.multiple_of(me * length + rows.start, rows.size), rows.size)
-        db_ref[mine, :] = norm_back(grad * gain_ref[...], branch, scale).astype(BF)
-
-    tiles(length, 16, finish)
-    sends = [
-        remote(block(me), block(me), ss.at[k], rs.at[k], (dp, a)) for k, a in enumerate(ahead + [partner])
+        db_ref[rows, :] = norm_back(grad * gain_ref[...], branch, scale).astype(BF)
+
+    load.wait()
+    tall = acc.shape[0]
+    blocks = width // tall
+    each = -(-blocks // (n_dp - 1))
+
+    def grads(step):
+        @pl.loop(min(step * each, blocks), min((step + 1) * each, blocks))
+        def _(j):
+            acc[...] = t_dot(all_ref[:, pl.ds(pl.multiple_of(j * tall, tall), tall)], dgu_ref[...])
+            for s in range(tall // rows):
+                r = j * (tall // rows) + s
+                part = slice(s * rows, (s + 1) * rows)
+                gg_ref[r % half, r // half] = acc[part, :fh].astype(BF)
+                gv_ref[r % half, r // half] = acc[part, fh:].astype(BF)
+
+    val, *line = line_refs
+    line_sum(n_dp, dp, me, make, val, dh_ref, *line, lambda: tiles(length, 16, finish), grads)
+    done(n_dp)
+    outs = [
+        pltpu.make_async_copy(ref, out, sem_out.at[i])
+        for i, (ref, out) in enumerate(((gg_ref, gg_out), (gv_ref, gv_out)))
     ]
-    for copy in sends:
+    for copy in outs:
         copy.start()
-    forwards = []
-    for k, b in enumerate(behind):
-        remote(block(b), block(b), ss.at[k], rs.at[k], (dp, b)).wait_recv()
-        forward = remote(block(b), block(b), fs.at[k], fr.at[k], (dp, partner))
-        forward.start()
-        forwards.append(forward)
-    remote(block(partner), block(partner), ss.at[half - 1], rs.at[half - 1], (dp, partner)).wait_recv()
-    for k, b in enumerate(behind):
-        other = b + 1 - 2 * parity
-        remote(block(other), block(other), fs.at[k], fr.at[k], (dp, partner)).wait_recv()
-    for copy in sends + forwards:
-        copy.wait_send()
-
-
-def ff_scatter(dgu, w_gu, h1_all, up, branch, gain, number):
+    load_wo.wait()
+
+    def mine(c):
+        return pl.ds(pl.multiple_of(c * length, length), length)
+
+    def send(k):
+        to = (me + k) % n
+        return remote(give_ref.at[to], do_ref.at[mine(me), :], ss.at[k - 1], rs.at[k - 1], (dp, to))
+
+    def receive(k):
+        source = (me + n - k) % n
+        return remote(give_ref.at[me], do_ref.at[mine(source), :], ss.at[k - 1], rs.at[k - 1], (dp, source))
+
+    own = rows // 2
+    share = n_dp * own
+    for c in range(n):
+        for d in range(n_dp):
+            start, source = c * share + d * own, (d * n + c) * own
+            mix_ref[:, start : start + own] = db_ref[:, source : source + own]
+
+    def share_of(c):
+        return mix_ref.at[:, pl.ds(pl.multiple_of(c * share, share), share)]
+
+    def send_share(k):
+        to = (me + k) % n
+        return remote(share_of(to), dc_ref.at[mine(me), :], sc.at[k - 1], rc.at[k - 1], (dp, to))
+
+    def receive_share(k):
+        source = (me + n - k) % n
+        return remote(share_of(me), dc_ref.at[mine(source), :], sc.at[k - 1], rc.at[k - 1], (dp, source))
+
+    stay = pltpu.make_async_copy(share_of(me), dc_ref.at[mine(me), :], sem_out.at[3])
+    stay.start()
+
+    @pl.loop(1, n)
+    def _(k):
+        to = (me + k) % n
+        send_share(k).start()
+        give_ref[to] = dot(db_ref[...], wo_ref[to]).astype(BF)
+        send(k).start()
+
+    do_ref[mine(me), :] = dot(db_ref[...], wo_ref[me]).astype(BF)
+    for k in range(1, n):
+        receive(k).wait_recv()
+        receive_share(k).wait_recv()
+    for k in range(1, n):
+        send(k).wait_send()
+        send_share(k).wait_send()
+    stay.wait()
+    for copy in outs:
+        copy.wait()
+
+
+def ff_scatter(dgu, w_gu, h1_all, wo_all, up, branch, gain, number):
     n_dp, n = lax.axis_size("dp"), lax.axis_size("ctx")
     length, width = up.shape
-    half = n // 2
+    hc = wo_all.shape[2]
     grad = jax.ShapeDtypeStruct(w_gu.shape[:3] + (w_gu.shape[3] // 2,), BF)
     return pl.pallas_call(
         functools.partial(ff_scatter_kernel, n_dp, n),
         out_shape=(
             jax.ShapeDtypeStruct((length, width), F32),
-            jax.ShapeDtypeStruct((n * length, width), BF),
+            jax.ShapeDtypeStruct((n * length, width // n), BF),
+            jax.ShapeDtypeStruct((n * length, hc), BF),
             jax.ShapeDtypeStruct((1, width), F32),
             grad,
             grad,
         ),
-        in_specs=[VMEM, ANY, ANY] + [VMEM] * 3,
-        out_specs=(VMEM,) * 5,
+        in_specs=[VMEM, ANY, ANY, ANY] + [VMEM] * 3,
+        out_specs=(VMEM,) * 4 + (ANY,) * 2,
         scratch_shapes=[
+            pltpu.VMEM(grad.shape, BF),
+            pltpu.VMEM(grad.shape, BF),
             pltpu.VMEM((width, w_gu.shape[3]), BF),
             pltpu.VMEM(h1_all.shape, BF),
+            pltpu.VMEM(wo_all.shape, BF),
+            pltpu.VMEM((n, length, hc), BF),
+            pltpu.VMEM((length, width), BF),
+            pltpu.VMEM((length, width), BF),
             pltpu.VMEM((256, w_gu.shape[3]), F32),
             pltpu.SemaphoreType.DMA((w_gu.shape[0] * n_dp,)),
             pltpu.SemaphoreType.DMA,
-            pltpu.SemaphoreType.DMA((half,)),
-            pltpu.SemaphoreType.DMA((half,)),
-            pltpu.SemaphoreType.DMA((half - 1,)),
-            pltpu.SemaphoreType.DMA((half - 1,)),
+            pltpu.SemaphoreType.DMA((4,)),
+            pltpu.SemaphoreType.DMA((n - 1,)),
+            pltpu.SemaphoreType.DMA((n - 1,)),
+            pltpu.SemaphoreType.DMA((n - 1,)),
+            pltpu.SemaphoreType.DMA((n - 1,)),
         ]
-        + give_scratch(n_dp, length, width),
-        compiler_params=params_of(number, 56),
+        + pair_scratch(n_dp, length, width)
+        + line_scratch(n_dp, length, width),
+        compiler_params=params_of(number, 60),
         cost_estimate=cost(50),
         name="ff_scatter",
-    )(dgu, w_gu, h1_all, up, branch, gain)
+    )(dgu, w_gu, h1_all, wo_all, up, branch, gain)
 
 
 def start_kernel(
@@ -829,7 +973,6 @@
     stay.start()
     sb[:, :, : 2 * hc] = qk_ref[...]
     sb[:, :, 2 * hc : 3 * hc] = wv_ref[...]
-    sb[:, :, 3 * hc :] = wo_ref[...]
     more, waits = swap(sb, ga_ref, sx, rx, n, me, lambda c: (dp, c))
     ga_ref[me] = sb[me]
 
@@ -840,7 +983,7 @@
             acc += block * block
         return jnp.sum(jnp.sum(acc, axis=0, keepdims=True), axis=1, keepdims=True)
 
-    total = squares(gg_ref) + squares(gd_ref)
+    total = squares(gg_ref) + squares(gd_ref) + squares(wo_ref)
     for copy in waits:
         copy.wait_recv()
     total += squares(ga_ref)
@@ -888,14 +1031,14 @@
     ga, gu, out = pl.pallas_call(
         functools.partial(total_kernel, n_dp, n),
         out_shape=(
-            jax.ShapeDtypeStruct((n, rows, 4 * hc), BF),
+            jax.ShapeDtypeStruct((n, rows, 3 * hc), BF),
             jax.ShapeDtypeStruct(u.shape, BF),
             jax.ShapeDtypeStruct(shape, F32),
         ),
         in_specs=[VMEM] * 3 + [ANY] + [VMEM] * 3,
         out_specs=(VMEM,) * 3,
         scratch_shapes=[
-            pltpu.VMEM((n, rows, 4 * hc), BF),
+            pltpu.VMEM((n, rows, 3 * hc), BF),
             pltpu.VMEM(shape, F32),
             pltpu.VMEM((n,) + shape, F32),
             pltpu.VMEM(shape, F32),
@@ -916,7 +1059,7 @@
     )(
         qk.reshape(n, rows, 2 * hc),
         wv.reshape(n, rows, hc),
-        wo.reshape(n, rows, hc),
+        wo[None],
         u,
         gg,
         gd,
@@ -925,15 +1068,16 @@
     return ga, gu, out[gain_rows, 0], out[:gain_rows].reshape(gain_part.shape)
 
 
-def adam_kernel(factor_ref, p_ref, m_ref, v_ref, ga_ref, gg_ref, gu_ref, gd_ref, po_ref, mo_ref, vo_ref, g_ref):
+def adam_kernel(factor_ref, p_ref, m_ref, v_ref, ga_ref, go_ref, gg_ref, gu_ref, gd_ref, po_ref, mo_ref, vo_ref, g_ref):
     part = pl.program_id(0)
-    n, _, four = ga_ref.shape
-    hc = four // 4
+    n, _, three = ga_ref.shape
+    hc = three // 3
     fs = gd_ref.shape[2]
 
     @pl.when(part == 0)
     def _():
-        for matrix in range(4):
+        g_ref[:, 3 * n * hc :] = go_ref[...].astype(F32)
+        for matrix in range(3):
             for c in range(n):
                 start = (matrix * n + c) * hc
                 g_ref[:, start : start + hc] = ga_ref[c, :, matrix * hc : (matrix + 1) * hc].astype(F32)
@@ -954,7 +1098,7 @@
     vo_ref[...] = new_v
 
 
-def adam(factor, params, first, second, ga, gg, gu, gd):
+def adam(factor, params, first, second, ga, go, gg, gu, gd):
     rows, columns = params.shape
     n, n_dp, fs = ga.shape[0], gd.shape[0], gd.shape[2]
     block = min(rows, 16)
@@ -970,6 +1114,7 @@
             wide,
             wide,
             pl.BlockSpec((n, block, ga.shape[2]), lambda i, r: (0, jnp.where(i == 0, r, steps - 1), 0)),
+            pl.BlockSpec((block, go.shape[1]), lambda i, r: (jnp.where(i == 0, r, steps - 1), 0)),
             *[
                 pl.BlockSpec(
                     (n_dp, block, fs),
@@ -986,7 +1131,7 @@
         scratch_shapes=[pltpu.VMEM((block, columns // 4), F32)],
         compiler_params=pltpu.CompilerParams(vmem_limit_bytes=48 * 1024 * 1024),
         name="adam",
-    )(factor.reshape(1, 1), params, first, second, ga, gg, gu, gd)
+    )(factor.reshape(1, 1), params, first, second, ga, go, gg, gu, gd)
 
 
 def arrange_kernel(n, count, p_ref, a_ref, o_ref, g_ref, d_ref):
@@ -1226,35 +1371,32 @@
 
 
 def attend_back_kernel(
-    n_dp, n, e_ref, w_ref, h_ref, o_ref, col_ref, row_ref, q_ref, k_ref, v_ref, lse_ref,
+    n_dp, n, e_ref, do_ref, h_ref, o_hbm, col_ref, row_ref, q_ref, k_ref, v_ref, lse_ref,
     dq_ref, dk_ref, dv_ref, h_out, wo_ref,
-    go_ref, co_ref, do_ref, sh, rh, local, sw, rw,
+    o_ref, go_ref, co_ref, sh, rh, local, sw, rw,
 ):
     dp, me = lax.axis_index("dp"), lax.axis_index("ctx")
     seq, hc = q_ref.shape
-    width = e_ref.shape[1]
+    load = pltpu.make_async_copy(o_hbm, o_ref, local.at[1])
+    load.start()
     block = min(seq, 256)
     count, index, place = group_of(n_dp, n, dp, me)
     greet_wide_group(n_dp, dp, me)
     swaps, receives = swap(h_ref, h_out, sh, rh, count, index, place)
-    stay = pltpu.make_async_copy(h_ref.at[index], h_out.at[index], local)
+    stay = pltpu.make_async_copy(h_ref.at[index], h_out.at[index], local.at[0])
     stay.start()
 
-    def product(part):
-        go_ref[part, :] = t_dot(e_ref[:, part], o_ref[...]).astype(BF)
-
-    tiles(width, 256, product)
+    load.wait()
+
+    @pl.loop(0, n)
+    def _(c):
+        go_ref[:, pl.ds(pl.multiple_of(c * hc, hc), hc)] = t_dot(e_ref[...], o_ref[c]).astype(BF)
+
     gives = slab_give(n_dp, dp, me, go_ref, co_ref, sw, rw)
-
-    def project(rows):
-        do_ref[rows, :] = dot(e_ref[rows, :], w_ref[...]).astype(BF)
-
-    tiles(seq, block, project)
     dk_ref[...] = jnp.zeros_like(dk_ref)
     dv_ref[...] = jnp.zeros_like(dv_ref)
 
-    @pl.loop(0, seq // block)
-    def _(i):
+    def attention(i):
         rows = pl.ds(pl.multiple_of(i * block, block), block)
         visible = mask_of(rows, col_ref, row_ref)
         for head in range(hc // HD):
@@ -1269,6 +1411,7 @@
             dk_ref[:, part] += t_dot(d_scores, query)
             dv_ref[:, part] += t_dot(probs.astype(BF), back)
 
+    pl.loop(0, seq // block)(attention)
     slab_sum(dp, gives, go_ref, co_ref, wo_ref)
     for copy in receives:
         copy.wait_recv()
@@ -1277,33 +1420,33 @@
     stay.wait()
 
 
-def attend_back(e, w, h, o, info_col, info_row, q, k, v, lse, number):
+def attend_back(e, do, h, o_all, info_col, info_row, q, k, v, lse, number):
     n_dp, n = lax.axis_size("dp"), lax.axis_size("ctx")
-    (seq, hc), width = q.shape, e.shape[1]
+    (seq, hc), share = q.shape, e.shape[1]
     dma = pltpu.SemaphoreType.DMA
     return pl.pallas_call(
         functools.partial(attend_back_kernel, n_dp, n),
         out_shape=(
             *[jax.ShapeDtypeStruct((seq, hc), F32)] * 3,
             jax.ShapeDtypeStruct(h.shape, BF),
-            jax.ShapeDtypeStruct((width // n_dp, hc), BF),
+            jax.ShapeDtypeStruct((share // n_dp, n * hc), BF),
         ),
-        in_specs=[VMEM, VMEM, ANY] + [VMEM] * 7,
+        in_specs=[VMEM, VMEM, ANY, ANY] + [VMEM] * 6,
         out_specs=(VMEM, VMEM, VMEM, ANY, VMEM),
         scratch_shapes=[
-            pltpu.VMEM((width, hc), BF),
-            pltpu.VMEM((n_dp - 1, width // n_dp, hc), BF),
-            pltpu.VMEM((seq, hc), BF),
+            pltpu.VMEM(o_all.shape, BF),
+            pltpu.VMEM((share, n * hc), BF),
+            pltpu.VMEM((n_dp - 1, share // n_dp, n * hc), BF),
             dma((2 * n_dp - 1,)),
             dma((2 * n_dp - 1,)),
-            dma,
+            dma((2,)),
             dma((n_dp - 1,)),
             dma((n_dp - 1,)),
         ],
         compiler_params=params_of(number),
         cost_estimate=cost(45),
         name="attend_back",
-    )(e, w, h, o, info_col, info_row, q, k, v, lse)
+    )(e, do, h, o_all, info_col, info_row, q, k, v, lse)
 
 
 def project_back_kernel(
@@ -1469,18 +1612,20 @@
         x_all, w_qkv, w_o.reshape(n_ctx * rows, hc), w_d, tokens, gains[2:3], *tables, 3
     )
 
-    result, d_mlp, g_ff_part, h1_all, gate_up, inner, w_d = ff_forward(
-        hidden1, upstream, gains[3:4], w_gu, w_d.reshape(n_dp, 2 * rows, fh), 4
-    )
+    result, d_mlp, g_ff_part, h1_all, gate_up, inner, w_d, w_o = ff_forward(
+        hidden1, upstream, gains[3:4], w_gu, w_d.reshape(n_dp, 2 * rows, fh), w_o, 4
+    )
+    attn_low, d_mlp = lax.optimization_barrier((attn_low, d_mlp))
+    attn_all = lax.all_gather(attn_low, "ctx", axis=0)
     d_gu, d_grad = ff_back(d_mlp, inner, w_d, gate_up, rows, 5)
     d_grad = scatter_pairs(d_grad)
-    d_h1, d_branch_all, g_attn_part, g_grad, u_grad = ff_scatter(
-        d_gu, w_gu, h1_all, upstream, branch, gains[2:3], 6
+    d_h1, d_branch, d_attn, g_attn_part, g_grad, u_grad = ff_scatter(
+        d_gu, w_gu, h1_all, w_o, upstream, branch, gains[2:3], 6
     )
     g_grad, u_grad = scatter_pairs(g_grad), scatter_pairs(u_grad)
 
     d_query, d_key, d_value, d_grad, wo_grad = attend_back(
-        d_branch_all, w_o, d_grad, attn_low, info_col, info_row, queries, keys, values, lse, 8
+        d_branch, d_attn, d_grad, attn_all, info_col, info_row, queries, keys, values, lse, 8
     )
     d_qkv, d_gain, qk_grad, wv_grad = project_back(
         d_query, d_key, d_value, x_all, my_gains, cos_tab, sine_tab, qk_pre, scales, 10
@@ -1502,7 +1647,7 @@
     grad_norm = jnp.sqrt(square_total + jnp.sum(gain_total * gain_total))
     factor = CLIP / (grad_norm + 1e-06)
     new_params, new_first, new_second = adam(
-        factor, params, first_moment, second_moment, attn_grad, g_grad, u_grad, d_grad
+        factor, params, first_moment, second_moment, attn_grad, wo_grad, g_grad, u_grad, d_grad
     )
     new_gains, new_gains_first, new_gains_second = adam_update(
         gains, gains_first, gains_second, gain_total * factor, GAIN_RATE, 0.0

time: 716 us -> 692 us (0.966)
  Pallas kernels: 664 us -> 639 us
    pallas_call x1, Pallas kernels: 85.5 us -> 69.6 us  [ff_scatter(): pl.pallas_call(functools.partial(ff_scatter_kernel, n_dp, n), out_shape=(...]
    pallas_call x1, Pallas kernels: 61.7 us -> 54 us  [ff_back(): pl.pallas_call(functools.partial(ff_back_kernel, n_dp), out_shape=(jax.Sh...]
  transfers between devices with their start and end apart: 4 -> 5, of which waited for: 0 -> 0; matrix products, arithmetic and copies ran while one was open for 0% -> 0% of each run, Pallas kernels for 52% -> 59%
where the time goes in v7:
time: 692 us; the launch traced here: 691 us
  Pallas kernels  639 us (92%)
  local copies, waits for them, and re-layouts  26.9 us (4%)
  between operations  16.7 us (2%)
  other arithmetic  7.59 us (1%)
    pallas_call x1, Pallas kernels, ff_forward(): pl.pallas_call(functools.partial(ff_forward_kernel, n_dp, n), out_shape=(...  117 us
    pallas_call x1, Pallas kernels, collect(): pl.pallas_call(functools.partial(collect_kernel, n_dp, n), out_shape=(jax...  70.7 us
    pallas_call x1, Pallas kernels, ff_scatter(): pl.pallas_call(functools.partial(ff_scatter_kernel, n_dp, n), out_shape=(...  69.6 us
    pallas_call x1, Pallas kernels, gather_dp(): pl.pallas_call(functools.partial(gather_dp_kernel, n), out_shape=jax.Shap...  63.5 us
    pallas_call x1, Pallas kernels, attend(): pl.pallas_call(functools.partial(attend_kernel, n_dp, n), out_shape=(jax....  59.4 us
    pallas_call x1, Pallas kernels, attend_back(): pl.pallas_call(functools.partial(attend_back_kernel, n_dp, n), out_shape=...  57.3 us
    pallas_call x1, Pallas kernels, ff_back(): pl.pallas_call(functools.partial(ff_back_kernel, n_dp), out_shape=(jax.Sh...  54 us
    pallas_call x1, Pallas kernels, start(): pl.pallas_call(functools.partial(start_kernel, n_dp, n), out_shape=(jax.S...  44.6 us
  transfers between devices with their start and end apart: 5, of which 0 were waited for; matrix products, arithmetic and copies ran while one was open for 0% of the time, Pallas kernels for 59%

profile of v7, /device:TPU:0, one launch (start us, length us, event | category | flops | bytes accessed | tf_op | source)
XLA Modules:
  0.0 691.1 jit_solution(2921298916656311174)
XLA Ops:
  7.2 0.0 all-gather.4.cloned.1.call-start
  7.2 4.2 arrange.1
  11.5 1.3 copy-done.3
  12.8 1.0 copy-done.6
  13.8 44.6 %start.1 = (bf16[8,64,2048]{2,1,0:T(8,128)(2,1)S(1)}, bf16[8,64,768]{2,1,0:T(8,128)(2,1)S(1)}, bf16[8,64,256]{2,1,0:T(8,128)(2,1)S(1)}, bf16[8,128,2048]{2,1,0:T(8,128)(2,1)}) custom-call(bf16[8,64,2048]{2,1,0:T(8,128)(2,1)} %copy-done.3, bf16[8,64,768]{2,1,0:T(8,128)(2,1)S(1)} %get-tuple-element.65.w_ref, bf16[8,64,256]{2,1,0:T(8,128)(2,1)S(1)} %get-tuple-element.66.v_ref, ...), custom_call_target="tpu_custom_call" | custom-call | bytes 162000000 | tf_op jit(solution)/shard_map/start/pallas_call | solution.py:866
  58.4 0.0 copy-start.4
  58.4 1.3 copy-done.4
  59.7 0.0 all-gather.4.cloned.1.call-update
  59.7 0.0 all-gather.6.cloned.1.call-start
  59.8 0.0 copy-start.27
  59.8 63.5 %gather_dp.1 = bf16[4,512,768]{2,1,0:T(8,128)(2,1)S(1)} custom-call(bf16[512,768]{1,0:T(8,128)(2,1)S(1)} %bitcast.35), custom_call_target="tpu_custom_call" | custom-call | bytes 216000000 | tf_op jit(solution)/shard_map/gather_dp/pallas_call | solution.py:152
  123.4 1.7 copy-done
  125.0 0.1 pad.5.clone
  125.1 0.1 select_reduce_fusion
  125.2 0.1 add_add_fusion
  125.3 0.2 copy.21.col_ref
  125.6 1.9 fusion.1
  127.5 0.3 pad_maximum_fusion
  127.8 0.6 fusion.15
  128.4 59.4 %attend.1 = (f32[128,2048]{1,0:T(8,128)}, f32[128,2048]{1,0:T(8,128)}, bf16[1024,256]{1,0:T(8,128)(2,1)S(1)}, bf16[1024,256]{1,0:T(8,128)(2,1)S(1)}, bf16[1024,2...) custom-call(bf16[1024,2048]{1,0:T(8,128)(2,1)} %bitcast.41, ...), custom_call_target="tpu_custom_call" | custom-call | bytes 216000000 | tf_op jit(solution)/shard_map/attend/pallas_call | solution.py:1305
  187.9 0.8 copy-done.13
  188.7 0.8 copy-done.15
  189.5 0.8 copy-done.17
  190.2 116.8 %ff_forward.1 = (bf16[128,2048]{1,0:T(8,128)(2,1)}, bf16[128,2048]{1,0:T(8,128)(2,1)}, f32[1,2048]{1,0:T(1,128)}, bf16[1024,2048]{1,0:T(8,128)(2,1)}, f32[1024,2...) custom-call(f32[128,2048]{1,0:T(8,128)} %get-tuple-element.71.h_ref, ...), custom_call_target="tpu_custom_call" | custom-call | bytes 324000000 | tf_op jit(solution)/shard_map/ff_forward/pallas_call | solution.py:547
  307.0 0.0 all-gather.6.cloned.1.call-update
  307.1 0.0 reduce-scatter.4.cloned.1.call-start
  307.1 54.0 %ff_back.1 = (bf16[1024,2048]{1,0:T(8,128)(2,1)}, bf16[4,4,128,1024]{3,2,1,0:T(8,128)(2,1)}) custom-call(bf16[128,2048]{1,0:T(8,128)(2,1)} %get-tuple-element.78.dm_ref, bf16[1024,1024]{1,0:T(8,128)(2,1)} %get-tuple-element.79.hid_ref, bf16[2048,1024]{1,0:T(8,128)(2,1)} %get-tuple-element.80.d_hbm, f32[1024,2048]{1,0:T(8,128)} %get-tuple-element.81.pre_hbm), custom_call_target="tpu_custom_call" | custom-call | bytes 162000000 | tf_op jit(solution)/shard_map/ff_back/pallas_call | solution.py:647
  361.1 0.0 reduce-scatter.4.cloned.1.call-update
  361.1 0.3 reduce-scatter.6.cloned.1.call-start
  361.4 69.6 %ff_scatter.1 = (f32[128,2048]{1,0:T(8,128)}, bf16[1024,256]{1,0:T(8,128)(2,1)}, bf16[1024,256]{1,0:T(8,128)(2,1)}, f32[1,2048]{1,0:T(1,128)}, bf16[4,4,128,1024...) custom-call(bf16[1024,2048]{1,0:T(8,128)(2,1)} %get-tuple-element.82.dgu_ref, bf16[4,4,128,2048]{3,2,1,0:T(8,128)(2,1)} %bitcast.40, ...), custom_call_target="tpu_custom_call" | custom-call | bytes 180000000 | tf_op jit(solution)/shard_map/ff_scatter/pallas_call | solution.py:782
  431.0 0.0 reduce-scatter.6.cloned.1.call-update
  431.0 0.3 reduce-scatter.8.cloned.1.call-start
  431.3 0.3 reduce-scatter.8.cloned.1.call-update
  431.6 0.0 all-gather.6.cloned.1.call-done
  431.7 0.0 reduce-scatter.4.cloned.1.call-done
  431.7 0.4 copy-done.14
  432.0 1.0 copy-done.16
  433.1 1.0 copy-done.18
  434.1 1.0 copy-done.19
  435.2 1.0 copy-done.20
  436.2 57.3 %attend_back.1 = (f32[1024,256]{1,0:T(8,128)S(1)}, f32[1024,256]{1,0:T(8,128)S(1)}, f32[1024,256]{1,0:T(8,128)}, bf16[8,64,1024]{2,1,0:T(8,128)(2,1)}, bf16[64,2048]{1,0:T(8,128)(2,1)S(1)}) custom-call(bf16[1024,256]{1,0:T(8,128)(2,1)S(1)} %copy-done.19, bf16[1024,256]{1,0:T(8,128)(2,1)S(1)} %copy-done.20, bf16[8,64,1024]{2,1,0:T(8,128)(2,1)} %bitcast.49, ...), custom_call_target="tpu_custom_call" | custom-call | bytes 162000000 | tf_op jit(solution)/shard_map/attend_back/pallas_call | solution.py:1427
  493.5 1.2 copy-done.8
  494.7 34.4 %project_back.1 = (bf16[1024,768]{1,0:T(8,128)(2,1)}, f32[2,256]{1,0:T(2,128)S(1)}, bf16[2048,512]{1,0:T(8,128)(2,1)}, bf16[512,256]{1,0:T(8,128)(2,1)S(1)}) custom-call(f32[1024,256]{1,0:T(8,128)S(1)} %get-tuple-element.95.dq_in, f32[1024,256]{1,0:T(8,128)S(1)} %get-tuple-element.96.dk_in, f32[1024,256]{1,0:T(8,128)S(1)} %copy-done.8, ...), custom_call_target="tpu_custom_call" | custom-call | bytes 108000000 | tf_op jit(solution)/shard_map/project_back/pallas_call | solution.py:1518
  529.1 0.7 copy-done.23
  529.9 0.0 reduce-scatter.6.cloned.1.call-done
  529.9 1.5 copy-done.5
  531.5 1.2 copy-done.7
  532.7 70.7 %collect.1 = (bf16[512,512]{1,0:T(8,128)(2,1)S(1)}, bf16[8,64,1024]{2,1,0:T(8,128)(2,1)S(1)}, f32[128,2048]{1,0:T(8,128)S(1)}) custom-call(bf16[2048,512]{1,0:T(8,128)(2,1)} %get-tuple-element.100.g_ref, bf16[8,64,1024]{2,1,0:T(8,128)(2,1)S(1)} %bitcast.33, bf16[1024,768]{1,0:T(8,128)(2,1)S(1)} %copy-done.5, bf16[2048,768]{1,0:T(8,128)(2,1)} %bitcast.28), custom_call_target="tpu_custom_call" | custom-call | bytes 252000000 | tf_op jit(solution)/shard_map/collect/pallas_call | solution.py:930
  603.4 1.0 copy-done.9
  604.4 0.8 copy-done.21
  605.2 1.2 copy-done.10
  606.4 1.0 copy-done.22
  607.5 0.9 copy-done.24
  608.4 41.9 %total.1 = (bf16[8,64,768]{2,1,0:T(8,128)(2,1)S(1)}, bf16[8,64,1024]{2,1,0:T(8,128)(2,1)S(1)}, f32[72,128]{1,0:T(8,128)S(1)}) custom-call(bf16[8,64,512]{2,1,0:T(8,128)(2,1)S(1)} %bitcast.36, bf16[8,64,256]{2,1,0:T(8,128)(2,1)S(1)} %bitcast.38, bf16[1,64,2048]{2,1,0:T(8,128)(2,1)S(1)} %bitcast.32, bf16[8,64,1024]{2,1,0:T(8,128)(2,1)S(1)} %bitcast.34, ...), custom_call_target="tpu_custom_call" | custom-call | bytes 126000000 | tf_op jit(solution)/shard_map/total/pallas_call | solution.py:1031
  650.4 0.9 copy-done.11
  651.2 0.5 slice.19
  651.7 0.6 multiply_reduce_fusion
  653.7 0.6 slice_multiply_fusion
  654.4 0.8 mul.101
  655.1 2.5 fusion
  657.6 1.5 multiply_subtract_fusion
  659.0 1.1 copy-done.12
  660.2 22.5 %adam.1 = (f32[64,32768]{1,0:T(8,128)}, f32[64,32768]{1,0:T(8,128)}, f32[64,32768]{1,0:T(8,128)}) custom-call(f32[1,1]{1,0:T(1,128)} %bitcast.24.factor_ref, f32[64,32768]{1,0:T(8,128)} %p_ref.3, f32[64,32768]{1,0:T(8,128)} %m_ref.1, f32[64,32768]{1,0:T(8,128)} %v_ref.1, bf16[8,64,768]{2,1,0:T(8,128)(2,1)S(1)} %copy-done.12, ...), custom_call_target="tpu_custom_call" | custom-call | tf_op jit(solution)/shard_map/adam/pallas_call | solution.py:1107
  682.7 0.8 copy.25
  (53 shorter events, 0.2 us)
Async XLA Ops:
  7.2 6.6 copy-start.2
  7.2 183.1 %all-gather.4.cloned.1.call-start = ((), (), s32[]{:S(2)}) async-start(), calls=%async_computation.3 | async-start | bytes 10485760 | tf_op jit(solution)/shard_map/all_gather | solution.py:1573
  11.5 1.3 copy-start.3
  12.8 1.0 copy-start.6
  13.8 111.3 %copy-start.31 = (s32[8]{0:T(128)S(1)}, s32[8]{0:T(128)}, u32[]{:S(2)}) copy-start(s32[8]{0:T(128)} %param.13) | copy-start | bytes 100
  13.8 111.5 %copy-start.30 = (s32[1,1024]{1,0:T(1,128)S(1)}, s32[1,1024]{1,0:T(1,128)}, u32[]{:S(2)}) copy-start(s32[1,1024]{1,0:T(1,128)} %param.12) | copy-start | bytes 12292
  58.4 1.3 copy-start.4
  59.7 65.8 %slice-start = ((f32[4,2048]{1,0:T(4,128)}), f32[2,2048]{1,0:T(2,128)S(1)}, s32[]{:S(2)}) async-start(f32[4,2048]{1,0:T(4,128)} %param.17), calls=%async_computation.8 | async-start | bytes 32768 | tf_op jit(solution)/shard_map/slice | solution.py:1608
  59.7 371.9 %all-gather.6.cloned.1.call-start = ((), (), s32[]{:S(2)}) async-start(), calls=%async_computation.7 | async-start | bytes 4718592 | tf_op jit(solution)/shard_map/all_gather | solution.py:1619
  59.8 68.0 %copy-start.27 = (f32[4,2048]{1,0:T(4,128)S(1)}, f32[4,2048]{1,0:T(4,128)}, u32[]{:S(2)}) copy-start(f32[4,2048]{1,0:T(4,128)} %param.17) | copy-start | bytes 98308
  123.4 1.7 copy-start
  128.4 59.4 %copy-start.25 = (f32[1,2048]{1,0:T(1,128)}, f32[1,2048]{1,0:T(1,128)S(1)}, u32[]{:S(2)}) copy-start(f32[1,2048]{1,0:T(1,128)S(1)} %get-tuple-element.123.norm_ref.gain_ref) | copy-start | bytes 24580
  187.9 0.8 copy-start.13
  188.7 0.8 copy-start.15
  189.5 0.8 copy-start.17
  307.1 124.6 %reduce-scatter.4.cloned.1.call-start = ((), (), s32[]{:S(2)}) async-start(), calls=%async_computation.4 | async-start | bytes 5242880 | tf_op jit(solution)/shard_map/reduce_scatter | solution.py:1579
  361.1 168.8 %reduce-scatter.6.cloned.1.call-start = ((), (), s32[]{:S(2)}) async-start(), calls=%async_computation.5 | async-start | bytes 5242880 | tf_op jit(solution)/shard_map/reduce_scatter | solution.py:1579
  431.0 1.0 copy-start.14
  431.0 174.2 %reduce-scatter.8.cloned.1.call-start = ((), (), s32[]{:S(2)}) async-start(), calls=%async_computation.6 | async-start | bytes 5242880 | tf_op jit(solution)/shard_map/reduce_scatter | solution.py:1579
  432.0 1.0 copy-start.16
  433.1 1.0 copy-start.18
  434.1 1.0 copy-start.19
  435.2 1.0 copy-start.20
  493.5 1.2 copy-start.8
  494.7 35.1 %copy-start.28 = (f32[1,2048]{1,0:T(1,128)S(1)}, f32[1,2048]{1,0:T(1,128)}, u32[]{:S(2)}) copy-start(f32[1,2048]{1,0:T(1,128)} %get-tuple-element.112) | copy-start | bytes 24580
  494.7 35.1 %copy-start.29 = (f32[1,2048]{1,0:T(1,128)S(1)}, f32[1,2048]{1,0:T(1,128)}, u32[]{:S(2)}) copy-start(f32[1,2048]{1,0:T(1,128)} %get-tuple-element.111) | copy-start | bytes 24580
  529.1 0.7 copy-start.23
  529.8 75.4 %copy-start.1 = (bf16[8,64,1024]{2,1,0:T(8,128)(2,1)S(1)}, bf16[8,64,1024]{2,1,0:T(8,128)(2,1)}, u32[]{:S(2)}) copy-start(bf16[8,64,1024]{2,1,0:T(8,128)(2,1)} %get-tuple-element.109.gd_ref) | copy-start | bytes 3145732
  529.9 1.5 copy-start.5
  531.5 1.2 copy-start.7
  603.4 1.0 copy-start.9
  604.4 0.8 copy-start.21
  605.2 1.2 copy-start.10
  606.4 1.0 copy-start.22
  607.5 0.9 copy-start.24
  650.4 0.9 copy-start.11
  659.0 1.1 copy-start.12
  660.2 22.5 %copy-start.26 = (bf16[128,2048]{1,0:T(8,128)(2,1)S(1)}, bf16[128,2048]{1,0:T(8,128)(2,1)}, u32[]{:S(2)}) copy-start(bf16[128,2048]{1,0:T(8,128)(2,1)} %get-tuple-element.75) | copy-start | bytes 1572868
Sparse Core Ops, SparseCore 0:
  59.9 97.6 all-gather.3
  307.2 38.9 all-gather.5
  361.2 53.2 reduce-scatter.3
  431.2 63.7 reduce-scatter.5
  497.8 60.0 reduce-scatter.7

commit v8 on v7

--- a/solution.py
+++ b/solution.py
@@ -173,10 +173,21 @@
     greet([(dp, (me + k) % n) for k in range(1, n)] + [(d, c) for d in others for c in (me, partner)])
 
 
+def across(mine, k, count):
+    if count & (count - 1):
+        return (mine + k) % count, (mine + count - k) % count
+    bit, other = 1, mine
+    while bit < count:
+        if k & bit:
+            other = other + bit - 2 * bit * ((other // bit) % 2)
+        bit *= 2
+    return other, other
+
+
 def swap(src, dst, send, recv, count, mine, place):
     sends, receives = [], []
     for k in range(1, count):
-        to, source = (mine + k) % count, (mine + count - k) % count
+        to, source = across(mine, k, count)
         sends.append(remote(src.at[to], dst.at[mine], send.at[k - 1], recv.at[k - 1], place(to)))
         receives.append(
             remote(src.at[mine], dst.at[source], send.at[k - 1], recv.at[k - 1], place(source))
@@ -194,7 +205,7 @@
         body(pl.ds(pl.multiple_of(j * tile, tile), tile))
 
 
-def reduce_ctx(n, dp, me, a_ref, w_ref, cols, o_ref, sa, ra, sb, rb, s1, r1, s2, r2):
+def reduce_ctx(n, dp, me, a_ref, w_ref, cols, o_ref, sa, ra, sb, rb, s1, r1, s2, r2, before=None):
     half, parity, pair, partner, ahead, behind = pairs_of(n, me)
     length, width = o_ref.shape
 
@@ -204,6 +215,8 @@
     first, second = [], []
     for k in range(half):
         target = (pair + k + 1) % half
+        if before is not None:
+            before(target, k == 0)
 
         def give(part):
             value = dot_t(a_ref[rows(2 * target + 1 - parity), :], w_ref[part, cols])
@@ -327,47 +340,51 @@
 
 
 def line_sum(n, dp, me, make, val, o_ref, buf, send, recv, sync, between=None):
-    rows_of = lambda ref, body: tiles(ref.shape[0], 32, body)
-
     def move(way, d):
         to = jnp.where(way == 1, dp + 1, dp - 1)
         return remote(buf.at[way, d], buf.at[way, d], send.at[way, d], recv.at[way, d], (to, me))
 
-    for j in range(1, n):
-
-        @pl.loop(0, 2)
-        def _(phase):
-            way = jnp.where(2 * dp < n, 1 - phase, phase)
-            d = jnp.where(way == 1, n - j, j - 1)
-            first = jnp.where(way == 1, 0, n - 1)
-            ahead = jnp.where(way == 1, d - dp, dp - d)
-
-            @pl.when(ahead > 0)
-            def _():
-                make(d, val)
-
-                @pl.when(dp == first)
+    def steps(body):
+        for j in range(1, n):
+
+            @pl.loop(0, 2)
+            def _(phase):
+                way = jnp.where(2 * dp < n, 1 - phase, phase)
+                d = jnp.where(way == 1, n - j, j - 1)
+                first = jnp.where(way == 1, 0, n - 1)
+                ahead = jnp.where(way == 1, d - dp, dp - d)
+
+                @pl.when(ahead > 0)
                 def _():
-                    def begin(part):
-                        buf[way, d, part, :] = val[part, :].astype(BF)
-
-                    rows_of(val, begin)
-
-                @pl.when(dp != first)
-                def _():
-                    move(way, d).wait_recv()
-
-                    def add(part):
-                        buf[way, d, part, :] = (val[part, :] + buf[way, d, part, :].astype(F32)).astype(BF)
-
-                    rows_of(val, add)
-
-                move(way, d).start()
-
-        if between is not None:
-            between(j - 1)
-
+                    body(way, d, dp == first)
+
+    def begin(way, d, starts):
+        make(d, val.at[d])
+
+        @pl.when(starts)
+        def _():
+            def put(part):
+                buf[way, d, part, :] = val[d, part, :].astype(BF)
+
+            tiles(val.shape[1], 32, put)
+            move(way, d).start()
+
+    def follow(way, d, starts):
+        @pl.when(jnp.logical_not(starts))
+        def _():
+            move(way, d).wait_recv()
+
+            def add(part):
+                buf[way, d, part, :] = (val[d, part, :] + buf[way, d, part, :].astype(F32)).astype(BF)
+
+            tiles(val.shape[1], 32, add)
+            move(way, d).start()
+
+    steps(begin)
     make(dp, o_ref)
+    steps(follow)
+    if between is not None:
+        between()
     for way, first in ((1, 0), (0, n - 1)):
 
         @pl.when(dp != first)
@@ -377,20 +394,15 @@
             def add(part):
                 o_ref[part, :] += buf[way, dp, part, :].astype(F32)
 
-            rows_of(val, add)
+            tiles(val.shape[1], 32, add)
 
     sync()
-    for j in range(1, n):
-        for way, d in ((1, n - j), (0, j - 1)):
-
-            @pl.when((d - dp if way == 1 else dp - d) > 0)
-            def _():
-                move(way, d).wait_send()
+    steps(lambda way, d, starts: move(way, d).wait_send())
 
 
 def line_scratch(n_dp, length, width):
     return [
-        pltpu.VMEM((length, width), F32),
+        pltpu.VMEM((n_dp, length, width), F32),
         pltpu.VMEM((2, n_dp, length, width), BF),
         pltpu.SemaphoreType.DMA((2, n_dp)),
         pltpu.SemaphoreType.DMA((2, n_dp)),
@@ -699,11 +711,9 @@
 
     load.wait()
     tall = acc.shape[0]
-    blocks = width // tall
-    each = -(-blocks // (n_dp - 1))
-
-    def grads(step):
-        @pl.loop(min(step * each, blocks), min((step + 1) * each, blocks))
+
+    def grads():
+        @pl.loop(0, width // tall)
         def _(j):
             acc[...] = t_dot(all_ref[:, pl.ds(pl.multiple_of(j * tall, tall), tall)], dgu_ref[...])
             for s in range(tall // rows):
@@ -818,30 +828,58 @@
 
 
 def start_kernel(
-    n_dp, n, g_ref, w_ref, v_ref, x_ref, h_ref, o_ref, p_ref, y_ref,
-    local, sg, rg, sa, ra, sv, rv, ss, rs, fs, fr,
+    n_dp, n, p_hbm, x_ref, h_ref, o_ref, p_ref, y_ref, d_ref,
+    p_all, g_ref, w_ref, v_ref, local, sg, rg, sa, ra, sv, rv, ss, rs, fs, fr,
 ):
     dp, me = lax.axis_index("dp"), lax.axis_index("ctx")
     half, parity, pair, partner, ahead, behind = pairs_of(n, me)
     count, mine, place = group_of(n_dp, n, dp, me)
+    columns = p_all.shape[2]
+    fh, hc = d_ref.shape[2], v_ref.shape[2]
+    loads = [
+        pltpu.make_async_copy(
+            p_hbm.at[:, pl.ds(part * columns, columns)], p_all.at[part], local.at[part]
+        )
+        for part in range(4)
+    ]
+    for part in (1, 2, 0, 3):
+        loads[part].start()
     greet_all(n_dp, n, dp, me)
-    owns = [
-        pltpu.make_async_copy(g_ref.at[mine], h_ref.at[mine], local.at[0]),
-        pltpu.make_async_copy(w_ref.at[me], o_ref.at[me], local.at[1]),
-        pltpu.make_async_copy(x_ref, y_ref.at[me], local.at[2]),
-        pltpu.make_async_copy(v_ref.at[me], p_ref.at[me], local.at[3]),
+    gathers = [
+        remote(x_ref, y_ref.at[me], ss.at[k], rs.at[k], (dp, a))
+        for k, a in enumerate(ahead + [partner])
     ]
+    own_x = pltpu.make_async_copy(x_ref, y_ref.at[me], local.at[4])
+    for copy in gathers + [own_x]:
+        copy.start()
+    for part in (1, 2):
+        loads[part].wait()
+        for j in range(count):
+            g_ref[j, :, (part - 1) * fh : part * fh] = p_all[part, :, j * fh : (j + 1) * fh].astype(BF)
     sends, receives = swap(g_ref, h_ref, sg, rg, count, mine, place)
+    loads[0].wait()
+    for c in range(n):
+        for matrix in range(4):
+            start = (matrix * n + c) * hc
+            value = p_all[0, :, start : start + hc].astype(BF)
+            if matrix < 3:
+                w_ref[c, :, matrix * hc : (matrix + 1) * hc] = value
+            else:
+                v_ref[c] = value
     for src, dst, send, recv in ((w_ref, o_ref, sa, ra), (v_ref, p_ref, sv, rv)):
         more, waits = swap(src, dst, send, recv, n, me, lambda c: (dp, c))
         sends += more
         receives += waits
-    gathers = [
-        remote(x_ref, y_ref.at[me], ss.at[k], rs.at[k], (dp, a))
-        for k, a in enumerate(ahead + [partner])
+    owns = [
+        pltpu.make_async_copy(g_ref.at[mine], h_ref.at[mine], local.at[5]),
+        pltpu.make_async_copy(w_ref.at[me], o_ref.at[me], local.at[6]),
+        pltpu.make_async_copy(v_ref.at[me], p_ref.at[me], local.at[7]),
     ]
-    for copy in gathers + owns:
+    for copy in owns:
         copy.start()
+    loads[3].wait()
+    for j in range(count):
+        d_ref[j] = p_all[3, :, j * fh : (j + 1) * fh].astype(BF)
     forwards = []
     for k, b in enumerate(behind):
         remote(x_ref, y_ref.at[b], ss.at[k], rs.at[k], (dp, b)).wait_recv()
@@ -855,70 +893,84 @@
         forward.wait()
     for copy in sends + gathers:
         copy.wait_send()
-    for copy in owns:
+    for copy in owns + [own_x]:
         copy.wait()
 
 
-def start(g, w, v, x, number):
+def start(params, x, number):
     n_dp, n = lax.axis_size("dp"), lax.axis_size("ctx")
-    half = n // 2
+    half, count = n // 2, 2 * n_dp
+    (rows, columns), width = params.shape, x.shape[1]
+    fh, hc = columns // 4 // count, width // n
     dma = pltpu.SemaphoreType.DMA
-    g_out, w_out, v_out, x_all = pl.pallas_call(
+    g, w, v = (count, rows, 2 * fh), (n, rows, 3 * hc), (n, rows, hc)
+    g_out, w_out, v_out, x_all, d_out = pl.pallas_call(
         functools.partial(start_kernel, n_dp, n),
         out_shape=(
-            jax.ShapeDtypeStruct(g.shape, g.dtype),
-            jax.ShapeDtypeStruct(w.shape, w.dtype),
-            jax.ShapeDtypeStruct(v.shape, v.dtype),
+            jax.ShapeDtypeStruct(g, BF),
+            jax.ShapeDtypeStruct(w, BF),
+            jax.ShapeDtypeStruct(v, BF),
             jax.ShapeDtypeStruct((n,) + x.shape, x.dtype),
+            jax.ShapeDtypeStruct((count, rows, fh), BF),
         ),
-        in_specs=[ANY] * 4,
-        out_specs=(ANY,) * 4,
-        scratch_shapes=[dma((4,))]
-        + [dma((2 * n_dp - 1,))] * 2
+        in_specs=[ANY] * 2,
+        out_specs=(ANY,) * 4 + (VMEM,),
+        scratch_shapes=[
+            pltpu.VMEM((4, rows, columns // 4), F32),
+            pltpu.VMEM(g, BF),
+            pltpu.VMEM(w, BF),
+            pltpu.VMEM(v, BF),
+            dma((8,)),
+        ]
+        + [dma((count - 1,))] * 2
         + [dma((n - 1,))] * 4
         + [dma((half,))] * 2
         + [dma((half - 1,))] * 2,
         compiler_params=params_of(number),
         cost_estimate=cost(45),
         name="start",
-    )(g, w, v, x)
-    return g_out, w_out, v_out, x_all.reshape(-1, x.shape[-1])
+    )(params, x)
+    return g_out, w_out, v_out, x_all.reshape(-1, width), d_out
 
 
 def collect_kernel(
     n_dp, n, g_ref, h_ref, a_ref, w_ref, o_ref, h_out, y_ref,
-    own, co_ref, pa, qa, pb, qb, local, sw, rw, s1, r1, s2, r2, sh, rh,
+    acc, pa, qa, pb, qb, local, s1, r1, s2, r2, sh, rh, *line_refs,
 ):
     dp, me = lax.axis_index("dp"), lax.axis_index("ctx")
-    tall = own.shape[0]
+    tall = acc.shape[0]
     count, index, place = group_of(n_dp, n, dp, me)
     greet_all(n_dp, n, dp, me)
-    gives = slab_give(n_dp, dp, me, g_ref, co_ref, sw, rw)
-    swaps, receives = swap(h_ref, h_out, sh, rh, count, index, place)
-    mine = g_ref.at[pl.ds(pl.multiple_of(dp * tall, tall), tall), :]
-    stays = [
-        pltpu.make_async_copy(mine, own, local.at[0]),
-        pltpu.make_async_copy(h_ref.at[index], h_out.at[index], local.at[1]),
-    ]
-    for copy in stays:
-        copy.start()
+
+    def make(d, out):
+        def put(part):
+            rows = pl.ds(pl.multiple_of(d * tall + part.start, part.size), part.size)
+            out[part, :] = g_ref[rows, :].astype(F32)
+
+        tiles(tall, 64, put)
+
     cols = slice(0, a_ref.shape[1])
-    sums = reduce_ctx(n, dp, me, a_ref, w_ref, cols, y_ref, pa, qa, pb, qb, s1, r1, s2, r2)
-    for copy in stays:
-        copy.wait()
-    for copy in gives:
-        copy.wait_recv()
-
-    def add(part):
-        total = own[part, :].astype(F32)
-        for k in range(n_dp - 1):
-            total = total + co_ref[k, part, :].astype(F32)
-        o_ref[part, :] = total.astype(BF)
-
-    tiles(tall, 64, add)
+    stay = pltpu.make_async_copy(h_ref.at[index], h_out.at[index], local)
+    stay.start()
+    later = []
+
+    def between():
+        later.extend(swap(h_ref, h_out, sh, rh, count, index, place))
+        later.append(reduce_ctx(n, dp, me, a_ref, w_ref, cols, y_ref, pa, qa, pb, qb, s1, r1, s2, r2))
+
+    def last():
+        def put(part):
+            o_ref[part, :] = acc[part, :].astype(BF)
+
+        tiles(tall, 64, put)
+
+    val, *line = line_refs
+    line_sum(n_dp, dp, me, make, val, acc, *line, last, between)
+    swaps, receives, sums = later
     for copy in receives:
         copy.wait_recv()
-    for copy in gives + swaps + sums:
+    stay.wait()
+    for copy in swaps + sums:
         copy.wait_send()
 
 
@@ -934,25 +986,23 @@
             jax.ShapeDtypeStruct(h.shape, BF),
             jax.ShapeDtypeStruct((length, features), F32),
         ),
-        in_specs=[ANY, ANY, VMEM, VMEM],
+        in_specs=[VMEM, ANY, VMEM, VMEM],
         out_specs=(VMEM, ANY, VMEM),
         scratch_shapes=[
-            pltpu.VMEM((tall, width), BF),
-            pltpu.VMEM((n_dp - 1, tall, width), BF),
+            pltpu.VMEM((tall, width), F32),
             pltpu.VMEM((half, length, features), BF),
             pltpu.VMEM((half, length, features), BF),
             pltpu.VMEM((half - 1, length, features), BF),
             pltpu.VMEM((half - 1, length, features), BF),
-            dma((2,)),
-            dma((n_dp - 1,)),
-            dma((n_dp - 1,)),
+            dma,
             dma((half,)),
             dma((half,)),
             dma((half - 1,)),
             dma((half - 1,)),
             dma((2 * n_dp - 1,)),
             dma((2 * n_dp - 1,)),
-        ],
+        ]
+        + line_scratch(n_dp, tall, width),
         compiler_params=params_of(number),
         cost_estimate=cost(70),
         name="collect",
@@ -960,11 +1010,10 @@
 
 
 def total_kernel(
-    n_dp, n, qk_ref, wv_ref, wo_ref, u_ref, gg_ref, gd_ref, gain_ref, ga_ref, gu_ref, o_ref,
+    n_dp, n, qk_ref, wv_ref, wo_ref, u_ref, gg_ref, gd_ref, qk_gain, attn_gain, ff_gain, ga_ref, gu_ref, o_ref,
     sb, mine, buf, part, all_parts, local, sx, rx, sh, rh, ss, rs, st, rt,
 ):
     dp, me = lax.axis_index("dp"), lax.axis_index("ctx")
-    gain_rows = gain_ref.shape[0]
     hc = wv_ref.shape[2]
     count, index, place = group_of(n_dp, n, dp, me)
     greet_all(n_dp, n, dp, me)
@@ -991,8 +1040,11 @@
         copy.wait_recv()
     stay.wait()
     total += squares(gu_ref)
-    mine[0:gain_rows, :] = gain_ref[...]
-    mine[gain_rows:, :] = jnp.broadcast_to(total, (8, 128))
+    mine[...] = jnp.zeros_like(mine)
+    mine[0:2, pl.ds(pl.multiple_of(me * hc, hc), hc)] = qk_gain[...]
+    mine[2:3, :] = attn_gain[...]
+    mine[3:4, :] = ff_gain[...]
+    mine[4:5, :] = jnp.broadcast_to(total, (1, mine.shape[1]))
     copies = swaps + more
     for k in range(1, n):
         copy = remote(mine, buf.at[me], ss.at[k - 1], rs.at[k - 1], (dp, (me + k) % n))
@@ -1022,20 +1074,19 @@
         copy.wait_send()
 
 
-def total_over(qk, wv, wo, u, gg, gd, gain_part, number):
+def total_over(qk, wv, wo, u, gg, gd, qk_gain, attn_gain, ff_gain, number):
     n_dp, n = lax.axis_size("dp"), lax.axis_size("ctx")
     rows, hc = qk.shape[0] // n, wv.shape[1]
-    gain_rows = gain_part.size // 128
-    shape = (gain_rows + 8, 128)
+    shape = (8, attn_gain.shape[1])
     dma = pltpu.SemaphoreType.DMA
-    ga, gu, out = pl.pallas_call(
+    return pl.pallas_call(
         functools.partial(total_kernel, n_dp, n),
         out_shape=(
             jax.ShapeDtypeStruct((n, rows, 3 * hc), BF),
             jax.ShapeDtypeStruct(u.shape, BF),
             jax.ShapeDtypeStruct(shape, F32),
         ),
-        in_specs=[VMEM] * 3 + [ANY] + [VMEM] * 3,
+        in_specs=[VMEM] * 3 + [ANY] + [VMEM] * 5,
         out_specs=(VMEM,) * 3,
         scratch_shapes=[
             pltpu.VMEM((n, rows, 3 * hc), BF),
@@ -1063,13 +1114,29 @@
         u,
         gg,
         gd,
-        gain_part.reshape(gain_rows, 128),
+        qk_gain,
+        attn_gain,
+        ff_gain,
     )
-    return ga, gu, out[gain_rows, 0], out[:gain_rows].reshape(gain_part.shape)
-
-
-def adam_kernel(factor_ref, p_ref, m_ref, v_ref, ga_ref, go_ref, gg_ref, gu_ref, gd_ref, po_ref, mo_ref, vo_ref, g_ref):
+
+
+def adam_kernel(
+    sum_ref, gp_ref, gm_ref, gv_ref, p_ref, m_ref, v_ref, ga_ref, go_ref, gg_ref, gu_ref, gd_ref,
+    norm_ref, gp_out, gm_out, gv_out, po_ref, mo_ref, vo_ref, g_ref, factor_ref,
+):
     part = pl.program_id(0)
+
+    @pl.when((part == 0) & (pl.program_id(1) == 0))
+    def _():
+        gain = sum_ref[0:4, :]
+        squares = jnp.sum(jnp.sum(gain * gain, axis=0, keepdims=True), axis=1, keepdims=True)
+        norm = jnp.sqrt(sum_ref[4:5, 0:1] + squares)
+        norm_ref[...] = norm
+        factor = CLIP / (norm + 1e-06)
+        factor_ref[...] = jnp.broadcast_to(factor, factor_ref.shape)
+        new = adam_update(gp_ref[...], gm_ref[...], gv_ref[...], gain * factor, GAIN_RATE, 0.0)
+        gp_out[...], gm_out[...], gv_out[...] = new
+
     n, _, three = ga_ref.shape
     hc = three // 3
     fs = gd_ref.shape[2]
@@ -1089,7 +1156,7 @@
             for d in range(ref.shape[0]):
                 g_ref[:, d * fs : (d + 1) * fs] = ref[d].astype(F32)
 
-    clipped = g_ref[...] * factor_ref[0, 0]
+    clipped = g_ref[...] * factor_ref[0:1, 0:1]
     new_m = BETA1 * m_ref[...] + (1.0 - BETA1) * clipped
     new_v = BETA2 * v_ref[...] + (1.0 - BETA2) * (clipped * clipped)
     root = jnp.sqrt(new_v * (1.0 / (1.0 - BETA2**STEP))) + ADAM_EPS
@@ -1098,18 +1165,24 @@
     vo_ref[...] = new_v
 
 
-def adam(factor, params, first, second, ga, go, gg, gu, gd):
+def adam(sums, gains, gains_first, gains_second, params, first, second, ga, go, gg, gu, gd):
     rows, columns = params.shape
     n, n_dp, fs = ga.shape[0], gd.shape[0], gd.shape[2]
     block = min(rows, 16)
     steps = rows // block
     wide = pl.BlockSpec((block, columns // 4), lambda i, r: (r, i))
+    small = pl.BlockSpec(gains.shape, lambda i, r: (0, 0))
     return pl.pallas_call(
         adam_kernel,
         grid=(4, steps),
-        out_shape=(jax.ShapeDtypeStruct(params.shape, F32),) * 3,
+        out_shape=(jax.ShapeDtypeStruct((1, 1), F32),)
+        + (jax.ShapeDtypeStruct(gains.shape, F32),) * 3
+        + (jax.ShapeDtypeStruct(params.shape, F32),) * 3,
         in_specs=[
-            pl.BlockSpec(memory_space=pltpu.SMEM),
+            pl.BlockSpec(sums.shape, lambda i, r: (0, 0)),
+            small,
+            small,
+            small,
             wide,
             wide,
             wide,
@@ -1127,52 +1200,11 @@
                 for part in (1, 2, 3)
             ],
         ],
-        out_specs=(wide, wide, wide),
-        scratch_shapes=[pltpu.VMEM((block, columns // 4), F32)],
+        out_specs=(pl.BlockSpec((1, 1), lambda i, r: (0, 0)),) + (small,) * 3 + (wide,) * 3,
+        scratch_shapes=[pltpu.VMEM((block, columns // 4), F32), pltpu.VMEM((8, 128), F32)],
         compiler_params=pltpu.CompilerParams(vmem_limit_bytes=48 * 1024 * 1024),
         name="adam",
-    )(factor.reshape(1, 1), params, first, second, ga, go, gg, gu, gd)
-
-
-def arrange_kernel(n, count, p_ref, a_ref, o_ref, g_ref, d_ref):
-    part = pl.program_id(0)
-    hc = o_ref.shape[2]
-    fs = d_ref.shape[2]
-
-    @pl.when(part == 0)
-    def _():
-        for matrix in range(4):
-            for c in range(n):
-                start = (matrix * n + c) * hc
-                value = p_ref[:, start : start + hc].astype(BF)
-                if matrix < 3:
-                    a_ref[c, :, matrix * hc : (matrix + 1) * hc] = value
-                else:
-                    o_ref[c] = value
-
-    for index, ref, first in ((1, g_ref, 0), (2, g_ref, fs), (3, d_ref, 0)):
-
-        @pl.when(part == index)
-        def _():
-            for d in range(count):
-                ref[d, :, first : first + fs] = p_ref[:, d * fs : (d + 1) * fs].astype(BF)
-
-
-def arrange(params, width):
-    count, n = 2 * lax.axis_size("dp"), lax.axis_size("ctx")
-    rows, columns = params.shape
-    fs, hc = columns // 4 // count, width // n
-    whole = lambda shape: pl.BlockSpec(shape, lambda i: (0,) * len(shape))
-    shapes = [(n, rows, 3 * hc), (n, rows, hc), (count, rows, 2 * fs), (count, rows, fs)]
-    return pl.pallas_call(
-        functools.partial(arrange_kernel, n, count),
-        grid=(4,),
-        out_shape=tuple(jax.ShapeDtypeStruct(s, BF) for s in shapes),
-        in_specs=[pl.BlockSpec((rows, columns // 4), lambda i: (0, i))],
-        out_specs=tuple(whole(s) for s in shapes),
-        compiler_params=pltpu.CompilerParams(vmem_limit_bytes=48 * 1024 * 1024),
-        name="arrange",
-    )(params)
+    )(sums, gains, gains_first, gains_second, params, first, second, ga, go, gg, gu, gd)
 
 
 def row_sums(value, row):
@@ -1233,7 +1265,7 @@
         pltpu.make_async_copy(d_ref.at[mine], d_out.at[mine], local.at[1]),
     ]
     behind_wo = [
-        remote(wo_ref, part_of(dp), sw.at[k - 1], rw.at[k - 1], ((dp + k) % n_dp, me))
+        remote(wo_ref, part_of(dp), sw.at[k - 1], rw.at[k - 1], (across(dp, k, n_dp)[0], me))
         for k in range(1, n_dp)
     ]
     for copy in behind_wo + owns:
@@ -1264,9 +1296,9 @@
                     turn(value * gain_ref[which : which + 1, part], cos, sine) * factor
                 ).astype(BF)
 
-    @pl.loop(0, seq // block)
-    def _(i):
-        rows = pl.ds(pl.multiple_of(i * block, block), block)
+    def attention(pair, first):
+        size = 2 * (seq // n)
+        rows = pl.ds(pl.multiple_of(pair * size, size), size)
         visible = mask_of(rows, col_ref, row_ref)
         for head in range(hc // HD):
             part = slice(head * HD, (head + 1) * HD)
@@ -1276,13 +1308,16 @@
             total = jnp.sum(weights, axis=1, keepdims=True)
             o_ref[rows, part] = (dot(weights.astype(BF), v_ref[:, part]) / total).astype(BF)
             lse_ref[rows, head : head + 1] = top + jnp.log(total)
-
-    owns[0].wait()
-    for k in range(1, n_dp):
-        source = (dp + n_dp - k) % n_dp
-        remote(wo_ref, part_of(source), sw.at[k - 1], rw.at[k - 1], (source, me)).wait_recv()
+        if first:
+            owns[0].wait()
+            for k in range(1, n_dp):
+                _, source = across(dp, k, n_dp)
+                remote(wo_ref, part_of(source), sw.at[k - 1], rw.at[k - 1], (source, me)).wait_recv()
+
     cols = slice(0, hc)
-    sums = reduce_ctx(n, dp, me, o_ref, wo_all, cols, y_ref, pa, qa, pb, qb, s1, r1, s2, r2)
+    sums = reduce_ctx(
+        n, dp, me, o_ref, wo_all, cols, y_ref, pa, qa, pb, qb, s1, r1, s2, r2, before=attention
+    )
 
     def finish(rows):
         branch = y_ref[rows, :]
@@ -1347,7 +1382,7 @@
     tall = co_ref.shape[1]
     gives = []
     for k in range(1, n_dp):
-        to = (dp + k) % n_dp
+        to, _ = across(dp, k, n_dp)
         part = pl.ds(pl.multiple_of(to * tall, tall), tall)
         copy = remote(g_ref.at[part, :], co_ref.at[k - 1], sw.at[k - 1], rw.at[k - 1], (to, me))
         copy.start()
@@ -1372,16 +1407,19 @@
 
 def attend_back_kernel(
     n_dp, n, e_ref, do_ref, h_ref, o_hbm, col_ref, row_ref, q_ref, k_ref, v_ref, lse_ref,
-    dq_ref, dk_ref, dv_ref, h_out, wo_ref,
-    o_ref, go_ref, co_ref, sh, rh, local, sw, rw,
+    x_ref, gain_ref, cos_ref, sin_ref, pre_ref, scale_ref,
+    d_ref, gain_out, g_ref, wv_ref, wo_ref, h_out,
+    o_ref, dq_ref, dk_ref, dv_ref, mean_ref, buf, go_ref, co_ref, gv_ref, cv_ref,
+    sh, rh, local, sw, rw, sv, rv, ss, rs,
 ):
     dp, me = lax.axis_index("dp"), lax.axis_index("ctx")
     seq, hc = q_ref.shape
     load = pltpu.make_async_copy(o_hbm, o_ref, local.at[1])
     load.start()
+    width = x_ref.shape[1]
     block = min(seq, 256)
     count, index, place = group_of(n_dp, n, dp, me)
-    greet_wide_group(n_dp, dp, me)
+    greet_all(n_dp, n, dp, me)
     swaps, receives = swap(h_ref, h_out, sh, rh, count, index, place)
     stay = pltpu.make_async_copy(h_ref.at[index], h_out.at[index], local.at[0])
     stay.start()
@@ -1412,62 +1450,14 @@
             dv_ref[:, part] += t_dot(probs.astype(BF), back)
 
     pl.loop(0, seq // block)(attention)
-    slab_sum(dp, gives, go_ref, co_ref, wo_ref)
-    for copy in receives:
-        copy.wait_recv()
-    for copy in swaps + gives:
-        copy.wait_send()
-    stay.wait()
-
-
-def attend_back(e, do, h, o_all, info_col, info_row, q, k, v, lse, number):
-    n_dp, n = lax.axis_size("dp"), lax.axis_size("ctx")
-    (seq, hc), share = q.shape, e.shape[1]
-    dma = pltpu.SemaphoreType.DMA
-    return pl.pallas_call(
-        functools.partial(attend_back_kernel, n_dp, n),
-        out_shape=(
-            *[jax.ShapeDtypeStruct((seq, hc), F32)] * 3,
-            jax.ShapeDtypeStruct(h.shape, BF),
-            jax.ShapeDtypeStruct((share // n_dp, n * hc), BF),
-        ),
-        in_specs=[VMEM, VMEM, ANY, ANY] + [VMEM] * 6,
-        out_specs=(VMEM, VMEM, VMEM, ANY, VMEM),
-        scratch_shapes=[
-            pltpu.VMEM(o_all.shape, BF),
-            pltpu.VMEM((share, n * hc), BF),
-            pltpu.VMEM((n_dp - 1, share // n_dp, n * hc), BF),
-            dma((2 * n_dp - 1,)),
-            dma((2 * n_dp - 1,)),
-            dma((2,)),
-            dma((n_dp - 1,)),
-            dma((n_dp - 1,)),
-        ],
-        compiler_params=params_of(number),
-        cost_estimate=cost(45),
-        name="attend_back",
-    )(e, do, h, o_all, info_col, info_row, q, k, v, lse)
-
-
-def project_back_kernel(
-    n_dp, n, dq_in, dk_in, dv_ref, x_ref, gain_ref, cos_ref, sin_ref, pre_ref, scale_ref,
-    d_ref, gain_out, g_ref, wv_ref,
-    dq_ref, dk_ref, mean_ref, buf, go_ref, co_ref, ss, rs, sw, rw,
-):
-    dp, me = lax.axis_index("dp"), lax.axis_index("ctx")
-    seq, hc = dv_ref.shape
-    width = x_ref.shape[1]
-    block = min(seq, 256)
-    greet(
-        [(dp, (me + k) % n) for k in range(1, n)] + [((dp + k) % n_dp, me) for k in range(1, n_dp)]
-    )
+
     d_ref[:, 2 * hc :] = dv_ref[...].astype(BF)
 
     def values(part):
-        go_ref[part, :] = t_dot(x_ref[:, part], d_ref[:, 2 * hc :]).astype(BF)
+        gv_ref[part, :] = t_dot(x_ref[:, part], d_ref[:, 2 * hc :]).astype(BF)
 
     tiles(width, 256, values)
-    gives = slab_give(n_dp, dp, me, go_ref, co_ref, sw, rw)
+    gives_v = slab_give(n_dp, dp, me, gv_ref, cv_ref, sv, rv)
     gain_out[...] = jnp.zeros_like(gain_out)
 
     @pl.loop(0, seq // block)
@@ -1475,15 +1465,12 @@
         rows = pl.ds(pl.multiple_of(i * block, block), block)
         cos, sine = cos_ref[rows, :], sin_ref[rows, :]
         sums = jnp.zeros((8, block), F32)
-        for which, source, ref, factor in (
-            (0, dq_in, dq_ref, HD ** (-0.5)),
-            (1, dk_in, dk_ref, 1.0),
-        ):
+        for which, ref, factor in ((0, dq_ref, HD ** (-0.5)), (1, dk_ref, 1.0)):
             scale = scale_ref[rows, which : which + 1]
             for start in range(0, hc, HD):
                 part = slice(start, start + HD)
                 pre = pre_ref[rows, which * hc + start : which * hc + start + HD]
-                value = turn(source[rows, part] * factor, cos, -sine)
+                value = turn(ref[rows, part] * factor, cos, -sine)
                 gain_out[which : which + 1, part] += jnp.sum(value * pre * scale, axis=0, keepdims=True)
                 value = value * gain_ref[which : which + 1, part]
                 ref[rows, part] = value
@@ -1506,41 +1493,56 @@
         g_ref[part, :] = t_dot(x_ref[:, part], d_ref[:, : 2 * hc]).astype(BF)
 
     tiles(width, 256, product)
-    slab_sum(dp, gives, go_ref, co_ref, wv_ref)
-    for copy in gives:
+    slab_sum(dp, gives, go_ref, co_ref, wo_ref)
+    slab_sum(dp, gives_v, gv_ref, cv_ref, wv_ref)
+    for copy in receives:
+        copy.wait_recv()
+    for copy in swaps + gives + gives_v:
         copy.wait_send()
-
-
-def project_back(dq, dk, dv, x, gain, cos, sine, pre, scale, number):
+    stay.wait()
+
+
+def attend_back(e, do, h, o_all, info_col, info_row, q, k, v, lse, x, gain, cos, sine, pre, scale, number):
     n_dp, n = lax.axis_size("dp"), lax.axis_size("ctx")
-    (seq, hc), width = dq.shape, x.shape[1]
+    (seq, hc), share, width = q.shape, e.shape[1], x.shape[1]
     dma = pltpu.SemaphoreType.DMA
     return pl.pallas_call(
-        functools.partial(project_back_kernel, n_dp, n),
+        functools.partial(attend_back_kernel, n_dp, n),
         out_shape=(
             jax.ShapeDtypeStruct((seq, 3 * hc), BF),
             jax.ShapeDtypeStruct((2, hc), F32),
             jax.ShapeDtypeStruct((width, 2 * hc), BF),
             jax.ShapeDtypeStruct((width // n_dp, hc), BF),
+            jax.ShapeDtypeStruct((share // n_dp, n * hc), BF),
+            jax.ShapeDtypeStruct(h.shape, BF),
         ),
-        in_specs=[VMEM] * 9,
-        out_specs=(VMEM,) * 4,
+        in_specs=[VMEM, VMEM, ANY, ANY] + [VMEM] * 12,
+        out_specs=(VMEM,) * 5 + (ANY,),
         scratch_shapes=[
+            pltpu.VMEM(o_all.shape, BF),
+            pltpu.VMEM((seq, hc), F32),
             pltpu.VMEM((seq, hc), F32),
             pltpu.VMEM((seq, hc), F32),
             pltpu.VMEM((seq, 8), F32),
             pltpu.VMEM((n, 8, seq), F32),
+            pltpu.VMEM((share, n * hc), BF),
+            pltpu.VMEM((n_dp - 1, share // n_dp, n * hc), BF),
             pltpu.VMEM((width, hc), BF),
             pltpu.VMEM((n_dp - 1, width // n_dp, hc), BF),
+            dma((2 * n_dp - 1,)),
+            dma((2 * n_dp - 1,)),
+            dma((2,)),
+            dma((n_dp - 1,)),
+            dma((n_dp - 1,)),
+            dma((n_dp - 1,)),
+            dma((n_dp - 1,)),
             dma((n - 1,)),
             dma((n - 1,)),
-            dma((n_dp - 1,)),
-            dma((n_dp - 1,)),
         ],
         compiler_params=params_of(number),
-        cost_estimate=cost(30),
-        name="project_back",
-    )(dq, dk, dv, x, gain, cos, sine, pre, scale)
+        cost_estimate=cost(75),
+        name="attend_back",
+    )(e, do, h, o_all, info_col, info_row, q, k, v, lse, x, gain, cos, sine, pre, scale)
 
 
 def shards(
@@ -1585,8 +1587,7 @@
         )
         return g.reshape(group, rows, g.shape[1])
 
-    w_qkv, w_o, w_gu, w_d = arrange(params, width)
-    w_gu, w_qkv, w_o, x_all = start(w_gu, w_qkv, w_o, tokens, 1)
+    w_gu, w_qkv, w_o, x_all, w_d = start(params, tokens, 1)
     w_gu = gather_pairs(w_gu)
     w_qkv = gather_dp(w_qkv.reshape(n_ctx * rows, 3 * hc), 2)
 
@@ -1624,38 +1625,24 @@
     )
     g_grad, u_grad = scatter_pairs(g_grad), scatter_pairs(u_grad)
 
-    d_query, d_key, d_value, d_grad, wo_grad = attend_back(
-        d_branch, d_attn, d_grad, attn_all, info_col, info_row, queries, keys, values, lse, 8
-    )
-    d_qkv, d_gain, qk_grad, wv_grad = project_back(
-        d_query, d_key, d_value, x_all, my_gains, cos_tab, sine_tab, qk_pre, scales, 10
+    d_qkv, d_gain, qk_grad, wv_grad, wo_grad, d_grad = attend_back(
+        d_branch, d_attn, d_grad, attn_all, info_col, info_row, queries, keys, values, lse,
+        x_all, my_gains, cos_tab, sine_tab, qk_pre, scales, 8,
     )
     qk_grad, g_grad, d_x = collect(qk_grad, g_grad, d_qkv, w_qkv, 9)
     d_input = d_h1 + d_x
 
-    gain_part = jnp.concatenate(
-        [
-            lax.dynamic_update_slice(jnp.zeros((2, width), F32), d_gain, (0, me_ctx * hc)),
-            g_attn_part,
-            g_ff_part,
-        ],
-        axis=0,
+    attn_grad, u_grad, sums = total_over(
+        qk_grad, wv_grad, wo_grad, u_grad, g_grad, d_grad, d_gain, g_attn_part, g_ff_part, 11
     )
-    attn_grad, u_grad, square_total, gain_total = total_over(
-        qk_grad, wv_grad, wo_grad, u_grad, g_grad, d_grad, gain_part, 11
-    )
-    grad_norm = jnp.sqrt(square_total + jnp.sum(gain_total * gain_total))
-    factor = CLIP / (grad_norm + 1e-06)
-    new_params, new_first, new_second = adam(
-        factor, params, first_moment, second_moment, attn_grad, wo_grad, g_grad, u_grad, d_grad
-    )
-    new_gains, new_gains_first, new_gains_second = adam_update(
-        gains, gains_first, gains_second, gain_total * factor, GAIN_RATE, 0.0
+    grad_norm, new_gains, new_gains_first, new_gains_second, new_params, new_first, new_second = adam(
+        sums, gains, gains_first, gains_second, params, first_moment, second_moment,
+        attn_grad, wo_grad, g_grad, u_grad, d_grad,
     )
     return (
         result[None],
         d_input.astype(BF)[None],
-        grad_norm,
+        grad_norm.reshape(()),
         new_params,
         new_first,
         new_second,

time: 692 us -> 653 us (0.944); the launches traced: 691 us -> 643 us
  Pallas kernels: 639 us -> 606 us
  local copies, waits for them, and re-layouts: 26.9 us -> 16.9 us
    pallas_call x2 -> x0, Pallas kernels: 38.6 us -> none  [the longest x1 34.4 us: project_back(): pl.pallas_call(functools.partial(project_back_kernel, n_dp, n), out_shape...]
    pallas_call x1, Pallas kernels: 57.3 us -> 74 us  [attend_back(): pl.pallas_call(functools.partial(attend_back_kernel, n_dp, n), out_shape=...]
    pallas_call x1, Pallas kernels: 117 us -> 108 us  [ff_forward(): pl.pallas_call(functools.partial(ff_forward_kernel, n_dp, n), out_shape=(...]
    unnamed x65 -> x55, local copies, waits for them, and re-layouts: 24.6 us -> 16 us
  transfers between devices with their start and end apart: 5 -> 5, of which waited for: 0 -> 0; matrix products, arithmetic and copies ran while one was open for 0% -> 1% of each run, Pallas kernels for 59% -> 60%
where the time goes in v8:
time: 653 us; the launch traced here: 643 us
  Pallas kernels  606 us (93%)
  local copies, waits for them, and re-layouts  16.9 us (3%)
  between operations  14.3 us (2%)
    pallas_call x1, Pallas kernels, ff_forward(): pl.pallas_call(functools.partial(ff_forward_kernel, n_dp, n), out_shape=(...  108 us
    pallas_call x1, Pallas kernels, attend_back(): pl.pallas_call(functools.partial(attend_back_kernel, n_dp, n), out_shape=...  74 us
    pallas_call x1, Pallas kernels, ff_scatter(): pl.pallas_call(functools.partial(ff_scatter_kernel, n_dp, n), out_shape=(...  73.4 us
    pallas_call x1, Pallas kernels, gather_dp(): pl.pallas_call(functools.partial(gather_dp_kernel, n), out_shape=jax.Shap...  65.3 us
    pallas_call x1, Pallas kernels, collect(): pl.pallas_call(functools.partial(collect_kernel, n_dp, n), out_shape=(jax...  65.1 us
    pallas_call x1, Pallas kernels, attend(): pl.pallas_call(functools.partial(attend_kernel, n_dp, n), out_shape=(jax....  58.3 us
    pallas_call x1, Pallas kernels, ff_back(): pl.pallas_call(functools.partial(ff_back_kernel, n_dp), out_shape=(jax.Sh...  51.3 us
    pallas_call x1, Pallas kernels, total_over(): pl.pallas_call(functools.partial(total_kernel, n_dp, n), out_shape=(jax.S...  43.4 us
  transfers between devices with their start and end apart: 5, of which 0 were waited for; matrix products, arithmetic and copies ran while one was open for 1% of the time, Pallas kernels for 60%

profile of v8, /device:TPU:0, one launch (start us, length us, event | category | flops | bytes accessed | tf_op | source)
XLA Modules:
  0.0 642.7 jit_solution(11987969534884475)
XLA Ops:
  7.2 0.0 all-gather.4.cloned.1.call-start
  7.2 0.0 copy-start.2
  7.2 1.0 copy-done.2
  8.3 42.8 %start.1 = (bf16[8,64,2048]{2,1,0:T(8,128)(2,1)}, bf16[8,64,768]{2,1,0:T(8,128)(2,1)S(1)}, bf16[8,64,256]{2,1,0:T(8,128)(2,1)S(1)}, bf16[8,128,2048]{2,1,0:T(8,128)(2,1)}, bf16[8,64,1024]{2,1,0:T(8,128)(2,1)S(1)}) custom-call(f32[64,32768]{1,0:T(8,128)} %p_ref.1, bf16[128,2048]{1,0:T(8,128)(2,1)S(1)} %bitcast.28), custom_call_target="tpu_custom_call" | custom-call | bytes 162000000 | tf_op jit(solution)/shard_map/start/pallas_call | solution.py:907
  51.1 0.0 copy-start.5
  51.1 1.0 copy-done.5
  52.0 0.0 all-gather.4.cloned.1.call-update
  52.1 0.0 all-gather.6.cloned.1.call-start
  52.1 0.1 pad.2.clone
  52.2 0.1 select_reduce_fusion
  52.3 0.0 copy-done.25
  52.3 0.1 add_add_fusion
  52.4 0.2 copy.21.col_ref
  52.6 0.0 copy-start.18
  52.6 0.0 copy-start.3
  52.6 65.3 %gather_dp.1 = bf16[4,512,768]{2,1,0:T(8,128)(2,1)S(1)} custom-call(bf16[512,768]{1,0:T(8,128)(2,1)S(1)} %bitcast.33), custom_call_target="tpu_custom_call" | custom-call | bytes 216000000 | tf_op jit(solution)/shard_map/gather_dp/pallas_call | solution.py:152
  117.9 0.0 copy-start
  117.9 1.7 copy-done
  119.6 0.0 slice-done
  119.6 1.9 fusion.1
  121.5 0.3 pad_maximum_fusion
  121.9 0.6 fusion.13
  122.5 58.3 %attend.1 = (f32[128,2048]{1,0:T(8,128)}, f32[128,2048]{1,0:T(8,128)}, bf16[1024,256]{1,0:T(8,128)(2,1)S(1)}, bf16[1024,256]{1,0:T(8,128)(2,1)S(1)}, bf16[1024,2...) custom-call(bf16[1024,2048]{1,0:T(8,128)(2,1)} %bitcast.39, ...), custom_call_target="tpu_custom_call" | custom-call | bytes 216000000 | tf_op jit(solution)/shard_map/attend/pallas_call | solution.py:1340
  180.8 0.0 copy-start.8
  180.8 0.8 copy-done.8
  181.6 0.8 copy-done.10
  182.4 0.8 copy-done.12
  183.2 107.6 %ff_forward.1 = (bf16[128,2048]{1,0:T(8,128)(2,1)}, bf16[128,2048]{1,0:T(8,128)(2,1)}, f32[1,2048]{1,0:T(1,128)}, bf16[1024,2048]{1,0:T(8,128)(2,1)}, f32[1024,2...) custom-call(f32[128,2048]{1,0:T(8,128)} %get-tuple-element.66.h_ref, ...), custom_call_target="tpu_custom_call" | custom-call | bytes 324000000 | tf_op jit(solution)/shard_map/ff_forward/pallas_call | solution.py:559
  290.8 0.0 all-gather.6.cloned.1.call-update
  290.8 0.0 reduce-scatter.4.cloned.1.call-start
  290.8 51.3 %ff_back.1 = (bf16[1024,2048]{1,0:T(8,128)(2,1)}, bf16[4,4,128,1024]{3,2,1,0:T(8,128)(2,1)}) custom-call(bf16[128,2048]{1,0:T(8,128)(2,1)} %get-tuple-element.73.dm_ref, bf16[1024,1024]{1,0:T(8,128)(2,1)} %get-tuple-element.74.hid_ref, bf16[2048,1024]{1,0:T(8,128)(2,1)} %get-tuple-element.75.d_hbm, f32[1024,2048]{1,0:T(8,128)} %get-tuple-element.76.pre_hbm), custom_call_target="tpu_custom_call" | custom-call | bytes 162000000 | tf_op jit(solution)/shard_map/ff_back/pallas_call | solution.py:659
  342.2 0.0 reduce-scatter.4.cloned.1.call-update
  342.2 0.0 reduce-scatter.6.cloned.1.call-start
  342.2 73.4 %ff_scatter.1 = (f32[128,2048]{1,0:T(8,128)}, bf16[1024,256]{1,0:T(8,128)(2,1)}, bf16[1024,256]{1,0:T(8,128)(2,1)}, f32[1,2048]{1,0:T(1,128)}, bf16[4,4,128,1024...) custom-call(bf16[1024,2048]{1,0:T(8,128)(2,1)} %get-tuple-element.77.dgu_ref, bf16[4,4,128,2048]{3,2,1,0:T(8,128)(2,1)} %bitcast.38, ...), custom_call_target="tpu_custom_call" | custom-call | bytes 180000000 | tf_op jit(solution)/shard_map/ff_scatter/pallas_call | solution.py:792
  415.6 0.0 copy-start.9
  415.6 0.0 reduce-scatter.6.cloned.1.call-update
  415.7 0.2 reduce-scatter.8.cloned.1.call-start
  415.9 0.4 reduce-scatter.8.cloned.1.call-update
  416.3 0.0 all-gather.6.cloned.1.call-done
  416.3 0.0 reduce-scatter.4.cloned.1.call-done
  416.3 0.4 copy-done.9
  416.7 1.0 copy-done.11
  417.7 1.0 copy-done.13
  418.8 1.0 copy-done.14
  419.8 1.0 copy-done.15
  420.8 74.0 %attend_back.1 = (bf16[1024,768]{1,0:T(8,128)(2,1)}, f32[2,256]{1,0:T(2,128)S(1)}, bf16[2048,512]{1,0:T(8,128)(2,1)}, bf16[512,256]{1,0:T(8,128)(2,1)S(1)}, bf16...) custom-call(bf16[1024,256]{1,0:T(8,128)(2,1)S(1)} %copy-done.14, bf16[1024,256]{1,0:T(8,128)(2,1)S(1)} %copy-done.15, ...), custom_call_target="tpu_custom_call" | custom-call | bytes 270000000 | tf_op jit(solution)/shard_map/attend_back/pallas_call | solution.py:1509
  494.9 0.0 copy-start.16
  494.9 0.7 copy-done.16
  495.6 1.4 copy-done.4
  497.0 1.3 copy-done.6
  498.3 65.1 %collect.1 = (bf16[512,512]{1,0:T(8,128)(2,1)S(1)}, bf16[8,64,1024]{2,1,0:T(8,128)(2,1)S(1)}, f32[128,2048]{1,0:T(8,128)S(1)}) custom-call(bf16[2048,512]{1,0:T(8,128)(2,1)} %get-tuple-element.92.g_ref, bf16[8,64,1024]{2,1,0:T(8,128)(2,1)S(1)} %bitcast.31, bf16[1024,768]{1,0:T(8,128)(2,1)S(1)} %copy-done.4, bf16[2048,768]{1,0:T(8,128)(2,1)} %bitcast.27), custom_call_target="tpu_custom_call" | custom-call | bytes 252000000 | tf_op jit(solution)/shard_map/collect/pallas_call | solution.py:982
  563.4 0.0 copy-start.20
  563.4 0.0 copy-start.21
  563.4 2.1 fusion
  565.5 0.0 copy-done.23
  565.5 0.0 copy-start.7
  565.6 1.2 copy-done.7
  566.8 43.4 %total.1 = (bf16[8,64,768]{2,1,0:T(8,128)(2,1)S(1)}, bf16[8,64,1024]{2,1,0:T(8,128)(2,1)S(1)}, f32[8,2048]{1,0:T(8,128)S(1)}) custom-call(bf16[8,64,512]{2,1,0:T(8,128)(2,1)S(1)} %bitcast.34, bf16[8,64,256]{2,1,0:T(8,128)(2,1)S(1)} %bitcast.36, bf16[1,64,2048]{2,1,0:T(8,128)(2,1)S(1)} %bitcast.30, bf16[8,64,1024]{2,1,0:T(8,128)(2,1)S(1)} %bitcast.32, ...), custom_call_target="tpu_custom_call" | custom-call | bytes 126000000 | tf_op jit(solution)/shard_map/total/pallas_call | solution.py:1082
  610.2 0.0 copy-done.20
  610.2 0.0 copy-done.21
  610.2 0.0 copy-start.24
  610.2 25.0 %adam.1 = (f32[1,1]{1,0:T(1,128)}, f32[4,2048]{1,0:T(4,128)}, f32[4,2048]{1,0:T(4,128)}, f32[4,2048]{1,0:T(4,128)}, f32[64,32768]{1,0:T(8,128)}, /*index=5*/f32[64,32768]{1,0:T(8,128)}, f32[64,32768]{1,0:T(8,128)}) custom-call(f32[8,2048]{1,0:T(8,128)S(1)} %get-tuple-element.105.sum_ref, f32[4,2048]{1,0:T(4,128)S(1)} %copy-done.18, ...), custom_call_target="tpu_custom_call" | custom-call | tf_op jit(solution)/shard_map/adam/pallas_call | solution.py:1175
  635.2 0.0 copy-done.24
  635.2 0.8 copy.24
  (32 shorter events, 0.1 us)
Async XLA Ops:
  7.2 176.0 %all-gather.4.cloned.1.call-start = ((), (), s32[]{:S(2)}) async-start(), calls=%async_computation.3 | async-start | bytes 10485760 | tf_op jit(solution)/shard_map/all_gather | solution.py:1575
  7.2 1.0 copy-start.2
  8.3 43.9 %copy-start.26 = (s32[8]{0:T(128)S(1)}, s32[8]{0:T(128)}, u32[]{:S(2)}) copy-start(s32[8]{0:T(128)} %param.13) | copy-start | bytes 100
  8.3 44.1 %copy-start.25 = (s32[1,1024]{1,0:T(1,128)S(1)}, s32[1,1024]{1,0:T(1,128)}, u32[]{:S(2)}) copy-start(s32[1,1024]{1,0:T(1,128)} %param.12) | copy-start | bytes 12292
  51.1 1.0 copy-start.5
  52.0 67.6 %slice-start = ((f32[4,2048]{1,0:T(4,128)}), f32[2,2048]{1,0:T(2,128)S(1)}, s32[]{:S(2)}) async-start(f32[4,2048]{1,0:T(4,128)} %gp_ref.1), calls=%async_computation.8 | async-start | bytes 32768 | tf_op jit(solution)/shard_map/slice | solution.py:1609
  52.1 364.2 %all-gather.6.cloned.1.call-start = ((), (), s32[]{:S(2)}) async-start(), calls=%async_computation.7 | async-start | bytes 4718592 | tf_op jit(solution)/shard_map/all_gather | solution.py:1620
  52.6 69.3 %copy-start.18 = (f32[4,2048]{1,0:T(4,128)S(1)}, f32[4,2048]{1,0:T(4,128)}, u32[]{:S(2)}) copy-start(f32[4,2048]{1,0:T(4,128)} %gp_ref.1) | copy-start | bytes 98308
  52.6 69.9 %copy-start.3 = (bf16[1,128,2048]{2,1,0:T(8,128)(2,1)S(1)}, bf16[1,128,2048]{2,1,0:T(8,128)(2,1)}, u32[]{:S(2)}) copy-start(bf16[1,128,2048]{2,1,0:T(8,128)(2,1)} %param.10) | copy-start | bytes 1572868
  117.9 1.7 copy-start
  122.5 58.3 %copy-start.19 = (f32[1,2048]{1,0:T(1,128)}, f32[1,2048]{1,0:T(1,128)S(1)}, u32[]{:S(2)}) copy-start(f32[1,2048]{1,0:T(1,128)S(1)} %get-tuple-element.116.norm_ref.gain_ref) | copy-start | bytes 24580
  180.8 0.8 copy-start.8
  181.6 0.8 copy-start.10
  182.4 0.8 copy-start.12
  290.8 125.5 %reduce-scatter.4.cloned.1.call-start = ((), (), s32[]{:S(2)}) async-start(), calls=%async_computation.4 | async-start | bytes 5242880 | tf_op jit(solution)/shard_map/reduce_scatter | solution.py:1581
  342.2 153.4 %reduce-scatter.6.cloned.1.call-start = ((), (), s32[]{:S(2)}) async-start(), calls=%async_computation.5 | async-start | bytes 5242880 | tf_op jit(solution)/shard_map/reduce_scatter | solution.py:1581
  415.6 1.0 copy-start.9
  415.7 149.9 %reduce-scatter.8.cloned.1.call-start = ((), (), s32[]{:S(2)}) async-start(), calls=%async_computation.6 | async-start | bytes 5242880 | tf_op jit(solution)/shard_map/reduce_scatter | solution.py:1581
  416.7 1.0 copy-start.11
  417.7 1.0 copy-start.13
  418.8 1.0 copy-start.14
  419.8 1.0 copy-start.15
  494.9 0.7 copy-start.16
  495.6 1.4 copy-start.4
  497.0 1.3 copy-start.6
  498.3 67.3 %copy-start.1 = (bf16[8,64,1024]{2,1,0:T(8,128)(2,1)S(1)}, bf16[8,64,1024]{2,1,0:T(8,128)(2,1)}, u32[]{:S(2)}) copy-start(bf16[8,64,1024]{2,1,0:T(8,128)(2,1)} %get-tuple-element.101.gd_ref) | copy-start | bytes 3145732
  498.3 67.3 %copy-start.17 = (bf16[512,256]{1,0:T(8,128)(2,1)S(1)}, bf16[512,256]{1,0:T(8,128)(2,1)}, u32[]{:S(2)}) copy-start(bf16[512,256]{1,0:T(8,128)(2,1)} %copy-done.16) | copy-start | bytes 786436
  498.3 67.3 %copy-start.22 = (f32[1,2048]{1,0:T(1,128)S(1)}, f32[1,2048]{1,0:T(1,128)}, u32[]{:S(2)}) copy-start(f32[1,2048]{1,0:T(1,128)} %get-tuple-element.104.ff_gain) | copy-start | bytes 24580
  498.3 67.3 %copy-start.23 = (f32[1,2048]{1,0:T(1,128)S(1)}, f32[1,2048]{1,0:T(1,128)}, u32[]{:S(2)}) copy-start(f32[1,2048]{1,0:T(1,128)} %get-tuple-element.103.attn_gain) | copy-start | bytes 24580
  563.4 46.9 %copy-start.20 = (f32[4,2048]{1,0:T(4,128)S(1)}, f32[4,2048]{1,0:T(4,128)}, u32[]{:S(2)}) copy-start(f32[4,2048]{1,0:T(4,128)} %gm_ref.1) | copy-start | bytes 98308
  563.4 46.9 %copy-start.21 = (f32[4,2048]{1,0:T(4,128)S(1)}, f32[4,2048]{1,0:T(4,128)}, u32[]{:S(2)}) copy-start(f32[4,2048]{1,0:T(4,128)} %gv_ref.1) | copy-start | bytes 98308
  565.5 1.2 copy-start.7
  610.2 25.0 %copy-start.24 = (bf16[128,2048]{1,0:T(8,128)(2,1)S(1)}, bf16[128,2048]{1,0:T(8,128)(2,1)}, u32[]{:S(2)}) copy-start(bf16[128,2048]{1,0:T(8,128)(2,1)} %get-tuple-element.70) | copy-start | bytes 1572868
Sparse Core Ops, SparseCore 0:
  52.2 98.8 all-gather.3
  290.9 36.6 all-gather.5
  342.3 53.5 reduce-scatter.3
  415.8 54.8 reduce-scatter.5
  473.5 70.3 reduce-scatter.7

commit v9 on v8

--- a/solution.py
+++ b/solution.py
@@ -23,6 +23,7 @@
 MESH = pl.DeviceIdType.MESH
 ANY = pl.BlockSpec(memory_space=pl.ANY)
 VMEM = pl.BlockSpec(memory_space=pltpu.VMEM)
+HBM = pl.BlockSpec(memory_space=pltpu.HBM)
 
 
 def rms_scale(values):
@@ -680,8 +681,8 @@
 
 
 def ff_scatter_kernel(
-    n_dp, n, dgu_ref, gu_hbm, all_hbm, wo_hbm, up_ref, branch_ref, gain_ref, dh_ref, dc_ref, do_ref, gp_ref, gg_out, gv_out,
-    gg_ref, gv_ref, gu_ref, all_ref, wo_ref, give_ref, db_ref, mix_ref, acc, sem_gu, sem_all, sem_out, ss, rs, sc, rc, *rest,
+    n_dp, n, dgu_ref, gu_hbm, all_hbm, dh_ref, gg_out, gv_out,
+    gg_ref, gv_ref, gu_ref, all_ref, acc, sem_gu, sem_all, sem_out, *rest,
 ):
     dp, me = lax.axis_index("dp"), lax.axis_index("ctx")
     length, width = dh_ref.shape
@@ -691,24 +692,11 @@
     loads = load_rows(gu_hbm, gu_ref, sem_gu)
     load = pltpu.make_async_copy(all_hbm, all_ref, sem_all)
     load.start()
-    load_wo = pltpu.make_async_copy(wo_hbm, wo_ref, sem_out.at[2])
-    load_wo.start()
-    greet(
-        [(dp, (me + k) % n) for k in range(1, n)] + [((dp + k) % n_dp, me) for k in range(1, n_dp)]
-    )
+    greet_group(n_dp, dp, me)
     for copy in loads:
         copy.wait()
 
     make, done = part_of_pair(dp, me, dgu_ref, gu_ref, length, *pair_refs)
-    gp_ref[...] = jnp.zeros_like(gp_ref)
-
-    def finish(rows):
-        grad, branch = dh_ref[rows, :] + up_ref[rows, :].astype(F32), branch_ref[rows, :]
-        scale = rms_scale(branch)
-        dh_ref[rows, :] = grad
-        gp_ref[...] += jnp.sum(grad * branch * scale, axis=0, keepdims=True)
-        db_ref[rows, :] = norm_back(grad * gain_ref[...], branch, scale).astype(BF)
-
     load.wait()
     tall = acc.shape[0]
 
@@ -723,7 +711,7 @@
                 gv_ref[r % half, r // half] = acc[part, fh:].astype(BF)
 
     val, *line = line_refs
-    line_sum(n_dp, dp, me, make, val, dh_ref, *line, lambda: tiles(length, 16, finish), grads)
+    line_sum(n_dp, dp, me, make, val, dh_ref, *line, lambda: None, grads)
     done(n_dp)
     outs = [
         pltpu.make_async_copy(ref, out, sem_out.at[i])
@@ -731,100 +719,39 @@
     ]
     for copy in outs:
         copy.start()
-    load_wo.wait()
-
-    def mine(c):
-        return pl.ds(pl.multiple_of(c * length, length), length)
-
-    def send(k):
-        to = (me + k) % n
-        return remote(give_ref.at[to], do_ref.at[mine(me), :], ss.at[k - 1], rs.at[k - 1], (dp, to))
-
-    def receive(k):
-        source = (me + n - k) % n
-        return remote(give_ref.at[me], do_ref.at[mine(source), :], ss.at[k - 1], rs.at[k - 1], (dp, source))
-
-    own = rows // 2
-    share = n_dp * own
-    for c in range(n):
-        for d in range(n_dp):
-            start, source = c * share + d * own, (d * n + c) * own
-            mix_ref[:, start : start + own] = db_ref[:, source : source + own]
-
-    def share_of(c):
-        return mix_ref.at[:, pl.ds(pl.multiple_of(c * share, share), share)]
-
-    def send_share(k):
-        to = (me + k) % n
-        return remote(share_of(to), dc_ref.at[mine(me), :], sc.at[k - 1], rc.at[k - 1], (dp, to))
-
-    def receive_share(k):
-        source = (me + n - k) % n
-        return remote(share_of(me), dc_ref.at[mine(source), :], sc.at[k - 1], rc.at[k - 1], (dp, source))
-
-    stay = pltpu.make_async_copy(share_of(me), dc_ref.at[mine(me), :], sem_out.at[3])
-    stay.start()
-
-    @pl.loop(1, n)
-    def _(k):
-        to = (me + k) % n
-        send_share(k).start()
-        give_ref[to] = dot(db_ref[...], wo_ref[to]).astype(BF)
-        send(k).start()
-
-    do_ref[mine(me), :] = dot(db_ref[...], wo_ref[me]).astype(BF)
-    for k in range(1, n):
-        receive(k).wait_recv()
-        receive_share(k).wait_recv()
-    for k in range(1, n):
-        send(k).wait_send()
-        send_share(k).wait_send()
-    stay.wait()
     for copy in outs:
         copy.wait()
 
 
-def ff_scatter(dgu, w_gu, h1_all, wo_all, up, branch, gain, number):
+def ff_scatter(dgu, w_gu, h1_all, length, number):
     n_dp, n = lax.axis_size("dp"), lax.axis_size("ctx")
-    length, width = up.shape
-    hc = wo_all.shape[2]
+    width = h1_all.shape[1]
     grad = jax.ShapeDtypeStruct(w_gu.shape[:3] + (w_gu.shape[3] // 2,), BF)
     return pl.pallas_call(
         functools.partial(ff_scatter_kernel, n_dp, n),
         out_shape=(
             jax.ShapeDtypeStruct((length, width), F32),
-            jax.ShapeDtypeStruct((n * length, width // n), BF),
-            jax.ShapeDtypeStruct((n * length, hc), BF),
-            jax.ShapeDtypeStruct((1, width), F32),
             grad,
             grad,
         ),
-        in_specs=[VMEM, ANY, ANY, ANY] + [VMEM] * 3,
-        out_specs=(VMEM,) * 4 + (ANY,) * 2,
+        in_specs=[VMEM, ANY, ANY],
+        out_specs=(VMEM,) + (ANY,) * 2,
         scratch_shapes=[
             pltpu.VMEM(grad.shape, BF),
             pltpu.VMEM(grad.shape, BF),
             pltpu.VMEM((width, w_gu.shape[3]), BF),
             pltpu.VMEM(h1_all.shape, BF),
-            pltpu.VMEM(wo_all.shape, BF),
-            pltpu.VMEM((n, length, hc), BF),
-            pltpu.VMEM((length, width), BF),
-            pltpu.VMEM((length, width), BF),
             pltpu.VMEM((256, w_gu.shape[3]), F32),
             pltpu.SemaphoreType.DMA((w_gu.shape[0] * n_dp,)),
             pltpu.SemaphoreType.DMA,
-            pltpu.SemaphoreType.DMA((4,)),
-            pltpu.SemaphoreType.DMA((n - 1,)),
-            pltpu.SemaphoreType.DMA((n - 1,)),
-            pltpu.SemaphoreType.DMA((n - 1,)),
-            pltpu.SemaphoreType.DMA((n - 1,)),
+            pltpu.SemaphoreType.DMA((2,)),
         ]
         + pair_scratch(n_dp, length, width)
         + line_scratch(n_dp, length, width),
         compiler_params=params_of(number, 60),
         cost_estimate=cost(50),
         name="ff_scatter",
-    )(dgu, w_gu, h1_all, wo_all, up, branch, gain)
+    )(dgu, w_gu, h1_all)
 
 
 def start_kernel(
@@ -934,8 +861,8 @@
 
 
 def collect_kernel(
-    n_dp, n, g_ref, h_ref, a_ref, w_ref, o_ref, h_out, y_ref,
-    acc, pa, qa, pb, qb, local, s1, r1, s2, r2, sh, rh, *line_refs,
+    n_dp, n, g_ref, h_ref, a_ref, w_ref, b_ref, o_ref, h_out, y_ref,
+    sum_ref, acc, pa, qa, pb, qb, local, s1, r1, s2, r2, sh, rh, *line_refs,
 ):
     dp, me = lax.axis_index("dp"), lax.axis_index("ctx")
     tall = acc.shape[0]
@@ -956,7 +883,7 @@
 
     def between():
         later.extend(swap(h_ref, h_out, sh, rh, count, index, place))
-        later.append(reduce_ctx(n, dp, me, a_ref, w_ref, cols, y_ref, pa, qa, pb, qb, s1, r1, s2, r2))
+        later.append(reduce_ctx(n, dp, me, a_ref, w_ref, cols, sum_ref, pa, qa, pb, qb, s1, r1, s2, r2))
 
     def last():
         def put(part):
@@ -964,9 +891,13 @@
 
         tiles(tall, 64, put)
 
+    def join(part):
+        y_ref[part, :] = (sum_ref[part, :] + b_ref[part, :]).astype(BF)
+
     val, *line = line_refs
     line_sum(n_dp, dp, me, make, val, acc, *line, last, between)
     swaps, receives, sums = later
+    tiles(y_ref.shape[0], 32, join)
     for copy in receives:
         copy.wait_recv()
     stay.wait()
@@ -974,7 +905,7 @@
         copy.wait_send()
 
 
-def collect(g, h, a, w, number):
+def collect(g, h, a, w, b, number):
     n_dp, n = lax.axis_size("dp"), lax.axis_size("ctx")
     tall, width = g.shape[0] // n_dp, g.shape[1]
     half, length, features = n // 2, a.shape[0] // n, w.shape[0]
@@ -984,11 +915,12 @@
         out_shape=(
             jax.ShapeDtypeStruct((tall, width), BF),
             jax.ShapeDtypeStruct(h.shape, BF),
-            jax.ShapeDtypeStruct((length, features), F32),
+            jax.ShapeDtypeStruct((length, features), BF),
         ),
-        in_specs=[VMEM, ANY, VMEM, VMEM],
+        in_specs=[VMEM, ANY, VMEM, VMEM, VMEM],
         out_specs=(VMEM, ANY, VMEM),
         scratch_shapes=[
+            pltpu.VMEM((length, features), F32),
             pltpu.VMEM((tall, width), F32),
             pltpu.VMEM((half, length, features), BF),
             pltpu.VMEM((half, length, features), BF),
@@ -1006,12 +938,14 @@
         compiler_params=params_of(number),
         cost_estimate=cost(70),
         name="collect",
-    )(g, h, a, w)
+    )(g, h, a, w, b)
 
 
 def total_kernel(
-    n_dp, n, qk_ref, wv_ref, wo_ref, u_ref, gg_ref, gd_ref, qk_gain, attn_gain, ff_gain, ga_ref, gu_ref, o_ref,
-    sb, mine, buf, part, all_parts, local, sx, rx, sh, rh, ss, rs, st, rt,
+    n_dp, n, qk_ref, wv_ref, wo_ref, u_ref, gg_ref, gd_ref, qk_gain, attn_gain, ff_gain, p_hbm, m_hbm, v_hbm,
+    ga_ref, gu_ref, o_ref, p_out, m_out, v_out,
+    sb, mine, buf, part, all_parts, square, buf_s, part_s, all_s, local, sx, rx, sh, rh,
+    ss, rs, st, rt, s1, r1, s2, r2, sem_copy,
 ):
     dp, me = lax.axis_index("dp"), lax.axis_index("ctx")
     hc = wv_ref.shape[2]
@@ -1020,6 +954,12 @@
     swaps, receives = swap(u_ref, gu_ref, sh, rh, count, index, place)
     stay = pltpu.make_async_copy(u_ref.at[index], gu_ref.at[index], local)
     stay.start()
+    moves = [
+        pltpu.make_async_copy(source, target, sem_copy.at[i])
+        for i, (source, target) in enumerate(((p_hbm, p_out), (m_hbm, m_out), (v_hbm, v_out)))
+    ]
+    for copy in moves:
+        copy.start()
     sb[:, :, : 2 * hc] = qk_ref[...]
     sb[:, :, 2 * hc : 3 * hc] = wv_ref[...]
     more, waits = swap(sb, ga_ref, sx, rx, n, me, lambda c: (dp, c))
@@ -1032,6 +972,40 @@
             acc += block * block
         return jnp.sum(jnp.sum(acc, axis=0, keepdims=True), axis=1, keepdims=True)
 
+    copies = swaps + more
+
+    def sum_all(value, rows, along, columns, send, recv, send_dp, recv_dp):
+        for k in range(1, n):
+            copy = remote(value, rows.at[me], send.at[k - 1], recv.at[k - 1], (dp, (me + k) % n))
+            copy.start()
+            copies.append(copy)
+        rows[me] = value[...]
+        for k in range(1, n):
+            source = (me + n - k) % n
+            remote(value, rows.at[source], send.at[k - 1], recv.at[k - 1], (dp, source)).wait_recv()
+        acc = rows[0]
+        for j in range(1, n):
+            acc = acc + rows[j]
+        along[...] = acc
+        columns[dp] = acc
+        for k in range(1, n_dp):
+            to = (dp + k) % n_dp
+            copy = remote(along, columns.at[dp], send_dp.at[k - 1], recv_dp.at[k - 1], (to, me))
+            copy.start()
+            copies.append(copy)
+        for k in range(1, n_dp):
+            source = (dp + n_dp - k) % n_dp
+            remote(along, columns.at[source], send_dp.at[k - 1], recv_dp.at[k - 1], (source, me)).wait_recv()
+        acc = columns[0]
+        for j in range(1, n_dp):
+            acc = acc + columns[j]
+        return acc
+
+    mine[...] = jnp.zeros_like(mine)
+    mine[0:2, pl.ds(pl.multiple_of(me * hc, hc), hc)] = qk_gain[...]
+    mine[2:3, :] = attn_gain[...]
+    mine[3:4, :] = ff_gain[...]
+    o_ref[...] = sum_all(mine, buf, part, all_parts, ss, rs, st, rt)
     total = squares(gg_ref) + squares(gd_ref) + squares(wo_ref)
     for copy in waits:
         copy.wait_recv()
@@ -1040,41 +1014,16 @@
         copy.wait_recv()
     stay.wait()
     total += squares(gu_ref)
-    mine[...] = jnp.zeros_like(mine)
-    mine[0:2, pl.ds(pl.multiple_of(me * hc, hc), hc)] = qk_gain[...]
-    mine[2:3, :] = attn_gain[...]
-    mine[3:4, :] = ff_gain[...]
-    mine[4:5, :] = jnp.broadcast_to(total, (1, mine.shape[1]))
-    copies = swaps + more
-    for k in range(1, n):
-        copy = remote(mine, buf.at[me], ss.at[k - 1], rs.at[k - 1], (dp, (me + k) % n))
-        copy.start()
-        copies.append(copy)
-    buf[me] = mine[...]
-    for k in range(1, n):
-        source = (me + n - k) % n
-        remote(mine, buf.at[source], ss.at[k - 1], rs.at[k - 1], (dp, source)).wait_recv()
-    acc = buf[0]
-    for j in range(1, n):
-        acc = acc + buf[j]
-    part[...] = acc
-    all_parts[dp] = acc
-    for k in range(1, n_dp):
-        copy = remote(part, all_parts.at[dp], st.at[k - 1], rt.at[k - 1], ((dp + k) % n_dp, me))
-        copy.start()
-        copies.append(copy)
-    for k in range(1, n_dp):
-        source = (dp + n_dp - k) % n_dp
-        remote(part, all_parts.at[source], st.at[k - 1], rt.at[k - 1], (source, me)).wait_recv()
-    acc = all_parts[0]
-    for j in range(1, n_dp):
-        acc = acc + all_parts[j]
-    o_ref[...] = acc
+    square[...] = jnp.broadcast_to(total, square.shape)
+    total = sum_all(square, buf_s, part_s, all_s, s1, r1, s2, r2)
+    o_ref[4:5, :] = jnp.broadcast_to(total[0:1, 0:1], (1, o_ref.shape[1]))
     for copy in copies:
         copy.wait_send()
-
-
-def total_over(qk, wv, wo, u, gg, gd, qk_gain, attn_gain, ff_gain, number):
+    for copy in moves:
+        copy.wait()
+
+
+def total_over(qk, wv, wo, u, gg, gd, qk_gain, attn_gain, ff_gain, masters, number):
     n_dp, n = lax.axis_size("dp"), lax.axis_size("ctx")
     rows, hc = qk.shape[0] // n, wv.shape[1]
     shape = (8, attn_gain.shape[1])
@@ -1085,15 +1034,20 @@
             jax.ShapeDtypeStruct((n, rows, 3 * hc), BF),
             jax.ShapeDtypeStruct(u.shape, BF),
             jax.ShapeDtypeStruct(shape, F32),
+            *[jax.ShapeDtypeStruct(a.shape, F32) for a in masters],
         ),
-        in_specs=[VMEM] * 3 + [ANY] + [VMEM] * 5,
-        out_specs=(VMEM,) * 3,
+        in_specs=[VMEM] * 3 + [ANY] + [VMEM] * 5 + [HBM] * 3,
+        out_specs=(VMEM,) * 3 + (ANY,) * 3,
         scratch_shapes=[
             pltpu.VMEM((n, rows, 3 * hc), BF),
             pltpu.VMEM(shape, F32),
             pltpu.VMEM((n,) + shape, F32),
             pltpu.VMEM(shape, F32),
             pltpu.VMEM((n_dp,) + shape, F32),
+            pltpu.VMEM((8, 128), F32),
+            pltpu.VMEM((n, 8, 128), F32),
+            pltpu.VMEM((8, 128), F32),
+            pltpu.VMEM((n_dp, 8, 128), F32),
             dma,
             dma((n - 1,)),
             dma((n - 1,)),
@@ -1103,8 +1057,13 @@
             dma((n - 1,)),
             dma((n_dp - 1,)),
             dma((n_dp - 1,)),
+            dma((n - 1,)),
+            dma((n - 1,)),
+            dma((n_dp - 1,)),
+            dma((n_dp - 1,)),
+            dma((3,)),
         ],
-        compiler_params=params_of(number),
+        compiler_params=params_of(number, 14),
         cost_estimate=cost(35),
         name="total",
     )(
@@ -1117,6 +1076,7 @@
         qk_gain,
         attn_gain,
         ff_gain,
+        *masters,
     )
 
 
@@ -1159,8 +1119,10 @@
     clipped = g_ref[...] * factor_ref[0:1, 0:1]
     new_m = BETA1 * m_ref[...] + (1.0 - BETA1) * clipped
     new_v = BETA2 * v_ref[...] + (1.0 - BETA2) * (clipped * clipped)
-    root = jnp.sqrt(new_v * (1.0 / (1.0 - BETA2**STEP))) + ADAM_EPS
-    po_ref[...] = p_ref[...] * (1.0 - RATE * DECAY) - (new_m * (RATE / (1.0 - BETA1**STEP))) / root
+    hat = new_v * (1.0 / (1.0 - BETA2**STEP))
+    root = hat * lax.rsqrt(jnp.maximum(hat, 1e-36)) + ADAM_EPS
+    change = (new_m * (RATE / (1.0 - BETA1**STEP))) * pl.reciprocal(root, approx=True)
+    po_ref[...] = p_ref[...] * (1.0 - RATE * DECAY) - change
     mo_ref[...] = new_m
     vo_ref[...] = new_v
 
@@ -1168,7 +1130,7 @@
 def adam(sums, gains, gains_first, gains_second, params, first, second, ga, go, gg, gu, gd):
     rows, columns = params.shape
     n, n_dp, fs = ga.shape[0], gd.shape[0], gd.shape[2]
-    block = min(rows, 16)
+    block = min(rows, 32)
     steps = rows // block
     wide = pl.BlockSpec((block, columns // 4), lambda i, r: (r, i))
     small = pl.BlockSpec(gains.shape, lambda i, r: (0, 0))
@@ -1202,7 +1164,7 @@
         ],
         out_specs=(pl.BlockSpec((1, 1), lambda i, r: (0, 0)),) + (small,) * 3 + (wide,) * 3,
         scratch_shapes=[pltpu.VMEM((block, columns // 4), F32), pltpu.VMEM((8, 128), F32)],
-        compiler_params=pltpu.CompilerParams(vmem_limit_bytes=48 * 1024 * 1024),
+        compiler_params=pltpu.CompilerParams(vmem_limit_bytes=22 * 1024 * 1024),
         name="adam",
     )(sums, gains, gains_first, gains_second, params, first, second, ga, go, gg, gu, gd)
 
@@ -1406,17 +1368,23 @@
 
 
 def attend_back_kernel(
-    n_dp, n, e_ref, do_ref, h_ref, o_hbm, col_ref, row_ref, q_ref, k_ref, v_ref, lse_ref,
-    x_ref, gain_ref, cos_ref, sin_ref, pre_ref, scale_ref,
-    d_ref, gain_out, g_ref, wv_ref, wo_ref, h_out,
-    o_ref, dq_ref, dk_ref, dv_ref, mean_ref, buf, go_ref, co_ref, gv_ref, cv_ref,
-    sh, rh, local, sw, rw, sv, rv, ss, rs,
+    n_dp, n, sum_ref, up_ref, branch_ref, norm_ref, wo_hbm, h_ref, o_hbm, col_ref, row_ref, q_ref, k_ref, v_ref, lse_ref,
+    x_hbm, gain_ref, cos_ref, sin_ref, pre_hbm, scale_ref,
+    dh_ref, gp_ref, d_ref, gain_out, g_ref, wv_ref, wo_ref, h_out,
+    x_ref, pre_ref, wall_ref, db_ref, mix_ref, give_ref, e_ref, do_ref, o_ref, dq_ref, dk_ref, dv_ref, mean_ref, buf, go_ref, co_ref, gv_ref, cv_ref,
+    sh, rh, local, sw, rw, sv, rv, ss, rs, sc, rc, sx, rx,
 ):
     dp, me = lax.axis_index("dp"), lax.axis_index("ctx")
     seq, hc = q_ref.shape
+    load_wo = pltpu.make_async_copy(wo_hbm, wall_ref, local.at[2])
+    load_wo.start()
+    later = [
+        pltpu.make_async_copy(src, dst, local.at[i])
+        for i, (src, dst) in enumerate(((x_hbm, x_ref), (pre_hbm, pre_ref)), 4)
+    ]
     load = pltpu.make_async_copy(o_hbm, o_ref, local.at[1])
     load.start()
-    width = x_ref.shape[1]
+    length, width = dh_ref.shape
     block = min(seq, 256)
     count, index, place = group_of(n_dp, n, dp, me)
     greet_all(n_dp, n, dp, me)
@@ -1424,7 +1392,68 @@
     stay = pltpu.make_async_copy(h_ref.at[index], h_out.at[index], local.at[0])
     stay.start()
 
+    gp_ref[...] = jnp.zeros_like(gp_ref)
+
+    def finish(rows):
+        grad, branch = sum_ref[rows, :] + up_ref[rows, :].astype(F32), branch_ref[rows, :]
+        scale = rms_scale(branch)
+        dh_ref[rows, :] = grad
+        gp_ref[...] += jnp.sum(grad * branch * scale, axis=0, keepdims=True)
+        db_ref[rows, :] = norm_back(grad * norm_ref[...], branch, scale).astype(BF)
+
+    tiles(length, 16, finish)
+    load_wo.wait()
+
+    def mine(c):
+        return pl.ds(pl.multiple_of(c * length, length), length)
+
+    def send(k):
+        to = (me + k) % n
+        return remote(give_ref.at[to], do_ref.at[mine(me), :], sx.at[k - 1], rx.at[k - 1], (dp, to))
+
+    def receive(k):
+        source = (me + n - k) % n
+        return remote(give_ref.at[me], do_ref.at[mine(source), :], sx.at[k - 1], rx.at[k - 1], (dp, source))
+
+    share = width // n
+    own = share // n_dp
+    for c in range(n):
+        for d in range(n_dp):
+            start, source = c * share + d * own, (d * n + c) * own
+            mix_ref[:, start : start + own] = db_ref[:, source : source + own]
+
+    def share_of(c):
+        return mix_ref.at[:, pl.ds(pl.multiple_of(c * share, share), share)]
+
+    def send_share(k):
+        to = (me + k) % n
+        return remote(share_of(to), e_ref.at[mine(me), :], sc.at[k - 1], rc.at[k - 1], (dp, to))
+
+    def receive_share(k):
+        source = (me + n - k) % n
+        return remote(share_of(me), e_ref.at[mine(source), :], sc.at[k - 1], rc.at[k - 1], (dp, source))
+
+    stay_share = pltpu.make_async_copy(share_of(me), e_ref.at[mine(me), :], local.at[3])
+    stay_share.start()
+
+    @pl.loop(1, n)
+    def _(k):
+        to = (me + k) % n
+        send_share(k).start()
+        give_ref[to] = dot(db_ref[...], wall_ref[to]).astype(BF)
+        send(k).start()
+
+    do_ref[mine(me), :] = dot(db_ref[...], wall_ref[me]).astype(BF)
+    for k in range(1, n):
+        receive(k).wait_recv()
+        receive_share(k).wait_recv()
+    for k in range(1, n):
+        send(k).wait_send()
+        send_share(k).wait_send()
+    stay_share.wait()
     load.wait()
+    for copy in later:
+        copy.start()
 
     @pl.loop(0, n)
     def _(c):
@@ -1451,6 +1480,8 @@
 
     pl.loop(0, seq // block)(attention)
 
+    for copy in later:
+        copy.wait()
     d_ref[:, 2 * hc :] = dv_ref[...].astype(BF)
 
     def values(part):
@@ -1502,13 +1533,16 @@
     stay.wait()
 
 
-def attend_back(e, do, h, o_all, info_col, info_row, q, k, v, lse, x, gain, cos, sine, pre, scale, number):
+def attend_back(sums, up, branch, norm, wo_all, h, o_all, info_col, info_row, q, k, v, lse, x, gain, cos, sine, pre, scale, number):
     n_dp, n = lax.axis_size("dp"), lax.axis_size("ctx")
-    (seq, hc), share, width = q.shape, e.shape[1], x.shape[1]
+    (seq, hc), (length, width) = q.shape, branch.shape
+    share = width // n
     dma = pltpu.SemaphoreType.DMA
     return pl.pallas_call(
         functools.partial(attend_back_kernel, n_dp, n),
         out_shape=(
+            jax.ShapeDtypeStruct((length, width), F32),
+            jax.ShapeDtypeStruct((1, width), F32),
             jax.ShapeDtypeStruct((seq, 3 * hc), BF),
             jax.ShapeDtypeStruct((2, hc), F32),
             jax.ShapeDtypeStruct((width, 2 * hc), BF),
@@ -1516,9 +1550,17 @@
             jax.ShapeDtypeStruct((share // n_dp, n * hc), BF),
             jax.ShapeDtypeStruct(h.shape, BF),
         ),
-        in_specs=[VMEM, VMEM, ANY, ANY] + [VMEM] * 12,
-        out_specs=(VMEM,) * 5 + (ANY,),
+        in_specs=[VMEM] * 4 + [ANY] * 3 + [VMEM] * 6 + [ANY] + [VMEM] * 3 + [ANY, VMEM],
+        out_specs=(VMEM,) * 7 + (ANY,),
         scratch_shapes=[
+            pltpu.VMEM(x.shape, BF),
+            pltpu.VMEM(pre.shape, F32),
+            pltpu.VMEM(wo_all.shape, BF),
+            pltpu.VMEM((length, width), BF),
+            pltpu.VMEM((length, width), BF),
+            pltpu.VMEM((n, length, hc), BF),
+            pltpu.VMEM((seq, share), BF),
+            pltpu.VMEM((seq, hc), BF),
             pltpu.VMEM(o_all.shape, BF),
             pltpu.VMEM((seq, hc), F32),
             pltpu.VMEM((seq, hc), F32),
@@ -1531,18 +1573,22 @@
             pltpu.VMEM((n_dp - 1, width // n_dp, hc), BF),
             dma((2 * n_dp - 1,)),
             dma((2 * n_dp - 1,)),
-            dma((2,)),
+            dma((6,)),
             dma((n_dp - 1,)),
             dma((n_dp - 1,)),
             dma((n_dp - 1,)),
             dma((n_dp - 1,)),
             dma((n - 1,)),
             dma((n - 1,)),
+            dma((n - 1,)),
+            dma((n - 1,)),
+            dma((n - 1,)),
+            dma((n - 1,)),
         ],
-        compiler_params=params_of(number),
+        compiler_params=params_of(number, 56),
         cost_estimate=cost(75),
         name="attend_back",
-    )(e, do, h, o_all, info_col, info_row, q, k, v, lse, x, gain, cos, sine, pre, scale)
+    )(sums, up, branch, norm, wo_all, h, o_all, info_col, info_row, q, k, v, lse, x, gain, cos, sine, pre, scale)
 
 
 def shards(
@@ -1620,28 +1666,26 @@
     attn_all = lax.all_gather(attn_low, "ctx", axis=0)
     d_gu, d_grad = ff_back(d_mlp, inner, w_d, gate_up, rows, 5)
     d_grad = scatter_pairs(d_grad)
-    d_h1, d_branch, d_attn, g_attn_part, g_grad, u_grad = ff_scatter(
-        d_gu, w_gu, h1_all, w_o, upstream, branch, gains[2:3], 6
-    )
+    d_sums, g_grad, u_grad = ff_scatter(d_gu, w_gu, h1_all, length, 6)
     g_grad, u_grad = scatter_pairs(g_grad), scatter_pairs(u_grad)
 
-    d_qkv, d_gain, qk_grad, wv_grad, wo_grad, d_grad = attend_back(
-        d_branch, d_attn, d_grad, attn_all, info_col, info_row, queries, keys, values, lse,
+    d_h1, g_attn_part, d_qkv, d_gain, qk_grad, wv_grad, wo_grad, d_grad = attend_back(
+        d_sums, upstream, branch, gains[2:3], w_o, d_grad, attn_all, info_col, info_row, queries, keys, values, lse,
         x_all, my_gains, cos_tab, sine_tab, qk_pre, scales, 8,
     )
-    qk_grad, g_grad, d_x = collect(qk_grad, g_grad, d_qkv, w_qkv, 9)
-    d_input = d_h1 + d_x
-
-    attn_grad, u_grad, sums = total_over(
-        qk_grad, wv_grad, wo_grad, u_grad, g_grad, d_grad, d_gain, g_attn_part, g_ff_part, 11
+    qk_grad, g_grad, d_input = collect(qk_grad, g_grad, d_qkv, w_qkv, d_h1, 9)
+
+    attn_grad, u_grad, sums, *masters = total_over(
+        qk_grad, wv_grad, wo_grad, u_grad, g_grad, d_grad, d_gain, g_attn_part, g_ff_part,
+        (params, first_moment, second_moment), 11,
     )
     grad_norm, new_gains, new_gains_first, new_gains_second, new_params, new_first, new_second = adam(
-        sums, gains, gains_first, gains_second, params, first_moment, second_moment,
+        sums, gains, gains_first, gains_second, *masters,
         attn_grad, wo_grad, g_grad, u_grad, d_grad,
     )
     return (
         result[None],
-        d_input.astype(BF)[None],
+        d_input[None],
         grad_norm.reshape(()),
         new_params,
         new_first,

time: 653 us -> 640 us (0.980)
  Pallas kernels: 606 us -> 593 us
    pallas_call x1, Pallas kernels: 73.4 us -> 62.2 us  [ff_scatter(): pl.pallas_call(functools.partial(ff_scatter_kernel, n_dp, n), out_shape=(...]
    pallas_call x1, Pallas kernels: 25 us -> 15.5 us  [adam(): pl.pallas_call(adam_kernel, grid=(4, steps), out_shape=(jax.ShapeDtypeStr...]
    unnamed x55 -> x66, local copies, waits for them, and re-layouts: 16 us -> 18.8 us
where the time goes in v9:
time: 640 us; the launch traced here: 631 us
  Pallas kernels  593 us (93%)
  local copies, waits for them, and re-layouts  19.8 us (3%)
  between operations  14.4 us (2%)
    pallas_call x1, Pallas kernels, ff_forward(): pl.pallas_call(functools.partial(ff_forward_kernel, n_dp, n), out_shape=(...  108 us
    pallas_call x1, Pallas kernels, attend_back(): pl.pallas_call(functools.partial(attend_back_kernel, n_dp, n), out_shape=...  78.4 us
    pallas_call x1, Pallas kernels, collect(): pl.pallas_call(functools.partial(collect_kernel, n_dp, n), out_shape=(jax...  65.8 us
    pallas_call x1, Pallas kernels, gather_dp(): pl.pallas_call(functools.partial(gather_dp_kernel, n), out_shape=jax.Shap...  65.3 us
    pallas_call x1, Pallas kernels, ff_scatter(): pl.pallas_call(functools.partial(ff_scatter_kernel, n_dp, n), out_shape=(...  62.2 us
    pallas_call x1, Pallas kernels, attend(): pl.pallas_call(functools.partial(attend_kernel, n_dp, n), out_shape=(jax....  58.3 us
    pallas_call x1, Pallas kernels, ff_back(): pl.pallas_call(functools.partial(ff_back_kernel, n_dp), out_shape=(jax.Sh...  51.3 us
    pallas_call x1, Pallas kernels, total_over(): pl.pallas_call(functools.partial(total_kernel, n_dp, n), out_shape=(jax.S...  45.9 us
  transfers between devices with their start and end apart: 5, of which 0 were waited for; matrix products, arithmetic and copies ran while one was open for 1% of the time, Pallas kernels for 60%

profile of v9, /device:TPU:0, one launch (start us, length us, event | category | flops | bytes accessed | tf_op | source)
XLA Modules:
  0.0 630.6 jit_solution(17781699476729823407)
XLA Ops:
  7.2 0.0 all-gather.4.cloned.1.call-start
  7.2 0.0 copy-start.6
  7.2 1.0 copy-done.6
  8.3 42.8 %start.1 = (bf16[8,64,2048]{2,1,0:T(8,128)(2,1)}, bf16[8,64,768]{2,1,0:T(8,128)(2,1)S(1)}, bf16[8,64,256]{2,1,0:T(8,128)(2,1)S(1)}, bf16[8,128,2048]{2,1,0:T(8,128)(2,1)}, bf16[8,64,1024]{2,1,0:T(8,128)(2,1)S(1)}) custom-call(f32[64,32768]{1,0:T(8,128)} %p_hbm.3, bf16[128,2048]{1,0:T(8,128)(2,1)S(1)} %bitcast.27), custom_call_target="tpu_custom_call" | custom-call | bytes 162000000 | tf_op jit(solution)/shard_map/start/pallas_call | solution.py:834
  51.1 0.0 copy-start.10
  51.1 1.0 copy-done.10
  52.0 0.0 all-gather.4.cloned.1.call-update
  52.1 0.0 all-gather.6.cloned.1.call-start
  52.1 0.1 pad.2.clone
  52.2 0.0 copy-done.31
  52.2 0.1 select_reduce_fusion
  52.3 0.0 copy-done.30
  52.3 0.1 add_add_fusion
  52.4 0.2 copy.21.col_ref
  52.6 0.0 copy-start.4
  52.6 0.0 copy-start.21
  52.6 0.0 copy-start.7
  52.7 65.3 %gather_dp.1 = bf16[4,512,768]{2,1,0:T(8,128)(2,1)S(1)} custom-call(bf16[512,768]{1,0:T(8,128)(2,1)S(1)} %bitcast.32), custom_call_target="tpu_custom_call" | custom-call | bytes 216000000 | tf_op jit(solution)/shard_map/gather_dp/pallas_call | solution.py:153
  117.9 0.0 copy-start.1
  118.0 1.7 copy-done.1
  119.6 0.0 slice-done
  119.6 0.0 copy-start.25
  119.7 1.9 fusion
  121.6 0.3 pad_maximum_fusion
  121.9 0.7 fusion.12
  122.6 58.3 %attend.1 = (f32[128,2048]{1,0:T(8,128)}, f32[128,2048]{1,0:T(8,128)}, bf16[1024,256]{1,0:T(8,128)(2,1)S(1)}, bf16[1024,256]{1,0:T(8,128)(2,1)S(1)}, bf16[1024,2...) custom-call(bf16[1024,2048]{1,0:T(8,128)(2,1)} %bitcast.39, ...), custom_call_target="tpu_custom_call" | custom-call | bytes 216000000 | tf_op jit(solution)/shard_map/attend/pallas_call | solution.py:1302
  180.9 0.0 copy-done.4
  180.9 0.0 copy-done.25
  180.9 0.0 copy-done.2
  181.0 0.0 copy-done.3
  181.0 0.0 copy-done.22
  181.0 0.0 copy-start.14
  181.0 0.8 copy-done.14
  181.8 0.8 copy-done.15
  182.6 0.8 copy-done.16
  183.4 0.8 copy-done.17
  184.2 0.8 copy-done.18
  185.0 107.6 %ff_forward.1 = (bf16[128,2048]{1,0:T(8,128)(2,1)}, bf16[128,2048]{1,0:T(8,128)(2,1)}, f32[1,2048]{1,0:T(1,128)}, bf16[1024,2048]{1,0:T(8,128)(2,1)}, f32[1024,2...) custom-call(f32[128,2048]{1,0:T(8,128)} %get-tuple-element.68.h_ref, ...), custom_call_target="tpu_custom_call" | custom-call | bytes 324000000 | tf_op jit(solution)/shard_map/ff_forward/pallas_call | solution.py:560
  292.6 0.0 all-gather.6.cloned.1.call-update
  292.7 0.0 reduce-scatter.4.cloned.1.call-start
  292.7 51.3 %ff_back.1 = (bf16[1024,2048]{1,0:T(8,128)(2,1)}, bf16[4,4,128,1024]{3,2,1,0:T(8,128)(2,1)}) custom-call(bf16[128,2048]{1,0:T(8,128)(2,1)} %get-tuple-element.75.dm_ref, bf16[1024,1024]{1,0:T(8,128)(2,1)} %get-tuple-element.76.hid_ref, bf16[2048,1024]{1,0:T(8,128)(2,1)} %get-tuple-element.77.d_hbm, f32[1024,2048]{1,0:T(8,128)} %get-tuple-element.78.pre_hbm), custom_call_target="tpu_custom_call" | custom-call | bytes 162000000 | tf_op jit(solution)/shard_map/ff_back/pallas_call | solution.py:660
  344.0 0.0 reduce-scatter.4.cloned.1.call-update
  344.0 0.0 reduce-scatter.6.cloned.1.call-start
  344.1 62.2 %ff_scatter.1 = (f32[128,2048]{1,0:T(8,128)}, bf16[4,4,128,1024]{3,2,1,0:T(8,128)(2,1)}, bf16[4,4,128,1024]{3,2,1,0:T(8,128)(2,1)}) custom-call(bf16[1024,2048]{1,0:T(8,128)(2,1)} %get-tuple-element.79.dgu_ref, bf16[4,4,128,2048]{3,2,1,0:T(8,128)(2,1)} %bitcast.38, bf16[1024,2048]{1,0:T(8,128)(2,1)} %get-tuple-element.80.all_hbm), custom_call_target="tpu_custom_call" | custom-call | bytes 180000000 | tf_op jit(solution)/shard_map/ff_scatter/pallas_call | solution.py:730
  406.3 0.0 reduce-scatter.6.cloned.1.call-update
  406.3 0.2 reduce-scatter.8.cloned.1.call-start
  406.6 0.4 reduce-scatter.8.cloned.1.call-update
  406.9 0.0 all-gather.6.cloned.1.call-done
  407.0 0.0 reduce-scatter.4.cloned.1.call-done
  407.0 78.4 %attend_back.1 = (f32[128,2048]{1,0:T(8,128)}, f32[1,2048]{1,0:T(1,128)}, bf16[1024,768]{1,0:T(8,128)(2,1)}, f32[2,256]{1,0:T(2,128)}, bf16[2048,512]{1,0:T(8,12...) custom-call(f32[128,2048]{1,0:T(8,128)} %get-tuple-element.81.sum_ref, ...), custom_call_target="tpu_custom_call" | custom-call | bytes 270000000 | tf_op jit(solution)/shard_map/attend_back/pallas_call | solution.py:1541
  485.4 0.0 reduce-scatter.6.cloned.1.call-done
  485.5 1.4 copy-done.8
  486.9 1.3 copy-done.12
  488.2 1.2 copy-done.13
  489.5 65.8 %collect.1 = (bf16[512,512]{1,0:T(8,128)(2,1)S(1)}, bf16[8,64,1024]{2,1,0:T(8,128)(2,1)S(1)}, bf16[128,2048]{1,0:T(8,128)(2,1)S(1)}) custom-call(bf16[2048,512]{1,0:T(8,128)(2,1)} %get-tuple-element.92.g_ref, bf16[8,64,1024]{2,1,0:T(8,128)(2,1)S(1)} %bitcast.31, bf16[1024,768]{1,0:T(8,128)(2,1)S(1)} %copy-done.8, bf16[2048,768]{1,0:T(8,128)(2,1)} %bitcast.26, ...), custom_call_target="tpu_custom_call" | custom-call | bytes 252000000 | tf_op jit(solution)/shard_map/collect/pallas_call | solution.py:913
  555.3 0.0 reduce-scatter.8.cloned.1.call-done
  555.4 0.0 copy-start
  555.4 3.4 copy-done
  558.7 1.2 copy-done.11
  560.0 0.9 copy-done.20
  560.9 45.9 %total.1 = (bf16[8,64,768]{2,1,0:T(8,128)(2,1)S(1)}, bf16[8,64,1024]{2,1,0:T(8,128)(2,1)S(1)}, f32[8,2048]{1,0:T(8,128)S(1)}, f32[64,32768]{1,0:T(8,128)S(1)}, f...) custom-call(bf16[8,64,512]{2,1,0:T(8,128)(2,1)S(1)} %bitcast.33, bf16[8,64,256]{2,1,0:T(8,128)(2,1)S(1)} %bitcast.35, ...), custom_call_target="tpu_custom_call" | custom-call | bytes 126000000 | tf_op jit(solution)/shard_map/total/pallas_call | solution.py:1031
  606.8 15.5 %adam.1 = (f32[1,1]{1,0:T(1,128)}, f32[4,2048]{1,0:T(4,128)}, f32[4,2048]{1,0:T(4,128)}, f32[4,2048]{1,0:T(4,128)}, f32[64,32768]{1,0:T(8,128)}, /*index=5*/f32[64,32768]{1,0:T(8,128)}, f32[64,32768]{1,0:T(8,128)}) custom-call(f32[8,2048]{1,0:T(8,128)S(1)} %get-tuple-element.106.sum_ref, f32[4,2048]{1,0:T(4,128)S(1)} %copy-done.21, ...), custom_call_target="tpu_custom_call" | custom-call | tf_op jit(solution)/shard_map/adam/pallas_call | solution.py:1137
  622.3 0.8 copy.25
  623.1 0.8 copy.26
  (42 shorter events, 0.1 us)
Async XLA Ops:
  7.2 177.8 %all-gather.4.cloned.1.call-start = ((), (), s32[]{:S(2)}) async-start(), calls=%async_computation.3 | async-start | bytes 10485760 | tf_op jit(solution)/shard_map/all_gather | solution.py:1621
  7.2 1.0 copy-start.6
  8.3 43.9 %copy-start.31 = (s32[8]{0:T(128)S(1)}, s32[8]{0:T(128)}, u32[]{:S(2)}) copy-start(s32[8]{0:T(128)} %param.13) | copy-start | bytes 100
  8.3 44.1 %copy-start.30 = (s32[1,1024]{1,0:T(1,128)S(1)}, s32[1,1024]{1,0:T(1,128)}, u32[]{:S(2)}) copy-start(s32[1,1024]{1,0:T(1,128)} %param.12) | copy-start | bytes 12292
  51.1 1.0 copy-start.10
  52.0 67.6 %slice-start = ((f32[4,2048]{1,0:T(4,128)}), f32[2,2048]{1,0:T(2,128)S(1)}, s32[]{:S(2)}) async-start(f32[4,2048]{1,0:T(4,128)} %gp_ref.1), calls=%async_computation.8 | async-start | bytes 32768 | tf_op jit(solution)/shard_map/slice | solution.py:1655
  52.1 354.9 %all-gather.6.cloned.1.call-start = ((), (), s32[]{:S(2)}) async-start(), calls=%async_computation.7 | async-start | bytes 4718592 | tf_op jit(solution)/shard_map/all_gather | solution.py:1666
  52.4 70.2 %copy-start.19 = (s32[8,1024]{1,0:T(8,128)}, s32[8,1024]{1,0:T(8,128)S(1)}, u32[]{:S(2)}) copy-start(s32[8,1024]{1,0:T(8,128)S(1)} %get-tuple-element.121.row_ref) | copy-start | bytes 98308
  52.6 128.3 %copy-start.4 = (s32[1024,8]{1,0:T(8,128)}, s32[1024,8]{1,0:T(8,128)S(1)}, u32[]{:S(2)}) copy-start(s32[1024,8]{1,0:T(8,128)S(1)} %copy.21.col_ref) | copy-start | bytes 98308
  52.6 69.3 %copy-start.21 = (f32[4,2048]{1,0:T(4,128)S(1)}, f32[4,2048]{1,0:T(4,128)}, u32[]{:S(2)}) copy-start(f32[4,2048]{1,0:T(4,128)} %gp_ref.1) | copy-start | bytes 98308
  52.6 70.0 %copy-start.7 = (bf16[1,128,2048]{2,1,0:T(8,128)(2,1)S(1)}, bf16[1,128,2048]{2,1,0:T(8,128)(2,1)}, u32[]{:S(2)}) copy-start(bf16[1,128,2048]{2,1,0:T(8,128)(2,1)} %param.10) | copy-start | bytes 1572868
  117.9 1.7 copy-start.1
  119.6 61.3 %copy-start.25 = (f32[2,256]{1,0:T(2,128)}, f32[2,256]{1,0:T(2,128)S(1)}, u32[]{:S(2)}) copy-start(f32[2,256]{1,0:T(2,128)S(1)} %constant_dynamic-slice_fusion.gain_ref) | copy-start | bytes 6148
  121.9 59.0 %copy-start.2 = (f32[1024,128]{1,0:T(8,128)}, f32[1024,128]{1,0:T(8,128)S(1)}, u32[]{:S(2)}) copy-start(f32[1024,128]{1,0:T(8,128)S(1)} %get-tuple-element.128.cos_ref) | copy-start | bytes 1572868
  121.9 59.0 %copy-start.3 = (f32[1024,128]{1,0:T(8,128)}, f32[1024,128]{1,0:T(8,128)S(1)}, u32[]{:S(2)}) copy-start(f32[1024,128]{1,0:T(8,128)S(1)} %get-tuple-element.129.sin_ref) | copy-start | bytes 1572868
  122.6 58.3 %copy-start.22 = (f32[1,2048]{1,0:T(1,128)}, f32[1,2048]{1,0:T(1,128)S(1)}, u32[]{:S(2)}) copy-start(f32[1,2048]{1,0:T(1,128)S(1)} %get-tuple-element.120.norm_ref) | copy-start | bytes 24580
  181.0 0.8 copy-start.14
  181.8 0.8 copy-start.15
  182.6 0.8 copy-start.16
  183.4 0.8 copy-start.17
  184.2 0.8 copy-start.18
  292.7 114.3 %reduce-scatter.4.cloned.1.call-start = ((), (), s32[]{:S(2)}) async-start(), calls=%async_computation.4 | async-start | bytes 5242880 | tf_op jit(solution)/shard_map/reduce_scatter | solution.py:1627
  344.0 141.4 %reduce-scatter.6.cloned.1.call-start = ((), (), s32[]{:S(2)}) async-start(), calls=%async_computation.5 | async-start | bytes 5242880 | tf_op jit(solution)/shard_map/reduce_scatter | solution.py:1627
  406.3 149.0 %reduce-scatter.8.cloned.1.call-start = ((), (), s32[]{:S(2)}) async-start(), calls=%async_computation.6 | async-start | bytes 5242880 | tf_op jit(solution)/shard_map/reduce_scatter | solution.py:1627
  485.5 1.4 copy-start.8
  486.9 1.3 copy-start.12
  488.2 1.2 copy-start.13
  489.4 65.9 %copy-start.5 = (bf16[8,64,1024]{2,1,0:T(8,128)(2,1)S(1)}, bf16[8,64,1024]{2,1,0:T(8,128)(2,1)}, u32[]{:S(2)}) copy-start(bf16[8,64,1024]{2,1,0:T(8,128)(2,1)} %get-tuple-element.102.gd_ref) | copy-start | bytes 3145732
  489.4 65.9 %copy-start.9 = (bf16[64,2048]{1,0:T(8,128)(2,1)S(1)}, bf16[64,2048]{1,0:T(8,128)(2,1)}, u32[]{:S(2)}) copy-start(bf16[64,2048]{1,0:T(8,128)(2,1)} %get-tuple-element.99.go_ref) | copy-start | bytes 786436
  489.4 65.9 %copy-start.26 = (f32[1,2048]{1,0:T(1,128)S(1)}, f32[1,2048]{1,0:T(1,128)}, u32[]{:S(2)}) copy-start(f32[1,2048]{1,0:T(1,128)} %get-tuple-element.105.ff_gain) | copy-start | bytes 24580
  489.4 65.9 %copy-start.27 = (f32[1,2048]{1,0:T(1,128)S(1)}, f32[1,2048]{1,0:T(1,128)}, u32[]{:S(2)}) copy-start(f32[1,2048]{1,0:T(1,128)} %get-tuple-element.104.attn_gain) | copy-start | bytes 24580
  489.4 65.9 %copy-start.28 = (f32[2,256]{1,0:T(2,128)S(1)}, f32[2,256]{1,0:T(2,128)}, u32[]{:S(2)}) copy-start(f32[2,256]{1,0:T(2,128)} %get-tuple-element.103.qk_gain) | copy-start | bytes 6148
  555.4 3.4 copy-start
  558.7 1.2 copy-start.11
  560.0 0.9 copy-start.20
  560.9 45.9 %copy-start.23 = (f32[4,2048]{1,0:T(4,128)S(1)}, f32[4,2048]{1,0:T(4,128)}, u32[]{:S(2)}) copy-start(f32[4,2048]{1,0:T(4,128)} %gm_ref.1) | copy-start | bytes 98308
  560.9 45.9 %copy-start.24 = (f32[4,2048]{1,0:T(4,128)S(1)}, f32[4,2048]{1,0:T(4,128)}, u32[]{:S(2)}) copy-start(f32[4,2048]{1,0:T(4,128)} %gv_ref.1) | copy-start | bytes 98308
  606.8 15.5 %copy-start.29 = (bf16[128,2048]{1,0:T(8,128)(2,1)S(1)}, bf16[128,2048]{1,0:T(8,128)(2,1)}, u32[]{:S(2)}) copy-start(bf16[128,2048]{1,0:T(8,128)(2,1)} %get-tuple-element.72) | copy-start | bytes 1572868
Sparse Core Ops, SparseCore 0:
  52.2 98.8 all-gather.3
  292.8 36.6 all-gather.5
  344.1 53.6 reduce-scatter.3
  406.5 65.9 reduce-scatter.5
  475.2 68.2 reduce-scatter.7

commit v10 on v9

--- a/solution.py
+++ b/solution.py
@@ -2,6 +2,7 @@
 
 import jax
 import jax.numpy as jnp
+import numpy as np
 from jax import lax
 from jax.experimental import pallas as pl
 from jax.experimental.pallas import tpu as pltpu
@@ -36,13 +37,6 @@
     )
 
 
-def rope_tables(positions, head_size):
-    half_size = head_size // 2
-    freqs = THETA ** (-jnp.arange(half_size, dtype=jnp.float32) * 2.0 / head_size)
-    angles = positions.astype(jnp.float32)[:, None] * freqs[None, :]
-    return (jnp.cos(angles), jnp.sin(angles))
-
-
 def adam_update(weight, first_in, second_in, clipped, rate, decay):
     new_first = BETA1 * first_in + (1.0 - BETA1) * clipped
     new_second = BETA2 * second_in + (1.0 - BETA2) * clipped * clipped
@@ -64,6 +58,13 @@
     return lax.dot_general(a, b, (((0,), (0,)), ((), ())), preferred_element_type=F32)
 
 
+def loads_of(pairs, sems, first=0):
+    copies = [pltpu.make_async_copy(a, b, sems.at[first + i]) for i, (a, b) in enumerate(pairs)]
+    for copy in copies:
+        copy.start()
+    return copies
+
+
 def greet(peers):
     barrier = pltpu.get_barrier_semaphore()
     for peer in peers:
@@ -81,13 +82,13 @@
     return pl.CostEstimate(flops=0, bytes_accessed=us * 3_600_000, transcendentals=0)
 
 
-def params_of(number, vmem=48):
+def params_of(number, vmem=62):
     return pltpu.CompilerParams(
         collective_id=number, has_side_effects=True, vmem_limit_bytes=vmem * 1024 * 1024
     )
 
 
-def line_steps(n, me, make_right, make_left):
+def line_steps(n, me, make_right, make_left, meanwhile):
     for s in range(n - 1):
 
         @pl.when((me < n - 1) & (me >= s))
@@ -97,6 +98,9 @@
         @pl.when((me > 0) & (me + s < n))
         def _():
             make_left(s).start()
+
+        if s == 0:
+            meanwhile()
 
         @pl.when(me - 1 - s >= 0)
         def _():
@@ -126,7 +130,10 @@
     return half, parity, pair, partner, ahead, behind
 
 
-def gather_dp_kernel(n, x_ref, o_ref, local, sr, rr, sl, rl):
+def gather_dp_kernel(
+    n, n_ctx, place_ref, doc_ref, freq_ref, x_ref, cos_ref, sin_ref, row_ref, col_ref, o_ref,
+    local, sr, rr, sl, rl,
+):
     me, ctx = lax.axis_index("dp"), lax.axis_index("ctx")
 
     def here(d):
@@ -144,23 +151,47 @@
         b = me + s if block is None else block
         return remote(x_ref if s == 0 else o_ref.at[b], o_ref.at[b], sl.at[s], rl.at[s], here(me - 1))
 
-    line_steps(n, me, right, left)
+    def tables():
+        length = cos_ref.shape[0] // n_ctx
+        head = cos_ref.shape[1]
+        sign = jnp.where(lax.broadcasted_iota(jnp.int32, (length, head), 1) < head // 2, -1.0, 1.0)
+        row_ref[...] = jnp.zeros_like(row_ref)
+        row_ref[1:2, :] = doc_ref[...].astype(F32)
+        for c in range(n_ctx):
+            rows = slice(c * length, (c + 1) * length)
+            base = place_ref[c] * length
+            angles = (base + lax.broadcasted_iota(jnp.int32, (length, head), 0)).astype(F32) * freq_ref[...]
+            cos_ref[rows, :] = jnp.cos(angles)
+            sin_ref[rows, :] = jnp.sin(angles) * sign
+            row_ref[0:1, rows] = (base + lax.broadcasted_iota(jnp.int32, (1, length), 1)).astype(F32)
+        col_ref[...] = jnp.transpose(row_ref[...])
+
+    line_steps(n, me, right, left, tables)
     own.wait()
 
 
-def gather_dp(x, number):
-    n = lax.axis_size("dp")
-    out = pl.pallas_call(
-        functools.partial(gather_dp_kernel, n),
-        out_shape=jax.ShapeDtypeStruct((n,) + x.shape, x.dtype),
-        in_specs=[ANY],
-        out_specs=ANY,
+def gather_dp(x, places, docs, number):
+    n, n_ctx = lax.axis_size("dp"), lax.axis_size("ctx")
+    seq = docs.shape[1]
+    half = np.arange(HD // 2, dtype=np.float64) * 2.0 / HD
+    freqs = np.tile(THETA**-half, 2)[None].astype(np.float32)
+    *tables, out = pl.pallas_call(
+        functools.partial(gather_dp_kernel, n, n_ctx),
+        out_shape=(
+            jax.ShapeDtypeStruct((seq, HD), F32),
+            jax.ShapeDtypeStruct((seq, HD), F32),
+            jax.ShapeDtypeStruct((8, seq), F32),
+            jax.ShapeDtypeStruct((seq, 8), F32),
+            jax.ShapeDtypeStruct((n,) + x.shape, x.dtype),
+        ),
+        in_specs=[pl.BlockSpec(memory_space=pltpu.SMEM), VMEM, VMEM, ANY],
+        out_specs=(VMEM,) * 4 + (ANY,),
         scratch_shapes=[pltpu.SemaphoreType.DMA] + [pltpu.SemaphoreType.DMA((n - 1,))] * 4,
         compiler_params=params_of(number),
         cost_estimate=cost(60),
         name="gather_dp",
-    )(x)
-    return out.reshape((n * x.shape[0],) + x.shape[1:])
+    )(places, docs, jnp.asarray(freqs), x)
+    return out.reshape((n * x.shape[0],) + x.shape[1:]), tables
 
 
 def group_of(n_dp, n, dp, me):
@@ -591,7 +622,7 @@
         + gather_sems(n_dp)
         + pair_scratch(n_dp, length, width)
         + line_scratch(n_dp, length, width),
-        compiler_params=params_of(number, 58),
+        compiler_params=params_of(number),
         cost_estimate=cost(90),
         name="ff_forward",
     )(h1, up, gain, w_gu, w_d, w_o)
@@ -606,8 +637,8 @@
 
 
 def ff_back_kernel(
-    n_dp, dm_ref, hid_ref, d_hbm, pre_hbm, dgu_ref, gd_ref,
-    all_ref, d_ref, pre_ref, acc, sem_d, sem_p, *gather,
+    n_dp, dm_ref, hid_ref, d_hbm, pre_hbm, dgu_out, gd_out,
+    dgu_ref, gd_ref, sem_out, all_ref, d_ref, pre_ref, acc, sem_d, sem_p, *gather,
 ):
     dp, me = lax.axis_index("dp"), lax.axis_index("ctx")
     length, width = dm_ref.shape
@@ -650,7 +681,10 @@
         tiles(width, 256, product)
 
     gather_group(n_dp, dp, me, all_ref, length, *gather, process)
+    outs = loads_of(((dgu_ref, dgu_out),), sem_out)
     store_rows(n_dp, lambda part: acc[part, :], gd_ref)
+    for copy in outs + loads_of(((gd_ref, gd_out),), sem_out, 1):
+        copy.wait()
 
 
 def ff_back(dm, hid, w_d, pre, rows, number):
@@ -664,8 +698,11 @@
             jax.ShapeDtypeStruct((half, n_dp, 2 * rows, fh), BF),
         ),
         in_specs=[VMEM, VMEM, ANY, ANY],
-        out_specs=(VMEM,) * 2,
+        out_specs=(ANY,) * 2,
         scratch_shapes=[
+            pltpu.VMEM((tokens, 2 * fh), BF),
+            pltpu.VMEM((half, n_dp, 2 * rows, fh), BF),
+            pltpu.SemaphoreType.DMA((2,)),
             pltpu.VMEM((tokens, width), BF),
             pltpu.VMEM((width, fh), BF),
             pltpu.VMEM((tokens, 2 * fh), F32),
@@ -674,22 +711,22 @@
             pltpu.SemaphoreType.DMA((n_dp,)),
         ]
         + gather_sems(n_dp),
-        compiler_params=params_of(number, 58),
+        compiler_params=params_of(number),
         cost_estimate=cost(45),
         name="ff_back",
     )(dm, hid, w_d, pre)
 
 
 def ff_scatter_kernel(
-    n_dp, n, dgu_ref, gu_hbm, all_hbm, dh_ref, gg_out, gv_out,
-    gg_ref, gv_ref, gu_ref, all_ref, acc, sem_gu, sem_all, sem_out, *rest,
+    n_dp, n, dgu_hbm, gu_hbm, all_hbm, dh_ref, gg_out, gv_out,
+    gg_ref, gv_ref, dgu_ref, gu_ref, all_ref, acc, sem_gu, sem_all, sem_out, *rest,
 ):
     dp, me = lax.axis_index("dp"), lax.axis_index("ctx")
     length, width = dh_ref.shape
     pair_refs, line_refs = rest[:4], rest[4:]
     half, parity, pair, partner, ahead, behind = pairs_of(n, me)
     _, _, rows, fh = gg_ref.shape
-    loads = load_rows(gu_hbm, gu_ref, sem_gu)
+    loads = load_rows(gu_hbm, gu_ref, sem_gu) + loads_of(((dgu_hbm, dgu_ref),), sem_out, 2)
     load = pltpu.make_async_copy(all_hbm, all_ref, sem_all)
     load.start()
     greet_group(n_dp, dp, me)
@@ -734,21 +771,22 @@
             grad,
             grad,
         ),
-        in_specs=[VMEM, ANY, ANY],
+        in_specs=[ANY] * 3,
         out_specs=(VMEM,) + (ANY,) * 2,
         scratch_shapes=[
             pltpu.VMEM(grad.shape, BF),
             pltpu.VMEM(grad.shape, BF),
+            pltpu.VMEM(dgu.shape, BF),
             pltpu.VMEM((width, w_gu.shape[3]), BF),
             pltpu.VMEM(h1_all.shape, BF),
             pltpu.VMEM((256, w_gu.shape[3]), F32),
             pltpu.SemaphoreType.DMA((w_gu.shape[0] * n_dp,)),
             pltpu.SemaphoreType.DMA,
-            pltpu.SemaphoreType.DMA((2,)),
+            pltpu.SemaphoreType.DMA((3,)),
         ]
         + pair_scratch(n_dp, length, width)
         + line_scratch(n_dp, length, width),
-        compiler_params=params_of(number, 60),
+        compiler_params=params_of(number),
         cost_estimate=cost(50),
         name="ff_scatter",
     )(dgu, w_gu, h1_all)
@@ -861,10 +899,11 @@
 
 
 def collect_kernel(
-    n_dp, n, g_ref, h_ref, a_ref, w_ref, b_ref, o_ref, h_out, y_ref,
-    sum_ref, acc, pa, qa, pb, qb, local, s1, r1, s2, r2, sh, rh, *line_refs,
+    n_dp, n, g_ref, h_ref, a_hbm, w_hbm, b_hbm, o_ref, h_out, y_ref,
+    a_ref, w_ref, b_ref, sem_in, sum_ref, acc, pa, qa, pb, qb, local, s1, r1, s2, r2, sh, rh, *line_refs,
 ):
     dp, me = lax.axis_index("dp"), lax.axis_index("ctx")
+    loads = loads_of(((a_hbm, a_ref), (w_hbm, w_ref), (b_hbm, b_ref)), sem_in)
     tall = acc.shape[0]
     count, index, place = group_of(n_dp, n, dp, me)
     greet_all(n_dp, n, dp, me)
@@ -883,6 +922,8 @@
 
     def between():
         later.extend(swap(h_ref, h_out, sh, rh, count, index, place))
+        for copy in loads:
+            copy.wait()
         later.append(reduce_ctx(n, dp, me, a_ref, w_ref, cols, sum_ref, pa, qa, pb, qb, s1, r1, s2, r2))
 
     def last():
@@ -917,9 +958,13 @@
             jax.ShapeDtypeStruct(h.shape, BF),
             jax.ShapeDtypeStruct((length, features), BF),
         ),
-        in_specs=[VMEM, ANY, VMEM, VMEM, VMEM],
+        in_specs=[VMEM] + [ANY] * 4,
         out_specs=(VMEM, ANY, VMEM),
         scratch_shapes=[
+            pltpu.VMEM(a.shape, BF),
+            pltpu.VMEM(w.shape, BF),
+            pltpu.VMEM(b.shape, F32),
+            dma((3,)),
             pltpu.VMEM((length, features), F32),
             pltpu.VMEM((tall, width), F32),
             pltpu.VMEM((half, length, features), BF),
@@ -1063,7 +1108,7 @@
             dma((n_dp - 1,)),
             dma((3,)),
         ],
-        compiler_params=params_of(number, 14),
+        compiler_params=params_of(number, 19),
         cost_estimate=cost(35),
         name="total",
     )(
@@ -1207,11 +1252,13 @@
 
 
 def attend_kernel(
-    n_dp, n, x_ref, w_ref, wo_ref, d_ref, t_ref, norm_ref, gain_ref, cos_ref, sin_ref, col_ref, row_ref,
-    y_ref, h_ref, q_ref, k_ref, v_ref, o_ref, pre_ref, scale_ref, lse_ref, wo_all, d_out,
+    n_dp, n, x_hbm, w_hbm, wo_ref, d_ref, t_ref, norm_ref, gain_ref, cos_ref, sin_ref, col_ref, row_ref,
+    y_ref, h_ref, q_out, k_out, v_out, o_ref, pre_out, scale_ref, lse_ref, wo_all, d_out,
     buf, pa, qa, pb, qb, ss, rs, s1, r1, s2, r2, sw, rw, sd, rd, local,
+    x_ref, w_ref, q_ref, k_ref, v_ref, pre_ref, sem_in, sem_out,
 ):
     dp, me = lax.axis_index("dp"), lax.axis_index("ctx")
+    loads = loads_of(((x_hbm, x_ref), (w_hbm, w_ref)), sem_in)
     seq, width = x_ref.shape
     hc = o_ref.shape[1]
     block = min(seq, 256)
@@ -1233,6 +1280,9 @@
     for copy in behind_wo + owns:
         copy.start()
     behind_d, receives = swap(d_ref, d_out, sd, rd, count, mine, place)
+
+    for copy in loads:
+        copy.wait()
 
     @pl.loop(0, seq // block)
     def _(i):
@@ -1276,6 +1326,7 @@
                 _, source = across(dp, k, n_dp)
                 remote(wo_ref, part_of(source), sw.at[k - 1], rw.at[k - 1], (source, me)).wait_recv()
 
+    outs = loads_of(((pre_ref, pre_out), (q_ref, q_out), (k_ref, k_out), (v_ref, v_out)), sem_out)
     cols = slice(0, hc)
     sums = reduce_ctx(
         n, dp, me, o_ref, wo_all, cols, y_ref, pa, qa, pb, qb, s1, r1, s2, r2, before=attention
@@ -1290,7 +1341,8 @@
         copy.wait_recv()
     for copy in sums + behind_wo + behind_d:
         copy.wait_send()
-    owns[1].wait()
+    for copy in outs + owns[1:]:
+        copy.wait()
 
 
 def attend(x_all, w, wo, d, tokens, norm, gain, cos, sine, info_col, info_row, number):
@@ -1314,8 +1366,8 @@
             jax.ShapeDtypeStruct((width, hc), BF),
             jax.ShapeDtypeStruct(d.shape, BF),
         ),
-        in_specs=[VMEM] * 2 + [ANY] * 2 + [VMEM] * 7,
-        out_specs=(VMEM,) * 10 + (ANY,),
+        in_specs=[ANY] * 4 + [VMEM] * 7,
+        out_specs=(VMEM,) * 2 + (ANY,) * 3 + (VMEM, ANY) + (VMEM,) * 3 + (ANY,),
         scratch_shapes=[
             pltpu.VMEM((n, 8, seq), F32),
             pltpu.VMEM((half, length, width), BF),
@@ -1333,6 +1385,12 @@
             dma((2 * n_dp - 1,)),
             dma((2 * n_dp - 1,)),
             dma((2,)),
+            pltpu.VMEM(x_all.shape, BF),
+            pltpu.VMEM(w.shape, BF),
+            *[pltpu.VMEM((seq, hc), BF)] * 3,
+            pltpu.VMEM((seq, 2 * hc), F32),
+            dma((2,)),
+            dma((4,)),
         ],
         compiler_params=params_of(number),
         cost_estimate=cost(60),
@@ -1368,10 +1426,10 @@
 
 
 def attend_back_kernel(
-    n_dp, n, sum_ref, up_ref, branch_ref, norm_ref, wo_hbm, h_ref, o_hbm, col_ref, row_ref, q_ref, k_ref, v_ref, lse_ref,
-    x_hbm, gain_ref, cos_ref, sin_ref, pre_hbm, scale_ref,
+    n_dp, n, sum_ref, up_ref, branch_ref, norm_ref, wo_hbm, h_ref, o_hbm, col_ref, row_ref, q_hbm, k_hbm, v_hbm, lse_ref,
+    x_hbm, gain_ref, cos_hbm, sin_hbm, pre_hbm, scale_ref,
     dh_ref, gp_ref, d_ref, gain_out, g_ref, wv_ref, wo_ref, h_out,
-    x_ref, pre_ref, wall_ref, db_ref, mix_ref, give_ref, e_ref, do_ref, o_ref, dq_ref, dk_ref, dv_ref, mean_ref, buf, go_ref, co_ref, gv_ref, cv_ref,
+    q_ref, k_ref, v_ref, cos_ref, sin_ref, x_ref, pre_ref, wall_ref, db_ref, mix_ref, give_ref, e_ref, do_ref, o_ref, dq_ref, dk_ref, dv_ref, mean_ref, buf, go_ref, co_ref, gv_ref, cv_ref,
     sh, rh, local, sw, rw, sv, rv, ss, rs, sc, rc, sx, rx,
 ):
     dp, me = lax.axis_index("dp"), lax.axis_index("ctx")
@@ -1384,6 +1442,8 @@
     ]
     load = pltpu.make_async_copy(o_hbm, o_ref, local.at[1])
     load.start()
+    tables = ((q_hbm, q_ref), (k_hbm, k_ref), (v_hbm, v_ref), (cos_hbm, cos_ref), (sin_hbm, sin_ref))
+    loads = loads_of(tables, local, 6)
     length, width = dh_ref.shape
     block = min(seq, 256)
     count, index, place = group_of(n_dp, n, dp, me)
@@ -1478,6 +1538,8 @@
             dk_ref[:, part] += t_dot(d_scores, query)
             dv_ref[:, part] += t_dot(probs.astype(BF), back)
 
+    for copy in loads:
+        copy.wait()
     pl.loop(0, seq // block)(attention)
 
     for copy in later:
@@ -1550,9 +1612,11 @@
             jax.ShapeDtypeStruct((share // n_dp, n * hc), BF),
             jax.ShapeDtypeStruct(h.shape, BF),
         ),
-        in_specs=[VMEM] * 4 + [ANY] * 3 + [VMEM] * 6 + [ANY] + [VMEM] * 3 + [ANY, VMEM],
+        in_specs=[VMEM] * 4 + [ANY] * 3 + [VMEM] * 2 + [ANY] * 3 + [VMEM, ANY, VMEM] + [ANY] * 3 + [VMEM],
         out_specs=(VMEM,) * 7 + (ANY,),
         scratch_shapes=[
+            *[pltpu.VMEM((seq, hc), BF)] * 3,
+            *[pltpu.VMEM(cos.shape, F32)] * 2,
             pltpu.VMEM(x.shape, BF),
             pltpu.VMEM(pre.shape, F32),
             pltpu.VMEM(wo_all.shape, BF),
@@ -1573,7 +1637,7 @@
             pltpu.VMEM((n_dp - 1, width // n_dp, hc), BF),
             dma((2 * n_dp - 1,)),
             dma((2 * n_dp - 1,)),
-            dma((6,)),
+            dma((11,)),
             dma((n_dp - 1,)),
             dma((n_dp - 1,)),
             dma((n_dp - 1,)),
@@ -1585,7 +1649,7 @@
             dma((n - 1,)),
             dma((n - 1,)),
         ],
-        compiler_params=params_of(number, 56),
+        compiler_params=params_of(number),
         cost_estimate=cost(75),
         name="attend_back",
     )(sums, up, branch, norm, wo_all, h, o_all, info_col, info_row, q, k, v, lse, x, gain, cos, sine, pre, scale)
@@ -1635,23 +1699,9 @@
 
     w_gu, w_qkv, w_o, x_all, w_d = start(params, tokens, 1)
     w_gu = gather_pairs(w_gu)
-    w_qkv = gather_dp(w_qkv.reshape(n_ctx * rows, 3 * hc), 2)
-
-    indices = jnp.arange(seq, dtype=jnp.int32)
-    owners = indices // length
-    placed = jnp.sum(
-        jnp.where(
-            owners[:, None] == jnp.arange(n_ctx, dtype=jnp.int32)[None, :], block_place[None, :], 0
-        ),
-        axis=1,
+    w_qkv, (cos_tab, sine_tab, info_row, info_col) = gather_dp(
+        w_qkv.reshape(n_ctx * rows, 3 * hc), block_place, documents, 2
     )
-    pos = placed * length + indices % length
-    docs = documents[0]
-    info_row = jnp.concatenate([pos[None], docs[None], jnp.zeros((6, seq), jnp.int32)])
-    info_col = info_row.T
-    cos_tab, sine_tab = rope_tables(pos, HD)
-    cos_tab = jnp.concatenate([cos_tab, cos_tab], axis=1)
-    sine_tab = jnp.concatenate([-sine_tab, sine_tab], axis=1)
     my_gains = lax.dynamic_slice_in_dim(gains[:2], me_ctx * hc, hc, axis=1)
     tables = (my_gains, cos_tab, sine_tab, info_col, info_row)
 

time: 640 us -> 630 us (0.984)
  local copies, waits for them, and re-layouts: 19.8 us -> 6.33 us
    unnamed x66 -> x32, local copies, waits for them, and re-layouts: 18.8 us -> 5.12 us
    pallas_call x1, Pallas kernels: 45.9 us -> 54.1 us  [total_over(): pl.pallas_call(functools.partial(total_kernel, n_dp, n), out_shape=(jax.S...]
  transfers between devices with their start and end apart: 5 -> 5, of which waited for: 0 -> 0; matrix products, arithmetic and copies ran while one was open for 1% -> 0% of each run, Pallas kernels for 60% -> 61%
where the time goes in v10:
time: 630 us; the launch traced here: 621 us
  Pallas kernels  599 us (95%)
  between operations  14.3 us (2%)
  local copies, waits for them, and re-layouts  6.33 us (1%)
    pallas_call x1, Pallas kernels, ff_forward(): pl.pallas_call(functools.partial(ff_forward_kernel, n_dp, n), out_shape=(...  107 us
    pallas_call x1, Pallas kernels, attend_back(): pl.pallas_call(functools.partial(attend_back_kernel, n_dp, n), out_shape=...  77.6 us
    pallas_call x1, Pallas kernels, gather_dp(): pl.pallas_call(functools.partial(gather_dp_kernel, n, n_ctx), out_shape=(...  67.7 us
    pallas_call x1, Pallas kernels, collect(): pl.pallas_call(functools.partial(collect_kernel, n_dp, n), out_shape=(jax...  65 us
    pallas_call x1, Pallas kernels, ff_scatter(): pl.pallas_call(functools.partial(ff_scatter_kernel, n_dp, n), out_shape=(...  60 us
    pallas_call x1, Pallas kernels, attend(): pl.pallas_call(functools.partial(attend_kernel, n_dp, n), out_shape=(jax....  56.8 us
    pallas_call x1, Pallas kernels, total_over(): pl.pallas_call(functools.partial(total_kernel, n_dp, n), out_shape=(jax.S...  54.1 us
    pallas_call x1, Pallas kernels, ff_back(): pl.pallas_call(functools.partial(ff_back_kernel, n_dp), out_shape=(jax.Sh...  50.9 us
  transfers between devices with their start and end apart: 5, of which 0 were waited for; matrix products, arithmetic and copies ran while one was open for 0% of the time, Pallas kernels for 61%

profile of v10, /device:TPU:0, one launch (start us, length us, event | category | flops | bytes accessed | tf_op | source)
XLA Modules:
  0.0 620.5 jit_solution(4923730895914052192)
XLA Ops:
  7.2 0.0 all-gather.4.cloned.1.call-start
  7.2 0.0 slice-start
  7.2 0.0 copy-start.7
  7.2 44.0 %start.1 = (bf16[8,64,2048]{2,1,0:T(8,128)(2,1)}, bf16[8,64,768]{2,1,0:T(8,128)(2,1)}, bf16[8,64,256]{2,1,0:T(8,128)(2,1)}, bf16[8,128,2048]{2,1,0:T(8,128)(2,1)}, bf16[8,64,1024]{2,1,0:T(8,128)(2,1)}) custom-call(f32[64,32768]{1,0:T(8,128)} %p_hbm.3, bf16[128,2048]{1,0:T(8,128)(2,1)} %bitcast.36), custom_call_target="tpu_custom_call" | custom-call | bytes 162000000 | tf_op jit(solution)/shard_map/start/pallas_call | solution.py:872
  51.2 0.0 all-gather.4.cloned.1.call-update
  51.2 0.0 all-gather.6.cloned.1.call-start
  51.3 67.7 %gather_dp.1 = (f32[1024,128]{1,0:T(8,128)}, f32[1024,128]{1,0:T(8,128)}, f32[8,1024]{1,0:T(8,128)}, f32[1024,8]{1,0:T(8,128)}, bf16[4,512,768]{2,1,0:T(8,128)(2,1)}) custom-call(s32[8]{0:T(128)} %place_ref.1, s32[1,1024]{1,0:T(1,128)} %doc_ref.1, f32[1,128]{1,0:T(1,128)} %constant.12.clone.freq_ref, bf16[512,768]{1,0:T(8,128)(2,1)} %bitcast.44), custom_call_target="tpu_custom_call" | custom-call | bytes 216000000 | tf_op jit(solution)/shard_map/gather_dp/pallas_call | solution.py:178
  119.0 0.0 slice-done
  119.0 0.6 constant_dynamic-slice_fusion.gain_ref
  119.6 0.0 copy-done.7
  119.6 0.6 fusion
  120.3 56.8 %attend.1 = (f32[128,2048]{1,0:T(8,128)}, f32[128,2048]{1,0:T(8,128)}, bf16[1024,256]{1,0:T(8,128)(2,1)}, bf16[1024,256]{1,0:T(8,128)(2,1)}, bf16[1024,256]{1,0:...) custom-call(bf16[1024,2048]{1,0:T(8,128)(2,1)} %bitcast.28, ...), custom_call_target="tpu_custom_call" | custom-call | bytes 216000000 | tf_op jit(solution)/shard_map/attend/pallas_call | solution.py:1354
  177.0 0.0 all-gather.4.cloned.1.call-done
  177.1 107.4 %ff_forward.1 = (bf16[128,2048]{1,0:T(8,128)(2,1)}, bf16[128,2048]{1,0:T(8,128)(2,1)}, f32[1,2048]{1,0:T(1,128)}, bf16[1024,2048]{1,0:T(8,128)(2,1)}, f32[1024,2...) custom-call(f32[128,2048]{1,0:T(8,128)} %get-tuple-element.78.h_ref, ...), custom_call_target="tpu_custom_call" | custom-call | bytes 324000000 | tf_op jit(solution)/shard_map/ff_forward/pallas_call | solution.py:591
  284.5 0.0 all-gather.6.cloned.1.call-update
  284.5 0.0 reduce-scatter.4.cloned.1.call-start
  284.5 50.9 %ff_back.1 = (bf16[1024,2048]{1,0:T(8,128)(2,1)}, bf16[4,4,128,1024]{3,2,1,0:T(8,128)(2,1)}) custom-call(bf16[128,2048]{1,0:T(8,128)(2,1)} %get-tuple-element.85.dm_ref, bf16[1024,1024]{1,0:T(8,128)(2,1)} %get-tuple-element.86.hid_ref, bf16[2048,1024]{1,0:T(8,128)(2,1)} %get-tuple-element.87.d_hbm, f32[1024,2048]{1,0:T(8,128)} %get-tuple-element.88.pre_hbm), custom_call_target="tpu_custom_call" | custom-call | bytes 162000000 | tf_op jit(solution)/shard_map/ff_back/pallas_call | solution.py:694
  335.5 0.0 reduce-scatter.4.cloned.1.call-update
  335.5 0.0 reduce-scatter.6.cloned.1.call-start
  335.5 60.0 %ff_scatter.1 = (f32[128,2048]{1,0:T(8,128)}, bf16[4,4,128,1024]{3,2,1,0:T(8,128)(2,1)}, bf16[4,4,128,1024]{3,2,1,0:T(8,128)(2,1)}) custom-call(bf16[1024,2048]{1,0:T(8,128)(2,1)} %get-tuple-element.89.dgu_hbm, bf16[4,4,128,2048]{3,2,1,0:T(8,128)(2,1)} %bitcast.27, bf16[1024,2048]{1,0:T(8,128)(2,1)} %get-tuple-element.90.all_hbm), custom_call_target="tpu_custom_call" | custom-call | bytes 180000000 | tf_op jit(solution)/shard_map/ff_scatter/pallas_call | solution.py:767
  395.6 0.0 reduce-scatter.6.cloned.1.call-update
  395.6 0.2 reduce-scatter.8.cloned.1.call-start
  395.8 0.4 reduce-scatter.8.cloned.1.call-update
  396.2 0.0 all-gather.6.cloned.1.call-done
  396.2 0.0 reduce-scatter.4.cloned.1.call-done
  396.2 77.6 %attend_back.1 = (f32[128,2048]{1,0:T(8,128)}, f32[1,2048]{1,0:T(1,128)}, bf16[1024,768]{1,0:T(8,128)(2,1)}, f32[2,256]{1,0:T(2,128)}, bf16[2048,512]{1,0:T(8,12...) custom-call(f32[128,2048]{1,0:T(8,128)} %get-tuple-element.91.sum_ref, ...), custom_call_target="tpu_custom_call" | custom-call | bytes 270000000 | tf_op jit(solution)/shard_map/attend_back/pallas_call | solution.py:1603
  473.8 0.0 reduce-scatter.6.cloned.1.call-done
  473.9 0.0 copy-start
  473.9 0.0 copy-start.3
  473.9 0.0 copy-start.6
  473.9 0.0 copy-start.10
  473.9 0.0 copy-start.11
  473.9 0.0 copy-start.12
  473.9 65.0 %collect.1 = (bf16[512,512]{1,0:T(8,128)(2,1)}, bf16[8,64,1024]{2,1,0:T(8,128)(2,1)}, bf16[128,2048]{1,0:T(8,128)(2,1)}) custom-call(bf16[2048,512]{1,0:T(8,128)(2,1)} %get-tuple-element.102.g_ref, bf16[8,64,1024]{2,1,0:T(8,128)(2,1)} %bitcast.42, bf16[1024,768]{1,0:T(8,128)(2,1)} %get-tuple-element.104.a_hbm, bf16[2048,768]{1,0:T(8,128)(2,1)} %bitcast.31, ...), custom_call_target="tpu_custom_call" | custom-call | bytes 252000000 | tf_op jit(solution)/shard_map/collect/pallas_call | solution.py:954
  539.0 0.0 reduce-scatter.8.cloned.1.call-done
  539.0 0.0 copy-done
  539.0 0.0 copy-done.3
  539.0 0.0 copy-done.6
  539.0 0.0 copy-done.10
  539.0 0.0 copy-done.11
  539.0 0.0 copy-done.12
  539.0 0.0 copy-start.1
  539.1 1.2 copy-done.1
  540.3 0.0 copy-start.4
  540.3 1.2 copy-done.4
  541.5 0.0 copy-start.5
  541.5 1.0 copy-done.5
  542.5 0.0 copy-start.2
  542.5 0.0 copy-start.8
  542.5 0.0 copy-start.9
  542.5 54.1 %total.1 = (bf16[8,64,768]{2,1,0:T(8,128)(2,1)S(1)}, bf16[8,64,1024]{2,1,0:T(8,128)(2,1)S(1)}, f32[8,2048]{1,0:T(8,128)S(1)}, f32[64,32768]{1,0:T(8,128)S(1)}, f...) custom-call(bf16[8,64,512]{2,1,0:T(8,128)(2,1)S(1)} %bitcast.24, bf16[8,64,256]{2,1,0:T(8,128)(2,1)S(1)} %bitcast.25, ...), custom_call_target="tpu_custom_call" | custom-call | bytes 126000000 | tf_op jit(solution)/shard_map/total/pallas_call | solution.py:1076
  596.7 0.0 copy-done.2
  596.7 0.0 copy-done.8
  596.7 0.0 copy-done.9
  596.7 0.0 copy-start.13
  596.7 0.0 copy-start.14
  596.7 15.5 %adam.1 = (f32[1,1]{1,0:T(1,128)}, f32[4,2048]{1,0:T(4,128)}, f32[4,2048]{1,0:T(4,128)}, f32[4,2048]{1,0:T(4,128)}, f32[64,32768]{1,0:T(8,128)}, /*index=5*/f32[64,32768]{1,0:T(8,128)}, f32[64,32768]{1,0:T(8,128)}) custom-call(f32[8,2048]{1,0:T(8,128)S(1)} %get-tuple-element.116.sum_ref, f32[4,2048]{1,0:T(4,128)S(1)} %copy-done.7, f32[4,2048]{1,0:T(4,128)S(1)} %copy-done.8, ...), custom_call_target="tpu_custom_call" | custom-call | tf_op jit(solution)/shard_map/adam/pallas_call | solution.py:1182
  612.2 0.0 copy-done.13
  612.2 0.8 copy.22
  613.0 0.0 copy-done.14
  613.0 0.8 copy.23
Async XLA Ops:
  7.2 169.9 %all-gather.4.cloned.1.call-start = ((), (), s32[]{:S(2)}) async-start(), calls=%async_computation.3 | async-start | bytes 10485760 | tf_op jit(solution)/shard_map/all_gather | solution.py:1685
  7.2 111.8 %slice-start = ((f32[4,2048]{1,0:T(4,128)}), f32[2,2048]{1,0:T(2,128)S(1)}, s32[]{:S(2)}) async-start(f32[4,2048]{1,0:T(4,128)} %gp_ref.1), calls=%async_computation.8 | async-start | bytes 32768 | tf_op jit(solution)/shard_map/slice | solution.py:1705
  7.2 112.4 %copy-start.7 = (f32[4,2048]{1,0:T(4,128)S(1)}, f32[4,2048]{1,0:T(4,128)}, u32[]{:S(2)}) copy-start(f32[4,2048]{1,0:T(4,128)} %gp_ref.1) | copy-start | bytes 98308
  51.2 345.0 %all-gather.6.cloned.1.call-start = ((), (), s32[]{:S(2)}) async-start(), calls=%async_computation.7 | async-start | bytes 4718592 | tf_op jit(solution)/shard_map/all_gather | solution.py:1716
  284.5 111.8 %reduce-scatter.4.cloned.1.call-start = ((), (), s32[]{:S(2)}) async-start(), calls=%async_computation.4 | async-start | bytes 5242880 | tf_op jit(solution)/shard_map/reduce_scatter | solution.py:1691
  335.5 138.4 %reduce-scatter.6.cloned.1.call-start = ((), (), s32[]{:S(2)}) async-start(), calls=%async_computation.5 | async-start | bytes 5242880 | tf_op jit(solution)/shard_map/reduce_scatter | solution.py:1691
  395.6 143.4 %reduce-scatter.8.cloned.1.call-start = ((), (), s32[]{:S(2)}) async-start(), calls=%async_computation.6 | async-start | bytes 5242880 | tf_op jit(solution)/shard_map/reduce_scatter | solution.py:1691
  473.9 65.1 %copy-start = (bf16[8,64,1024]{2,1,0:T(8,128)(2,1)S(1)}, bf16[8,64,1024]{2,1,0:T(8,128)(2,1)}, u32[]{:S(2)}) copy-start(bf16[8,64,1024]{2,1,0:T(8,128)(2,1)} %get-tuple-element.112.gd_ref) | copy-start | bytes 3145732
  473.9 65.1 %copy-start.3 = (bf16[64,2048]{1,0:T(8,128)(2,1)S(1)}, bf16[64,2048]{1,0:T(8,128)(2,1)}, u32[]{:S(2)}) copy-start(bf16[64,2048]{1,0:T(8,128)(2,1)} %get-tuple-element.109.go_ref) | copy-start | bytes 786436
  473.9 65.1 %copy-start.6 = (bf16[512,256]{1,0:T(8,128)(2,1)S(1)}, bf16[512,256]{1,0:T(8,128)(2,1)}, u32[]{:S(2)}) copy-start(bf16[512,256]{1,0:T(8,128)(2,1)} %get-tuple-element.108) | copy-start | bytes 786436
  473.9 65.1 %copy-start.10 = (f32[1,2048]{1,0:T(1,128)S(1)}, f32[1,2048]{1,0:T(1,128)}, u32[]{:S(2)}) copy-start(f32[1,2048]{1,0:T(1,128)} %get-tuple-element.115.ff_gain) | copy-start | bytes 24580
  473.9 65.1 %copy-start.11 = (f32[1,2048]{1,0:T(1,128)S(1)}, f32[1,2048]{1,0:T(1,128)}, u32[]{:S(2)}) copy-start(f32[1,2048]{1,0:T(1,128)} %get-tuple-element.114.attn_gain) | copy-start | bytes 24580
  473.9 65.1 %copy-start.12 = (f32[2,256]{1,0:T(2,128)S(1)}, f32[2,256]{1,0:T(2,128)}, u32[]{:S(2)}) copy-start(f32[2,256]{1,0:T(2,128)} %get-tuple-element.113.qk_gain) | copy-start | bytes 6148
  539.0 1.2 copy-start.1
  540.3 1.2 copy-start.4
  541.5 1.0 copy-start.5
  542.5 54.1 %copy-start.2 = (bf16[8,64,1024]{2,1,0:T(8,128)(2,1)S(1)}, bf16[8,64,1024]{2,1,0:T(8,128)(2,1)}, u32[]{:S(2)}) copy-start(bf16[8,64,1024]{2,1,0:T(8,128)(2,1)} %get-tuple-element.111.gg_ref) | copy-start | bytes 3145732
  542.5 54.2 %copy-start.8 = (f32[4,2048]{1,0:T(4,128)S(1)}, f32[4,2048]{1,0:T(4,128)}, u32[]{:S(2)}) copy-start(f32[4,2048]{1,0:T(4,128)} %gm_ref.1) | copy-start | bytes 98308
  542.5 54.2 %copy-start.9 = (f32[4,2048]{1,0:T(4,128)S(1)}, f32[4,2048]{1,0:T(4,128)}, u32[]{:S(2)}) copy-start(f32[4,2048]{1,0:T(4,128)} %gv_ref.1) | copy-start | bytes 98308
  596.7 15.5 %copy-start.13 = (bf16[128,2048]{1,0:T(8,128)(2,1)S(1)}, bf16[128,2048]{1,0:T(8,128)(2,1)}, u32[]{:S(2)}) copy-start(bf16[128,2048]{1,0:T(8,128)(2,1)} %get-tuple-element.82) | copy-start | bytes 1572868
  596.7 16.3 %copy-start.14 = (bf16[128,2048]{1,0:T(8,128)(2,1)S(1)}, bf16[128,2048]{1,0:T(8,128)(2,1)}, u32[]{:S(2)}) copy-start(bf16[128,2048]{1,0:T(8,128)(2,1)} %get-tuple-element.106) | copy-start | bytes 1572868
Sparse Core Ops, SparseCore 0:
  51.4 98.8 all-gather.3
  284.6 36.6 all-gather.5
  335.6 53.4 reduce-scatter.3
  395.7 65.7 reduce-scatter.5
  464.4 65.1 reduce-scatter.7

commit v11 on v10

--- a/solution.py
+++ b/solution.py
@@ -131,8 +131,8 @@
 
 
 def gather_dp_kernel(
-    n, n_ctx, place_ref, doc_ref, freq_ref, x_ref, cos_ref, sin_ref, row_ref, col_ref, o_ref,
-    local, sr, rr, sl, rl,
+    n, n_ctx, place_ref, doc_ref, freq_ref, x_ref, cos_out, sin_out, row_ref, col_ref, o_ref,
+    cos_ref, sin_ref, sem_out, local, sr, rr, sl, rl,
 ):
     me, ctx = lax.axis_index("dp"), lax.axis_index("ctx")
 
@@ -150,6 +150,8 @@
     def left(s, block=None):
         b = me + s if block is None else block
         return remote(x_ref if s == 0 else o_ref.at[b], o_ref.at[b], sl.at[s], rl.at[s], here(me - 1))
+
+    outs = []
 
     def tables():
         length = cos_ref.shape[0] // n_ctx
@@ -165,9 +167,11 @@
             sin_ref[rows, :] = jnp.sin(angles) * sign
             row_ref[0:1, rows] = (base + lax.broadcasted_iota(jnp.int32, (1, length), 1)).astype(F32)
         col_ref[...] = jnp.transpose(row_ref[...])
+        outs.extend(loads_of(((cos_ref, cos_out), (sin_ref, sin_out)), sem_out))
 
     line_steps(n, me, right, left, tables)
-    own.wait()
+    for copy in outs + [own]:
+        copy.wait()
 
 
 def gather_dp(x, places, docs, number):
@@ -185,8 +189,10 @@
             jax.ShapeDtypeStruct((n,) + x.shape, x.dtype),
         ),
         in_specs=[pl.BlockSpec(memory_space=pltpu.SMEM), VMEM, VMEM, ANY],
-        out_specs=(VMEM,) * 4 + (ANY,),
-        scratch_shapes=[pltpu.SemaphoreType.DMA] + [pltpu.SemaphoreType.DMA((n - 1,))] * 4,
+        out_specs=(ANY,) * 2 + (VMEM,) * 2 + (ANY,),
+        scratch_shapes=[pltpu.VMEM((seq, HD), F32)] * 2
+        + [pltpu.SemaphoreType.DMA((2,))]
+        + [pltpu.SemaphoreType.DMA] + [pltpu.SemaphoreType.DMA((n - 1,))] * 4,
         compiler_params=params_of(number),
         cost_estimate=cost(60),
         name="gather_dp",
@@ -899,11 +905,10 @@
 
 
 def collect_kernel(
-    n_dp, n, g_ref, h_ref, a_hbm, w_hbm, b_hbm, o_ref, h_out, y_ref,
-    a_ref, w_ref, b_ref, sem_in, sum_ref, acc, pa, qa, pb, qb, local, s1, r1, s2, r2, sh, rh, *line_refs,
+    n_dp, n, g_ref, h_ref, a_ref, w_ref, b_ref, o_ref, h_out, y_ref,
+    sum_ref, acc, pa, qa, pb, qb, local, s1, r1, s2, r2, sh, rh, *line_refs,
 ):
     dp, me = lax.axis_index("dp"), lax.axis_index("ctx")
-    loads = loads_of(((a_hbm, a_ref), (w_hbm, w_ref), (b_hbm, b_ref)), sem_in)
     tall = acc.shape[0]
     count, index, place = group_of(n_dp, n, dp, me)
     greet_all(n_dp, n, dp, me)
@@ -922,8 +927,6 @@
 
     def between():
         later.extend(swap(h_ref, h_out, sh, rh, count, index, place))
-        for copy in loads:
-            copy.wait()
         later.append(reduce_ctx(n, dp, me, a_ref, w_ref, cols, sum_ref, pa, qa, pb, qb, s1, r1, s2, r2))
 
     def last():
@@ -958,13 +961,9 @@
             jax.ShapeDtypeStruct(h.shape, BF),
             jax.ShapeDtypeStruct((length, features), BF),
         ),
-        in_specs=[VMEM] + [ANY] * 4,
+        in_specs=[VMEM, ANY, VMEM, VMEM, VMEM],
         out_specs=(VMEM, ANY, VMEM),
         scratch_shapes=[
-            pltpu.VMEM(a.shape, BF),
-            pltpu.VMEM(w.shape, BF),
-            pltpu.VMEM(b.shape, F32),
-            dma((3,)),
             pltpu.VMEM((length, features), F32),
             pltpu.VMEM((tall, width), F32),
             pltpu.VMEM((half, length, features), BF),

time: 630 us -> 623 us (0.989)
  Pallas kernels: 599 us -> 592 us
    pallas_call x1, Pallas kernels: 54.1 us -> 46 us  [total_over(): pl.pallas_call(functools.partial(total_kernel, n_dp, n), out_shape=(jax.S...]
  transfers between devices with their start and end apart: 5 -> 5, of which waited for: 0 -> 0; matrix products, arithmetic and copies ran while one was open for 0% -> 0% of each run, Pallas kernels for 61% -> 62%
where the time goes in v11:
time: 623 us; the launch traced here: 614 us
  Pallas kernels  592 us (95%)
  between operations  14.3 us (2%)
  local copies, waits for them, and re-layouts  6.33 us (1%)
    pallas_call x1, Pallas kernels, ff_forward(): pl.pallas_call(functools.partial(ff_forward_kernel, n_dp, n), out_shape=(...  107 us
    pallas_call x1, Pallas kernels, attend_back(): pl.pallas_call(functools.partial(attend_back_kernel, n_dp, n), out_shape=...  77.6 us
    pallas_call x1, Pallas kernels, gather_dp(): pl.pallas_call(functools.partial(gather_dp_kernel, n, n_ctx), out_shape=(...  67.4 us
    pallas_call x1, Pallas kernels, collect(): pl.pallas_call(functools.partial(collect_kernel, n_dp, n), out_shape=(jax...  66.8 us
    pallas_call x1, Pallas kernels, ff_scatter(): pl.pallas_call(functools.partial(ff_scatter_kernel, n_dp, n), out_shape=(...  60 us
    pallas_call x1, Pallas kernels, attend(): pl.pallas_call(functools.partial(attend_kernel, n_dp, n), out_shape=(jax....  57.1 us
    pallas_call x1, Pallas kernels, ff_back(): pl.pallas_call(functools.partial(ff_back_kernel, n_dp), out_shape=(jax.Sh...  50.9 us
    pallas_call x1, Pallas kernels, total_over(): pl.pallas_call(functools.partial(total_kernel, n_dp, n), out_shape=(jax.S...  46 us
  transfers between devices with their start and end apart: 5, of which 0 were waited for; matrix products, arithmetic and copies ran while one was open for 0% of the time, Pallas kernels for 62%

profile of v11, /device:TPU:0, one launch (start us, length us, event | category | flops | bytes accessed | tf_op | source)
XLA Modules:
  0.0 613.8 jit_solution(15926604775934691276)
XLA Ops:
  7.2 0.0 all-gather.4.cloned.1.call-start
  7.2 0.0 slice-start
  7.2 0.0 copy-start.7
  7.2 44.0 %start.1 = (bf16[8,64,2048]{2,1,0:T(8,128)(2,1)}, bf16[8,64,768]{2,1,0:T(8,128)(2,1)}, bf16[8,64,256]{2,1,0:T(8,128)(2,1)}, bf16[8,128,2048]{2,1,0:T(8,128)(2,1)}, bf16[8,64,1024]{2,1,0:T(8,128)(2,1)}) custom-call(f32[64,32768]{1,0:T(8,128)} %p_hbm.3, bf16[128,2048]{1,0:T(8,128)(2,1)} %bitcast.36), custom_call_target="tpu_custom_call" | custom-call | bytes 162000000 | tf_op jit(solution)/shard_map/start/pallas_call | solution.py:878
  51.2 0.0 all-gather.4.cloned.1.call-update
  51.2 0.0 all-gather.6.cloned.1.call-start
  51.3 67.4 %gather_dp.1 = (f32[1024,128]{1,0:T(8,128)}, f32[1024,128]{1,0:T(8,128)}, f32[8,1024]{1,0:T(8,128)}, f32[1024,8]{1,0:T(8,128)}, bf16[4,512,768]{2,1,0:T(8,128)(2,1)}) custom-call(s32[8]{0:T(128)} %place_ref.1, s32[1,1024]{1,0:T(1,128)} %doc_ref.1, f32[1,128]{1,0:T(1,128)} %constant.12.clone.freq_ref, bf16[512,768]{1,0:T(8,128)(2,1)} %bitcast.44), custom_call_target="tpu_custom_call" | custom-call | bytes 216000000 | tf_op jit(solution)/shard_map/gather_dp/pallas_call | solution.py:182
  118.7 0.0 slice-done
  118.7 0.6 constant_dynamic-slice_fusion.gain_ref
  119.3 0.0 copy-done.7
  119.3 0.6 fusion
  119.9 57.1 %attend.1 = (f32[128,2048]{1,0:T(8,128)}, f32[128,2048]{1,0:T(8,128)}, bf16[1024,256]{1,0:T(8,128)(2,1)}, bf16[1024,256]{1,0:T(8,128)(2,1)}, bf16[1024,256]{1,0:...) custom-call(bf16[1024,2048]{1,0:T(8,128)(2,1)} %bitcast.28, ...), custom_call_target="tpu_custom_call" | custom-call | bytes 216000000 | tf_op jit(solution)/shard_map/attend/pallas_call | solution.py:1353
  177.0 0.0 all-gather.4.cloned.1.call-done
  177.1 107.0 %ff_forward.1 = (bf16[128,2048]{1,0:T(8,128)(2,1)}, bf16[128,2048]{1,0:T(8,128)(2,1)}, f32[1,2048]{1,0:T(1,128)}, bf16[1024,2048]{1,0:T(8,128)(2,1)}, f32[1024,2...) custom-call(f32[128,2048]{1,0:T(8,128)} %get-tuple-element.78.h_ref, ...), custom_call_target="tpu_custom_call" | custom-call | bytes 324000000 | tf_op jit(solution)/shard_map/ff_forward/pallas_call | solution.py:597
  284.1 0.0 all-gather.6.cloned.1.call-update
  284.1 0.0 reduce-scatter.4.cloned.1.call-start
  284.2 50.9 %ff_back.1 = (bf16[1024,2048]{1,0:T(8,128)(2,1)}, bf16[4,4,128,1024]{3,2,1,0:T(8,128)(2,1)}) custom-call(bf16[128,2048]{1,0:T(8,128)(2,1)} %get-tuple-element.85.dm_ref, bf16[1024,1024]{1,0:T(8,128)(2,1)} %get-tuple-element.86.hid_ref, bf16[2048,1024]{1,0:T(8,128)(2,1)} %get-tuple-element.87.d_hbm, f32[1024,2048]{1,0:T(8,128)} %get-tuple-element.88.pre_hbm), custom_call_target="tpu_custom_call" | custom-call | bytes 162000000 | tf_op jit(solution)/shard_map/ff_back/pallas_call | solution.py:700
  335.1 0.0 reduce-scatter.4.cloned.1.call-update
  335.1 0.0 reduce-scatter.6.cloned.1.call-start
  335.2 60.0 %ff_scatter.1 = (f32[128,2048]{1,0:T(8,128)}, bf16[4,4,128,1024]{3,2,1,0:T(8,128)(2,1)}, bf16[4,4,128,1024]{3,2,1,0:T(8,128)(2,1)}) custom-call(bf16[1024,2048]{1,0:T(8,128)(2,1)} %get-tuple-element.89.dgu_hbm, bf16[4,4,128,2048]{3,2,1,0:T(8,128)(2,1)} %bitcast.27, bf16[1024,2048]{1,0:T(8,128)(2,1)} %get-tuple-element.90.all_hbm), custom_call_target="tpu_custom_call" | custom-call | bytes 180000000 | tf_op jit(solution)/shard_map/ff_scatter/pallas_call | solution.py:773
  395.2 0.0 reduce-scatter.6.cloned.1.call-update
  395.2 0.2 reduce-scatter.8.cloned.1.call-start
  395.5 0.4 reduce-scatter.8.cloned.1.call-update
  395.8 0.0 all-gather.6.cloned.1.call-done
  395.9 0.0 reduce-scatter.4.cloned.1.call-done
  395.9 77.6 %attend_back.1 = (f32[128,2048]{1,0:T(8,128)}, f32[1,2048]{1,0:T(1,128)}, bf16[1024,768]{1,0:T(8,128)(2,1)}, f32[2,256]{1,0:T(2,128)}, bf16[2048,512]{1,0:T(8,12...) custom-call(f32[128,2048]{1,0:T(8,128)} %get-tuple-element.91.sum_ref, ...), custom_call_target="tpu_custom_call" | custom-call | bytes 270000000 | tf_op jit(solution)/shard_map/attend_back/pallas_call | solution.py:1602
  473.5 0.0 reduce-scatter.6.cloned.1.call-done
  473.5 0.0 copy-start
  473.5 0.0 copy-start.3
  473.5 0.0 copy-start.6
  473.5 0.0 copy-start.10
  473.5 0.0 copy-start.11
  473.5 0.0 copy-start.12
  473.5 66.8 %collect.1 = (bf16[512,512]{1,0:T(8,128)(2,1)}, bf16[8,64,1024]{2,1,0:T(8,128)(2,1)}, bf16[128,2048]{1,0:T(8,128)(2,1)}) custom-call(bf16[2048,512]{1,0:T(8,128)(2,1)} %get-tuple-element.102.g_ref, bf16[8,64,1024]{2,1,0:T(8,128)(2,1)} %bitcast.42, bf16[1024,768]{1,0:T(8,128)(2,1)} %get-tuple-element.104.a_ref, bf16[2048,768]{1,0:T(8,128)(2,1)} %bitcast.31, ...), custom_call_target="tpu_custom_call" | custom-call | bytes 252000000 | tf_op jit(solution)/shard_map/collect/pallas_call | solution.py:957
  540.4 0.0 reduce-scatter.8.cloned.1.call-done
  540.4 0.0 copy-done
  540.4 0.0 copy-done.3
  540.4 0.0 copy-done.6
  540.4 0.0 copy-done.10
  540.4 0.0 copy-done.11
  540.5 0.0 copy-done.12
  540.5 0.0 copy-start.1
  540.5 1.2 copy-done.1
  541.7 0.0 copy-start.4
  541.7 1.2 copy-done.4
  542.9 0.0 copy-start.5
  542.9 1.0 copy-done.5
  544.0 0.0 copy-start.2
  544.0 0.0 copy-start.8
  544.0 0.0 copy-start.9
  544.0 46.0 %total.1 = (bf16[8,64,768]{2,1,0:T(8,128)(2,1)S(1)}, bf16[8,64,1024]{2,1,0:T(8,128)(2,1)S(1)}, f32[8,2048]{1,0:T(8,128)S(1)}, f32[64,32768]{1,0:T(8,128)S(1)}, f...) custom-call(bf16[8,64,512]{2,1,0:T(8,128)(2,1)S(1)} %bitcast.24, bf16[8,64,256]{2,1,0:T(8,128)(2,1)S(1)} %bitcast.25, ...), custom_call_target="tpu_custom_call" | custom-call | bytes 126000000 | tf_op jit(solution)/shard_map/total/pallas_call | solution.py:1075
  590.0 0.0 copy-done.2
  590.0 0.0 copy-done.8
  590.0 0.0 copy-done.9
  590.0 0.0 copy-start.13
  590.0 0.0 copy-start.14
  590.0 15.5 %adam.1 = (f32[1,1]{1,0:T(1,128)}, f32[4,2048]{1,0:T(4,128)}, f32[4,2048]{1,0:T(4,128)}, f32[4,2048]{1,0:T(4,128)}, f32[64,32768]{1,0:T(8,128)}, /*index=5*/f32[64,32768]{1,0:T(8,128)}, f32[64,32768]{1,0:T(8,128)}) custom-call(f32[8,2048]{1,0:T(8,128)S(1)} %get-tuple-element.116.sum_ref, f32[4,2048]{1,0:T(4,128)S(1)} %copy-done.7, f32[4,2048]{1,0:T(4,128)S(1)} %copy-done.8, ...), custom_call_target="tpu_custom_call" | custom-call | tf_op jit(solution)/shard_map/adam/pallas_call | solution.py:1181
  605.5 0.0 copy-done.13
  605.5 0.8 copy.22
  606.3 0.0 copy-done.14
  606.3 0.8 copy.23
Async XLA Ops:
  7.2 169.9 %all-gather.4.cloned.1.call-start = ((), (), s32[]{:S(2)}) async-start(), calls=%async_computation.3 | async-start | bytes 10485760 | tf_op jit(solution)/shard_map/all_gather | solution.py:1684
  7.2 111.5 %slice-start = ((f32[4,2048]{1,0:T(4,128)}), f32[2,2048]{1,0:T(2,128)S(1)}, s32[]{:S(2)}) async-start(f32[4,2048]{1,0:T(4,128)} %gp_ref.1), calls=%async_computation.8 | async-start | bytes 32768 | tf_op jit(solution)/shard_map/slice | solution.py:1704
  7.2 112.1 %copy-start.7 = (f32[4,2048]{1,0:T(4,128)S(1)}, f32[4,2048]{1,0:T(4,128)}, u32[]{:S(2)}) copy-start(f32[4,2048]{1,0:T(4,128)} %gp_ref.1) | copy-start | bytes 98308
  51.2 344.6 %all-gather.6.cloned.1.call-start = ((), (), s32[]{:S(2)}) async-start(), calls=%async_computation.7 | async-start | bytes 4718592 | tf_op jit(solution)/shard_map/all_gather | solution.py:1715
  284.1 111.8 %reduce-scatter.4.cloned.1.call-start = ((), (), s32[]{:S(2)}) async-start(), calls=%async_computation.4 | async-start | bytes 5242880 | tf_op jit(solution)/shard_map/reduce_scatter | solution.py:1690
  335.1 138.4 %reduce-scatter.6.cloned.1.call-start = ((), (), s32[]{:S(2)}) async-start(), calls=%async_computation.5 | async-start | bytes 5242880 | tf_op jit(solution)/shard_map/reduce_scatter | solution.py:1690
  395.2 145.2 %reduce-scatter.8.cloned.1.call-start = ((), (), s32[]{:S(2)}) async-start(), calls=%async_computation.6 | async-start | bytes 5242880 | tf_op jit(solution)/shard_map/reduce_scatter | solution.py:1690
  473.5 66.9 %copy-start = (bf16[8,64,1024]{2,1,0:T(8,128)(2,1)S(1)}, bf16[8,64,1024]{2,1,0:T(8,128)(2,1)}, u32[]{:S(2)}) copy-start(bf16[8,64,1024]{2,1,0:T(8,128)(2,1)} %get-tuple-element.112.gd_ref) | copy-start | bytes 3145732
  473.5 66.9 %copy-start.3 = (bf16[64,2048]{1,0:T(8,128)(2,1)S(1)}, bf16[64,2048]{1,0:T(8,128)(2,1)}, u32[]{:S(2)}) copy-start(bf16[64,2048]{1,0:T(8,128)(2,1)} %get-tuple-element.109.go_ref) | copy-start | bytes 786436
  473.5 66.9 %copy-start.6 = (bf16[512,256]{1,0:T(8,128)(2,1)S(1)}, bf16[512,256]{1,0:T(8,128)(2,1)}, u32[]{:S(2)}) copy-start(bf16[512,256]{1,0:T(8,128)(2,1)} %get-tuple-element.108) | copy-start | bytes 786436
  473.5 66.9 %copy-start.10 = (f32[1,2048]{1,0:T(1,128)S(1)}, f32[1,2048]{1,0:T(1,128)}, u32[]{:S(2)}) copy-start(f32[1,2048]{1,0:T(1,128)} %get-tuple-element.115.ff_gain) | copy-start | bytes 24580
  473.5 66.9 %copy-start.11 = (f32[1,2048]{1,0:T(1,128)S(1)}, f32[1,2048]{1,0:T(1,128)}, u32[]{:S(2)}) copy-start(f32[1,2048]{1,0:T(1,128)} %get-tuple-element.114.attn_gain) | copy-start | bytes 24580
  473.5 66.9 %copy-start.12 = (f32[2,256]{1,0:T(2,128)S(1)}, f32[2,256]{1,0:T(2,128)}, u32[]{:S(2)}) copy-start(f32[2,256]{1,0:T(2,128)} %get-tuple-element.113.qk_gain) | copy-start | bytes 6148
  540.5 1.2 copy-start.1
  541.7 1.2 copy-start.4
  542.9 1.0 copy-start.5
  544.0 46.0 %copy-start.2 = (bf16[8,64,1024]{2,1,0:T(8,128)(2,1)S(1)}, bf16[8,64,1024]{2,1,0:T(8,128)(2,1)}, u32[]{:S(2)}) copy-start(bf16[8,64,1024]{2,1,0:T(8,128)(2,1)} %get-tuple-element.111.gg_ref) | copy-start | bytes 3145732
  544.0 46.0 %copy-start.8 = (f32[4,2048]{1,0:T(4,128)S(1)}, f32[4,2048]{1,0:T(4,128)}, u32[]{:S(2)}) copy-start(f32[4,2048]{1,0:T(4,128)} %gm_ref.1) | copy-start | bytes 98308
  544.0 46.0 %copy-start.9 = (f32[4,2048]{1,0:T(4,128)S(1)}, f32[4,2048]{1,0:T(4,128)}, u32[]{:S(2)}) copy-start(f32[4,2048]{1,0:T(4,128)} %gv_ref.1) | copy-start | bytes 98308
  590.0 15.5 %copy-start.13 = (bf16[128,2048]{1,0:T(8,128)(2,1)S(1)}, bf16[128,2048]{1,0:T(8,128)(2,1)}, u32[]{:S(2)}) copy-start(bf16[128,2048]{1,0:T(8,128)(2,1)} %get-tuple-element.82) | copy-start | bytes 1572868
  590.0 16.3 %copy-start.14 = (bf16[128,2048]{1,0:T(8,128)(2,1)S(1)}, bf16[128,2048]{1,0:T(8,128)(2,1)}, u32[]{:S(2)}) copy-start(bf16[128,2048]{1,0:T(8,128)(2,1)} %get-tuple-element.106) | copy-start | bytes 1572868
Sparse Core Ops, SparseCore 0:
  51.4 99.2 all-gather.3
  284.2 36.6 all-gather.5
  335.2 53.5 reduce-scatter.3
  395.4 65.8 reduce-scatter.5
  464.1 65.7 reduce-scatter.7

commit v12 on v11

--- a/solution.py
+++ b/solution.py
@@ -458,14 +458,14 @@
         def give(part):
             sa[d, :, part] = dot_t(a_ref[rows(1 - parity), :], w_ref[part, :]).astype(BF)
 
-        tiles(out.shape[1], 512, give)
+        tiles(out.shape[1], 2048, give)
         copy = remote(sa.at[d], ra.at[d], s1.at[d], r1.at[d], (dp, partner))
         copy.start()
 
         def keep(part):
             out[:, part] = dot_t(a_ref[rows(parity), :], w_ref[part, :])
 
-        tiles(out.shape[1], 512, keep)
+        tiles(out.shape[1], 2048, keep)
         copy.wait_recv()
 
         def add(part):

time: 623 us -> 631 us (1.013)
  starting transfers between devices: 0.38 us -> 10.9 us
    reduce_scatter x3, starting transfers between devices: 0.3 us -> 10.8 us  [scatter_pairs(): lax.psum_scatter(g.reshape(width, g.shape[3]), 'ctx', scatter_dimension=0...]
  transfers between devices with their start and end apart: 5 -> 5, of which waited for: 0 -> 0; matrix products, arithmetic and copies ran while one was open for 0% -> 0% of each run, Pallas kernels for 62% -> 61%
where the time goes in v12:
time: 631 us; the launch traced here: 622 us
  Pallas kernels  589 us (93%)
  between operations  14.5 us (2%)
  starting transfers between devices  10.9 us (2%)
  local copies, waits for them, and re-layouts  6.33 us (1%)
    pallas_call x1, Pallas kernels, ff_forward(): pl.pallas_call(functools.partial(ff_forward_kernel, n_dp, n), out_shape=(...  108 us
    pallas_call x1, Pallas kernels, attend_back(): pl.pallas_call(functools.partial(attend_back_kernel, n_dp, n), out_shape=...  77 us
    pallas_call x1, Pallas kernels, collect(): pl.pallas_call(functools.partial(collect_kernel, n_dp, n), out_shape=(jax...  67.6 us
    pallas_call x1, Pallas kernels, gather_dp(): pl.pallas_call(functools.partial(gather_dp_kernel, n, n_ctx), out_shape=(...  67.4 us
    pallas_call x1, Pallas kernels, attend(): pl.pallas_call(functools.partial(attend_kernel, n_dp, n), out_shape=(jax....  57.1 us
    pallas_call x1, Pallas kernels, ff_scatter(): pl.pallas_call(functools.partial(ff_scatter_kernel, n_dp, n), out_shape=(...  57 us
    pallas_call x1, Pallas kernels, ff_back(): pl.pallas_call(functools.partial(ff_back_kernel, n_dp), out_shape=(jax.Sh...  50.5 us
    pallas_call x1, Pallas kernels, total_over(): pl.pallas_call(functools.partial(total_kernel, n_dp, n), out_shape=(jax.S...  45.7 us
  transfers between devices with their start and end apart: 5, of which 0 were waited for; matrix products, arithmetic and copies ran while one was open for 0% of the time, Pallas kernels for 61%

profile of v12, /device:TPU:0, one launch (start us, length us, event | category | flops | bytes accessed | tf_op | source)
XLA Modules:
  0.0 621.8 jit_solution(16926645242533546708)
XLA Ops:
  7.2 0.0 all-gather.4.cloned.1.call-start
  7.2 0.0 slice-start
  7.2 0.0 copy-start.7
  7.2 44.0 %start.1 = (bf16[8,64,2048]{2,1,0:T(8,128)(2,1)}, bf16[8,64,768]{2,1,0:T(8,128)(2,1)}, bf16[8,64,256]{2,1,0:T(8,128)(2,1)}, bf16[8,128,2048]{2,1,0:T(8,128)(2,1)}, bf16[8,64,1024]{2,1,0:T(8,128)(2,1)}) custom-call(f32[64,32768]{1,0:T(8,128)} %p_hbm.3, bf16[128,2048]{1,0:T(8,128)(2,1)} %bitcast.36), custom_call_target="tpu_custom_call" | custom-call | bytes 162000000 | tf_op jit(solution)/shard_map/start/pallas_call | solution.py:878
  51.2 0.0 all-gather.4.cloned.1.call-update
  51.2 0.0 all-gather.6.cloned.1.call-start
  51.3 67.4 %gather_dp.1 = (f32[1024,128]{1,0:T(8,128)}, f32[1024,128]{1,0:T(8,128)}, f32[8,1024]{1,0:T(8,128)}, f32[1024,8]{1,0:T(8,128)}, bf16[4,512,768]{2,1,0:T(8,128)(2,1)}) custom-call(s32[8]{0:T(128)} %place_ref.1, s32[1,1024]{1,0:T(1,128)} %doc_ref.1, f32[1,128]{1,0:T(1,128)} %constant.12.clone.freq_ref, bf16[512,768]{1,0:T(8,128)(2,1)} %bitcast.44), custom_call_target="tpu_custom_call" | custom-call | bytes 216000000 | tf_op jit(solution)/shard_map/gather_dp/pallas_call | solution.py:182
  118.7 0.0 slice-done
  118.7 0.6 constant_dynamic-slice_fusion.gain_ref
  119.3 0.0 copy-done.7
  119.3 0.6 fusion
  119.9 57.1 %attend.1 = (f32[128,2048]{1,0:T(8,128)}, f32[128,2048]{1,0:T(8,128)}, bf16[1024,256]{1,0:T(8,128)(2,1)}, bf16[1024,256]{1,0:T(8,128)(2,1)}, bf16[1024,256]{1,0:...) custom-call(bf16[1024,2048]{1,0:T(8,128)(2,1)} %bitcast.28, ...), custom_call_target="tpu_custom_call" | custom-call | bytes 216000000 | tf_op jit(solution)/shard_map/attend/pallas_call | solution.py:1353
  177.0 0.0 all-gather.4.cloned.1.call-done
  177.1 107.7 %ff_forward.1 = (bf16[128,2048]{1,0:T(8,128)(2,1)}, bf16[128,2048]{1,0:T(8,128)(2,1)}, f32[1,2048]{1,0:T(1,128)}, bf16[1024,2048]{1,0:T(8,128)(2,1)}, f32[1024,2...) custom-call(f32[128,2048]{1,0:T(8,128)} %get-tuple-element.78.h_ref, ...), custom_call_target="tpu_custom_call" | custom-call | bytes 324000000 | tf_op jit(solution)/shard_map/ff_forward/pallas_call | solution.py:597
  284.8 0.0 all-gather.6.cloned.1.call-update
  284.8 0.0 reduce-scatter.4.cloned.1.call-start
  284.8 50.5 %ff_back.1 = (bf16[1024,2048]{1,0:T(8,128)(2,1)}, bf16[4,4,128,1024]{3,2,1,0:T(8,128)(2,1)}) custom-call(bf16[128,2048]{1,0:T(8,128)(2,1)} %get-tuple-element.85.dm_ref, bf16[1024,1024]{1,0:T(8,128)(2,1)} %get-tuple-element.86.hid_ref, bf16[2048,1024]{1,0:T(8,128)(2,1)} %get-tuple-element.87.d_hbm, f32[1024,2048]{1,0:T(8,128)} %get-tuple-element.88.pre_hbm), custom_call_target="tpu_custom_call" | custom-call | bytes 162000000 | tf_op jit(solution)/shard_map/ff_back/pallas_call | solution.py:700
  335.4 0.0 reduce-scatter.4.cloned.1.call-update
  335.4 10.7 %reduce-scatter.6.cloned.1.call-start = ((), (), s32[]{:S(2)}) async-start(), calls=%async_computation.5 | async-start | bytes 5242880 | tf_op jit(solution)/shard_map/reduce_scatter | solution.py:1690
  346.1 57.0 %ff_scatter.1 = (f32[128,2048]{1,0:T(8,128)}, bf16[4,4,128,1024]{3,2,1,0:T(8,128)(2,1)}, bf16[4,4,128,1024]{3,2,1,0:T(8,128)(2,1)}) custom-call(bf16[1024,2048]{1,0:T(8,128)(2,1)} %get-tuple-element.89.dgu_hbm, bf16[4,4,128,2048]{3,2,1,0:T(8,128)(2,1)} %bitcast.27, bf16[1024,2048]{1,0:T(8,128)(2,1)} %get-tuple-element.90.all_hbm), custom_call_target="tpu_custom_call" | custom-call | bytes 180000000 | tf_op jit(solution)/shard_map/ff_scatter/pallas_call | solution.py:773
  403.1 0.0 reduce-scatter.6.cloned.1.call-update
  403.2 0.0 reduce-scatter.8.cloned.1.call-start
  403.2 0.5 reduce-scatter.8.cloned.1.call-update
  403.8 0.0 all-gather.6.cloned.1.call-done
  403.8 0.0 reduce-scatter.4.cloned.1.call-done
  403.8 77.0 %attend_back.1 = (f32[128,2048]{1,0:T(8,128)}, f32[1,2048]{1,0:T(1,128)}, bf16[1024,768]{1,0:T(8,128)(2,1)}, f32[2,256]{1,0:T(2,128)}, bf16[2048,512]{1,0:T(8,12...) custom-call(f32[128,2048]{1,0:T(8,128)} %get-tuple-element.91.sum_ref, ...), custom_call_target="tpu_custom_call" | custom-call | bytes 270000000 | tf_op jit(solution)/shard_map/attend_back/pallas_call | solution.py:1602
  480.8 0.0 reduce-scatter.6.cloned.1.call-done
  480.8 0.0 copy-start
  480.8 0.0 copy-start.3
  480.8 0.0 copy-start.6
  480.9 0.0 copy-start.10
  480.9 0.0 copy-start.11
  480.9 0.0 copy-start.12
  480.9 67.6 %collect.1 = (bf16[512,512]{1,0:T(8,128)(2,1)}, bf16[8,64,1024]{2,1,0:T(8,128)(2,1)}, bf16[128,2048]{1,0:T(8,128)(2,1)}) custom-call(bf16[2048,512]{1,0:T(8,128)(2,1)} %get-tuple-element.102.g_ref, bf16[8,64,1024]{2,1,0:T(8,128)(2,1)} %bitcast.42, bf16[1024,768]{1,0:T(8,128)(2,1)} %get-tuple-element.104.a_ref, bf16[2048,768]{1,0:T(8,128)(2,1)} %bitcast.31, ...), custom_call_target="tpu_custom_call" | custom-call | bytes 252000000 | tf_op jit(solution)/shard_map/collect/pallas_call | solution.py:957
  548.4 0.0 reduce-scatter.8.cloned.1.call-done
  548.5 0.0 copy-done
  548.5 0.0 copy-done.3
  548.5 0.0 copy-done.6
  548.5 0.0 copy-done.10
  548.5 0.0 copy-done.11
  548.5 0.0 copy-done.12
  548.5 0.0 copy-start.1
  548.5 1.2 copy-done.1
  549.8 0.0 copy-start.4
  549.8 1.2 copy-done.4
  551.0 0.0 copy-start.5
  551.0 1.0 copy-done.5
  552.0 0.0 copy-start.2
  552.0 0.0 copy-start.8
  552.0 0.0 copy-start.9
  552.0 45.7 %total.1 = (bf16[8,64,768]{2,1,0:T(8,128)(2,1)S(1)}, bf16[8,64,1024]{2,1,0:T(8,128)(2,1)S(1)}, f32[8,2048]{1,0:T(8,128)S(1)}, f32[64,32768]{1,0:T(8,128)S(1)}, f...) custom-call(bf16[8,64,512]{2,1,0:T(8,128)(2,1)S(1)} %bitcast.24, bf16[8,64,256]{2,1,0:T(8,128)(2,1)S(1)} %bitcast.25, ...), custom_call_target="tpu_custom_call" | custom-call | bytes 126000000 | tf_op jit(solution)/shard_map/total/pallas_call | solution.py:1075
  597.7 0.0 copy-done.2
  597.8 0.0 copy-done.8
  597.8 0.0 copy-done.9
  597.8 0.0 copy-start.13
  597.8 0.0 copy-start.14
  597.8 15.5 %adam.1 = (f32[1,1]{1,0:T(1,128)}, f32[4,2048]{1,0:T(4,128)}, f32[4,2048]{1,0:T(4,128)}, f32[4,2048]{1,0:T(4,128)}, f32[64,32768]{1,0:T(8,128)}, /*index=5*/f32[64,32768]{1,0:T(8,128)}, f32[64,32768]{1,0:T(8,128)}) custom-call(f32[8,2048]{1,0:T(8,128)S(1)} %get-tuple-element.116.sum_ref, f32[4,2048]{1,0:T(4,128)S(1)} %copy-done.7, f32[4,2048]{1,0:T(4,128)S(1)} %copy-done.8, ...), custom_call_target="tpu_custom_call" | custom-call | tf_op jit(solution)/shard_map/adam/pallas_call | solution.py:1181
  613.3 0.0 copy-done.13
  613.3 0.8 copy.22
  614.1 0.0 copy-done.14
  614.1 0.8 copy.23
Async XLA Ops:
  7.2 169.9 %all-gather.4.cloned.1.call-start = ((), (), s32[]{:S(2)}) async-start(), calls=%async_computation.3 | async-start | bytes 10485760 | tf_op jit(solution)/shard_map/all_gather | solution.py:1684
  7.2 111.5 %slice-start = ((f32[4,2048]{1,0:T(4,128)}), f32[2,2048]{1,0:T(2,128)S(1)}, s32[]{:S(2)}) async-start(f32[4,2048]{1,0:T(4,128)} %gp_ref.1), calls=%async_computation.8 | async-start | bytes 32768 | tf_op jit(solution)/shard_map/slice | solution.py:1704
  7.2 112.1 %copy-start.7 = (f32[4,2048]{1,0:T(4,128)S(1)}, f32[4,2048]{1,0:T(4,128)}, u32[]{:S(2)}) copy-start(f32[4,2048]{1,0:T(4,128)} %gp_ref.1) | copy-start | bytes 98308
  51.2 352.5 %all-gather.6.cloned.1.call-start = ((), (), s32[]{:S(2)}) async-start(), calls=%async_computation.7 | async-start | bytes 4718592 | tf_op jit(solution)/shard_map/all_gather | solution.py:1715
  284.8 119.0 %reduce-scatter.4.cloned.1.call-start = ((), (), s32[]{:S(2)}) async-start(), calls=%async_computation.4 | async-start | bytes 5242880 | tf_op jit(solution)/shard_map/reduce_scatter | solution.py:1690
  335.4 145.4 %reduce-scatter.6.cloned.1.call-start = ((), (), s32[]{:S(2)}) async-start(), calls=%async_computation.5 | async-start | bytes 5242880 | tf_op jit(solution)/shard_map/reduce_scatter | solution.py:1690
  403.2 145.3 %reduce-scatter.8.cloned.1.call-start = ((), (), s32[]{:S(2)}) async-start(), calls=%async_computation.6 | async-start | bytes 5242880 | tf_op jit(solution)/shard_map/reduce_scatter | solution.py:1690
  480.8 67.7 %copy-start = (bf16[8,64,1024]{2,1,0:T(8,128)(2,1)S(1)}, bf16[8,64,1024]{2,1,0:T(8,128)(2,1)}, u32[]{:S(2)}) copy-start(bf16[8,64,1024]{2,1,0:T(8,128)(2,1)} %get-tuple-element.112.gd_ref) | copy-start | bytes 3145732
  480.8 67.7 %copy-start.3 = (bf16[64,2048]{1,0:T(8,128)(2,1)S(1)}, bf16[64,2048]{1,0:T(8,128)(2,1)}, u32[]{:S(2)}) copy-start(bf16[64,2048]{1,0:T(8,128)(2,1)} %get-tuple-element.109.go_ref) | copy-start | bytes 786436
  480.8 67.7 %copy-start.6 = (bf16[512,256]{1,0:T(8,128)(2,1)S(1)}, bf16[512,256]{1,0:T(8,128)(2,1)}, u32[]{:S(2)}) copy-start(bf16[512,256]{1,0:T(8,128)(2,1)} %get-tuple-element.108) | copy-start | bytes 786436
  480.9 67.7 %copy-start.10 = (f32[1,2048]{1,0:T(1,128)S(1)}, f32[1,2048]{1,0:T(1,128)}, u32[]{:S(2)}) copy-start(f32[1,2048]{1,0:T(1,128)} %get-tuple-element.115.ff_gain) | copy-start | bytes 24580
  480.9 67.7 %copy-start.11 = (f32[1,2048]{1,0:T(1,128)S(1)}, f32[1,2048]{1,0:T(1,128)}, u32[]{:S(2)}) copy-start(f32[1,2048]{1,0:T(1,128)} %get-tuple-element.114.attn_gain) | copy-start | bytes 24580
  480.9 67.7 %copy-start.12 = (f32[2,256]{1,0:T(2,128)S(1)}, f32[2,256]{1,0:T(2,128)}, u32[]{:S(2)}) copy-start(f32[2,256]{1,0:T(2,128)} %get-tuple-element.113.qk_gain) | copy-start | bytes 6148
  548.5 1.2 copy-start.1
  549.8 1.2 copy-start.4
  551.0 1.0 copy-start.5
  552.0 45.7 %copy-start.2 = (bf16[8,64,1024]{2,1,0:T(8,128)(2,1)S(1)}, bf16[8,64,1024]{2,1,0:T(8,128)(2,1)}, u32[]{:S(2)}) copy-start(bf16[8,64,1024]{2,1,0:T(8,128)(2,1)} %get-tuple-element.111.gg_ref) | copy-start | bytes 3145732
  552.0 45.7 %copy-start.8 = (f32[4,2048]{1,0:T(4,128)S(1)}, f32[4,2048]{1,0:T(4,128)}, u32[]{:S(2)}) copy-start(f32[4,2048]{1,0:T(4,128)} %gm_ref.1) | copy-start | bytes 98308
  552.0 45.7 %copy-start.9 = (f32[4,2048]{1,0:T(4,128)S(1)}, f32[4,2048]{1,0:T(4,128)}, u32[]{:S(2)}) copy-start(f32[4,2048]{1,0:T(4,128)} %gv_ref.1) | copy-start | bytes 98308
  597.8 15.5 %copy-start.13 = (bf16[128,2048]{1,0:T(8,128)(2,1)S(1)}, bf16[128,2048]{1,0:T(8,128)(2,1)}, u32[]{:S(2)}) copy-start(bf16[128,2048]{1,0:T(8,128)(2,1)} %get-tuple-element.82) | copy-start | bytes 1572868
  597.8 16.3 %copy-start.14 = (bf16[128,2048]{1,0:T(8,128)(2,1)S(1)}, bf16[128,2048]{1,0:T(8,128)(2,1)}, u32[]{:S(2)}) copy-start(bf16[128,2048]{1,0:T(8,128)(2,1)} %get-tuple-element.106) | copy-start | bytes 1572868
Sparse Core Ops, SparseCore 0:
  51.4 99.2 all-gather.3
  284.9 35.9 all-gather.5
  335.5 53.2 reduce-scatter.3
  403.3 65.6 reduce-scatter.5
  471.7 66.0 reduce-scatter.7
